TPU v7x, 32 devices: a whole 2x2x4 slice. The times are simulated.
32 devices in a mesh: gx: 4 (over x, core), gy: 2 (over y), gz: 4 (over z).
Axes of the slice: x: 2, y: 2, z: 4, core: 2. Of those that a mesh axis runs over, the one named last changes fastest.
Arguments:
- right_side: float32 [3, 512, 1024], P(None, None, ('gx', 'gy', 'gz')), may hold values from -6 to 6
- geometry: float32 [6, 32, 32, 512], P(None, 'gx', 'gy', 'gz'), may hold values from -1.4 to 4, as said below
- viscosity: float32 [32, 32, 512], P('gx', 'gy', 'gz'), may hold values from 0.3 to 3
- eig_low: float32 [1], replicated, may hold values from 0.2 to 2
- eig_high: float32 [1], replicated, may hold values from 8 to 12
- element_slot: int32 [32, 32], P(('gx', 'gy', 'gz')), may hold values from 0 to 31, each once within a row
- dirichlet: int32 [2, 3, 32, 512], P(None, None, 'gy', 'gz'), may hold values 0 or 1
Outputs:
- solution_field: float32 [3, 512, 1024], P(None, None, ('gx', 'gy', 'gz'))
Inputs may be any that keep to these rules, and one draw needn't show every extreme that they name: `element_slot`: each row holds each number from 0 to 31 once. `geometry`: the six entries of each node, in the order xx, yy, zz, xy, xz, yz, form a symmetric positive definite matrix.
All inputs are finite; a program needn't handle non-finite values. No bound on the sum of `dirichlet` on one device may be relied on, other than what follows from the above.
Results may differ from a plain program's by a relative error of at most 0.0003.
Values sent between devices are 32-bit elements; how exact they have to be, the bound alone decides.
No kernel may reach another device: no remote copies, remote signals or barrier semaphores. Data moves between devices by JAX's collectives and lax.ppermute only.
A program may use at most 64 MiB of HBM per device.

v0:
```python
import jax
import jax.numpy as jnp
import numpy as np
from jax import lax
from jax.sharding import PartitionSpec as P

DEGREE = 7
ITERS = 3


helm_coefficient = 10.0


def extended_2(x, sides, width):
    for axis, dim in sides:
        size, length = (lax.axis_size(axis), x.shape[dim])
        up = [(i, (i + 1) % size) for i in range(size - 1)]
        down = [(j, i) for i, j in up]
        last = lax.slice_in_dim(x, length - width, length, axis=dim)
        first = lax.slice_in_dim(x, 0, width, axis=dim)
        before = lax.ppermute(last, axis, up)
        after = lax.ppermute(first, axis, down)
        x = jnp.concatenate([before, x, after], axis=dim)
    return x


def legendre_pair(values, degree):
    previous = 0.0 * values + 1.0
    current = values.copy()
    for order in range(2, degree + 1):
        previous, current = (
            current,
            ((2 * order - 1) * values * current - (order - 1) * previous) / order,
        )
    return (current, previous)


def gll_tables(degree):
    start = np.cos(np.pi * np.arange(degree + 1) / degree)
    nodes_now = start.copy()
    for sweep in range(80):
        top_value, lower_value = legendre_pair(nodes_now, degree)
        nodes_now = nodes_now - (nodes_now * top_value - lower_value) / ((degree + 1) * top_value)
    gll_nodes = nodes_now[::-1].copy()
    gll_nodes[0] = -1.0
    gll_nodes[degree] = 1.0
    legendre_values = legendre_pair(gll_nodes, degree)[0]
    weights = 2.0 / (degree * (degree + 1) * legendre_values**2)
    differences = gll_nodes[:, None] - gll_nodes[None, :] + np.eye(degree + 1)
    derivative = legendre_values[:, None] / legendre_values[None, :] / differences
    derivative = derivative * (1.0 - np.eye(degree + 1))
    derivative[0, 0] = -degree * (degree + 1) / 4.0
    derivative[degree, degree] = degree * (degree + 1) / 4.0
    return (weights, derivative)


def fold_rims(extended, dimension, points):
    length = extended.shape[dimension] - 2
    center = lax.slice_in_dim(extended, 1, length + 1, axis=dimension)
    upper_side = lax.slice_in_dim(extended, 2, length + 2, axis=dimension)
    lower_side = lax.slice_in_dim(extended, 0, length, axis=dimension)
    shape_ones = [1] * extended.ndim
    shape_ones[dimension] = length
    position = (jnp.arange(length, dtype=jnp.int32) % points).reshape(tuple(shape_ones))
    upper_flag = (position == points - 1).astype(extended.dtype)
    lower_flag = (position == 0).astype(extended.dtype)
    return center + upper_flag * upper_side + lower_flag * lower_side


def assemble_lattice(lattice, points):
    extended = extended_2(lattice, (("gx", 1),), 1)
    folded = fold_rims(extended, 1, points)
    extended = extended_2(folded, (("gy", 2),), 1)
    folded = fold_rims(extended, 2, points)
    extended = extended_2(folded, (("gz", 3),), 1)
    return fold_rims(extended, 3, points)


def along_first(lattice, matrix, points):
    blocked = lattice.reshape(
        lattice.shape[0], lattice.shape[1] // points, points, lattice.shape[2], lattice.shape[3]
    )
    result = jnp.einsum("ai,cpiyz->cpayz", matrix, blocked, precision=lax.Precision.HIGHEST)
    return result.reshape(lattice.shape)


def along_second(lattice, matrix, points):
    blocked = lattice.reshape(
        lattice.shape[0], lattice.shape[1], lattice.shape[2] // points, points, lattice.shape[3]
    )
    result = jnp.einsum("ai,cxpiz->cxpaz", matrix, blocked, precision=lax.Precision.HIGHEST)
    return result.reshape(lattice.shape)


def along_third(lattice, block_table):
    return jnp.dot(
        lattice, block_table, precision=lax.Precision.HIGHEST, preferred_element_type=jnp.float32
    )


def helmholtz(lattice, geometry, weighted, mass, tables, points):
    forward, backward, forward_third, backward_third = tables
    slope_first = along_first(lattice, forward, points)
    slope_second = along_second(lattice, forward, points)
    slope_third = along_third(lattice, forward_third)
    flux_first = weighted * (
        geometry[0] * slope_first + geometry[3] * slope_second + geometry[4] * slope_third
    )
    flux_second = weighted * (
        geometry[3] * slope_first + geometry[1] * slope_second + geometry[5] * slope_third
    )
    flux_third = weighted * (
        geometry[4] * slope_first + geometry[5] * slope_second + geometry[2] * slope_third
    )
    return (
        along_first(flux_first, backward, points)
        + along_second(flux_second, backward, points)
        + along_third(flux_third, backward_third)
        + mass * lattice
    )


def shards(right_side, geometry, viscosity, eig_low, eig_high, element_slot, dirichlet):
    points = DEGREE + 1
    weights, derivative = gll_tables(DEGREE)
    components = right_side.shape[0]
    size_first, size_second, size_third = viscosity.shape
    blocks_first = size_first // points
    blocks_second = size_second // points
    blocks_third = size_third // points
    forward = jnp.asarray(derivative, jnp.float32)
    backward = forward.T
    squared = forward * forward
    identity_third = jnp.eye(blocks_third, dtype=jnp.float32)
    tables = (
        forward,
        backward,
        jnp.kron(identity_third, backward),
        jnp.kron(identity_third, forward),
    )
    weight_table = jnp.asarray(weights, jnp.float32)
    diagonal_table = jnp.diagonal(forward)
    quadrature = (
        jnp.tile(weight_table, blocks_first)[:, None, None]
        * jnp.tile(weight_table, blocks_second)[None, :, None]
        * jnp.tile(weight_table, blocks_third)[None, None, :]
    )
    weighted = quadrature * viscosity
    determinant = (
        geometry[0] * (geometry[1] * geometry[2] - geometry[5] * geometry[5])
        - geometry[3] * (geometry[3] * geometry[2] - geometry[5] * geometry[4])
        + geometry[4] * (geometry[3] * geometry[5] - geometry[1] * geometry[4])
    )
    mass = helm_coefficient * quadrature * determinant
    end_first = jnp.tile(diagonal_table, blocks_first)[:, None, None]
    end_second = jnp.tile(diagonal_table, blocks_second)[None, :, None]
    end_third = jnp.tile(diagonal_table, blocks_third)[None, None, :]
    cross = (
        2.0
        * weighted
        * (
            end_first * end_second * geometry[3]
            + end_first * end_third * geometry[4]
            + end_second * end_third * geometry[5]
        )
    )
    diagonal_local = (
        (
            along_first((weighted * geometry[0])[None], squared.T, points)
            + along_second((weighted * geometry[1])[None], squared.T, points)
            + along_third((weighted * geometry[2])[None], jnp.kron(identity_third, squared))
        )[0]
        + cross
        + mass
    )
    slot_bricks = element_slot[0]
    elements = slot_bricks.shape[0]
    slot_index = jnp.arange(elements, dtype=jnp.int32)
    inverse = jnp.sum(
        jnp.where(slot_bricks[:, None] == slot_index[None, :], slot_index[:, None], 0), axis=0
    )
    bricks = jnp.take(right_side, inverse, axis=2)
    rhs_lattice = (
        bricks.reshape(
            components, points, points, points, blocks_first, blocks_second, blocks_third
        )
        .transpose(0, 4, 1, 5, 2, 6, 3)
        .reshape(components, size_first, size_second, size_third)
    )
    row_index = lax.axis_index("gx")
    low_plane = jnp.where(row_index == 0, dirichlet[0], 0).astype(jnp.float32)
    high_plane = jnp.where(row_index == lax.axis_size("gx") - 1, dirichlet[1], 0).astype(
        jnp.float32
    )
    middle = jnp.zeros((components, size_first - 2, size_second, size_third), jnp.float32)
    indicator = jnp.concatenate([low_plane[:, None], middle, high_plane[:, None]], axis=1)
    stacked = jnp.concatenate([rhs_lattice, diagonal_local[None], indicator], axis=0)
    assembled = assemble_lattice(stacked, points)
    keep = jnp.where(assembled[components + 1 :] > 0.5, 0.0, 1.0).astype(jnp.float32)
    residual = keep * assembled[:components]
    scaling = keep / assembled[components][None]
    midpoint = (eig_high[0] + eig_low[0]) * 0.5
    halfwidth = (eig_high[0] - eig_low[0]) * 0.5
    ratio_start = midpoint / halfwidth
    damping = 1.0 / ratio_start
    direction = scaling * residual / midpoint
    solution = jnp.zeros_like(residual)
    for iteration in range(ITERS):
        solution = solution + direction
        if iteration < ITERS - 1:
            image = assemble_lattice(
                helmholtz(direction, geometry, weighted, mass, tables, points), points
            )
            residual = residual - keep * image
            damping_next = 1.0 / (2.0 * ratio_start - damping)
            direction = damping_next * damping * direction + 2.0 * damping_next / halfwidth * (
                scaling * residual
            )
            damping = damping_next
    back_bricks = (
        solution.reshape(
            components, blocks_first, points, blocks_second, points, blocks_third, points
        )
        .transpose(0, 2, 4, 6, 1, 3, 5)
        .reshape(components, points * points * points, elements)
    )
    return jnp.take(back_bricks, slot_bricks, axis=2)


def solution(mesh):
    return jax.shard_map(
        shards,
        mesh=mesh,
        in_specs=(
            P(None, None, ("gx", "gy", "gz")),
            P(None, "gx", "gy", "gz"),
            P("gx", "gy", "gz"),
            P(),
            P(),
            P(("gx", "gy", "gz"), None),
            P(None, None, "gy", "gz"),
        ),
        out_specs=P(None, None, ("gx", "gy", "gz")),
        check_vma=False,
    )
```

profile of v0, /device:TPU:30, one launch (start us, length us, event | category | flops | bytes accessed | tf_op | source)
XLA Modules:
  0.0 120.3 jit_solution(1742536167034099552)
XLA Ops:
  6.5 1.7 %fusion.112 = (f32[1,8,16,128]{3,2,1,0:T(8,128)}, f32[1,8,16,128]{3,2,1,0:T(8,128)}, f32[1,8,16,128]{3,2,1,0:T(8,128)}, f32[1,8,16,128]{3,2,1,0:T(8,128)}, f32[1...) fusion(f32[6,8,16,128]{3,2,1,0:T(8,128)} %param.12), kind=kLoop, calls=%fused_computation.201 | loop fusion | bytes 786432 | tf_op jit(solution)/shard_map/slice | solution.py:164
  11.9 2.1 %reshape.373 = f32[3,8,8,8,1,2,16]{6,5,3,2,1,0,4:T(2,128)} reshape(f32[3,512,32]{2,1,0:T(8,128)S(1)} %copy.84) | data formatting | bytes 393216 | tf_op jit(solution)/shard_map/reshape | solution.py:184
  14.0 2.9 %copy.139 = f32[3,1,8,2,8,16,8]{6,5,2,4,3,0,1:T(8,128)S(1)} copy(f32[3,1,8,2,8,16,8]{5,3,6,4,2,0,1:T(2,128)} %bitcast.171) | data formatting | bytes 393216 | tf_op jit(solution)/shard_map/reshape | solution.py:188
  16.8 2.1 %reshape.427 = f32[3,8,16,128]{3,1,2,0:T(8,128)} reshape(f32[3,1,8,2,8,16,8]{6,5,2,4,3,0,1:T(8,128)S(1)} %copy.139) | data formatting | bytes 393216 | tf_op jit(solution)/shard_map/reshape | solution.py:188
  19.1 2.3 %broadcast_multiply_fusion = (f32[16,8,16,8]{3,2,1,0:T(8,128)S(1)}, f32[16,8,16,8]{3,2,1,0:T(8,128)S(1)}, f32[16,8,16,8]{3,2,1,0:T(8,128)}) fusion(f32[8,8]{1,0:T(8,128)S(1)} %copy-done.1, f32[16,16]{1,0:T(8,128)} %fusion.106, f32[8,8]{1,0:T(8,128)} %constant.105, f32[8,8]{1,0:T(8,128)} %constant.121), kind=kLoop, calls=%fused_computation.24 | loop fusion | flops 49152 | bytes 198400 | tf_op jit(solution)/shard_map/jit(kron)/mul | solution.py:139
  21.4 1.6 %reshape.422 = f32[128,128,1]{1,0,2:T(8,128)S(1)} reshape(f32[16,8,16,8]{3,2,1,0:T(8,128)} %get-tuple-element.47) | data formatting | bytes 131072 | tf_op jit(solution)/shard_map/jit(kron)/mul | solution.py:171
  23.8 1.9 %collective-permute-start = (f32[7,1,16,128]{3,1,2,0:T(1,128)S(1)}, f32[7,1,16,128]{3,1,2,0:T(1,128)S(1)}, u32[]{:S(2)}, u32[]{:S(2)}) collective-permute-start(f32[7,1,16,128]{3,1,2,0:T(1,128)S(1)} %get-tuple-element.16), channel_id=1, source_target_pairs={{8,0},{16,8},{24,16},{9,1},{17,9},{25,17},{10,2},{18,10},{26,18},{... | collective-permute-start | bytes 172040 | tf_op jit(solution)/shard_map/ppermute | solution.py:22
  25.8 2.4 %collective-permute-start.1 = (f32[7,1,16,128]{3,1,2,0:T(1,128)S(1)}, f32[7,1,16,128]{3,1,2,0:T(1,128)S(1)}, u32[]{:S(2)}, u32[]{:S(2)}) collective-permute-start(f32[7,1,16,128]{3,1,2,0:T(1,128)S(1)} %get-tuple-element.17), channel_id=1, source_target_pairs={{0,8},{8,16},{16,24},{1,9},{9,17},{17,25},{2,10},{10,18},{18,26},{... | collective-permute-start | bytes 172040 | tf_op jit(solution)/shard_map/ppermute | solution.py:21
  28.2 1.8 %copy_bitcast_fusion.3 = (f32[8,16,128]{2,0,1:T(8,128)}, f32[8,16,128]{2,0,1:T(8,128)}, f32[8,16,128]{2,0,1:T(8,128)}, f32[8,16,128]{2,0,1:T(8,128)}, f32[8,16,1...) fusion(f32[1,8,16,128]{3,2,1,0:T(8,128)} %get-tuple-element.21, ...), kind=kLoop, calls=%fused_computation.168 | loop fusion | flops 278528 | bytes 852992 | tf_op jit(solution)/shard_map/squeeze | solution.py:171
  31.6 2.4 %collective-permute-start.2 = (f32[7,8,1,128]{3,1,2,0:T(8,128)S(1)}, f32[7,8,1,128]{3,1,2,0:T(8,128)S(1)}, u32[]{:S(2)}, u32[]{:S(2)}) collective-permute-start(f32[7,8,1,128]{3,1,2,0:T(8,128)S(1)} %get-tuple-element.14), channel_id=1, source_target_pairs={{4,0},{5,1},{6,2},{7,3},{12,8},{13,9},{14,10},{15,11},{20,16},{21,... | collective-permute-start | bytes 86024 | tf_op jit(solution)/shard_map/ppermute | solution.py:22
  35.6 4.2 %collective-permute-done.3 = f32[7,8,1,128]{3,1,2,0:T(8,128)S(1)} collective-permute-done((f32[7,8,1,128]{3,1,2,0:T(8,128)S(1)}, f32[7,8,1,128]{3,1,2,0:T(8,128)S(1)}, u32[]{:S(2)}, u32[]{:S(2)}) %collective-permute-start.3) | collective-permute-done | bytes 28704 | tf_op jit(solution)/shard_map/ppermute | solution.py:21
  41.1 3.3 %collective-permute-start.4 = (f32[7,8,16,1]{3,1,2,0:T(8,128)}, f32[7,8,16,1]{3,1,2,0:T(8,128)}, u32[]{:S(2)}, u32[]{:S(2)}) collective-permute-start(f32[7,8,16,1]{3,1,2,0:T(8,128)} %get-tuple-element.12), channel_id=1, source_target_pairs={{1,0},{2,1},{3,2},{5,4},{6,5},{7,6},{9,8},{10,9},{11,10},{13,12},{... | collective-permute-start | bytes 10760 | tf_op jit(solution)/shard_map/ppermute | solution.py:22
  47.9 2.6 %collective-permute-done.4 = f32[7,8,16,1]{3,1,2,0:T(8,128)} collective-permute-done((f32[7,8,16,1]{3,1,2,0:T(8,128)}, f32[7,8,16,1]{3,1,2,0:T(8,128)}, u32[]{:S(2)}, u32[]{:S(2)}) %collective-permute-start.4) | collective-permute-done | bytes 3616 | tf_op jit(solution)/shard_map/ppermute | solution.py:22
  50.5 4.9 %collective-permute-done.5 = f32[7,8,16,1]{3,1,2,0:T(8,128)} collective-permute-done((f32[7,8,16,1]{3,1,2,0:T(8,128)}, f32[7,8,16,1]{3,1,2,0:T(8,128)}, u32[]{:S(2)}, u32[]{:S(2)}) %collective-permute-start.5) | collective-permute-done | bytes 3616 | tf_op jit(solution)/shard_map/ppermute | solution.py:21
  55.4 1.6 %fusion.9 = f32[7,8,16,128]{3,1,2,0:T(8,128)S(1)} fusion(f32[7,8,16,128]{3,1,2,0:T(8,128)S(1)} %fusion.13, f32[7,8,16,1]{3,1,2,0:T(8,128)} %collective-permute-done.5, f32[7,8,16,1]{3,1,2,0:T(8,128)} %collective-permute-done.4, f32[128]{0:T(128)S(1)} %get-tuple-element.58, f32[128]{0:T(128)S(1)} %get-tuple-element.59), kind=kLoop, calls=%fused_computation.29 | loop fusion | flops 688128 | bytes 925696 | tf_op jit(solution)/shard_map/add | solution.py:67
  59.3 3.0 %collective-permute-start.6 = (f32[3,1,16,128]{3,1,2,0:T(1,128)S(1)}, f32[3,1,16,128]{3,1,2,0:T(1,128)S(1)}, u32[]{:S(2)}, u32[]{:S(2)}) collective-permute-start(f32[3,1,16,128]{3,1,2,0:T(1,128)S(1)} %get-tuple-element.34), channel_id=1, source_target_pairs={{8,0},{16,8},{24,16},{9,1},{17,9},{25,17},{10,2},{18,10},{26,18},{... | collective-permute-start | bytes 73736 | tf_op jit(solution)/shard_map/ppermute | solution.py:22
  62.3 1.9 %collective-permute-start.7 = (f32[3,1,16,128]{3,1,2,0:T(1,128)S(1)}, f32[3,1,16,128]{3,1,2,0:T(1,128)S(1)}, u32[]{:S(2)}, u32[]{:S(2)}) collective-permute-start(f32[3,1,16,128]{3,1,2,0:T(1,128)S(1)} %get-tuple-element.35), channel_id=1, source_target_pairs={{0,8},{8,16},{16,24},{1,9},{9,17},{17,25},{2,10},{10,18},{18,26},{... | collective-permute-start | bytes 73736 | tf_op jit(solution)/shard_map/ppermute | solution.py:21
  64.3 3.2 %collective-permute-done.7 = f32[3,1,16,128]{3,1,2,0:T(1,128)S(1)} collective-permute-done((f32[3,1,16,128]{3,1,2,0:T(1,128)S(1)}, f32[3,1,16,128]{3,1,2,0:T(1,128)S(1)}, u32[]{:S(2)}, u32[]{:S(2)}) %collective-permute-start.7) | collective-permute-done | bytes 24608 | tf_op jit(solution)/shard_map/ppermute | solution.py:21
  70.5 4.2 %collective-permute-done.9 = f32[3,8,1,128]{3,1,2,0:T(8,128)S(1)} collective-permute-done((f32[3,8,1,128]{3,1,2,0:T(8,128)S(1)}, f32[3,8,1,128]{3,1,2,0:T(8,128)S(1)}, u32[]{:S(2)}, u32[]{:S(2)}) %collective-permute-start.9) | collective-permute-done | bytes 12320 | tf_op jit(solution)/shard_map/ppermute | solution.py:21
  74.9 1.6 %collective-permute-start.10 = (f32[3,8,16,1]{3,1,2,0:T(8,128)S(1)}, f32[3,8,16,1]{3,1,2,0:T(8,128)S(1)}, u32[]{:S(2)}, u32[]{:S(2)}) collective-permute-start(f32[3,8,16,1]{3,1,2,0:T(8,128)S(1)} %get-tuple-element.30), channel_id=1, source_target_pairs={{1,0},{2,1},{3,2},{5,4},{6,5},{7,6},{9,8},{10,9},{11,10},{13,12},{... | collective-permute-start | bytes 4616 | tf_op jit(solution)/shard_map/ppermute | solution.py:22
  79.7 4.4 %collective-permute-done.11 = f32[3,8,16,1]{3,1,2,0:T(8,128)S(1)} collective-permute-done((f32[3,8,16,1]{3,1,2,0:T(8,128)S(1)}, f32[3,8,16,1]{3,1,2,0:T(8,128)S(1)}, u32[]{:S(2)}, u32[]{:S(2)}) %collective-permute-start.11) | collective-permute-done | bytes 1568 | tf_op jit(solution)/shard_map/ppermute | solution.py:21
  86.5 1.9 %collective-permute-start.12 = (f32[3,1,16,128]{3,1,2,0:T(1,128)S(1)}, f32[3,1,16,128]{3,1,2,0:T(1,128)S(1)}, u32[]{:S(2)}, u32[]{:S(2)}) collective-permute-start(f32[3,1,16,128]{3,1,2,0:T(1,128)S(1)} %get-tuple-element.28), channel_id=1, source_target_pairs={{8,0},{16,8},{24,16},{9,1},{17,9},{25,17},{10,2},{18,10},{26,18},{... | collective-permute-start | bytes 73736 | tf_op jit(solution)/shard_map/ppermute | solution.py:22
  88.5 2.4 %collective-permute-start.13 = (f32[3,1,16,128]{3,1,2,0:T(1,128)S(1)}, f32[3,1,16,128]{3,1,2,0:T(1,128)S(1)}, u32[]{:S(2)}, u32[]{:S(2)}) collective-permute-start(f32[3,1,16,128]{3,1,2,0:T(1,128)S(1)} %get-tuple-element.29), channel_id=1, source_target_pairs={{0,8},{8,16},{16,24},{1,9},{9,17},{17,25},{2,10},{10,18},{18,26},{... | collective-permute-start | bytes 73736 | tf_op jit(solution)/shard_map/ppermute | solution.py:21
  90.9 2.7 %collective-permute-done.13 = f32[3,1,16,128]{3,1,2,0:T(1,128)S(1)} collective-permute-done((f32[3,1,16,128]{3,1,2,0:T(1,128)S(1)}, f32[3,1,16,128]{3,1,2,0:T(1,128)S(1)}, u32[]{:S(2)}, u32[]{:S(2)}) %collective-permute-start.13) | collective-permute-done | bytes 24608 | tf_op jit(solution)/shard_map/ppermute | solution.py:21
  93.7 1.6 %collective-permute-start.14 = (f32[3,8,1,128]{3,1,2,0:T(8,128)S(1)}, f32[3,8,1,128]{3,1,2,0:T(8,128)S(1)}, u32[]{:S(2)}, u32[]{:S(2)}) collective-permute-start(f32[3,8,1,128]{3,1,2,0:T(8,128)S(1)} %get-tuple-element.26), channel_id=1, source_target_pairs={{4,0},{5,1},{6,2},{7,3},{12,8},{13,9},{14,10},{15,11},{20,16},{21,... | collective-permute-start | bytes 36872 | tf_op jit(solution)/shard_map/ppermute | solution.py:22
  96.8 4.2 %collective-permute-done.15 = f32[3,8,1,128]{3,1,2,0:T(8,128)S(1)} collective-permute-done((f32[3,8,1,128]{3,1,2,0:T(8,128)S(1)}, f32[3,8,1,128]{3,1,2,0:T(8,128)S(1)}, u32[]{:S(2)}, u32[]{:S(2)}) %collective-permute-start.15) | collective-permute-done | bytes 12320 | tf_op jit(solution)/shard_map/ppermute | solution.py:21
  101.2 2.9 %collective-permute-start.16 = (f32[3,8,16,1]{3,1,2,0:T(8,128)S(1)}, f32[3,8,16,1]{3,1,2,0:T(8,128)S(1)}, u32[]{:S(2)}, u32[]{:S(2)}) collective-permute-start(f32[3,8,16,1]{3,1,2,0:T(8,128)S(1)} %get-tuple-element.24), channel_id=1, source_target_pairs={{1,0},{2,1},{3,2},{5,4},{6,5},{7,6},{9,8},{10,9},{11,10},{13,12},{... | collective-permute-start | bytes 4616 | tf_op jit(solution)/shard_map/ppermute | solution.py:22
  105.5 1.8 %collective-permute-done.16 = f32[3,8,16,1]{3,1,2,0:T(8,128)S(1)} collective-permute-done((f32[3,8,16,1]{3,1,2,0:T(8,128)S(1)}, f32[3,8,16,1]{3,1,2,0:T(8,128)S(1)}, u32[]{:S(2)}, u32[]{:S(2)}) %collective-permute-start.16) | collective-permute-done | bytes 1568 | tf_op jit(solution)/shard_map/ppermute | solution.py:22
  107.2 4.4 %collective-permute-done.17 = f32[3,8,16,1]{3,1,2,0:T(8,128)S(1)} collective-permute-done((f32[3,8,16,1]{3,1,2,0:T(8,128)S(1)}, f32[3,8,16,1]{3,1,2,0:T(8,128)S(1)}, u32[]{:S(2)}, u32[]{:S(2)}) %collective-permute-start.17) | collective-permute-done | bytes 1568 | tf_op jit(solution)/shard_map/ppermute | solution.py:21
  111.9 1.7 %reshape.390 = f32[3,1,8,2,8,16,8]{6,5,4,3,2,0,1:T(8,128)S(1)} reshape(f32[3,8,16,128]{3,2,1,0:T(8,128)S(1)} %copy.120) | data formatting | bytes 393216 | tf_op jit(solution)/shard_map/reshape | solution.py:221
  113.6 2.4 %copy.121 = f32[3,8,8,8,1,2,16]{6,5,3,2,1,0,4:T(2,128)} copy(f32[3,8,8,8,1,2,16]{3,6,2,5,1,0,4:T(8,128)S(1)} %bitcast.168) | data formatting | bytes 393216 | tf_op jit(solution)/shard_map/transpose | solution.py:224
  116.0 2.3 %reshape.391 = f32[3,512,32]{2,1,0:T(8,128)S(1)} reshape(f32[3,8,8,8,1,2,16]{6,5,3,2,1,0,4:T(2,128)} %copy.121) | data formatting | bytes 393216 | tf_op jit(solution)/shard_map/reshape | solution.py:225
  (136 shorter events, 33.4 us)
Async XLA Ops:
  0.0 10.7 %copy-start = (f32[3,512,32]{1,2,0:T(8,128)S(1)}, f32[3,512,32]{1,2,0:T(8,128)}, u32[]{:S(2)}) copy-start(f32[3,512,32]{1,2,0:T(8,128)} %param.11) | copy-start | bytes 589828
  5.2 4.9 %copy-start.18 = (f32[128]{0:T(128)}, f32[128]{0:T(128)S(1)}, u32[]{:S(2)}) copy-start(f32[128]{0:T(128)S(1)} %mul.690) | copy-start | bytes 1540
  8.2 15.1 %copy-start.3 = (f32[1,8,16,128]{3,2,1,0:T(8,128)}, f32[1,8,16,128]{3,2,1,0:T(8,128)S(1)}, u32[]{:S(2)}) copy-start(f32[1,8,16,128]{3,2,1,0:T(8,128)S(1)} %get-tuple-element.23) | copy-start | bytes 196612
  14.0 5.0 %copy-start.1 = (f32[8,8]{1,0:T(8,128)S(1)}, f32[8,8]{1,0:T(8,128)}, u32[]{:S(2)}) copy-start(f32[8,8]{1,0:T(8,128)} %constant.101.clone) | copy-start | bytes 772
  19.0 4.3 %copy-start.8 = (f32[1,8,16,128]{3,2,1,0:T(8,128)S(1)}, f32[1,8,16,128]{3,2,1,0:T(8,128)}, u32[]{:S(2)}) copy-start(f32[1,8,16,128]{3,2,1,0:T(8,128)} %get-tuple-element.18) | copy-start | bytes 196612
  19.0 4.3 %copy-start.9 = (f32[1,8,16,128]{3,2,1,0:T(8,128)S(1)}, f32[1,8,16,128]{3,2,1,0:T(8,128)}, u32[]{:S(2)}) copy-start(f32[1,8,16,128]{3,2,1,0:T(8,128)} %get-tuple-element.19) | copy-start | bytes 196612
  19.0 4.3 %copy-start.10 = (f32[1,8,16,128]{3,2,1,0:T(8,128)S(1)}, f32[1,8,16,128]{3,2,1,0:T(8,128)}, u32[]{:S(2)}) copy-start(f32[1,8,16,128]{3,2,1,0:T(8,128)} %get-tuple-element.20) | copy-start | bytes 196612
  19.0 4.3 %copy-start.11 = (f32[1,8,16,128]{3,2,1,0:T(8,128)S(1)}, f32[1,8,16,128]{3,2,1,0:T(8,128)}, u32[]{:S(2)}) copy-start(f32[1,8,16,128]{3,2,1,0:T(8,128)} %get-tuple-element.21) | copy-start | bytes 196612
  19.1 4.6 %copy-start.2 = (f32[3,8,16,128]{3,1,2,0:T(8,128)S(1)}, f32[3,8,16,128]{3,1,2,0:T(8,128)}, u32[]{:S(2)}) copy-start(f32[3,8,16,128]{3,1,2,0:T(8,128)} %reshape.427) | copy-start | bytes 589828
  23.8 6.1 %collective-permute-start = (f32[7,1,16,128]{3,1,2,0:T(1,128)S(1)}, f32[7,1,16,128]{3,1,2,0:T(1,128)S(1)}, u32[]{:S(2)}, u32[]{:S(2)}) collective-permute-start(f32[7,1,16,128]{3,1,2,0:T(1,128)S(1)} %get-tuple-element.16), channel_id=1, source_target_pairs={{8,0},{16,8},{24,16},{9,1},{17,9},{25,17},{10,2},{18,10},{26,18},{... | collective-permute-start | bytes 172040 | tf_op jit(solution)/shard_map/ppermute | solution.py:22
  25.8 5.5 %collective-permute-start.1 = (f32[7,1,16,128]{3,1,2,0:T(1,128)S(1)}, f32[7,1,16,128]{3,1,2,0:T(1,128)S(1)}, u32[]{:S(2)}, u32[]{:S(2)}) collective-permute-start(f32[7,1,16,128]{3,1,2,0:T(1,128)S(1)} %get-tuple-element.17), channel_id=1, source_target_pairs={{0,8},{8,16},{16,24},{1,9},{9,17},{17,25},{2,10},{10,18},{18,26},{... | collective-permute-start | bytes 172040 | tf_op jit(solution)/shard_map/ppermute | solution.py:21
  31.6 4.0 %collective-permute-start.2 = (f32[7,8,1,128]{3,1,2,0:T(8,128)S(1)}, f32[7,8,1,128]{3,1,2,0:T(8,128)S(1)}, u32[]{:S(2)}, u32[]{:S(2)}) collective-permute-start(f32[7,8,1,128]{3,1,2,0:T(8,128)S(1)} %get-tuple-element.14), channel_id=1, source_target_pairs={{4,0},{5,1},{6,2},{7,3},{12,8},{13,9},{14,10},{15,11},{20,16},{21,... | collective-permute-start | bytes 86024 | tf_op jit(solution)/shard_map/ppermute | solution.py:22
  34.0 5.8 %collective-permute-start.3 = (f32[7,8,1,128]{3,1,2,0:T(8,128)S(1)}, f32[7,8,1,128]{3,1,2,0:T(8,128)S(1)}, u32[]{:S(2)}, u32[]{:S(2)}) collective-permute-start(f32[7,8,1,128]{3,1,2,0:T(8,128)S(1)} %get-tuple-element.15), channel_id=1, source_target_pairs={{0,4},{1,5},{2,6},{3,7},{8,12},{9,13},{10,14},{11,15},{16,20},{17,... | collective-permute-start | bytes 86024 | tf_op jit(solution)/shard_map/ppermute | solution.py:21
  40.0 17.1 %copy-start.13 = (f32[8,8,1,1]{1,0,3,2:T(8,128)S(1)}, f32[8,8,1,1]{1,0,3,2:T(8,128)}, u32[]{:S(2)}) copy-start(f32[8,8,1,1]{1,0,3,2:T(8,128)} %constant.122) | copy-start | bytes 772
  40.0 17.4 %copy-start.14 = (f32[8,8,1,1,1]{1,0,4,3,2:T(8,128)S(1)}, f32[8,8,1,1,1]{1,0,4,3,2:T(8,128)}, u32[]{:S(2)}) copy-start(f32[8,8,1,1,1]{1,0,4,3,2:T(8,128)} %constant.123) | copy-start | bytes 772
  41.0 16.7 %copy-start.7 = (f32[8,16,128]{2,0,1:T(8,128)S(1)}, f32[8,16,128]{2,0,1:T(8,128)}, u32[]{:S(2)}) copy-start(f32[8,16,128]{2,0,1:T(8,128)} %get-tuple-element.39) | copy-start | bytes 196612
  41.1 9.4 %collective-permute-start.4 = (f32[7,8,16,1]{3,1,2,0:T(8,128)}, f32[7,8,16,1]{3,1,2,0:T(8,128)}, u32[]{:S(2)}, u32[]{:S(2)}) collective-permute-start(f32[7,8,16,1]{3,1,2,0:T(8,128)} %get-tuple-element.12), channel_id=1, source_target_pairs={{1,0},{2,1},{3,2},{5,4},{6,5},{7,6},{9,8},{10,9},{11,10},{13,12},{... | collective-permute-start | bytes 10760 | tf_op jit(solution)/shard_map/ppermute | solution.py:22
  44.3 11.0 %collective-permute-start.5 = (f32[7,8,16,1]{3,1,2,0:T(8,128)}, f32[7,8,16,1]{3,1,2,0:T(8,128)}, u32[]{:S(2)}, u32[]{:S(2)}) collective-permute-start(f32[7,8,16,1]{3,1,2,0:T(8,128)} %get-tuple-element.13), channel_id=1, source_target_pairs={{0,1},{1,2},{2,3},{4,5},{5,6},{6,7},{8,9},{9,10},{10,11},{12,13},{... | collective-permute-start | bytes 10760 | tf_op jit(solution)/shard_map/ppermute | solution.py:21
  47.9 10.6 %copy-start.6 = (f32[8,16,128]{2,0,1:T(8,128)S(1)}, f32[8,16,128]{2,0,1:T(8,128)}, u32[]{:S(2)}) copy-start(f32[8,16,128]{2,0,1:T(8,128)} %get-tuple-element.38) | copy-start | bytes 196612
  59.3 4.9 %collective-permute-start.6 = (f32[3,1,16,128]{3,1,2,0:T(1,128)S(1)}, f32[3,1,16,128]{3,1,2,0:T(1,128)S(1)}, u32[]{:S(2)}, u32[]{:S(2)}) collective-permute-start(f32[3,1,16,128]{3,1,2,0:T(1,128)S(1)} %get-tuple-element.34), channel_id=1, source_target_pairs={{8,0},{16,8},{24,16},{9,1},{17,9},{25,17},{10,2},{18,10},{26,18},{... | collective-permute-start | bytes 73736 | tf_op jit(solution)/shard_map/ppermute | solution.py:22
  62.3 5.1 %collective-permute-start.7 = (f32[3,1,16,128]{3,1,2,0:T(1,128)S(1)}, f32[3,1,16,128]{3,1,2,0:T(1,128)S(1)}, u32[]{:S(2)}, u32[]{:S(2)}) collective-permute-start(f32[3,1,16,128]{3,1,2,0:T(1,128)S(1)} %get-tuple-element.35), channel_id=1, source_target_pairs={{0,8},{8,16},{16,24},{1,9},{9,17},{17,25},{2,10},{10,18},{18,26},{... | collective-permute-start | bytes 73736 | tf_op jit(solution)/shard_map/ppermute | solution.py:21
  67.6 2.9 %collective-permute-start.8 = (f32[3,8,1,128]{3,1,2,0:T(8,128)S(1)}, f32[3,8,1,128]{3,1,2,0:T(8,128)S(1)}, u32[]{:S(2)}, u32[]{:S(2)}) collective-permute-start(f32[3,8,1,128]{3,1,2,0:T(8,128)S(1)} %get-tuple-element.32), channel_id=1, source_target_pairs={{4,0},{5,1},{6,2},{7,3},{12,8},{13,9},{14,10},{15,11},{20,16},{21,... | collective-permute-start | bytes 36872 | tf_op jit(solution)/shard_map/ppermute | solution.py:22
  69.1 5.6 %collective-permute-start.9 = (f32[3,8,1,128]{3,1,2,0:T(8,128)S(1)}, f32[3,8,1,128]{3,1,2,0:T(8,128)S(1)}, u32[]{:S(2)}, u32[]{:S(2)}) collective-permute-start(f32[3,8,1,128]{3,1,2,0:T(8,128)S(1)} %get-tuple-element.33), channel_id=1, source_target_pairs={{0,4},{1,5},{2,6},{3,7},{8,12},{9,13},{10,14},{11,15},{16,20},{17,... | collective-permute-start | bytes 36872 | tf_op jit(solution)/shard_map/ppermute | solution.py:21
  74.9 4.8 %collective-permute-start.10 = (f32[3,8,16,1]{3,1,2,0:T(8,128)S(1)}, f32[3,8,16,1]{3,1,2,0:T(8,128)S(1)}, u32[]{:S(2)}, u32[]{:S(2)}) collective-permute-start(f32[3,8,16,1]{3,1,2,0:T(8,128)S(1)} %get-tuple-element.30), channel_id=1, source_target_pairs={{1,0},{2,1},{3,2},{5,4},{6,5},{7,6},{9,8},{10,9},{11,10},{13,12},{... | collective-permute-start | bytes 4616 | tf_op jit(solution)/shard_map/ppermute | solution.py:22
  76.5 7.6 %collective-permute-start.11 = (f32[3,8,16,1]{3,1,2,0:T(8,128)S(1)}, f32[3,8,16,1]{3,1,2,0:T(8,128)S(1)}, u32[]{:S(2)}, u32[]{:S(2)}) collective-permute-start(f32[3,8,16,1]{3,1,2,0:T(8,128)S(1)} %get-tuple-element.31), channel_id=1, source_target_pairs={{0,1},{1,2},{2,3},{4,5},{5,6},{6,7},{8,9},{9,10},{10,11},{12,13},{... | collective-permute-start | bytes 4616 | tf_op jit(solution)/shard_map/ppermute | solution.py:21
  84.3 6.6 %copy-start.21 = (s32[1,32]{1,0:T(1,128)S(1)}, s32[1,32]{1,0:T(1,128)}, u32[]{:S(2)}) copy-start(s32[1,32]{1,0:T(1,128)} %param.16) | copy-start | bytes 388
  86.5 4.4 %collective-permute-start.12 = (f32[3,1,16,128]{3,1,2,0:T(1,128)S(1)}, f32[3,1,16,128]{3,1,2,0:T(1,128)S(1)}, u32[]{:S(2)}, u32[]{:S(2)}) collective-permute-start(f32[3,1,16,128]{3,1,2,0:T(1,128)S(1)} %get-tuple-element.28), channel_id=1, source_target_pairs={{8,0},{16,8},{24,16},{9,1},{17,9},{25,17},{10,2},{18,10},{26,18},{... | collective-permute-start | bytes 73736 | tf_op jit(solution)/shard_map/ppermute | solution.py:22
  88.5 5.1 %collective-permute-start.13 = (f32[3,1,16,128]{3,1,2,0:T(1,128)S(1)}, f32[3,1,16,128]{3,1,2,0:T(1,128)S(1)}, u32[]{:S(2)}, u32[]{:S(2)}) collective-permute-start(f32[3,1,16,128]{3,1,2,0:T(1,128)S(1)} %get-tuple-element.29), channel_id=1, source_target_pairs={{0,8},{8,16},{16,24},{1,9},{9,17},{17,25},{2,10},{10,18},{18,26},{... | collective-permute-start | bytes 73736 | tf_op jit(solution)/shard_map/ppermute | solution.py:21
  93.7 3.0 %collective-permute-start.14 = (f32[3,8,1,128]{3,1,2,0:T(8,128)S(1)}, f32[3,8,1,128]{3,1,2,0:T(8,128)S(1)}, u32[]{:S(2)}, u32[]{:S(2)}) collective-permute-start(f32[3,8,1,128]{3,1,2,0:T(8,128)S(1)} %get-tuple-element.26), channel_id=1, source_target_pairs={{4,0},{5,1},{6,2},{7,3},{12,8},{13,9},{14,10},{15,11},{20,16},{21,... | collective-permute-start | bytes 36872 | tf_op jit(solution)/shard_map/ppermute | solution.py:22
  95.4 5.6 %collective-permute-start.15 = (f32[3,8,1,128]{3,1,2,0:T(8,128)S(1)}, f32[3,8,1,128]{3,1,2,0:T(8,128)S(1)}, u32[]{:S(2)}, u32[]{:S(2)}) collective-permute-start(f32[3,8,1,128]{3,1,2,0:T(8,128)S(1)} %get-tuple-element.27), channel_id=1, source_target_pairs={{0,4},{1,5},{2,6},{3,7},{8,12},{9,13},{10,14},{11,15},{16,20},{17,... | collective-permute-start | bytes 36872 | tf_op jit(solution)/shard_map/ppermute | solution.py:21
  101.2 6.0 %collective-permute-start.16 = (f32[3,8,16,1]{3,1,2,0:T(8,128)S(1)}, f32[3,8,16,1]{3,1,2,0:T(8,128)S(1)}, u32[]{:S(2)}, u32[]{:S(2)}) collective-permute-start(f32[3,8,16,1]{3,1,2,0:T(8,128)S(1)} %get-tuple-element.24), channel_id=1, source_target_pairs={{1,0},{2,1},{3,2},{5,4},{6,5},{7,6},{9,8},{10,9},{11,10},{13,12},{... | collective-permute-start | bytes 4616 | tf_op jit(solution)/shard_map/ppermute | solution.py:22
  104.1 7.6 %collective-permute-start.17 = (f32[3,8,16,1]{3,1,2,0:T(8,128)S(1)}, f32[3,8,16,1]{3,1,2,0:T(8,128)S(1)}, u32[]{:S(2)}, u32[]{:S(2)}) collective-permute-start(f32[3,8,16,1]{3,1,2,0:T(8,128)S(1)} %get-tuple-element.25), channel_id=1, source_target_pairs={{0,1},{1,2},{2,3},{4,5},{5,6},{6,7},{8,9},{9,10},{10,11},{12,13},{... | collective-permute-start | bytes 4616 | tf_op jit(solution)/shard_map/ppermute | solution.py:21
  (8 other events, 29.2 us)
where the time goes:
time: 121 us; the launch traced here: 120 us
  waiting for transfers between devices  39.8 us (33%)
  starting transfers between devices  34.7 us (29%)
  local copies, waits for them, and re-layouts  26.2 us (22%)
  other arithmetic  11.9 us (10%)
  matrix products  5.33 us (4%)
  between operations  2.42 us (2%)
    ppermute x9, waiting for transfers between devices, extended_2(): before = lax.ppermute(last, axis, up)  33.5 us
    ppermute x9, starting transfers between devices, extended_2(): after = lax.ppermute(first, axis, down)  20.1 us
    ppermute x9, starting transfers between devices, extended_2(): before = lax.ppermute(last, axis, up)  14.6 us
    ppermute x9, waiting for transfers between devices, extended_2(): after = lax.ppermute(first, axis, down)  6.24 us
    reshape x2, local copies, waits for them, and re-layouts, shards(): rhs_lattice = bricks.reshape(components, points, points, points, blocks_f...  4.99 us
    reshape x2, local copies, waits for them, and re-layouts, shards(): back_bricks = solution.reshape(components, blocks_first, points, blocks_s...  2.65 us
    add x7, other arithmetic, fold_rims(): return center + upper_flag * upper_side + lower_flag * lower_side  2.47 us
    transpose x1, local copies, waits for them, and re-layouts, shards(): back_bricks = solution.reshape(components, blocks_first, points, blocks_s...  2.43 us
  transfers between devices with their start and end apart: 18, of which 15 were waited for; matrix products, arithmetic and copies ran while one was open for 2% of the time, Pallas kernels for 0%

commit v1 on v0

v1 whole, which is shorter than its diff:
```python
import functools
import math

import jax
import jax.numpy as jnp
import numpy as np
from jax import lax
from jax.experimental import pallas as pl
from jax.experimental.pallas import tpu as pltpu
from jax.sharding import PartitionSpec as P

DEGREE = 7
ITERS = 3


helm_coefficient = 10.0


def legendre_pair(values, degree):
    previous = 0.0 * values + 1.0
    current = values.copy()
    for order in range(2, degree + 1):
        previous, current = (
            current,
            ((2 * order - 1) * values * current - (order - 1) * previous) / order,
        )
    return (current, previous)


def gll_tables(degree):
    start = np.cos(np.pi * np.arange(degree + 1) / degree)
    nodes_now = start.copy()
    for sweep in range(80):
        top_value, lower_value = legendre_pair(nodes_now, degree)
        nodes_now = nodes_now - (nodes_now * top_value - lower_value) / ((degree + 1) * top_value)
    gll_nodes = nodes_now[::-1].copy()
    gll_nodes[0] = -1.0
    gll_nodes[degree] = 1.0
    legendre_values = legendre_pair(gll_nodes, degree)[0]
    weights = 2.0 / (degree * (degree + 1) * legendre_values**2)
    differences = gll_nodes[:, None] - gll_nodes[None, :] + np.eye(degree + 1)
    derivative = legendre_values[:, None] / legendre_values[None, :] / differences
    derivative = derivative * (1.0 - np.eye(degree + 1))
    derivative[0, 0] = -degree * (degree + 1) / 4.0
    derivative[degree, degree] = degree * (degree + 1) / 4.0
    return (weights, derivative)


HALO = 2
F32 = jnp.float32
BF16 = jnp.bfloat16


def pairings(names, sizes, dim):
    size = sizes[dim]
    if size == 1:
        return []
    if size % 2:
        shifts = (1, size - 1)
        partners = [[(i + shift) % size for i in range(size)] for shift in shifts]
    else:
        partners = [[i ^ 1 for i in range(size)]]
        if size > 2:
            partners.append([((i + 1) ^ 1) - 1 for i in range(size)])
    result = []
    for partner in partners:
        pairs = []
        for flat in range(math.prod(sizes)):
            place = list(np.unravel_index(flat, sizes))
            to = partner[place[dim]]
            if 0 <= to < size:
                place[dim] = to
            elif len(sizes) > 1 and sizes[1 - dim] % 2 == 0:
                place[1 - dim] ^= 1
            else:
                place[dim] = size - 1 - place[dim]
            pairs.append((flat, int(np.ravel_multi_index(place, sizes))))
        result.append(pairs)
    return result


def roles(name, size):
    if size == 1:
        return []
    index = lax.axis_index(name)
    low, high = index > 0, index < size - 1
    if size % 2:
        yes = index >= 0
        no = index < 0
        return [(yes, no, low), (no, yes, high)]
    even = lax.rem(index, 2) == 0
    odd = jnp.logical_not(even)
    result = [(even, even, index >= 0)]
    if size > 2:
        result.append((odd, odd, jnp.logical_or(jnp.logical_and(odd, high), jnp.logical_and(even, low))))
    return result


def both_sides(received, role):
    low, high = 0.0, 0.0
    for data, (_, from_high, used) in zip(received, role):
        high = high + jnp.where(jnp.logical_and(used, from_high), data, 0.0)
        low = low + jnp.where(jnp.logical_and(used, jnp.logical_not(from_high)), data, 0.0)
    return low, high


def split(x):
    upper = x.astype(BF16)
    return upper, (x - upper.astype(F32)).astype(BF16)


def dot2(x, table):
    upper, lower = split(x)
    return jnp.dot(upper, table, preferred_element_type=F32) + jnp.dot(
        lower, table, preferred_element_type=F32
    )


class Plan:
    def __init__(self, components, viscosity_shape, mesh_sizes):
        points = DEGREE + 1
        self.p, self.c = points, components
        self.sizes = mesh_sizes
        ex, ey, ez = (n // points for n in viscosity_shape)
        assert ex == 1 and ez >= HALO
        self.ey, self.ez = ey, ez
        self.rows = points**3
        self.block = points * points
        self.step3, self.step4 = components * ey, (components + 1) * ey
        self.n3, self.n4 = (ez + 2 * HALO) * self.step3, ez * self.step4
        self.w3, self.w4 = -(-self.n3 // 128) * 128, -(-self.n4 // 128) * 128
        self.halo4 = HALO * self.step4
        assert points * self.halo4 <= self.w4 and 2 * self.halo4 <= self.w4
        weights, derivative = gll_tables(DEGREE)
        self.forward = derivative.astype(np.float32)
        self.squared = self.forward * self.forward
        self.weights = weights.astype(np.float32)
        self.end = np.diagonal(self.forward)
        self.tables()

    def lane3(self, g, c, f):
        return (g + HALO) * self.step3 + c * self.ey + f

    def lane4(self, g, c, f):
        return g * self.step4 + c * self.ey + f

    def tables(self):
        p, c, ey, ez = self.p, self.c, self.ey, self.ez
        lanes = ez * p
        every = [(g, cc, f) for g in range(ez) for cc in range(c) for f in range(ey)]
        spread = np.zeros((ey * lanes, self.w3), np.float32)
        flags = np.zeros((c * ey * lanes, self.w4), np.float32)
        diagonal = np.zeros((self.w3, self.w4), np.float32)
        widen = np.zeros((2 * self.w4, 2 * self.w3), np.float32)
        self.id3 = np.full((self.w3, 128), -1, np.int32)
        self.id4 = np.full((self.w4, 128), -1, np.int32)
        for g, cc, f in every:
            for k in range(p):
                spread[f * lanes + g * p + k, self.lane3(g, cc, f)] = 1
                flags[(cc * ey + f) * lanes + g * p + k, self.lane4(g, cc, f)] = 1
            diagonal[self.lane3(g, 0, f), self.lane4(g, c, f)] = 1
            widen[self.lane4(g, cc, f), self.lane3(g, cc, f)] = 1
            widen[self.lane4(g, c, f), self.w3 + self.lane3(g, cc, f)] = 1
            self.id3[self.lane3(g, cc, f), cc] = f * ez + g
            self.id4[self.lane4(g, cc, f), cc] = f * ez + g
        fields = 7
        part = HALO * p
        self.part = part
        assert fields * part <= lanes
        halo = np.zeros((2 * ey * lanes, fields * self.w3), np.float32)
        for side, first in ((0, -HALO), (1, ez)):
            for g in range(HALO):
                for cc in range(c):
                    for f in range(ey):
                        at = self.lane3(first + g, cc, f)
                        row = self.w4 + side * self.halo4 + g * self.step4
                        widen[row + cc * ey + f, at] = 1
                        widen[row + c * ey + f, self.w3 + at] = 1
                        for q in range(fields):
                            for k in range(p):
                                halo[(side * ey + f) * lanes + q * part + g * p + k, q * self.w3 + at] = 1
        self.spread, self.flags, self.diagonal, self.widen, self.halo = (
            x.astype(jnp.bfloat16) for x in (spread, flags, diagonal, widen, halo)
        )
        rolled = []
        for matrix in (self.forward, self.forward.T, self.squared.T):
            for d in range(p):
                rolled += [matrix[a, (a + d) % p] for a in range(p)]
        node = [(j, k) for j in range(p) for k in range(p)]
        wjk = [self.weights[j] * self.weights[k] for j, k in node]
        second = [self.end[j] for j, k in node]
        third = [self.end[k] for j, k in node]
        column = np.asarray(rolled + wjk + second + third, np.float32)
        self.table = np.ascontiguousarray(np.broadcast_to(column[:, None], (column.size, 128)))


    def rolled(self, table, which):
        p = self.p
        return [table[(which * p + d) * p : (which * p + d + 1) * p, :] for d in range(p)]

    def node_table(self, table, which):
        start = 3 * self.p * self.p + which * self.block
        return table[start : start + self.block, :]

    def along_j(self, x, matrix):
        p = self.p
        x = x.reshape(p, p, x.shape[-1])
        out = []
        for a in range(p):
            total = None
            for i in range(p):
                value = float(matrix[a, i])
                if value != 0.0:
                    term = value * x[i]
                    total = term if total is None else total + term
            out.append(total)
        return jnp.concatenate(out, axis=0)

    def along_k(self, x, coefficients):
        p = self.p
        x3 = x.reshape(p, p, x.shape[-1])
        total = coefficients[0][None] * x3
        for d in range(1, p):
            total = total + coefficients[d][None] * pltpu.roll(x3, p - d, 1)
        return total.reshape(x.shape)

    def along_i(self, source, matrix, write):
        p = self.p

        def body(j, carry):
            at = pl.multiple_of(j * p, p)
            x = [source[pl.ds(i * self.block + at, p), :] for i in range(p)]
            for a in range(p):
                total = None
                for i in range(p):
                    value = float(matrix[a, i])
                    if value != 0.0:
                        term = value * x[i]
                        total = term if total is None else total + term
                write(a * self.block + at, total)
            return carry

        lax.fori_loop(0, p, body, 0)

    def operator(self, v, g, out, slope, flux, table):
        p, block = self.p, self.block
        ahead, back = self.rolled(table, 0), self.rolled(table, 1)

        def store(row, value):
            slope[pl.ds(row, p), :] = value

        self.along_i(v, self.forward, store)

        def body(i, carry):
            at = pl.ds(pl.multiple_of(i * block, block), block)
            x = v[at, :]
            s1 = slope[at, :]
            s2 = self.along_j(x, self.forward)
            s3 = self.along_k(x, ahead)
            xy, xz, yz = g[3, at, :], g[4, at, :], g[5, at, :]
            flux[at, :] = g[0, at, :] * s1 + xy * s2 + xz * s3
            f2 = xy * s1 + g[1, at, :] * s2 + yz * s3
            f3 = xz * s1 + yz * s2 + g[2, at, :] * s3
            out[at, :] = (
                self.along_j(f2, self.forward.T) + self.along_k(f3, back) + g[6, at, :] * x
            )
            return carry

        lax.fori_loop(0, p, body, 0)

        def add(row, value):
            out[pl.ds(row, p), :] += value

        self.along_i(flux, self.forward.T, add)

    def fold_second(self, u):
        if self.ey == 1:
            return
        p, width = self.p, u.shape[-1]
        lane = lax.broadcasted_iota(jnp.int32, (p, width), 1)
        f = lax.rem(lane, self.ey)
        for start in range(0, u.shape[0], self.block):
            first, last = u[start : start + p, :], u[start + self.block - p : start + self.block, :]
            u[start + self.block - p : start + self.block, :] = last + jnp.where(
                f < self.ey - 1, pltpu.roll(first, width - 1, 1), 0.0
            )
            u[start : start + p, :] = first + jnp.where(f > 0, pltpu.roll(last, 1, 1), 0.0)

    def fold_third(self, u, step, take_upper, take_lower):
        p, (rows, width) = self.p, u.shape
        count = rows // p
        lane = lax.broadcasted_iota(jnp.int32, (count, width), 1)
        first, last = u[pl.ds(0, count, stride=p), :], u[pl.ds(p - 1, count, stride=p), :]
        u[pl.ds(p - 1, count, stride=p), :] = last + jnp.where(
            take_upper(lane), pltpu.roll(first, width - step, 1), 0.0
        )
        u[pl.ds(0, count, stride=p), :] = first + jnp.where(
            take_lower(lane), pltpu.roll(last, step, 1), 0.0
        )

    def emit(self, u, x_out, y_out):
        p, block = self.p, self.block
        for out, (high, _, _) in zip(x_out, roles("gx", self.sizes["gx"])):
            out[...] = jnp.where(high, u[self.rows - block :, :], u[:block, :])
        for out, (high, _, _) in zip(y_out, roles("gy", self.sizes["gy"])):
            for i in range(p):
                start = i * block
                out[i * p : (i + 1) * p, :] = jnp.where(
                    high, u[start + block - p : start + block, :], u[start : start + p, :]
                )

    def subtract_shared(self, t, scale, x_in, y_in):
        p, block, rows = self.p, self.block, self.rows
        low, high = both_sides([x[...] for x in x_in], roles("gx", self.sizes["gx"]))
        if x_in:
            t[:block, :] -= scale[:block, :] * low
            t[rows - block :, :] -= scale[rows - block :, :] * high
        low, high = both_sides([y[...] for y in y_in], roles("gy", self.sizes["gy"]))
        if y_in:
            for i in range(p):
                at, end = i * block, (i + 1) * block
                t[at : at + p, :] -= scale[at : at + p, :] * low[i * p : (i + 1) * p]
                t[end - p : end, :] -= scale[end - p : end, :] * high[i * p : (i + 1) * p]

    def iteration_fold(self, u):
        self.fold_second(u)
        last = self.n3 - self.step3
        self.fold_third(u, self.step3, lambda l: l < last, lambda l: (l >= self.step3) & (l < self.n3))

    def expand(self, source, upper, lower):
        p, ey = self.p, self.ey

        def body(i, carry):
            block = source(i)
            width = block.shape[-1]
            lane = lax.broadcasted_iota(jnp.int32, (p, width), 1)
            keep = lax.rem(lane, p) == lax.broadcasted_iota(jnp.int32, (p, width), 0)
            for f in range(ey):
                for j in range(0, p, 2):
                    row = f * p + j
                    x = jnp.concatenate(
                        [
                            jnp.where(keep, jnp.broadcast_to(block[r : r + 1, :], (p, width)), 0.0)
                            for r in (row, row + 1)
                        ],
                        axis=0,
                    )
                    at = pl.ds(pl.multiple_of(i * self.block + j * p, 2 * p), 2 * p)
                    first, second = split(x)
                    upper[at, f * width : (f + 1) * width] = first
                    lower[at, f * width : (f + 1) * width] = second
            return carry

        lax.fori_loop(0, p, body, 0)


    def pack_geometry(self, geometry, viscosity, *out):
        width = geometry.shape[-1]
        rows = self.p * self.ey * self.p
        role = roles("gz", self.sizes["gz"])
        lane = lax.broadcasted_iota(jnp.int32, (rows, width), 1)
        for target, (high, _, _) in zip(out, role):
            total = jnp.zeros((rows, width), F32)
            for q in range(7):
                field = (geometry[q] if q < 6 else viscosity[...]).reshape(rows, width)
                start = q * self.part
                upper = pltpu.roll(field, start + self.part, 1)
                lower = pltpu.roll(field, start, 1) if start else field
                here = (lane >= start) & (lane < start + self.part)
                total = jnp.where(here, jnp.where(high, upper, lower), total)
            target[...] = total

    def prepare(self, n_x, n_y, *refs):
        (right, slots, geometry, viscosity, dirichlet, low, high, spread, flags, diagonal, ids, table) = refs[:12]
        s4, ind, raw, coef = refs[12:16]
        x_out, y_out = refs[16 : 16 + n_x], refs[16 + n_x : 16 + n_x + n_y]
        upper, lower, stiff, work = refs[16 + n_x + n_y :]
        p, c, block, rows = self.p, self.c, self.block, self.rows
        top, bottom = jnp.full((8, 128), high[0], F32), jnp.full((8, 128), low[0], F32)
        midpoint, halfwidth = (top + bottom) * 0.5, (top - bottom) * 0.5
        ratio = midpoint / halfwidth
        damping = 1.0 / ratio
        coef[0:8, :] = 1.0 / midpoint
        for n in range(ITERS - 1):
            following = 1.0 / (2.0 * ratio - damping)
            coef[8 * (2 * n + 1) : 8 * (2 * n + 2), :] = following * damping
            coef[8 * (2 * n + 2) : 8 * (2 * n + 3), :] = 2.0 * following / halfwidth
            damping = following
        def convert(q, source):
            self.expand(source, upper, lower)
            raw[q] = jnp.dot(upper[...], spread[...], preferred_element_type=F32) + jnp.dot(
                lower[...], spread[...], preferred_element_type=F32
            )

        def each(q, carry):
            convert(q, lambda i: geometry[q, i])
            return carry

        lax.fori_loop(0, 6, each, 0)
        convert(6, lambda i: viscosity[i])
        wjk, second, third = (self.node_table(table, n) for n in range(3))
        square = self.rolled(table, 2)
        for i in range(p):
            at = slice(i * block, (i + 1) * block)
            xx, yy, zz, xy, xz, yz = (raw[q, at, :] for q in range(6))
            quadrature = float(self.weights[i]) * wjk
            weighted = quadrature * raw[6, at, :]
            mass = (helm_coefficient * quadrature) * (
                xx * (yy * zz - yz * yz) - xy * (xy * zz - yz * xz) + xz * (xy * yz - yy * xz)
            )
            cross = second * third * yz
            end = float(self.end[i])
            if end != 0.0:
                cross = cross + end * (second * xy + third * xz)
            stiff[at, :] = weighted * xx
            work[at, :] = (
                self.along_j(weighted * yy, self.squared.T)
                + self.along_k(weighted * zz, square)
                + (2.0 * weighted) * cross
                + mass
            )

        def add(row, value):
            work[pl.ds(row, p), :] += value

        self.along_i(stiff, self.squared.T, add)
        total = dot2(work[...], diagonal[...])
        for cc in range(c):
            hot = jnp.where(slots[...] == ids[:, cc : cc + 1], 1.0, 0.0).astype(BF16)
            for part in split(right[cc]):
                total = total + lax.dot_general(
                    part, hot, (((1,), (1,)), ((), ())), preferred_element_type=F32
                )
        s4[...] = total
        ends = (lax.axis_index("gx") == 0, lax.axis_index("gx") == self.sizes["gx"] - 1)
        width = dirichlet.shape[-1]
        lane = lax.broadcasted_iota(jnp.int32, (p, width), 1)
        keep = lax.rem(lane, p) == lax.broadcasted_iota(jnp.int32, (p, width), 0)
        for n, here in enumerate(ends):
            plane = jnp.zeros((block, self.w4), F32)
            for cc in range(c):
                face = dirichlet[n, cc].astype(F32)
                for f in range(self.ey):
                    x = jnp.concatenate(
                        [
                            jnp.where(keep, jnp.broadcast_to(face[f * p + j : f * p + j + 1, :], (p, width)), 0.0)
                            for j in range(p)
                        ],
                        axis=0,
                    ).astype(BF16)
                    start = (cc * self.ey + f) * width
                    plane = plane + jnp.dot(x, flags[start : start + width, :], preferred_element_type=F32)
            ind[n * block : (n + 1) * block, :] = jnp.where(here, plane, 0.0)
        last = self.n4 - self.step4
        for u in (s4, ind):
            self.fold_second(u)
            self.fold_third(u, self.step4, lambda l: l < last, lambda l: (l >= self.step4) & (l < self.n4))
        self.emit(s4, x_out, y_out)
        for out, (up, _, _) in zip(y_out, roles("gy", self.sizes["gy"])):
            for n in range(2):
                start = n * block
                out[block + n * p : block + (n + 1) * p, :] = jnp.where(
                    up, ind[start + block - p : start + block, :], ind[start : start + p, :]
                )

    def halo_geometry(self, n_z, *refs):
        raw, halo, table = refs[:3]
        z_in, g = refs[3 : 3 + n_z], refs[3 + n_z]
        upper, lower, sides = refs[4 + n_z :]
        p, block, rows, ey = self.p, self.block, self.rows, self.ey
        if n_z:
            low, high = both_sides([z[...] for z in z_in], roles("gz", self.sizes["gz"]))
            sides[0], sides[1] = low, high
            width = low.shape[-1]
            for side in range(2):
                at = slice(side * ey * width, (side + 1) * ey * width)
                self.expand(
                    lambda i: sides[side, pl.ds(pl.multiple_of(i * ey * p, ey * p), ey * p), :],
                    upper.at[:, at],
                    lower.at[:, at],
                )
        wjk = self.node_table(table, 0)
        fields = []
        for q in range(7):
            field = raw[q]
            if n_z:
                columns = halo[:, q * self.w3 : (q + 1) * self.w3]
                field = field + (
                    jnp.dot(upper[...], columns, preferred_element_type=F32)
                    + jnp.dot(lower[...], columns, preferred_element_type=F32)
                )
            g[q] = field
        for i in range(p):
            at = slice(i * block, (i + 1) * block)
            xx, yy, zz, xy, xz, yz = (g[q, at, :] for q in range(6))
            quadrature = float(self.weights[i]) * wjk
            weighted = quadrature * g[6, at, :]
            g[6, at, :] = (helm_coefficient * quadrature) * (
                xx * (yy * zz - yz * yz) - xy * (xy * zz - yz * xz) + xz * (xy * yz - yy * xz)
            )
            for q, entry in enumerate((xx, yy, zz, xy, xz, yz)):
                g[q, at, :] = weighted * entry

    def join(self, n_x, n_y, *refs):
        x_in, y_raw, y_out = refs[:n_x], refs[n_x : n_x + n_y], refs[n_x + n_y :]
        p, block, ey = self.p, self.block, self.ey
        low, high = both_sides([x[...] for x in x_in], roles("gx", self.sizes["gx"]))
        for raw, out, (up, _, _) in zip(y_raw, y_out, roles("gy", self.sizes["gy"])):
            width = raw.shape[-1]
            face = raw[...]
            if n_x:
                first, last = (jnp.where(up, x[block - p :], x[:p]) for x in (low, high))
                parts = [face[:p] + first, face[p : block - p], face[block - p : block] + last]
                parts += [face[block:]] if face.shape[0] > block else []
                face = jnp.concatenate(parts, axis=0)
            f = lax.rem(lax.broadcasted_iota(jnp.int32, face.shape, 1), ey)
            if ey > 1:
                to_first = jnp.where(f == 0, pltpu.roll(face, width - (ey - 1), 1), 0.0)
                to_last = jnp.where(f == ey - 1, pltpu.roll(face, ey - 1, 1), 0.0)
                face = jnp.where(up, to_first, to_last)
            out[...] = face

    def pack(self, n_x, n_y, *refs):
        s4, ind = refs[:2]
        x_in, y_in = refs[2 : 2 + n_x], refs[2 + n_x : 2 + n_x + n_y]
        s_out, i_out = refs[2 + n_x + n_y : 4 + n_x + n_y]
        z_out = refs[4 + n_x + n_y :]
        p, block, rows = self.p, self.block, self.rows
        s_out[...] = s4[...]
        i_out[...] = ind[...]
        if n_x:
            low, high = both_sides([x[...] for x in x_in], roles("gx", self.sizes["gx"]))
            s_out[:block, :] += low
            s_out[rows - block :, :] += high
        if n_y:
            low, high = both_sides([y[...] for y in y_in], roles("gy", self.sizes["gy"]))
            for u, first, count in ((s_out, 0, p), (i_out, p, 2)):
                for i in range(count):
                    at, end, row = i * block, (i + 1) * block, (first + i) * p
                    u[at : at + p, :] += low[row : row + p]
                    u[end - p : end, :] += high[row : row + p]
        width, size = self.w4, self.halo4
        for out, (up, _, _) in zip(z_out, roles("gz", self.sizes["gz"])):
            for u, count, start in ((s_out, block, 0), (i_out, p, block)):
                groups = u.shape[0] // count
                lane = lax.broadcasted_iota(jnp.int32, (count, width), 1)
                for section in range(0, groups, p):
                    total = jnp.zeros((count, width), F32)
                    for n in range(p):
                        at = (section + n) * count
                        x = u[at : at + count, :]
                        shift = n * size
                        below = pltpu.roll(x, shift, 1) if shift else x
                        above = pltpu.roll(x, (shift + width - self.n4 + size) % width, 1)
                        here = (lane >= shift) & (lane < shift + size)
                        total = jnp.where(here, jnp.where(up, above, below), total)
                    row = start + section // p * count
                    out[row : row + count, :] = total

    def wide(self, own, low, high, groups, count, put):
        size, width = self.halo4, self.w4
        lane = lax.broadcasted_iota(jnp.int32, (count, width), 1)
        for n in range(groups):
            shift = (width - (n % self.p) * size) % width
            row = (n // self.p) * count
            first = pltpu.roll(low[row : row + count], shift, 1) if shift else low[row : row + count]
            second = pltpu.roll(high[row : row + count], (shift + size) % width, 1)
            beside = jnp.where(lane < size, first, jnp.where(lane < 2 * size, second, 0.0))
            put(n * count, jnp.concatenate([own[n * count : (n + 1) * count, :], beside], axis=1))

    def start(self, n_x, n_y, n_z, *refs):
        s4, ind, g, coef, widen, table = refs[:6]
        z_in = refs[6 : 6 + n_z]
        t, d, scale, v = refs[6 + n_z : 10 + n_z]
        refs = refs[10 + n_z :]
        x_out, y_out = refs[:n_x], refs[n_x : n_x + n_y]
        upper, lower, flag_lhs, r, flag, slope, flux = refs[n_x + n_y :]
        p, block, rows, w3 = self.p, self.block, self.rows, self.w3
        size = self.sizes["gz"]
        if n_z:
            low, high = both_sides([z[...] for z in z_in], roles("gz", size))
        else:
            low = high = jnp.zeros((block + 2 * p, self.w4), F32)

        def put(at, x):
            first, second = split(x)
            upper[at : at + block, :] = first
            lower[at : at + block, :] = second

        self.wide(s4, low, high, p, block, put)

        def put_flag(at, x):
            flag_lhs[at : at + p, :] = x

        self.wide(ind, low[block:], high[block:], 2 * p, p, put_flag)
        both = jnp.dot(upper[...], widen[...], preferred_element_type=F32) + jnp.dot(
            lower[...], widen[...], preferred_element_type=F32
        )
        r[...] = both[:, :w3]
        scale[...] = both[:, w3:]
        flag[...] = jnp.dot(flag_lhs[...].astype(BF16), widen[:, :w3], preferred_element_type=F32)
        step, first_own, end_own = self.step3, HALO * self.step3, self.n3 - HALO * self.step3
        for u in (r, scale, flag):
            self.fold_third(
                u,
                step,
                lambda l: ((l >= first_own - step) & (l < first_own)) | ((l >= end_own - step) & (l < end_own)),
                lambda l: ((l >= first_own) & (l < first_own + step)) | ((l >= end_own) & (l < end_own + step)),
            )
        index = lax.axis_index("gz")
        begin = jnp.where(index > 0, 0, first_own)
        end = jnp.where(index < size - 1, self.n3, end_own)
        lane = lax.broadcasted_iota(jnp.int32, (block, w3), 1)
        valid = (lane >= begin) & (lane < end)
        middle = coef[0:1, :]
        for i in range(p):
            at = slice(i * block, (i + 1) * block)
            factor = jnp.where(valid, 1.0 / jnp.where(valid, scale[at, :], 1.0), 0.0)
            if i in (0, p - 1):
                row = 0 if i == 0 else block
                factor = jnp.where(flag[row : row + block, :] > 0.5, 0.0, factor)
            scale[at, :] = factor
            scaled = factor * r[at, :]
            t[at, :] = scaled
            d[at, :] = scaled * middle
        self.operator(d, g, v, slope, flux, table)
        self.iteration_fold(v)
        self.emit(v, x_out, y_out)

    def advance(self, t, t_new, d, v, scale, coef, which, x_in, y_in, put):
        t_new[...] = t[...] - scale[...] * v[...]
        self.subtract_shared(t_new, scale, x_in, y_in)
        keep, gain = (coef[8 * (2 * which + n) : 8 * (2 * which + n) + 1, :] for n in (1, 2))
        for i in range(self.p):
            at = slice(i * self.block, (i + 1) * self.block)
            put(at, keep * d[at, :] + gain * t_new[at, :])

    def middle(self, n_x, n_y, which, *refs):
        t, d, scale, v, total, g, coef, table = refs[:8]
        refs = refs[8:]
        x_in, y_in, refs = refs[:n_x], refs[n_x : n_x + n_y], refs[n_x + n_y :]
        t_new, d_new, v_new, total_new = refs[:4]
        x_out, y_out = refs[4 : 4 + n_x], refs[4 + n_x : 4 + n_x + n_y]
        slope, flux = refs[4 + n_x + n_y :]

        def put(at, x):
            d_new[at, :] = x
            total_new[at, :] = total[at, :] + x

        self.advance(t, t_new, d, v, scale, coef, which, x_in, y_in, put)
        self.operator(d_new, g, v_new, slope, flux, table)
        self.iteration_fold(v_new)
        self.emit(v_new, x_out, y_out)

    def finish(self, n_x, n_y, which, *refs):
        t, d, scale, v, total, coef, slots, ids = refs[:8]
        refs = refs[8:]
        x_in, y_in, refs = refs[:n_x], refs[n_x : n_x + n_y], refs[n_x + n_y :]
        out, t_new, field = refs

        def put(at, x):
            field[at, :] = total[at, :] + x

        self.advance(t, t_new, d, v, scale, coef, which, x_in, y_in, put)
        upper, lower = split(field[...])
        for cc in range(self.c):
            hot = jnp.where(slots[...] == ids[:, cc : cc + 1], 1.0, 0.0).astype(BF16)
            out[cc] = jnp.dot(upper, hot, preferred_element_type=F32) + jnp.dot(
                lower, hot, preferred_element_type=F32
            )


def shards(sizes, right_side, geometry, viscosity, eig_low, eig_high, element_slot, dirichlet):
    plan = Plan(right_side.shape[0], viscosity.shape, sizes)
    p, block, rows, w3, w4 = plan.p, plan.block, plan.rows, plan.w3, plan.w4
    x_pairs = pairings(("gx",), (sizes["gx"],), 0)
    y_pairs = pairings(("gy",), (sizes["gy"],), 0)
    z_pairs = pairings(("gy", "gz"), (sizes["gy"], sizes["gz"]), 1)
    n_x, n_y, n_z = len(x_pairs), len(y_pairs), len(z_pairs)

    def send(arrays, axis, pairs):
        return [lax.ppermute(x, axis, pair) for x, pair in zip(arrays, pairs)]

    def shape(*size, dtype=F32):
        return jax.ShapeDtypeStruct(size, dtype)

    def call(kernel, outputs, operands, scratch=(), scalars=(), flops=0, name=None):
        specs = [
            pl.BlockSpec(memory_space=pltpu.SMEM if n in scalars else pltpu.VMEM)
            for n in range(len(operands))
        ]
        return list(pl.pallas_call(
            kernel,
            out_shape=list(outputs),
            in_specs=specs,
            out_specs=[pl.BlockSpec(memory_space=pltpu.VMEM)] * len(outputs),
            scratch_shapes=list(scratch),
            compiler_params=pltpu.CompilerParams(vmem_limit_bytes=40 * 1024 * 1024),
            cost_estimate=pl.CostEstimate(flops=flops, bytes_accessed=0, transcendentals=0),
            name=name,
        )(*operands))

    def vmem(*size, dtype=F32):
        return pltpu.VMEM(size, dtype)

    lanes = plan.ez * p
    table = jnp.asarray(plan.table)
    faces = [shape(plan.p * plan.ey * p, lanes)] * n_z
    z_geometry = call(plan.pack_geometry, faces, (geometry, viscosity), name="pack_geometry") if n_z else []
    z_geometry = send(z_geometry, ("gy", "gz"), z_pairs)

    field3, field4 = shape(rows, w3), shape(rows, w4)
    results = call(
        functools.partial(plan.prepare, n_x, n_y),
        [field4, shape(2 * block, w4), shape(7, rows, w3), shape(8 * (2 * ITERS - 1), 128)]
        + [shape(block, w4)] * n_x
        + [shape(block + 2 * p, w4)] * n_y,
        (
            right_side,
            element_slot,
            geometry,
            viscosity,
            dirichlet,
            eig_low,
            eig_high,
            jnp.asarray(plan.spread),
            jnp.asarray(plan.flags),
            jnp.asarray(plan.diagonal),
            jnp.asarray(plan.id4),
            table,
        ),
        scratch=[vmem(rows, plan.ey * lanes, dtype=BF16)] * 2 + [vmem(rows, w3)] * 2,
        scalars=(5, 6),
        name="prepare",
    )
    s4, ind, raw, coef = results[:4]
    x_out, y_raw = results[4 : 4 + n_x], results[4 + n_x :]
    x_in = send(x_out, "gx", x_pairs)

    g = call(
        functools.partial(plan.halo_geometry, n_z),
        [shape(7, rows, w3)],
        [raw, jnp.asarray(plan.halo), table] + z_geometry,
        scratch=[vmem(rows, 2 * plan.ey * lanes, dtype=BF16)] * 2 + [vmem(2, plan.p * plan.ey * p, lanes)],
        flops=2000000,
        name="halo_geometry",
    )[0]

    def second(x_in, y_raw):
        if not y_raw:
            return []
        faces = [shape(*y.shape) for y in y_raw]
        return send(call(functools.partial(plan.join, n_x, n_y), faces, x_in + y_raw, name="join"), "gy", y_pairs)

    y_in = second(x_in, y_raw)
    results = call(
        functools.partial(plan.pack, n_x, n_y),
        [field4, shape(2 * block, w4)] + [shape(block + 2 * p, w4)] * n_z,
        [s4, ind] + x_in + y_in,
        name="pack",
    )
    s4, ind = results[:2]
    z_in = send(results[2:], ("gy", "gz"), z_pairs)

    messages = [shape(block, w3)] * (n_x + n_y)
    results = call(
        functools.partial(plan.start, n_x, n_y, n_z),
        [field3] * 4 + messages,
        [s4, ind, g, coef, jnp.asarray(plan.widen), table] + z_in,
        scratch=[vmem(rows, 2 * w4, dtype=BF16)] * 2
        + [vmem(2 * block, 2 * w4), vmem(rows, w3), vmem(2 * block, w3), vmem(rows, w3), vmem(rows, w3)],
        name="first_direction",
    )
    t, d, scale, v = results[:4]
    total = d
    for n in range(ITERS - 1):
        x_out, y_raw = results[4 : 4 + n_x], results[4 + n_x :]
        x_in = send(x_out, "gx", x_pairs)
        y_in = second(x_in, y_raw)
        if n < ITERS - 2:
            results = call(
                functools.partial(plan.middle, n_x, n_y, n),
                [field3] * 4 + messages,
                [t, d, scale, v, total, g, coef, table] + x_in + y_in,
                scratch=[vmem(rows, w3)] * 2,
                name="direction",
            )
            t, d, v, total = results[:4]
        else:
            return call(
                functools.partial(plan.finish, n_x, n_y, n),
                [shape(*right_side.shape)],
                [t, d, scale, v, total, coef, element_slot, jnp.asarray(plan.id3)] + x_in + y_in,
                scratch=[vmem(rows, w3)] * 2,
                name="field",
            )[0]


def solution(mesh):
    sizes = {name: mesh.shape[name] for name in ("gx", "gy", "gz")}
    return jax.shard_map(
        functools.partial(shards, sizes),
        mesh=mesh,
        in_specs=(
            P(None, None, ("gx", "gy", "gz")),
            P(None, "gx", "gy", "gz"),
            P("gx", "gy", "gz"),
            P(),
            P(),
            P(("gx", "gy", "gz"), None),
            P(None, None, "gy", "gz"),
        ),
        out_specs=P(None, None, ("gx", "gy", "gz")),
        check_vma=False,
    )
```

time: 121 us -> 51.7 us (0.43)
  the two profiles are of different devices: /device:TPU:30 before, /device:TPU:0 now
where the time goes in v1:
time: 51.7 us; the launch traced here: 51.2 us
  starting transfers between devices  14.9 us (29%)
  waiting for transfers between devices  12.9 us (25%)
  Pallas kernels  12.2 us (24%)
  local copies, waits for them, and re-layouts  9.75 us (19%)
  between operations  1.46 us (3%)
    ppermute x13, starting transfers between devices, send(): return [lax.ppermute(x, axis, pair) for x, pair in zip(arrays, pairs)]  14.9 us
    ppermute x13, waiting for transfers between devices, send(): return [lax.ppermute(x, axis, pair) for x, pair in zip(arrays, pairs)]  12.9 us
    pallas_call x10, Pallas kernels, call(): pl.pallas_call(kernel, out_shape=list(outputs), in_specs=specs, out_specs...  12.2 us
    unnamed x29, local copies, waits for them, and re-layouts  8.83 us
  transfers between devices with their start and end apart: 13, of which 7 were waited for; matrix products, arithmetic and copies ran while one was open for 0% of the time, Pallas kernels for 7%

profile of v1, /device:TPU:0, one launch (start us, length us, event | category | flops | bytes accessed | tf_op | source)
XLA Modules:
  0.0 51.2 jit_solution(16489715378877608568)
XLA Ops:
  1.3 1.2 %copy.16.refs_0_ = f32[3,512,32]{2,1,0:T(8,128)S(1)} copy(f32[3,512,32]{1,2,0:T(8,128)} %param.15) | data formatting | bytes 393216 | tf_op args[0]
  2.6 0.9 %copy-done = f32[384,128]{1,0:T(8,128)S(1)} copy-done((f32[384,128]{1,0:T(8,128)S(1)}, f32[384,128]{1,0:T(8,128)}, u32[]{:S(2)}) %copy-start) | copy-done | bytes 196632
  3.5 1.0 %copy-done.2 = f32[6,8,16,128]{3,2,1,0:T(8,128)S(1)} copy-done((f32[6,8,16,128]{3,2,1,0:T(8,128)S(1)}, f32[6,8,16,128]{3,2,1,0:T(8,128)}, u32[]{:S(2)}) %copy-start.2) | copy-done | bytes 393240
  4.5 0.8 %copy-done.4 = f32[8,16,128]{2,1,0:T(8,128)S(1)} copy-done((f32[8,16,128]{2,1,0:T(8,128)S(1)}, f32[8,16,128]{2,1,0:T(8,128)}, u32[]{:S(2)}) %copy-start.4) | copy-done | bytes 65560
  5.3 0.9 %copy-done.5 = bf16[768,128]{1,0:T(8,128)(2,1)S(1)} copy-done((bf16[768,128]{1,0:T(8,128)(2,1)S(1)}, bf16[768,128]{1,0:T(8,128)(2,1)}, u32[]{:S(2)}) %copy-start.5) | copy-done | bytes 196632
  6.2 0.8 %copy-done.8 = s32[128,128]{1,0:T(8,128)S(1)} copy-done((s32[128,128]{1,0:T(8,128)S(1)}, s32[128,128]{1,0:T(8,128)}, u32[]{:S(2)}) %copy-start.8) | copy-done | bytes 65560
  7.1 0.8 %copy-done.9 = bf16[256,128]{1,0:T(8,128)(2,1)S(1)} copy-done((bf16[256,128]{1,0:T(8,128)(2,1)S(1)}, bf16[256,128]{1,0:T(8,128)(2,1)}, u32[]{:S(2)}) %copy-start.9) | copy-done | bytes 65560
  7.9 0.8 %copy-done.10 = s32[2,3,16,128]{3,2,1,0:T(8,128)S(1)} copy-done((s32[2,3,16,128]{3,2,1,0:T(8,128)S(1)}, s32[2,3,16,128]{3,2,1,0:T(8,128)}, u32[]{:S(2)}) %copy-start.10) | copy-done | bytes 49176
  8.7 0.8 %copy-done.11 = bf16[128,128]{1,0:T(8,128)(2,1)S(1)} copy-done((bf16[128,128]{1,0:T(8,128)(2,1)S(1)}, bf16[128,128]{1,0:T(8,128)(2,1)}, u32[]{:S(2)}) %copy-start.11) | copy-done | bytes 32792
  9.5 0.7 %copy-done.12 = s32[1,32]{1,0:T(1,128)S(1)} copy-done((s32[1,32]{1,0:T(1,128)S(1)}, s32[1,32]{1,0:T(1,128)}, u32[]{:S(2)}) %copy-start.12) | copy-done | bytes 152
  10.1 4.7 %prepare.1 = (f32[512,128]{1,0:T(8,128)S(1)}, f32[128,128]{1,0:T(8,128)S(1)}, f32[7,512,128]{2,1,0:T(8,128)S(1)}, f32[40,128]{1,0:T(8,128)S(1)}, f32[64,128]{1,0...) custom-call(f32[3,512,32]{2,1,0:T(8,128)S(1)} %copy.16.refs_0_, s32[1,32]{1,0:T(1,128)S(1)} %copy-done.12, ...), custom_call_target="tpu_custom_call" | custom-call | tf_op jit(solution)/shard_map/prepare/pallas_call | solution.py:692
  14.8 0.5 %collective-permute-start = (f32[64,128]{1,0:T(8,128)S(1)}, f32[64,128]{1,0:T(8,128)S(1)}, u32[]{:S(2)}, u32[]{:S(2)}) collective-permute-start(f32[64,128]{1,0:T(8,128)S(1)} %get-tuple-element.34), channel_id=1, source_target_pairs={{0,8},{8,0},{16,24},{24,16},{1,9},{9,1},{17,25},{25,17},{2,10},{10... | collective-permute-start | bytes 98312 | tf_op jit(solution)/shard_map/ppermute | solution.py:682
  15.4 2.6 %collective-permute-start.1 = (f32[64,128]{1,0:T(8,128)S(1)}, f32[64,128]{1,0:T(8,128)S(1)}, u32[]{:S(2)}, u32[]{:S(2)}) collective-permute-start(f32[64,128]{1,0:T(8,128)S(1)} %get-tuple-element.35), channel_id=1, source_target_pairs={{0,24},{8,16},{16,8},{24,0},{1,25},{9,17},{17,9},{25,1},{2,26},{10... | collective-permute-start | bytes 98312 | tf_op jit(solution)/shard_map/ppermute | solution.py:682
  18.0 1.7 %collective-permute-done.1.refs_1_.refs_3_ = f32[64,128]{1,0:T(8,128)S(1)} collective-permute-done((f32[64,128]{1,0:T(8,128)S(1)}, f32[64,128]{1,0:T(8,128)S(1)}, u32[]{:S(2)}, u32[]{:S(2)}) %collective-permute-start.1) | collective-permute-done | bytes 32800 | tf_op jit(solution)/shard_map/ppermute | solution.py:682
  19.8 1.7 %collective-permute-start.2 = (f32[80,128]{1,0:T(8,128)S(1)}, f32[80,128]{1,0:T(8,128)S(1)}, u32[]{:S(2)}, u32[]{:S(2)}) collective-permute-start(f32[80,128]{1,0:T(8,128)S(1)} %join.3), channel_id=1, source_target_pairs={{0,4},{4,0},{1,5},{5,1},{2,6},{6,2},{3,7},{7,3},{8,12},{12,8},{9,1... | collective-permute-start | bytes 122888 | tf_op jit(solution)/shard_map/ppermute | solution.py:682
  21.5 0.5 pack_geometry.1
  22.0 1.6 %collective-permute-start.3 = (f32[128,128]{1,0:T(8,128)S(1)}, f32[128,128]{1,0:T(8,128)S(1)}, u32[]{:S(2)}, u32[]{:S(2)}) collective-permute-start(f32[128,128]{1,0:T(8,128)S(1)} %get-tuple-element.40), channel_id=1, source_target_pairs={{0,1},{1,0},{2,3},{3,2},{4,5},{5,4},{6,7},{7,6},{8,9},{9,8},{10,11... | collective-permute-start | bytes 196616 | tf_op jit(solution)/shard_map/ppermute | solution.py:682
  23.6 0.6 %collective-permute-start.4 = (f32[128,128]{1,0:T(8,128)S(1)}, f32[128,128]{1,0:T(8,128)S(1)}, u32[]{:S(2)}, u32[]{:S(2)}) collective-permute-start(f32[128,128]{1,0:T(8,128)S(1)} %get-tuple-element.41), channel_id=1, source_target_pairs={{0,4},{1,2},{2,1},{3,7},{4,0},{5,6},{6,5},{7,3},{8,12},{9,10},{10,... | collective-permute-start | bytes 196616 | tf_op jit(solution)/shard_map/ppermute | solution.py:682
  24.5 2.7 %collective-permute-start.5 = (f32[80,128]{1,0:T(8,128)S(1)}, f32[80,128]{1,0:T(8,128)S(1)}, u32[]{:S(2)}, u32[]{:S(2)}) collective-permute-start(f32[80,128]{1,0:T(8,128)S(1)} %get-tuple-element.43), channel_id=1, source_target_pairs={{0,1},{1,0},{2,3},{3,2},{4,5},{5,4},{6,7},{7,6},{8,9},{9,8},{10,11... | collective-permute-start | bytes 122888 | tf_op jit(solution)/shard_map/ppermute | solution.py:682
  27.9 2.5 %halo_geometry.1.refs_2_.refs_5_ = f32[7,512,128]{2,1,0:T(8,128)S(1)} custom-call(f32[7,512,128]{2,1,0:T(8,128)S(1)} %get-tuple-element.39.refs_0_, bf16[512,896]{1,0:T(8,128)(2,1)S(1)} %copy-done.3, f32[384,128]{1,0:T(8,128)S(1)} %copy-done.1, f32[128,128]{1,0:T(8,128)S(1)} %collective-permute-done.3.refs_3_, f32[128,128]{1,0:T(8,128)S(1)} %collective-permute-done.4.refs_4_), custom_call_target="tpu_custom_call" | custom-call | flops 2000000 | tf_op jit(solution)/shard_map/halo_geometry/pallas_call | solution.py:692
  30.4 0.8 %collective-permute-done.6.refs_7_ = f32[80,128]{1,0:T(8,128)S(1)} collective-permute-done((f32[80,128]{1,0:T(8,128)S(1)}, f32[80,128]{1,0:T(8,128)S(1)}, u32[]{:S(2)}, u32[]{:S(2)}) %collective-permute-start.6) | collective-permute-done | bytes 40992 | tf_op jit(solution)/shard_map/ppermute | solution.py:682
  31.2 1.9 %first_direction.1 = (f32[512,128]{1,0:T(8,128)S(1)}, f32[512,128]{1,0:T(8,128)S(1)}, f32[512,128]{1,0:T(8,128)S(1)}, f32[512,128]{1,0:T(8,128)S(1)}, f32[64,128...) custom-call(f32[512,128]{1,0:T(8,128)S(1)} %get-tuple-element.37.refs_0_, ...), custom_call_target="tpu_custom_call" | custom-call | tf_op jit(solution)/shard_map/first_direction/pallas_call | solution.py:692
  33.3 1.6 %collective-permute-start.8 = (f32[64,128]{1,0:T(8,128)S(1)}, f32[64,128]{1,0:T(8,128)S(1)}, u32[]{:S(2)}, u32[]{:S(2)}) collective-permute-start(f32[64,128]{1,0:T(8,128)S(1)} %get-tuple-element.50), channel_id=1, source_target_pairs={{0,24},{8,16},{16,8},{24,0},{1,25},{9,17},{17,9},{25,1},{2,26},{10... | collective-permute-start | bytes 98312 | tf_op jit(solution)/shard_map/ppermute | solution.py:682
  34.8 1.8 %collective-permute-done.8.refs_1_.refs_9_ = f32[64,128]{1,0:T(8,128)S(1)} collective-permute-done((f32[64,128]{1,0:T(8,128)S(1)}, f32[64,128]{1,0:T(8,128)S(1)}, u32[]{:S(2)}, u32[]{:S(2)}) %collective-permute-start.8) | collective-permute-done | bytes 32800 | tf_op jit(solution)/shard_map/ppermute | solution.py:682
  36.8 0.7 %collective-permute-start.9 = (f32[64,128]{1,0:T(8,128)S(1)}, f32[64,128]{1,0:T(8,128)S(1)}, u32[]{:S(2)}, u32[]{:S(2)}) collective-permute-start(f32[64,128]{1,0:T(8,128)S(1)} %join.4), channel_id=1, source_target_pairs={{0,4},{4,0},{1,5},{5,1},{2,6},{6,2},{3,7},{7,3},{8,12},{12,8},{9,1... | collective-permute-start | bytes 98312 | tf_op jit(solution)/shard_map/ppermute | solution.py:682
  37.5 3.3 %collective-permute-done.9.refs_10_ = f32[64,128]{1,0:T(8,128)S(1)} collective-permute-done((f32[64,128]{1,0:T(8,128)S(1)}, f32[64,128]{1,0:T(8,128)S(1)}, u32[]{:S(2)}, u32[]{:S(2)}) %collective-permute-start.9) | collective-permute-done | bytes 32800 | tf_op jit(solution)/shard_map/ppermute | solution.py:682
  40.8 1.5 %direction.1 = (f32[512,128]{1,0:T(8,128)S(1)}, f32[512,128]{1,0:T(8,128)S(1)}, f32[512,128]{1,0:T(8,128)S(1)}, f32[512,128]{1,0:T(8,128)S(1)}, f32[64,128]{1,0:...) custom-call(f32[512,128]{1,0:T(8,128)S(1)} %get-tuple-element.45.refs_0_, ...), custom_call_target="tpu_custom_call" | custom-call | tf_op jit(solution)/shard_map/direction/pallas_call | solution.py:692
  42.3 1.6 %collective-permute-start.11 = (f32[64,128]{1,0:T(8,128)S(1)}, f32[64,128]{1,0:T(8,128)S(1)}, u32[]{:S(2)}, u32[]{:S(2)}) collective-permute-start(f32[64,128]{1,0:T(8,128)S(1)} %get-tuple-element.57), channel_id=1, source_target_pairs={{0,24},{8,16},{16,8},{24,0},{1,25},{9,17},{17,9},{25,1},{2,26},{10... | collective-permute-start | bytes 98312 | tf_op jit(solution)/shard_map/ppermute | solution.py:682
  43.9 1.8 %collective-permute-done.11.refs_1_.refs_9_ = f32[64,128]{1,0:T(8,128)S(1)} collective-permute-done((f32[64,128]{1,0:T(8,128)S(1)}, f32[64,128]{1,0:T(8,128)S(1)}, u32[]{:S(2)}, u32[]{:S(2)}) %collective-permute-start.11) | collective-permute-done | bytes 32800 | tf_op jit(solution)/shard_map/ppermute | solution.py:682
  45.8 0.7 %collective-permute-start.12 = (f32[64,128]{1,0:T(8,128)S(1)}, f32[64,128]{1,0:T(8,128)S(1)}, u32[]{:S(2)}, u32[]{:S(2)}) collective-permute-start(f32[64,128]{1,0:T(8,128)S(1)} %join.5), channel_id=1, source_target_pairs={{0,4},{4,0},{1,5},{5,1},{2,6},{6,2},{3,7},{7,3},{8,12},{12,8},{9,1... | collective-permute-start | bytes 98312 | tf_op jit(solution)/shard_map/ppermute | solution.py:682
  46.5 3.3 %collective-permute-done.12.refs_10_ = f32[64,128]{1,0:T(8,128)S(1)} collective-permute-done((f32[64,128]{1,0:T(8,128)S(1)}, f32[64,128]{1,0:T(8,128)S(1)}, u32[]{:S(2)}, u32[]{:S(2)}) %collective-permute-start.12) | collective-permute-done | bytes 32800 | tf_op jit(solution)/shard_map/ppermute | solution.py:682
  50.3 0.9 %copy.17 = f32[3,512,32]{1,2,0:T(8,128)} copy(f32[3,512,32]{2,1,0:T(8,128)S(1)} %field.1) | data formatting | bytes 393216 | tf_op jit(solution)/shard_map/field/pallas_call | solution.py:692
  (34 shorter events, 1.9 us)
Async XLA Ops:
  1.3 26.6 %copy-start.1 = (f32[384,128]{1,0:T(8,128)S(1)}, f32[384,128]{1,0:T(8,128)}, u32[]{:S(2)}) copy-start(f32[384,128]{1,0:T(8,128)} %constant.16.clone.refs_11_.refs_2_.refs_5_.refs_7_) | copy-start | bytes 589828
  2.5 0.9 %copy-start = (f32[384,128]{1,0:T(8,128)S(1)}, f32[384,128]{1,0:T(8,128)}, u32[]{:S(2)}) copy-start(f32[384,128]{1,0:T(8,128)} %constant.16.clone.refs_11_.refs_2_.refs_5_.refs_7_) | copy-start | bytes 589828
  3.5 1.0 %copy-start.2 = (f32[6,8,16,128]{3,2,1,0:T(8,128)S(1)}, f32[6,8,16,128]{3,2,1,0:T(8,128)}, u32[]{:S(2)}) copy-start(f32[6,8,16,128]{3,2,1,0:T(8,128)} %geometry.1) | copy-start | bytes 1179652
  4.5 0.8 %copy-start.4 = (f32[8,16,128]{2,1,0:T(8,128)S(1)}, f32[8,16,128]{2,1,0:T(8,128)}, u32[]{:S(2)}) copy-start(f32[8,16,128]{2,1,0:T(8,128)} %viscosity.1) | copy-start | bytes 196612
  5.3 0.9 %copy-start.5 = (bf16[768,128]{1,0:T(8,128)(2,1)S(1)}, bf16[768,128]{1,0:T(8,128)(2,1)}, u32[]{:S(2)}) copy-start(bf16[768,128]{1,0:T(8,128)(2,1)} %constant.18.clone.refs_8_) | copy-start | bytes 589828
  6.2 0.8 %copy-start.8 = (s32[128,128]{1,0:T(8,128)S(1)}, s32[128,128]{1,0:T(8,128)}, u32[]{:S(2)}) copy-start(s32[128,128]{1,0:T(8,128)} %constant.20.clone.refs_10_) | copy-start | bytes 196612
  7.1 0.8 %copy-start.9 = (bf16[256,128]{1,0:T(8,128)(2,1)S(1)}, bf16[256,128]{1,0:T(8,128)(2,1)}, u32[]{:S(2)}) copy-start(bf16[256,128]{1,0:T(8,128)(2,1)} %constant.17.clone.refs_7_) | copy-start | bytes 196612
  7.9 0.8 %copy-start.10 = (s32[2,3,16,128]{3,2,1,0:T(8,128)S(1)}, s32[2,3,16,128]{3,2,1,0:T(8,128)}, u32[]{:S(2)}) copy-start(s32[2,3,16,128]{3,2,1,0:T(8,128)} %refs_4_.2) | copy-start | bytes 147460
  8.7 0.8 %copy-start.11 = (bf16[128,128]{1,0:T(8,128)(2,1)S(1)}, bf16[128,128]{1,0:T(8,128)(2,1)}, u32[]{:S(2)}) copy-start(bf16[128,128]{1,0:T(8,128)(2,1)} %constant.19.clone.refs_9_) | copy-start | bytes 98308
  9.5 0.7 %copy-start.12 = (s32[1,32]{1,0:T(1,128)S(1)}, s32[1,32]{1,0:T(1,128)}, u32[]{:S(2)}) copy-start(s32[1,32]{1,0:T(1,128)} %refs_6_.2) | copy-start | bytes 388
  10.1 17.7 %copy-start.3 = (bf16[512,896]{1,0:T(8,128)(2,1)S(1)}, bf16[512,896]{1,0:T(8,128)(2,1)}, u32[]{:S(2)}) copy-start(bf16[512,896]{1,0:T(8,128)(2,1)} %constant.21.clone.refs_1_) | copy-start | bytes 2752516
  14.8 3.2 %collective-permute-start = (f32[64,128]{1,0:T(8,128)S(1)}, f32[64,128]{1,0:T(8,128)S(1)}, u32[]{:S(2)}, u32[]{:S(2)}) collective-permute-start(f32[64,128]{1,0:T(8,128)S(1)} %get-tuple-element.34), channel_id=1, source_target_pairs={{0,8},{8,0},{16,24},{24,16},{1,9},{9,1},{17,25},{25,17},{2,10},{10... | collective-permute-start | bytes 98312 | tf_op jit(solution)/shard_map/ppermute | solution.py:682
  15.4 4.3 %collective-permute-start.1 = (f32[64,128]{1,0:T(8,128)S(1)}, f32[64,128]{1,0:T(8,128)S(1)}, u32[]{:S(2)}, u32[]{:S(2)}) collective-permute-start(f32[64,128]{1,0:T(8,128)S(1)} %get-tuple-element.35), channel_id=1, source_target_pairs={{0,24},{8,16},{16,8},{24,0},{1,25},{9,17},{17,9},{25,1},{2,26},{10... | collective-permute-start | bytes 98312 | tf_op jit(solution)/shard_map/ppermute | solution.py:682
  19.8 4.4 %collective-permute-start.2 = (f32[80,128]{1,0:T(8,128)S(1)}, f32[80,128]{1,0:T(8,128)S(1)}, u32[]{:S(2)}, u32[]{:S(2)}) collective-permute-start(f32[80,128]{1,0:T(8,128)S(1)} %join.3), channel_id=1, source_target_pairs={{0,4},{4,0},{1,5},{5,1},{2,6},{6,2},{3,7},{7,3},{8,12},{12,8},{9,1... | collective-permute-start | bytes 122888 | tf_op jit(solution)/shard_map/ppermute | solution.py:682
  22.0 5.8 %collective-permute-start.3 = (f32[128,128]{1,0:T(8,128)S(1)}, f32[128,128]{1,0:T(8,128)S(1)}, u32[]{:S(2)}, u32[]{:S(2)}) collective-permute-start(f32[128,128]{1,0:T(8,128)S(1)} %get-tuple-element.40), channel_id=1, source_target_pairs={{0,1},{1,0},{2,3},{3,2},{4,5},{5,4},{6,7},{7,6},{8,9},{9,8},{10,11... | collective-permute-start | bytes 196616 | tf_op jit(solution)/shard_map/ppermute | solution.py:682
  23.6 4.3 %collective-permute-start.4 = (f32[128,128]{1,0:T(8,128)S(1)}, f32[128,128]{1,0:T(8,128)S(1)}, u32[]{:S(2)}, u32[]{:S(2)}) collective-permute-start(f32[128,128]{1,0:T(8,128)S(1)} %get-tuple-element.41), channel_id=1, source_target_pairs={{0,4},{1,2},{2,1},{3,7},{4,0},{5,6},{6,5},{7,3},{8,12},{9,10},{10,... | collective-permute-start | bytes 196616 | tf_op jit(solution)/shard_map/ppermute | solution.py:682
  24.5 5.9 %collective-permute-start.5 = (f32[80,128]{1,0:T(8,128)S(1)}, f32[80,128]{1,0:T(8,128)S(1)}, u32[]{:S(2)}, u32[]{:S(2)}) collective-permute-start(f32[80,128]{1,0:T(8,128)S(1)} %get-tuple-element.43), channel_id=1, source_target_pairs={{0,1},{1,0},{2,3},{3,2},{4,5},{5,4},{6,7},{7,6},{8,9},{9,8},{10,11... | collective-permute-start | bytes 122888 | tf_op jit(solution)/shard_map/ppermute | solution.py:682
  27.2 4.0 %collective-permute-start.6 = (f32[80,128]{1,0:T(8,128)S(1)}, f32[80,128]{1,0:T(8,128)S(1)}, u32[]{:S(2)}, u32[]{:S(2)}) collective-permute-start(f32[80,128]{1,0:T(8,128)S(1)} %get-tuple-element.44), channel_id=1, source_target_pairs={{0,4},{1,2},{2,1},{3,7},{4,0},{5,6},{6,5},{7,3},{8,12},{9,10},{10,... | collective-permute-start | bytes 122888 | tf_op jit(solution)/shard_map/ppermute | solution.py:682
  27.9 3.4 %copy-start.6 = (bf16[256,256]{1,0:T(8,128)(2,1)S(1)}, bf16[256,256]{1,0:T(8,128)(2,1)}, u32[]{:S(2)}) copy-start(bf16[256,256]{1,0:T(8,128)(2,1)} %constant.22.clone.refs_4_) | copy-start | bytes 393220
  33.2 1.6 %collective-permute-start.7 = (f32[64,128]{1,0:T(8,128)S(1)}, f32[64,128]{1,0:T(8,128)S(1)}, u32[]{:S(2)}, u32[]{:S(2)}) collective-permute-start(f32[64,128]{1,0:T(8,128)S(1)} %get-tuple-element.49), channel_id=1, source_target_pairs={{0,8},{8,0},{16,24},{24,16},{1,9},{9,1},{17,25},{25,17},{2,10},{10... | collective-permute-start | bytes 98312 | tf_op jit(solution)/shard_map/ppermute | solution.py:682
  33.3 3.4 %collective-permute-start.8 = (f32[64,128]{1,0:T(8,128)S(1)}, f32[64,128]{1,0:T(8,128)S(1)}, u32[]{:S(2)}, u32[]{:S(2)}) collective-permute-start(f32[64,128]{1,0:T(8,128)S(1)} %get-tuple-element.50), channel_id=1, source_target_pairs={{0,24},{8,16},{16,8},{24,0},{1,25},{9,17},{17,9},{25,1},{2,26},{10... | collective-permute-start | bytes 98312 | tf_op jit(solution)/shard_map/ppermute | solution.py:682
  36.8 13.1 %copy-start.7 = (s32[128,128]{1,0:T(8,128)S(1)}, s32[128,128]{1,0:T(8,128)}, u32[]{:S(2)}) copy-start(s32[128,128]{1,0:T(8,128)} %constant.23.clone.refs_7_) | copy-start | bytes 196612
  36.8 13.0 %copy-start.13 = (s32[1,32]{1,0:T(1,128)S(1)}, s32[1,32]{1,0:T(1,128)}, u32[]{:S(2)}) copy-start(s32[1,32]{1,0:T(1,128)} %refs_6_.2) | copy-start | bytes 388
  36.8 4.0 %collective-permute-start.9 = (f32[64,128]{1,0:T(8,128)S(1)}, f32[64,128]{1,0:T(8,128)S(1)}, u32[]{:S(2)}, u32[]{:S(2)}) collective-permute-start(f32[64,128]{1,0:T(8,128)S(1)} %join.4), channel_id=1, source_target_pairs={{0,4},{4,0},{1,5},{5,1},{2,6},{6,2},{3,7},{7,3},{8,12},{12,8},{9,1... | collective-permute-start | bytes 98312 | tf_op jit(solution)/shard_map/ppermute | solution.py:682
  42.2 1.6 %collective-permute-start.10 = (f32[64,128]{1,0:T(8,128)S(1)}, f32[64,128]{1,0:T(8,128)S(1)}, u32[]{:S(2)}, u32[]{:S(2)}) collective-permute-start(f32[64,128]{1,0:T(8,128)S(1)} %get-tuple-element.56), channel_id=1, source_target_pairs={{0,8},{8,0},{16,24},{24,16},{1,9},{9,1},{17,25},{25,17},{2,10},{10... | collective-permute-start | bytes 98312 | tf_op jit(solution)/shard_map/ppermute | solution.py:682
  42.3 3.4 %collective-permute-start.11 = (f32[64,128]{1,0:T(8,128)S(1)}, f32[64,128]{1,0:T(8,128)S(1)}, u32[]{:S(2)}, u32[]{:S(2)}) collective-permute-start(f32[64,128]{1,0:T(8,128)S(1)} %get-tuple-element.57), channel_id=1, source_target_pairs={{0,24},{8,16},{16,8},{24,0},{1,25},{9,17},{17,9},{25,1},{2,26},{10... | collective-permute-start | bytes 98312 | tf_op jit(solution)/shard_map/ppermute | solution.py:682
  45.8 4.0 %collective-permute-start.12 = (f32[64,128]{1,0:T(8,128)S(1)}, f32[64,128]{1,0:T(8,128)S(1)}, u32[]{:S(2)}, u32[]{:S(2)}) collective-permute-start(f32[64,128]{1,0:T(8,128)S(1)} %join.5), channel_id=1, source_target_pairs={{0,4},{4,0},{1,5},{5,1},{2,6},{6,2},{3,7},{7,3},{8,12},{12,8},{9,1... | collective-permute-start | bytes 98312 | tf_op jit(solution)/shard_map/ppermute | solution.py:682

commit v2 on v1

--- a/solution.py
+++ b/solution.py
@@ -47,6 +47,9 @@
 
 
 HALO = 2
+FIELDS = 7
+VMEM_BYTES = 40 * 1024 * 1024
+FLOPS = 3 * 10**9
 F32 = jnp.float32
 BF16 = jnp.bfloat16
 
@@ -148,26 +151,20 @@
         p, c, ey, ez = self.p, self.c, self.ey, self.ez
         lanes = ez * p
         every = [(g, cc, f) for g in range(ez) for cc in range(c) for f in range(ey)]
-        spread = np.zeros((ey * lanes, self.w3), np.float32)
-        flags = np.zeros((c * ey * lanes, self.w4), np.float32)
         diagonal = np.zeros((self.w3, self.w4), np.float32)
         widen = np.zeros((2 * self.w4, 2 * self.w3), np.float32)
-        self.id3 = np.full((self.w3, 128), -1, np.int32)
-        self.id4 = np.full((self.w4, 128), -1, np.int32)
+        ids = np.full((2 * c, 128, 128), -1, np.int32)
         for g, cc, f in every:
-            for k in range(p):
-                spread[f * lanes + g * p + k, self.lane3(g, cc, f)] = 1
-                flags[(cc * ey + f) * lanes + g * p + k, self.lane4(g, cc, f)] = 1
             diagonal[self.lane3(g, 0, f), self.lane4(g, c, f)] = 1
             widen[self.lane4(g, cc, f), self.lane3(g, cc, f)] = 1
             widen[self.lane4(g, c, f), self.w3 + self.lane3(g, cc, f)] = 1
-            self.id3[self.lane3(g, cc, f), cc] = f * ez + g
-            self.id4[self.lane4(g, cc, f), cc] = f * ez + g
-        fields = 7
+            ids[cc, :, self.lane4(g, cc, f)] = f * ez + g
+            ids[c + cc, :, self.lane3(g, cc, f)] = f * ez + g
+        self.ids = np.ascontiguousarray(ids[:, :1, :]).reshape(2 * c, 128)
         part = HALO * p
         self.part = part
-        assert fields * part <= lanes
-        halo = np.zeros((2 * ey * lanes, fields * self.w3), np.float32)
+        assert FIELDS * part <= lanes and 2 * ey * part <= 128
+        halo = np.zeros((128, p, self.w3), np.float32)
         for side, first in ((0, -HALO), (1, ez)):
             for g in range(HALO):
                 for cc in range(c):
@@ -176,12 +173,10 @@
                         row = self.w4 + side * self.halo4 + g * self.step4
                         widen[row + cc * ey + f, at] = 1
                         widen[row + c * ey + f, self.w3 + at] = 1
-                        for q in range(fields):
-                            for k in range(p):
-                                halo[(side * ey + f) * lanes + q * part + g * p + k, q * self.w3 + at] = 1
-        self.spread, self.flags, self.diagonal, self.widen, self.halo = (
-            x.astype(jnp.bfloat16) for x in (spread, flags, diagonal, widen, halo)
-        )
+                        for k in range(p):
+                            halo[(side * ey + f) * part + g * p + k, k, at] = 1
+        self.halo = halo.reshape(128, -1).astype(jnp.bfloat16)
+        self.diagonal, self.widen = (x.astype(jnp.bfloat16) for x in (diagonal, widen))
         rolled = []
         for matrix in (self.forward, self.forward.T, self.squared.T):
             for d in range(p):
@@ -327,55 +322,151 @@
         last = self.n3 - self.step3
         self.fold_third(u, self.step3, lambda l: l < last, lambda l: (l >= self.step3) & (l < self.n3))
 
-    def expand(self, source, upper, lower):
-        p, ey = self.p, self.ey
-
-        def body(i, carry):
-            block = source(i)
-            width = block.shape[-1]
-            lane = lax.broadcasted_iota(jnp.int32, (p, width), 1)
-            keep = lax.rem(lane, p) == lax.broadcasted_iota(jnp.int32, (p, width), 0)
-            for f in range(ey):
-                for j in range(0, p, 2):
-                    row = f * p + j
-                    x = jnp.concatenate(
-                        [
-                            jnp.where(keep, jnp.broadcast_to(block[r : r + 1, :], (p, width)), 0.0)
-                            for r in (row, row + 1)
-                        ],
-                        axis=0,
-                    )
-                    at = pl.ds(pl.multiple_of(i * self.block + j * p, 2 * p), 2 * p)
-                    first, second = split(x)
-                    upper[at, f * width : (f + 1) * width] = first
-                    lower[at, f * width : (f + 1) * width] = second
-            return carry
-
-        lax.fori_loop(0, p, body, 0)
-
-
-    def pack_geometry(self, geometry, viscosity, *out):
-        width = geometry.shape[-1]
-        rows = self.p * self.ey * self.p
-        role = roles("gz", self.sizes["gz"])
-        lane = lax.broadcasted_iota(jnp.int32, (rows, width), 1)
-        for target, (high, _, _) in zip(out, role):
+
+    def pack_geometry(self, field, out):
+        for target, (high, _, _) in zip(out, roles("gz", self.sizes["gz"])):
+            rows, width = target.shape
+            lane = lax.broadcasted_iota(jnp.int32, (rows, width), 1)
             total = jnp.zeros((rows, width), F32)
-            for q in range(7):
-                field = (geometry[q] if q < 6 else viscosity[...]).reshape(rows, width)
+            for q in range(FIELDS):
                 start = q * self.part
-                upper = pltpu.roll(field, start + self.part, 1)
-                lower = pltpu.roll(field, start, 1) if start else field
+                upper = pltpu.roll(field(q), start + self.part, 1)
+                lower = pltpu.roll(field(q), start, 1) if start else field(q)
                 here = (lane >= start) & (lane < start + self.part)
                 total = jnp.where(here, jnp.where(high, upper, lower), total)
             target[...] = total
 
-    def prepare(self, n_x, n_y, *refs):
-        (right, slots, geometry, viscosity, dirichlet, low, high, spread, flags, diagonal, ids, table) = refs[:12]
-        s4, ind, raw, coef = refs[12:16]
-        x_out, y_out = refs[16 : 16 + n_x], refs[16 + n_x : 16 + n_x + n_y]
-        upper, lower, stiff, work = refs[16 + n_x + n_y :]
-        p, c, block, rows = self.p, self.c, self.block, self.rows
+    def by_nodes(self, upper, lower, table, store):
+        w3 = self.w3
+        for k in range(0, self.p, 2):
+            columns = table[:, k * w3 : (k + 2) * w3]
+            both = jnp.dot(upper[...], columns, preferred_element_type=F32) + jnp.dot(
+                lower[...], columns, preferred_element_type=F32
+            )
+            store(k, both[:, :w3])
+            store(k + 1, both[:, w3:])
+
+    def one_hot(self, slots, ids):
+        count = slots.shape[-1]
+        column = jnp.broadcast_to(slots[...], (count, count))
+        column = jnp.concatenate([column, jnp.zeros((count, 128 - count), jnp.int32)], axis=1)
+        column = jnp.concatenate([column, jnp.zeros((128 - count, 128), jnp.int32)], axis=0)
+        column = column.astype(F32).T[:count, :1]
+        return jnp.concatenate(
+            [jnp.where(column == ids[n : n + 1, :].astype(F32), 1.0, 0.0) for n in range(self.c)], axis=0
+        ).astype(BF16)
+
+    def spread_table(self, out):
+        p, ey, ez, w3 = self.p, self.ey, self.ez, self.w3
+        shape = (ey * ez * p, w3)
+        row = lax.broadcasted_iota(jnp.int32, shape, 0)
+        lane = lax.broadcasted_iota(jnp.int32, (1, w3), 1)
+        g = lane // self.step3 - HALO
+        element = jnp.where((g >= 0) & (g < ez), lax.rem(lane, ey) * ez + g, -1)
+        same = row // p == element
+        node = lax.rem(row, p)
+        for k in range(p):
+            out[:, k * w3 : (k + 1) * w3] = jnp.where(same & (node == k), 1.0, 0.0).astype(BF16)
+
+    def prepare(self, n_x, n_y, n_z, *refs):
+        geometry, viscosity, spread, dirichlet, table, diagonal, right, slots, ids = refs[:9]
+        s4, ind, raw, hot3 = refs[9:13]
+        refs = refs[13:]
+        x_out, y_out, z_out = refs[:n_x], refs[n_x : n_x + n_y], refs[n_x + n_y : n_x + n_y + n_z]
+        upper, lower, stiff, work = refs[n_x + n_y + n_z :]
+        p, c, block, rows, ey = self.p, self.c, self.block, self.rows, self.ey
+        width = geometry.shape[-1]
+
+        def field(q):
+            return (geometry[q] if q < FIELDS - 1 else viscosity[...]).reshape(p * ey * p, width)
+
+        for q in range(FIELDS):
+            value = field(q).reshape(p, ey, p, width)
+            for f in range(ey):
+                at = (slice(q * block, (q + 1) * block), slice(f * width, (f + 1) * width))
+                upper[at], lower[at] = split(value[:, f].reshape(block, width))
+        first_flag, flags = FIELDS * block, 2 * p
+        for cc in range(c):
+            for f in range(ey):
+                at = slice(f * p, (f + 1) * p)
+                face = jnp.concatenate([dirichlet[0, cc, at, :], dirichlet[1, cc, at, :]], axis=0)
+                to = slice(first_flag + cc * flags, first_flag + (cc + 1) * flags)
+                upper[to, f * width : (f + 1) * width] = face.astype(F32).astype(BF16)
+                lower[to, f * width : (f + 1) * width] = jnp.zeros((flags, width), BF16)
+        row = lax.broadcasted_iota(jnp.int32, (flags, self.w3), 0)
+        lane = lax.broadcasted_iota(jnp.int32, (flags, self.w3), 1)
+        ends = (lax.axis_index("gx") == 0, lax.axis_index("gx") == self.sizes["gx"] - 1)
+        here = ((row < p) & ends[0]) | ((row >= p) & ends[1])
+        owner = lax.rem(lane, self.step3) // ey
+
+        def store(k, value):
+            raw[pl.ds(k, first_flag, stride=p), :] = value[:first_flag]
+            total = jnp.zeros((flags, self.w3), F32)
+            for cc in range(c):
+                at = first_flag + cc * flags
+                total = jnp.where(owner == cc, value[at : at + flags], total)
+            ind[pl.ds(k, flags, stride=p), :] = jnp.where(here, total, 0.0)
+
+        self.by_nodes(upper, lower, spread, store)
+        self.pack_geometry(field, z_out)
+        wjk, second, third = (self.node_table(table, n) for n in range(3))
+        square = self.rolled(table, 2)
+        for i in range(p):
+            at = slice(i * block, (i + 1) * block)
+            xx, yy, zz, xy, xz, yz = (raw[q * rows + i * block : q * rows + (i + 1) * block, :] for q in range(6))
+            quadrature = float(self.weights[i]) * wjk
+            weighted = quadrature * raw[6 * rows + i * block : 6 * rows + (i + 1) * block, :]
+            mass = (helm_coefficient * quadrature) * (
+                xx * (yy * zz - yz * yz) - xy * (xy * zz - yz * xz) + xz * (xy * yz - yy * xz)
+            )
+            cross = second * third * yz
+            end = float(self.end[i])
+            if end != 0.0:
+                cross = cross + end * (second * xy + third * xz)
+            stiff[at, :] = weighted * xx
+            work[at, :] = (
+                self.along_j(weighted * yy, self.squared.T)
+                + self.along_k(weighted * zz, square)
+                + (2.0 * weighted) * cross
+                + mass
+            )
+
+        def add(row, value):
+            work[pl.ds(row, p), :] += value
+
+        self.along_i(stiff, self.squared.T, add)
+        total = dot2(work[...], diagonal[...])
+        hot = self.one_hot(slots, ids)
+        hot3[...] = self.one_hot(slots, ids[c:, :])
+        for part in split(right[...].reshape(hot.shape[0], rows)):
+            total = total + lax.dot_general(
+                part, hot, (((0,), (0,)), ((), ())), preferred_element_type=F32
+            )
+        s4[...] = total
+        self.fold_second(s4)
+        self.fold_second(ind)
+        last = self.n4 - self.step4
+        self.fold_third(s4, self.step4, lambda l: l < last, lambda l: (l >= self.step4) & (l < self.n4))
+        first_own, end_own = HALO * self.step3, self.n3 - HALO * self.step3
+        self.fold_third(
+            ind,
+            self.step3,
+            lambda l: (l >= first_own) & (l < end_own - self.step3),
+            lambda l: (l >= first_own + self.step3) & (l < end_own),
+        )
+        self.emit(s4, x_out, y_out)
+        for out, (up, _, _) in zip(y_out, roles("gy", self.sizes["gy"])):
+            for n in range(2):
+                start = n * block
+                out[block + n * p : block + (n + 1) * p, :] = jnp.where(
+                    up, ind[start + block - p : start + block, :], ind[start : start + p, :]
+                )
+
+    def halo_geometry(self, n_z, *refs):
+        raw, halo, table, low, high = refs[:5]
+        z_in, (g, coef) = refs[5 : 5 + n_z], refs[5 + n_z : 7 + n_z]
+        upper, lower, total = refs[7 + n_z :]
+        p, block, rows, ey = self.p, self.block, self.rows, self.ey
         top, bottom = jnp.full((8, 128), high[0], F32), jnp.full((8, 128), low[0], F32)
         midpoint, halfwidth = (top + bottom) * 0.5, (top - bottom) * 0.5
         ratio = midpoint / halfwidth
@@ -386,120 +477,42 @@
             coef[8 * (2 * n + 1) : 8 * (2 * n + 2), :] = following * damping
             coef[8 * (2 * n + 2) : 8 * (2 * n + 3), :] = 2.0 * following / halfwidth
             damping = following
-        def convert(q, source):
-            self.expand(source, upper, lower)
-            raw[q] = jnp.dot(upper[...], spread[...], preferred_element_type=F32) + jnp.dot(
-                lower[...], spread[...], preferred_element_type=F32
-            )
-
-        def each(q, carry):
-            convert(q, lambda i: geometry[q, i])
-            return carry
-
-        lax.fori_loop(0, 6, each, 0)
-        convert(6, lambda i: viscosity[i])
-        wjk, second, third = (self.node_table(table, n) for n in range(3))
-        square = self.rolled(table, 2)
+        source = raw
+        if n_z:
+            sides = both_sides([z[...] for z in z_in], roles("gz", self.sizes["gz"]))
+            width, part = sides[0].shape[-1], self.part
+            sides = [side.reshape(p, ey, p, width) for side in sides]
+            lane = lax.broadcasted_iota(jnp.int32, (block, width), 1)
+            for q in range(FIELDS):
+                value = jnp.zeros((block, width), F32)
+                for side in range(2):
+                    for f in range(ey):
+                        to = (side * ey + f) * part
+                        shift = (to - q * part) % width
+                        x = sides[side][:, f].reshape(block, width)
+                        x = pltpu.roll(x, shift, 1) if shift else x
+                        value = jnp.where((lane >= to) & (lane < to + part), x, value)
+                at = slice(q * block, (q + 1) * block)
+                upper[at, :], lower[at, :] = split(value)
+
+            def store(k, value):
+                at = pl.ds(k, FIELDS * block, stride=p)
+                total[at, :] = raw[at, :] + value
+
+            self.by_nodes(upper, lower, halo, store)
+            source = total
+        wjk = self.node_table(table, 0)
         for i in range(p):
             at = slice(i * block, (i + 1) * block)
-            xx, yy, zz, xy, xz, yz = (raw[q, at, :] for q in range(6))
+            entries = [source[q * rows + i * block : q * rows + (i + 1) * block, :] for q in range(FIELDS)]
+            xx, yy, zz, xy, xz, yz = entries[:6]
             quadrature = float(self.weights[i]) * wjk
-            weighted = quadrature * raw[6, at, :]
-            mass = (helm_coefficient * quadrature) * (
-                xx * (yy * zz - yz * yz) - xy * (xy * zz - yz * xz) + xz * (xy * yz - yy * xz)
-            )
-            cross = second * third * yz
-            end = float(self.end[i])
-            if end != 0.0:
-                cross = cross + end * (second * xy + third * xz)
-            stiff[at, :] = weighted * xx
-            work[at, :] = (
-                self.along_j(weighted * yy, self.squared.T)
-                + self.along_k(weighted * zz, square)
-                + (2.0 * weighted) * cross
-                + mass
-            )
-
-        def add(row, value):
-            work[pl.ds(row, p), :] += value
-
-        self.along_i(stiff, self.squared.T, add)
-        total = dot2(work[...], diagonal[...])
-        for cc in range(c):
-            hot = jnp.where(slots[...] == ids[:, cc : cc + 1], 1.0, 0.0).astype(BF16)
-            for part in split(right[cc]):
-                total = total + lax.dot_general(
-                    part, hot, (((1,), (1,)), ((), ())), preferred_element_type=F32
-                )
-        s4[...] = total
-        ends = (lax.axis_index("gx") == 0, lax.axis_index("gx") == self.sizes["gx"] - 1)
-        width = dirichlet.shape[-1]
-        lane = lax.broadcasted_iota(jnp.int32, (p, width), 1)
-        keep = lax.rem(lane, p) == lax.broadcasted_iota(jnp.int32, (p, width), 0)
-        for n, here in enumerate(ends):
-            plane = jnp.zeros((block, self.w4), F32)
-            for cc in range(c):
-                face = dirichlet[n, cc].astype(F32)
-                for f in range(self.ey):
-                    x = jnp.concatenate(
-                        [
-                            jnp.where(keep, jnp.broadcast_to(face[f * p + j : f * p + j + 1, :], (p, width)), 0.0)
-                            for j in range(p)
-                        ],
-                        axis=0,
-                    ).astype(BF16)
-                    start = (cc * self.ey + f) * width
-                    plane = plane + jnp.dot(x, flags[start : start + width, :], preferred_element_type=F32)
-            ind[n * block : (n + 1) * block, :] = jnp.where(here, plane, 0.0)
-        last = self.n4 - self.step4
-        for u in (s4, ind):
-            self.fold_second(u)
-            self.fold_third(u, self.step4, lambda l: l < last, lambda l: (l >= self.step4) & (l < self.n4))
-        self.emit(s4, x_out, y_out)
-        for out, (up, _, _) in zip(y_out, roles("gy", self.sizes["gy"])):
-            for n in range(2):
-                start = n * block
-                out[block + n * p : block + (n + 1) * p, :] = jnp.where(
-                    up, ind[start + block - p : start + block, :], ind[start : start + p, :]
-                )
-
-    def halo_geometry(self, n_z, *refs):
-        raw, halo, table = refs[:3]
-        z_in, g = refs[3 : 3 + n_z], refs[3 + n_z]
-        upper, lower, sides = refs[4 + n_z :]
-        p, block, rows, ey = self.p, self.block, self.rows, self.ey
-        if n_z:
-            low, high = both_sides([z[...] for z in z_in], roles("gz", self.sizes["gz"]))
-            sides[0], sides[1] = low, high
-            width = low.shape[-1]
-            for side in range(2):
-                at = slice(side * ey * width, (side + 1) * ey * width)
-                self.expand(
-                    lambda i: sides[side, pl.ds(pl.multiple_of(i * ey * p, ey * p), ey * p), :],
-                    upper.at[:, at],
-                    lower.at[:, at],
-                )
-        wjk = self.node_table(table, 0)
-        fields = []
-        for q in range(7):
-            field = raw[q]
-            if n_z:
-                columns = halo[:, q * self.w3 : (q + 1) * self.w3]
-                field = field + (
-                    jnp.dot(upper[...], columns, preferred_element_type=F32)
-                    + jnp.dot(lower[...], columns, preferred_element_type=F32)
-                )
-            g[q] = field
-        for i in range(p):
-            at = slice(i * block, (i + 1) * block)
-            xx, yy, zz, xy, xz, yz = (g[q, at, :] for q in range(6))
-            quadrature = float(self.weights[i]) * wjk
-            weighted = quadrature * g[6, at, :]
+            weighted = quadrature * entries[6]
             g[6, at, :] = (helm_coefficient * quadrature) * (
                 xx * (yy * zz - yz * yz) - xy * (xy * zz - yz * xz) + xz * (xy * yz - yy * xz)
             )
-            for q, entry in enumerate((xx, yy, zz, xy, xz, yz)):
-                g[q, at, :] = weighted * entry
+            for q in range(6):
+                g[q, at, :] = weighted * entries[q]
 
     def join(self, n_x, n_y, *refs):
         x_in, y_raw, y_out = refs[:n_x], refs[n_x : n_x + n_y], refs[n_x + n_y :]
@@ -540,33 +553,25 @@
                     u[at : at + p, :] += low[row : row + p]
                     u[end - p : end, :] += high[row : row + p]
         width, size = self.w4, self.halo4
+        own3, halo3 = HALO * self.step3, HALO * self.step3
         for out, (up, _, _) in zip(z_out, roles("gz", self.sizes["gz"])):
-            for u, count, start in ((s_out, block, 0), (i_out, p, block)):
-                groups = u.shape[0] // count
+            for u, count, first, last, start in (
+                (s_out, block, 0, self.n4 - size, 0),
+                (i_out, p, own3, self.n3 - 2 * halo3, block),
+            ):
                 lane = lax.broadcasted_iota(jnp.int32, (count, width), 1)
-                for section in range(0, groups, p):
+                for section in range(0, u.shape[0] // count, p):
                     total = jnp.zeros((count, width), F32)
                     for n in range(p):
                         at = (section + n) * count
                         x = u[at : at + count, :]
                         shift = n * size
-                        below = pltpu.roll(x, shift, 1) if shift else x
-                        above = pltpu.roll(x, (shift + width - self.n4 + size) % width, 1)
+                        below = pltpu.roll(x, (shift - first) % width, 1) if (shift - first) % width else x
+                        above = pltpu.roll(x, (shift - last) % width, 1)
                         here = (lane >= shift) & (lane < shift + size)
                         total = jnp.where(here, jnp.where(up, above, below), total)
                     row = start + section // p * count
                     out[row : row + count, :] = total
-
-    def wide(self, own, low, high, groups, count, put):
-        size, width = self.halo4, self.w4
-        lane = lax.broadcasted_iota(jnp.int32, (count, width), 1)
-        for n in range(groups):
-            shift = (width - (n % self.p) * size) % width
-            row = (n // self.p) * count
-            first = pltpu.roll(low[row : row + count], shift, 1) if shift else low[row : row + count]
-            second = pltpu.roll(high[row : row + count], (shift + size) % width, 1)
-            beside = jnp.where(lane < size, first, jnp.where(lane < 2 * size, second, 0.0))
-            put(n * count, jnp.concatenate([own[n * count : (n + 1) * count, :], beside], axis=1))
 
     def start(self, n_x, n_y, n_z, *refs):
         s4, ind, g, coef, widen, table = refs[:6]
@@ -574,32 +579,37 @@
         t, d, scale, v = refs[6 + n_z : 10 + n_z]
         refs = refs[10 + n_z :]
         x_out, y_out = refs[:n_x], refs[n_x : n_x + n_y]
-        upper, lower, flag_lhs, r, flag, slope, flux = refs[n_x + n_y :]
-        p, block, rows, w3 = self.p, self.block, self.rows, self.w3
-        size = self.sizes["gz"]
+        upper, lower, r, flag, slope, flux = refs[n_x + n_y :]
+        p, block, rows, w3, w4 = self.p, self.block, self.rows, self.w3, self.w4
+        step, first_own, end_own = self.step3, HALO * self.step3, self.n3 - HALO * self.step3
+        size, part = self.sizes["gz"], self.halo4
         if n_z:
             low, high = both_sides([z[...] for z in z_in], roles("gz", size))
         else:
-            low = high = jnp.zeros((block + 2 * p, self.w4), F32)
-
-        def put(at, x):
-            first, second = split(x)
-            upper[at : at + block, :] = first
-            lower[at : at + block, :] = second
-
-        self.wide(s4, low, high, p, block, put)
-
-        def put_flag(at, x):
-            flag_lhs[at : at + p, :] = x
-
-        self.wide(ind, low[block:], high[block:], 2 * p, p, put_flag)
+            low = high = jnp.zeros((block + 2 * p, w4), F32)
+        lane = lax.broadcasted_iota(jnp.int32, (block, w4), 1)
+        for n in range(p):
+            first = pltpu.roll(low[:block], w4 - n * part, 1) if n else low[:block]
+            second = pltpu.roll(high[:block], (part - n * part) % w4, 1) if n != 1 else high[:block]
+            beside = jnp.where(lane < part, first, jnp.where(lane < 2 * part, second, 0.0))
+            at = slice(n * block, (n + 1) * block)
+            upper[at, :w4], lower[at, :w4] = split(s4[at, :])
+            upper[at, w4:], lower[at, w4:] = split(beside)
         both = jnp.dot(upper[...], widen[...], preferred_element_type=F32) + jnp.dot(
             lower[...], widen[...], preferred_element_type=F32
         )
         r[...] = both[:, :w3]
         scale[...] = both[:, w3:]
-        flag[...] = jnp.dot(flag_lhs[...].astype(BF16), widen[:, :w3], preferred_element_type=F32)
-        step, first_own, end_own = self.step3, HALO * self.step3, self.n3 - HALO * self.step3
+        lane = lax.broadcasted_iota(jnp.int32, (p, w3), 1)
+        for n in range(2 * p):
+            row, shift = block + n // p * p, n % p * part
+            first = pltpu.roll(low[row : row + p], w3 - shift, 1) if shift else low[row : row + p]
+            second = pltpu.roll(high[row : row + p], (end_own - shift) % w3, 1)
+            flag[n * p : (n + 1) * p, :] = jnp.where(
+                lane < first_own,
+                first,
+                jnp.where(lane < end_own, ind[n * p : (n + 1) * p, :], jnp.where(lane < self.n3, second, 0.0)),
+            )
         for u in (r, scale, flag):
             self.fold_third(
                 u,
@@ -653,8 +663,8 @@
         self.emit(v_new, x_out, y_out)
 
     def finish(self, n_x, n_y, which, *refs):
-        t, d, scale, v, total, coef, slots, ids = refs[:8]
-        refs = refs[8:]
+        t, d, scale, v, total, coef, hot = refs[:7]
+        refs = refs[7:]
         x_in, y_in, refs = refs[:n_x], refs[n_x : n_x + n_y], refs[n_x + n_y :]
         out, t_new, field = refs
 
@@ -662,12 +672,13 @@
             field[at, :] = total[at, :] + x
 
         self.advance(t, t_new, d, v, scale, coef, which, x_in, y_in, put)
-        upper, lower = split(field[...])
-        for cc in range(self.c):
-            hot = jnp.where(slots[...] == ids[:, cc : cc + 1], 1.0, 0.0).astype(BF16)
-            out[cc] = jnp.dot(upper, hot, preferred_element_type=F32) + jnp.dot(
-                lower, hot, preferred_element_type=F32
-            )
+        value = None
+        for part in split(field[...]):
+            term = lax.dot_general(
+                hot[...], part, (((1,), (1,)), ((), ())), preferred_element_type=F32
+            )
+            value = term if value is None else value + term
+        out[...] = value.reshape(out.shape)
 
 
 def shards(sizes, right_side, geometry, viscosity, eig_low, eig_high, element_slot, dirichlet):
@@ -684,78 +695,83 @@
     def shape(*size, dtype=F32):
         return jax.ShapeDtypeStruct(size, dtype)
 
-    def call(kernel, outputs, operands, scratch=(), scalars=(), flops=0, name=None):
-        specs = [
-            pl.BlockSpec(memory_space=pltpu.SMEM if n in scalars else pltpu.VMEM)
-            for n in range(len(operands))
-        ]
-        return list(pl.pallas_call(
-            kernel,
-            out_shape=list(outputs),
-            in_specs=specs,
-            out_specs=[pl.BlockSpec(memory_space=pltpu.VMEM)] * len(outputs),
-            scratch_shapes=list(scratch),
-            compiler_params=pltpu.CompilerParams(vmem_limit_bytes=40 * 1024 * 1024),
-            cost_estimate=pl.CostEstimate(flops=flops, bytes_accessed=0, transcendentals=0),
-            name=name,
-        )(*operands))
+    def call(kernel, outputs, operands, scratch=(), spaces={}, flops=0, name=None):
+        specs = [pl.BlockSpec(memory_space=spaces.get(n, pltpu.VMEM)) for n in range(len(operands))]
+        return list(
+            pl.pallas_call(
+                kernel,
+                out_shape=list(outputs),
+                in_specs=specs,
+                out_specs=[pl.BlockSpec(memory_space=pltpu.VMEM)] * len(outputs),
+                scratch_shapes=list(scratch),
+                compiler_params=pltpu.CompilerParams(vmem_limit_bytes=VMEM_BYTES),
+                cost_estimate=pl.CostEstimate(flops=flops, bytes_accessed=0, transcendentals=0),
+                name=name,
+            )(*operands)
+        )
 
     def vmem(*size, dtype=F32):
         return pltpu.VMEM(size, dtype)
 
     lanes = plan.ez * p
     table = jnp.asarray(plan.table)
-    faces = [shape(plan.p * plan.ey * p, lanes)] * n_z
-    z_geometry = call(plan.pack_geometry, faces, (geometry, viscosity), name="pack_geometry") if n_z else []
-    z_geometry = send(z_geometry, ("gy", "gz"), z_pairs)
-
     field3, field4 = shape(rows, w3), shape(rows, w4)
+    elements = element_slot.shape[-1]
+    spread = call(
+        plan.spread_table, [shape(plan.ey * lanes, p * w3, dtype=BF16)], (), flops=FLOPS, name="spread_table"
+    )[0]
+    operands = (
+        geometry,
+        viscosity,
+        spread,
+        dirichlet,
+        table,
+        jnp.asarray(plan.diagonal),
+        jnp.swapaxes(right_side, 1, 2),
+        element_slot,
+        jnp.asarray(plan.ids),
+    )
+    lhs = FIELDS * block + 2 * plan.c * p
     results = call(
-        functools.partial(plan.prepare, n_x, n_y),
-        [field4, shape(2 * block, w4), shape(7, rows, w3), shape(8 * (2 * ITERS - 1), 128)]
+        functools.partial(plan.prepare, n_x, n_y, n_z),
+        [
+            field4,
+            shape(2 * block, w3),
+            shape(FIELDS * rows, w3),
+            shape(plan.c * elements, w3, dtype=BF16),
+        ]
         + [shape(block, w4)] * n_x
-        + [shape(block + 2 * p, w4)] * n_y,
-        (
-            right_side,
-            element_slot,
-            geometry,
-            viscosity,
-            dirichlet,
-            eig_low,
-            eig_high,
-            jnp.asarray(plan.spread),
-            jnp.asarray(plan.flags),
-            jnp.asarray(plan.diagonal),
-            jnp.asarray(plan.id4),
-            table,
-        ),
-        scratch=[vmem(rows, plan.ey * lanes, dtype=BF16)] * 2 + [vmem(rows, w3)] * 2,
-        scalars=(5, 6),
+        + [shape(block + 2 * p, w4)] * n_y
+        + [shape(p * plan.ey * p, lanes)] * n_z,
+        operands,
+        scratch=[vmem(lhs, plan.ey * lanes, dtype=BF16)] * 2 + [vmem(rows, w3)] * 2,
         name="prepare",
     )
-    s4, ind, raw, coef = results[:4]
-    x_out, y_raw = results[4 : 4 + n_x], results[4 + n_x :]
+    s4, ind, raw, hot3 = results[:4]
+    results = results[4:]
+    x_out, y_raw, z_geometry = results[:n_x], results[n_x : n_x + n_y], results[n_x + n_y :]
     x_in = send(x_out, "gx", x_pairs)
-
-    g = call(
-        functools.partial(plan.halo_geometry, n_z),
-        [shape(7, rows, w3)],
-        [raw, jnp.asarray(plan.halo), table] + z_geometry,
-        scratch=[vmem(rows, 2 * plan.ey * lanes, dtype=BF16)] * 2 + [vmem(2, plan.p * plan.ey * p, lanes)],
-        flops=2000000,
-        name="halo_geometry",
-    )[0]
-
-    def second(x_in, y_raw):
+    def joined(x_in, y_raw):
         if not y_raw:
             return []
         faces = [shape(*y.shape) for y in y_raw]
-        return send(call(functools.partial(plan.join, n_x, n_y), faces, x_in + y_raw, name="join"), "gy", y_pairs)
-
-    y_in = second(x_in, y_raw)
+        return call(functools.partial(plan.join, n_x, n_y), faces, x_in + y_raw, name="join")
+
+    y_in = send(joined(x_in, y_raw), "gy", y_pairs)
+    z_geometry = send(z_geometry, ("gy", "gz"), z_pairs)
+    g, coef = call(
+        functools.partial(plan.halo_geometry, n_z),
+        [shape(FIELDS, rows, w3), shape(8 * (2 * ITERS - 1), 128)],
+        [raw, jnp.asarray(plan.halo), table, eig_low, eig_high] + z_geometry,
+        scratch=[vmem(FIELDS * block, 128, dtype=BF16)] * 2 + [vmem(FIELDS * rows, w3)],
+        spaces={3: pltpu.SMEM, 4: pltpu.SMEM},
+        flops=2000000,
+        name="halo_geometry",
+    )
+
     results = call(
         functools.partial(plan.pack, n_x, n_y),
-        [field4, shape(2 * block, w4)] + [shape(block + 2 * p, w4)] * n_z,
+        [field4, shape(2 * block, w3)] + [shape(block + 2 * p, w4)] * n_z,
         [s4, ind] + x_in + y_in,
         name="pack",
     )
@@ -768,7 +784,7 @@
         [field3] * 4 + messages,
         [s4, ind, g, coef, jnp.asarray(plan.widen), table] + z_in,
         scratch=[vmem(rows, 2 * w4, dtype=BF16)] * 2
-        + [vmem(2 * block, 2 * w4), vmem(rows, w3), vmem(2 * block, w3), vmem(rows, w3), vmem(rows, w3)],
+        + [vmem(rows, w3), vmem(2 * block, w3), vmem(rows, w3), vmem(rows, w3)],
         name="first_direction",
     )
     t, d, scale, v = results[:4]
@@ -776,7 +792,7 @@
     for n in range(ITERS - 1):
         x_out, y_raw = results[4 : 4 + n_x], results[4 + n_x :]
         x_in = send(x_out, "gx", x_pairs)
-        y_in = second(x_in, y_raw)
+        y_in = send(joined(x_in, y_raw), "gy", y_pairs)
         if n < ITERS - 2:
             results = call(
                 functools.partial(plan.middle, n_x, n_y, n),
@@ -787,13 +803,14 @@
             )
             t, d, v, total = results[:4]
         else:
-            return call(
+            out = call(
                 functools.partial(plan.finish, n_x, n_y, n),
-                [shape(*right_side.shape)],
-                [t, d, scale, v, total, coef, element_slot, jnp.asarray(plan.id3)] + x_in + y_in,
+                [shape(plan.c, elements, rows)],
+                [t, d, scale, v, total, coef, hot3] + x_in + y_in,
                 scratch=[vmem(rows, w3)] * 2,
                 name="field",
             )[0]
+            return jnp.swapaxes(out, 1, 2)
 
 
 def solution(mesh):

time: 51.7 us -> 39 us (0.75)
  local copies, waits for them, and re-layouts: 9.75 us -> 1.03 us
  Pallas kernels: 12.2 us -> 8.85 us
  waiting for transfers between devices: 12.9 us -> 12.1 us
    unnamed x29 -> x20, local copies, waits for them, and re-layouts: 8.83 us -> 1.03 us
    pallas_call x10, Pallas kernels: 12.2 us -> 8.85 us  [call(): pl.pallas_call(kernel, out_shape=list(outputs), in_specs=specs, out_specs...]
    pallas_call x1 -> x0, local copies, waits for them, and re-layouts: 0.92 us -> none  [call(): pl.pallas_call(kernel, out_shape=list(outputs), in_specs=specs, out_specs...]
    ppermute x13, waiting for transfers between devices: 12.9 us -> 12.1 us  [send(): return [lax.ppermute(x, axis, pair) for x, pair in zip(arrays, pairs)]]
  transfers between devices with their start and end apart: 13 -> 13, of which waited for: 7 -> 7; matrix products, arithmetic and copies ran while one was open for 0% -> 0% of each run, Pallas kernels for 7% -> 5%
where the time goes in v2:
time: 39 us; the launch traced here: 38.8 us
  starting transfers between devices  15.4 us (39%)
  waiting for transfers between devices  12.1 us (31%)
  Pallas kernels  8.85 us (23%)
  between operations  1.48 us (4%)
  local copies, waits for them, and re-layouts  1.03 us (3%)
    ppermute x13, starting transfers between devices, send(): return [lax.ppermute(x, axis, pair) for x, pair in zip(arrays, pairs)]  15.4 us
    ppermute x13, waiting for transfers between devices, send(): return [lax.ppermute(x, axis, pair) for x, pair in zip(arrays, pairs)]  12.1 us
    pallas_call x10, Pallas kernels, call(): pl.pallas_call(kernel, out_shape=list(outputs), in_specs=specs, out_specs...  8.85 us
    unnamed x20, local copies, waits for them, and re-layouts  1.03 us
  transfers between devices with their start and end apart: 13, of which 7 were waited for; matrix products, arithmetic and copies ran while one was open for 0% of the time, Pallas kernels for 5%

profile of v2, /device:TPU:0, one launch (start us, length us, event | category | flops | bytes accessed | tf_op | source)
XLA Modules:
  0.0 38.8 jit_solution(14338196105373322129)
XLA Ops:
  0.0 0.2 spread_table.1.refs_2_
  0.3 0.7 %copy-done = f32[384,128]{1,0:T(8,128)S(1)} copy-done((f32[384,128]{1,0:T(8,128)S(1)}, f32[384,128]{1,0:T(8,128)}, u32[]{:S(2)}) %copy-start) | copy-done | bytes 196632
  1.0 0.2 copy-done.1
  1.3 2.2 %prepare.1 = (f32[512,128]{1,0:T(8,128)S(1)}, f32[128,128]{1,0:T(8,128)S(1)}, f32[3584,128]{1,0:T(8,128)S(1)}, bf16[96,128]{1,0:T(8,128)(2,1)S(1)}, f32[64,128]{...) custom-call(f32[6,8,16,128]{3,2,1,0:T(8,128)S(1)} %copy-done.1, ...), custom_call_target="tpu_custom_call" | custom-call | tf_op jit(solution)/shard_map/prepare/pallas_call | solution.py:701
  3.5 0.5 %collective-permute-start = (f32[64,128]{1,0:T(8,128)S(1)}, f32[64,128]{1,0:T(8,128)S(1)}, u32[]{:S(2)}, u32[]{:S(2)}) collective-permute-start(f32[64,128]{1,0:T(8,128)S(1)} %get-tuple-element.36), channel_id=1, source_target_pairs={{0,8},{8,0},{16,24},{24,16},{1,9},{9,1},{17,25},{25,17},{2,10},{10... | collective-permute-start | bytes 98312 | tf_op jit(solution)/shard_map/ppermute | solution.py:693
  4.1 2.6 %collective-permute-start.1 = (f32[64,128]{1,0:T(8,128)S(1)}, f32[64,128]{1,0:T(8,128)S(1)}, u32[]{:S(2)}, u32[]{:S(2)}) collective-permute-start(f32[64,128]{1,0:T(8,128)S(1)} %get-tuple-element.37), channel_id=1, source_target_pairs={{0,24},{8,16},{16,8},{24,0},{1,25},{9,17},{17,9},{25,1},{2,26},{10... | collective-permute-start | bytes 98312 | tf_op jit(solution)/shard_map/ppermute | solution.py:693
  6.7 1.7 %collective-permute-done.1.refs_1_.refs_3_ = f32[64,128]{1,0:T(8,128)S(1)} collective-permute-done((f32[64,128]{1,0:T(8,128)S(1)}, f32[64,128]{1,0:T(8,128)S(1)}, u32[]{:S(2)}, u32[]{:S(2)}) %collective-permute-start.1) | collective-permute-done | bytes 32800 | tf_op jit(solution)/shard_map/ppermute | solution.py:693
  8.3 0.1 join.3
  8.4 1.7 %collective-permute-start.2 = (f32[80,128]{1,0:T(8,128)S(1)}, f32[80,128]{1,0:T(8,128)S(1)}, u32[]{:S(2)}, u32[]{:S(2)}) collective-permute-start(f32[80,128]{1,0:T(8,128)S(1)} %join.3), channel_id=1, source_target_pairs={{0,4},{4,0},{1,5},{5,1},{2,6},{6,2},{3,7},{7,3},{8,12},{12,8},{9,1... | collective-permute-start | bytes 122888 | tf_op jit(solution)/shard_map/ppermute | solution.py:693
  10.1 1.6 %collective-permute-start.3 = (f32[128,128]{1,0:T(8,128)S(1)}, f32[128,128]{1,0:T(8,128)S(1)}, u32[]{:S(2)}, u32[]{:S(2)}) collective-permute-start(f32[128,128]{1,0:T(8,128)S(1)} %get-tuple-element.42), channel_id=1, source_target_pairs={{0,1},{1,0},{2,3},{3,2},{4,5},{5,4},{6,7},{7,6},{8,9},{9,8},{10,11... | collective-permute-start | bytes 196616 | tf_op jit(solution)/shard_map/ppermute | solution.py:693
  11.7 0.5 %collective-permute-start.4 = (f32[128,128]{1,0:T(8,128)S(1)}, f32[128,128]{1,0:T(8,128)S(1)}, u32[]{:S(2)}, u32[]{:S(2)}) collective-permute-start(f32[128,128]{1,0:T(8,128)S(1)} %get-tuple-element.43), channel_id=1, source_target_pairs={{0,4},{1,2},{2,1},{3,7},{4,0},{5,6},{6,5},{7,3},{8,12},{9,10},{10,... | collective-permute-start | bytes 196616 | tf_op jit(solution)/shard_map/ppermute | solution.py:693
  12.2 0.3 collective-permute-done.2.refs_4_
  12.5 0.4 pack.1
  12.9 2.4 %collective-permute-start.5 = (f32[80,128]{1,0:T(8,128)S(1)}, f32[80,128]{1,0:T(8,128)S(1)}, u32[]{:S(2)}, u32[]{:S(2)}) collective-permute-start(f32[80,128]{1,0:T(8,128)S(1)} %get-tuple-element.46), channel_id=1, source_target_pairs={{0,1},{1,0},{2,3},{3,2},{4,5},{5,4},{6,7},{7,6},{8,9},{9,8},{10,11... | collective-permute-start | bytes 122888 | tf_op jit(solution)/shard_map/ppermute | solution.py:693
  15.3 0.8 %collective-permute-start.6 = (f32[80,128]{1,0:T(8,128)S(1)}, f32[80,128]{1,0:T(8,128)S(1)}, u32[]{:S(2)}, u32[]{:S(2)}) collective-permute-start(f32[80,128]{1,0:T(8,128)S(1)} %get-tuple-element.47), channel_id=1, source_target_pairs={{0,4},{1,2},{2,1},{3,7},{4,0},{5,6},{6,5},{7,3},{8,12},{9,10},{10,... | collective-permute-start | bytes 122888 | tf_op jit(solution)/shard_map/ppermute | solution.py:693
  17.5 1.4 %halo_geometry.1 = (f32[7,512,128]{2,1,0:T(8,128)S(1)}, f32[40,128]{1,0:T(8,128)S(1)}) custom-call(f32[3584,128]{1,0:T(8,128)S(1)} %get-tuple-element.41.refs_0_, bf16[128,1024]{1,0:T(8,128)(2,1)S(1)} %copy-done.2, f32[384,128]{1,0:T(8,128)S(1)} %copy-done, f32[1]{0:T(128)S(6)} %copy.13.refs_3_, f32[1]{0:T(128)S(6)} %copy.14.refs_4_, ...), custom_call_target="tpu_custom_call" | custom-call | flops 2000000 | tf_op jit(solution)/shard_map/halo_geometry/pallas_call | solution.py:701
  18.9 0.4 collective-permute-done.6.refs_7_
  19.3 1.9 %first_direction.1 = (f32[512,128]{1,0:T(8,128)S(1)}, f32[512,128]{1,0:T(8,128)S(1)}, f32[512,128]{1,0:T(8,128)S(1)}, f32[512,128]{1,0:T(8,128)S(1)}, f32[64,128...) custom-call(f32[512,128]{1,0:T(8,128)S(1)} %get-tuple-element.39.refs_0_, ...), custom_call_target="tpu_custom_call" | custom-call | tf_op jit(solution)/shard_map/first_direction/pallas_call | solution.py:701
  21.2 0.1 collective-permute-start.7
  21.3 1.6 %collective-permute-start.8 = (f32[64,128]{1,0:T(8,128)S(1)}, f32[64,128]{1,0:T(8,128)S(1)}, u32[]{:S(2)}, u32[]{:S(2)}) collective-permute-start(f32[64,128]{1,0:T(8,128)S(1)} %get-tuple-element.53), channel_id=1, source_target_pairs={{0,24},{8,16},{16,8},{24,0},{1,25},{9,17},{17,9},{25,1},{2,26},{10... | collective-permute-start | bytes 98312 | tf_op jit(solution)/shard_map/ppermute | solution.py:693
  22.9 1.8 %collective-permute-done.8.refs_1_.refs_9_ = f32[64,128]{1,0:T(8,128)S(1)} collective-permute-done((f32[64,128]{1,0:T(8,128)S(1)}, f32[64,128]{1,0:T(8,128)S(1)}, u32[]{:S(2)}, u32[]{:S(2)}) %collective-permute-start.8) | collective-permute-done | bytes 32800 | tf_op jit(solution)/shard_map/ppermute | solution.py:693
  24.7 0.1 join.4
  24.8 0.9 %collective-permute-start.9 = (f32[64,128]{1,0:T(8,128)S(1)}, f32[64,128]{1,0:T(8,128)S(1)}, u32[]{:S(2)}, u32[]{:S(2)}) collective-permute-start(f32[64,128]{1,0:T(8,128)S(1)} %join.4), channel_id=1, source_target_pairs={{0,4},{4,0},{1,5},{5,1},{2,6},{6,2},{3,7},{7,3},{8,12},{12,8},{9,1... | collective-permute-start | bytes 98312 | tf_op jit(solution)/shard_map/ppermute | solution.py:693
  25.7 3.1 %collective-permute-done.9.refs_10_ = f32[64,128]{1,0:T(8,128)S(1)} collective-permute-done((f32[64,128]{1,0:T(8,128)S(1)}, f32[64,128]{1,0:T(8,128)S(1)}, u32[]{:S(2)}, u32[]{:S(2)}) %collective-permute-start.9) | collective-permute-done | bytes 32800 | tf_op jit(solution)/shard_map/ppermute | solution.py:693
  28.8 1.5 %direction.1 = (f32[512,128]{1,0:T(8,128)S(1)}, f32[512,128]{1,0:T(8,128)S(1)}, f32[512,128]{1,0:T(8,128)S(1)}, f32[512,128]{1,0:T(8,128)S(1)}, f32[64,128]{1,0:...) custom-call(f32[512,128]{1,0:T(8,128)S(1)} %get-tuple-element.48.refs_0_, ...), custom_call_target="tpu_custom_call" | custom-call | tf_op jit(solution)/shard_map/direction/pallas_call | solution.py:701
  30.3 0.1 collective-permute-start.10
  30.4 1.6 %collective-permute-start.11 = (f32[64,128]{1,0:T(8,128)S(1)}, f32[64,128]{1,0:T(8,128)S(1)}, u32[]{:S(2)}, u32[]{:S(2)}) collective-permute-start(f32[64,128]{1,0:T(8,128)S(1)} %get-tuple-element.61), channel_id=1, source_target_pairs={{0,24},{8,16},{16,8},{24,0},{1,25},{9,17},{17,9},{25,1},{2,26},{10... | collective-permute-start | bytes 98312 | tf_op jit(solution)/shard_map/ppermute | solution.py:693
  32.0 1.8 %collective-permute-done.11.refs_1_.refs_8_ = f32[64,128]{1,0:T(8,128)S(1)} collective-permute-done((f32[64,128]{1,0:T(8,128)S(1)}, f32[64,128]{1,0:T(8,128)S(1)}, u32[]{:S(2)}, u32[]{:S(2)}) %collective-permute-start.11) | collective-permute-done | bytes 32800 | tf_op jit(solution)/shard_map/ppermute | solution.py:693
  33.8 0.1 join.5
  33.9 0.9 %collective-permute-start.12 = (f32[64,128]{1,0:T(8,128)S(1)}, f32[64,128]{1,0:T(8,128)S(1)}, u32[]{:S(2)}, u32[]{:S(2)}) collective-permute-start(f32[64,128]{1,0:T(8,128)S(1)} %join.5), channel_id=1, source_target_pairs={{0,4},{4,0},{1,5},{5,1},{2,6},{6,2},{3,7},{7,3},{8,12},{12,8},{9,1... | collective-permute-start | bytes 98312 | tf_op jit(solution)/shard_map/ppermute | solution.py:693
  34.8 3.1 %collective-permute-done.12.refs_9_ = f32[64,128]{1,0:T(8,128)S(1)} collective-permute-done((f32[64,128]{1,0:T(8,128)S(1)}, f32[64,128]{1,0:T(8,128)S(1)}, u32[]{:S(2)}, u32[]{:S(2)}) %collective-permute-start.12) | collective-permute-done | bytes 32800 | tf_op jit(solution)/shard_map/ppermute | solution.py:693
  37.8 1.0 %field.1 = f32[3,32,512]{2,1,0:T(8,128)} custom-call(f32[512,128]{1,0:T(8,128)S(1)} %get-tuple-element.55.refs_0_, f32[512,128]{1,0:T(8,128)S(1)} %get-tuple-element.56.refs_1_, f32[512,128]{1,0:T(8,128)S(1)} %get-tuple-element.50.refs_2_, f32[512,128]{1,0:T(8,128)S(1)} %get-tuple-element.57.refs_3_, f32[512,128]{1,0:T(8,128)S(1)} %get-tuple-element.58.refs_4_, ...), custom_call_target="tpu_custom_call" | custom-call | tf_op jit(solution)/shard_map/field/pallas_call | solution.py:701
  (24 shorter events, 0.2 us)
Async XLA Ops:
  0.0 0.9 %copy-start = (f32[384,128]{1,0:T(8,128)S(1)}, f32[384,128]{1,0:T(8,128)}, u32[]{:S(2)}) copy-start(f32[384,128]{1,0:T(8,128)} %constant.10.clone.refs_4_.refs_2_.refs_5_.refs_7_) | copy-start | bytes 589828
  0.0 0.9 %copy-start.7 = (bf16[128,128]{1,0:T(8,128)(2,1)S(1)}, bf16[128,128]{1,0:T(8,128)(2,1)}, u32[]{:S(2)}) copy-start(bf16[128,128]{1,0:T(8,128)(2,1)} %constant.11.clone.refs_5_) | copy-start | bytes 98308
  0.0 0.9 %copy-start.8 = (s32[6,128]{1,0:T(8,128)S(1)}, s32[6,128]{1,0:T(8,128)}, u32[]{:S(2)}) copy-start(s32[6,128]{1,0:T(8,128)} %constant.12.clone.refs_8_) | copy-start | bytes 9220
  0.0 0.9 %copy-start.6 = (s32[2,3,16,128]{3,2,1,0:T(8,128)S(1)}, s32[2,3,16,128]{3,2,1,0:T(8,128)}, u32[]{:S(2)}) copy-start(s32[2,3,16,128]{3,2,1,0:T(8,128)} %refs_3_.2) | copy-start | bytes 147460
  0.0 0.9 %copy-start.9 = (s32[1,32]{1,0:T(1,128)S(1)}, s32[1,32]{1,0:T(1,128)}, u32[]{:S(2)}) copy-start(s32[1,32]{1,0:T(1,128)} %refs_7_.2) | copy-start | bytes 388
  0.0 1.0 %copy-start.5 = (f32[8,16,128]{2,1,0:T(8,128)S(1)}, f32[8,16,128]{2,1,0:T(8,128)}, u32[]{:S(2)}) copy-start(f32[8,16,128]{2,1,0:T(8,128)} %refs_1_.2) | copy-start | bytes 196612
  0.0 1.2 %copy-start.1 = (f32[6,8,16,128]{3,2,1,0:T(8,128)S(1)}, f32[6,8,16,128]{3,2,1,0:T(8,128)}, u32[]{:S(2)}) copy-start(f32[6,8,16,128]{3,2,1,0:T(8,128)} %refs_0_.1) | copy-start | bytes 1179652
  0.0 1.2 %copy-start.3 = (f32[3,512,32]{1,2,0:T(8,128)S(1)}, f32[3,512,32]{1,2,0:T(8,128)}, u32[]{:S(2)}) copy-start(f32[3,512,32]{1,2,0:T(8,128)} %param.12) | copy-start | bytes 589828
  0.2 17.3 %copy-start.2 = (bf16[128,1024]{1,0:T(8,128)(2,1)S(1)}, bf16[128,1024]{1,0:T(8,128)(2,1)}, u32[]{:S(2)}) copy-start(bf16[128,1024]{1,0:T(8,128)(2,1)} %constant.13.clone.refs_1_) | copy-start | bytes 786436
  3.5 15.8 %copy-start.4 = (bf16[256,256]{1,0:T(8,128)(2,1)S(1)}, bf16[256,256]{1,0:T(8,128)(2,1)}, u32[]{:S(2)}) copy-start(bf16[256,256]{1,0:T(8,128)(2,1)} %constant.14.clone.refs_4_) | copy-start | bytes 393220
  3.5 3.1 %collective-permute-start = (f32[64,128]{1,0:T(8,128)S(1)}, f32[64,128]{1,0:T(8,128)S(1)}, u32[]{:S(2)}, u32[]{:S(2)}) collective-permute-start(f32[64,128]{1,0:T(8,128)S(1)} %get-tuple-element.36), channel_id=1, source_target_pairs={{0,8},{8,0},{16,24},{24,16},{1,9},{9,1},{17,25},{25,17},{2,10},{10... | collective-permute-start | bytes 98312 | tf_op jit(solution)/shard_map/ppermute | solution.py:693
  4.1 4.3 %collective-permute-start.1 = (f32[64,128]{1,0:T(8,128)S(1)}, f32[64,128]{1,0:T(8,128)S(1)}, u32[]{:S(2)}, u32[]{:S(2)}) collective-permute-start(f32[64,128]{1,0:T(8,128)S(1)} %get-tuple-element.37), channel_id=1, source_target_pairs={{0,24},{8,16},{16,8},{24,0},{1,25},{9,17},{17,9},{25,1},{2,26},{10... | collective-permute-start | bytes 98312 | tf_op jit(solution)/shard_map/ppermute | solution.py:693
  8.4 4.1 %collective-permute-start.2 = (f32[80,128]{1,0:T(8,128)S(1)}, f32[80,128]{1,0:T(8,128)S(1)}, u32[]{:S(2)}, u32[]{:S(2)}) collective-permute-start(f32[80,128]{1,0:T(8,128)S(1)} %join.3), channel_id=1, source_target_pairs={{0,4},{4,0},{1,5},{5,1},{2,6},{6,2},{3,7},{7,3},{8,12},{12,8},{9,1... | collective-permute-start | bytes 122888 | tf_op jit(solution)/shard_map/ppermute | solution.py:693
  10.1 7.3 %collective-permute-start.3 = (f32[128,128]{1,0:T(8,128)S(1)}, f32[128,128]{1,0:T(8,128)S(1)}, u32[]{:S(2)}, u32[]{:S(2)}) collective-permute-start(f32[128,128]{1,0:T(8,128)S(1)} %get-tuple-element.42), channel_id=1, source_target_pairs={{0,1},{1,0},{2,3},{3,2},{4,5},{5,4},{6,7},{7,6},{8,9},{9,8},{10,11... | collective-permute-start | bytes 196616 | tf_op jit(solution)/shard_map/ppermute | solution.py:693
  11.7 5.8 %collective-permute-start.4 = (f32[128,128]{1,0:T(8,128)S(1)}, f32[128,128]{1,0:T(8,128)S(1)}, u32[]{:S(2)}, u32[]{:S(2)}) collective-permute-start(f32[128,128]{1,0:T(8,128)S(1)} %get-tuple-element.43), channel_id=1, source_target_pairs={{0,4},{1,2},{2,1},{3,7},{4,0},{5,6},{6,5},{7,3},{8,12},{9,10},{10,... | collective-permute-start | bytes 196616 | tf_op jit(solution)/shard_map/ppermute | solution.py:693
  12.9 6.1 %collective-permute-start.5 = (f32[80,128]{1,0:T(8,128)S(1)}, f32[80,128]{1,0:T(8,128)S(1)}, u32[]{:S(2)}, u32[]{:S(2)}) collective-permute-start(f32[80,128]{1,0:T(8,128)S(1)} %get-tuple-element.46), channel_id=1, source_target_pairs={{0,1},{1,0},{2,3},{3,2},{4,5},{5,4},{6,7},{7,6},{8,9},{9,8},{10,11... | collective-permute-start | bytes 122888 | tf_op jit(solution)/shard_map/ppermute | solution.py:693
  15.3 4.0 %collective-permute-start.6 = (f32[80,128]{1,0:T(8,128)S(1)}, f32[80,128]{1,0:T(8,128)S(1)}, u32[]{:S(2)}, u32[]{:S(2)}) collective-permute-start(f32[80,128]{1,0:T(8,128)S(1)} %get-tuple-element.47), channel_id=1, source_target_pairs={{0,4},{1,2},{2,1},{3,7},{4,0},{5,6},{6,5},{7,3},{8,12},{9,10},{10,... | collective-permute-start | bytes 122888 | tf_op jit(solution)/shard_map/ppermute | solution.py:693
  21.2 1.7 %collective-permute-start.7 = (f32[64,128]{1,0:T(8,128)S(1)}, f32[64,128]{1,0:T(8,128)S(1)}, u32[]{:S(2)}, u32[]{:S(2)}) collective-permute-start(f32[64,128]{1,0:T(8,128)S(1)} %get-tuple-element.52), channel_id=1, source_target_pairs={{0,8},{8,0},{16,24},{24,16},{1,9},{9,1},{17,25},{25,17},{2,10},{10... | collective-permute-start | bytes 98312 | tf_op jit(solution)/shard_map/ppermute | solution.py:693
  21.3 3.4 %collective-permute-start.8 = (f32[64,128]{1,0:T(8,128)S(1)}, f32[64,128]{1,0:T(8,128)S(1)}, u32[]{:S(2)}, u32[]{:S(2)}) collective-permute-start(f32[64,128]{1,0:T(8,128)S(1)} %get-tuple-element.53), channel_id=1, source_target_pairs={{0,24},{8,16},{16,8},{24,0},{1,25},{9,17},{17,9},{25,1},{2,26},{10... | collective-permute-start | bytes 98312 | tf_op jit(solution)/shard_map/ppermute | solution.py:693
  24.8 4.0 %collective-permute-start.9 = (f32[64,128]{1,0:T(8,128)S(1)}, f32[64,128]{1,0:T(8,128)S(1)}, u32[]{:S(2)}, u32[]{:S(2)}) collective-permute-start(f32[64,128]{1,0:T(8,128)S(1)} %join.4), channel_id=1, source_target_pairs={{0,4},{4,0},{1,5},{5,1},{2,6},{6,2},{3,7},{7,3},{8,12},{12,8},{9,1... | collective-permute-start | bytes 98312 | tf_op jit(solution)/shard_map/ppermute | solution.py:693
  30.3 1.7 %collective-permute-start.10 = (f32[64,128]{1,0:T(8,128)S(1)}, f32[64,128]{1,0:T(8,128)S(1)}, u32[]{:S(2)}, u32[]{:S(2)}) collective-permute-start(f32[64,128]{1,0:T(8,128)S(1)} %get-tuple-element.60), channel_id=1, source_target_pairs={{0,8},{8,0},{16,24},{24,16},{1,9},{9,1},{17,25},{25,17},{2,10},{10... | collective-permute-start | bytes 98312 | tf_op jit(solution)/shard_map/ppermute | solution.py:693
  30.4 3.4 %collective-permute-start.11 = (f32[64,128]{1,0:T(8,128)S(1)}, f32[64,128]{1,0:T(8,128)S(1)}, u32[]{:S(2)}, u32[]{:S(2)}) collective-permute-start(f32[64,128]{1,0:T(8,128)S(1)} %get-tuple-element.61), channel_id=1, source_target_pairs={{0,24},{8,16},{16,8},{24,0},{1,25},{9,17},{17,9},{25,1},{2,26},{10... | collective-permute-start | bytes 98312 | tf_op jit(solution)/shard_map/ppermute | solution.py:693
  33.9 4.0 %collective-permute-start.12 = (f32[64,128]{1,0:T(8,128)S(1)}, f32[64,128]{1,0:T(8,128)S(1)}, u32[]{:S(2)}, u32[]{:S(2)}) collective-permute-start(f32[64,128]{1,0:T(8,128)S(1)} %join.5), channel_id=1, source_target_pairs={{0,4},{4,0},{1,5},{5,1},{2,6},{6,2},{3,7},{7,3},{8,12},{12,8},{9,1... | collective-permute-start | bytes 98312 | tf_op jit(solution)/shard_map/ppermute | solution.py:693

commit v3 on v2

--- a/solution.py
+++ b/solution.py
@@ -177,94 +177,93 @@
                             halo[(side * ey + f) * part + g * p + k, k, at] = 1
         self.halo = halo.reshape(128, -1).astype(jnp.bfloat16)
         self.diagonal, self.widen = (x.astype(jnp.bfloat16) for x in (diagonal, widen))
-        rolled = []
-        for matrix in (self.forward, self.forward.T, self.squared.T):
-            for d in range(p):
-                rolled += [matrix[a, (a + d) % p] for a in range(p)]
+        self.third = [self.block_terms(matrix) for matrix in (self.forward, self.forward.T, self.squared.T)]
         node = [(j, k) for j in range(p) for k in range(p)]
         wjk = [self.weights[j] * self.weights[k] for j, k in node]
         second = [self.end[j] for j, k in node]
         third = [self.end[k] for j, k in node]
-        column = np.asarray(rolled + wjk + second + third, np.float32)
+        column = np.asarray(wjk + second + third, np.float32)
         self.table = np.ascontiguousarray(np.broadcast_to(column[:, None], (column.size, 128)))
 
-
-    def rolled(self, table, which):
+    def block_terms(self, matrix):
+        size = self.rows // 4
+        blocks = np.kron(np.eye(size // self.p), matrix).astype(np.float32)
+        upper = blocks.astype(jnp.bfloat16)
+        lower = (blocks - upper.astype(np.float32)).astype(jnp.bfloat16)
+        return np.concatenate([upper, upper, lower], axis=1)
+
+
+    def node_table(self, table, which):
+        start = which * self.block
+        return table[start : start + self.block, :]
+
+    def contract(self, x, matrix):
         p = self.p
-        return [table[(which * p + d) * p : (which * p + d + 1) * p, :] for d in range(p)]
-
-    def node_table(self, table, which):
-        start = 3 * self.p * self.p + which * self.block
-        return table[start : start + self.block, :]
+        sign = 1.0 if matrix[0, 0] * matrix[p - 1, p - 1] > 0 else -1.0
+        half = p // 2
+        sums = [x[i] + x[p - 1 - i] for i in range(half)]
+        differences = [x[i] - x[p - 1 - i] for i in range(half)]
+        out = [None] * p
+        for a in range(half):
+            even, odd = None, None
+            for i in range(half):
+                first, second = float(matrix[a, i]), float(matrix[a, p - 1 - i])
+                even = self.gather(even, 0.5 * (first + second), sums[i])
+                odd = self.gather(odd, 0.5 * (first - second), differences[i])
+            out[a] = odd + even
+            out[p - 1 - a] = even - odd if sign > 0 else odd - even
+        return out
+
+    @staticmethod
+    def gather(total, factor, x):
+        if factor == 0.0:
+            return total
+        return factor * x if total is None else total + factor * x
 
     def along_j(self, x, matrix):
-        p = self.p
-        x = x.reshape(p, p, x.shape[-1])
-        out = []
-        for a in range(p):
-            total = None
-            for i in range(p):
-                value = float(matrix[a, i])
-                if value != 0.0:
-                    term = value * x[i]
-                    total = term if total is None else total + term
-            out.append(total)
-        return jnp.concatenate(out, axis=0)
-
-    def along_k(self, x, coefficients):
-        p = self.p
-        x3 = x.reshape(p, p, x.shape[-1])
-        total = coefficients[0][None] * x3
-        for d in range(1, p):
-            total = total + coefficients[d][None] * pltpu.roll(x3, p - d, 1)
-        return total.reshape(x.shape)
+        x = x.reshape(self.p, self.p, x.shape[-1])
+        return jnp.concatenate(self.contract([x[j] for j in range(self.p)], matrix), axis=0)
 
     def along_i(self, source, matrix, write):
-        p = self.p
-
-        def body(j, carry):
-            at = pl.multiple_of(j * p, p)
-            x = [source[pl.ds(i * self.block + at, p), :] for i in range(p)]
-            for a in range(p):
-                total = None
-                for i in range(p):
-                    value = float(matrix[a, i])
-                    if value != 0.0:
-                        term = value * x[i]
-                        total = term if total is None else total + term
-                write(a * self.block + at, total)
-            return carry
-
-        lax.fori_loop(0, p, body, 0)
-
-    def operator(self, v, g, out, slope, flux, table):
         p, block = self.p, self.block
-        ahead, back = self.rolled(table, 0), self.rolled(table, 1)
+        for j in range(p):
+            rows = [i * block + j * p for i in range(p)]
+            for row, value in zip(rows, self.contract([source[r : r + p, :] for r in rows], matrix)):
+                write(row, value)
+
+    def along_k(self, source, table, out):
+        size = table.shape[0]
+        for start in range(0, self.rows, 2 * size):
+            pieces = [split(source[at : at + size, :]) for at in (start, start + size)]
+            upper, lower = (jnp.concatenate([piece[n] for piece in pieces], axis=1) for n in range(2))
+            both = jnp.dot(
+                table[...], jnp.concatenate([upper, lower, upper], axis=0), preferred_element_type=F32
+            )
+            width = source.shape[-1]
+            out[start : start + size, :] = both[:, :width]
+            out[start + size : start + 2 * size, :] = both[:, width:]
+
+    def operator(self, v, g, out, slope, flux, third, work, ahead, back):
+        block = self.block
 
         def store(row, value):
-            slope[pl.ds(row, p), :] = value
+            slope[row : row + self.p, :] = value
 
         self.along_i(v, self.forward, store)
-
-        def body(i, carry):
-            at = pl.ds(pl.multiple_of(i * block, block), block)
-            x = v[at, :]
-            s1 = slope[at, :]
+        self.along_k(v, ahead, third)
+        for i in range(self.p):
+            at = slice(i * block, (i + 1) * block)
+            x, s1, s3 = v[at, :], slope[at, :], third[at, :]
             s2 = self.along_j(x, self.forward)
-            s3 = self.along_k(x, ahead)
             xy, xz, yz = g[3, at, :], g[4, at, :], g[5, at, :]
             flux[at, :] = g[0, at, :] * s1 + xy * s2 + xz * s3
             f2 = xy * s1 + g[1, at, :] * s2 + yz * s3
-            f3 = xz * s1 + yz * s2 + g[2, at, :] * s3
-            out[at, :] = (
-                self.along_j(f2, self.forward.T) + self.along_k(f3, back) + g[6, at, :] * x
-            )
-            return carry
-
-        lax.fori_loop(0, p, body, 0)
+            work[at, :] = xz * s1 + yz * s2 + g[2, at, :] * s3
+            out[at, :] = self.along_j(f2, self.forward.T) + g[6, at, :] * x
+        self.along_k(work, back, third)
 
         def add(row, value):
-            out[pl.ds(row, p), :] += value
+            out[row : row + self.p, :] += value + third[row : row + self.p, :]
 
         self.along_i(flux, self.forward.T, add)
 
@@ -369,11 +368,11 @@
             out[:, k * w3 : (k + 1) * w3] = jnp.where(same & (node == k), 1.0, 0.0).astype(BF16)
 
     def prepare(self, n_x, n_y, n_z, *refs):
-        geometry, viscosity, spread, dirichlet, table, diagonal, right, slots, ids = refs[:9]
-        s4, ind, raw, hot3 = refs[9:13]
-        refs = refs[13:]
+        geometry, viscosity, spread, dirichlet, table, diagonal, right, slots, ids, square = refs[:10]
+        s4, ind, raw, hot3 = refs[10:14]
+        refs = refs[14:]
         x_out, y_out, z_out = refs[:n_x], refs[n_x : n_x + n_y], refs[n_x + n_y : n_x + n_y + n_z]
-        upper, lower, stiff, work = refs[n_x + n_y + n_z :]
+        upper, lower, stiff, third, work = refs[n_x + n_y + n_z :]
         p, c, block, rows, ey = self.p, self.c, self.block, self.rows, self.ey
         width = geometry.shape[-1]
 
@@ -409,8 +408,7 @@
 
         self.by_nodes(upper, lower, spread, store)
         self.pack_geometry(field, z_out)
-        wjk, second, third = (self.node_table(table, n) for n in range(3))
-        square = self.rolled(table, 2)
+        wjk, end_j, end_k = (self.node_table(table, n) for n in range(3))
         for i in range(p):
             at = slice(i * block, (i + 1) * block)
             xx, yy, zz, xy, xz, yz = (raw[q * rows + i * block : q * rows + (i + 1) * block, :] for q in range(6))
@@ -419,20 +417,17 @@
             mass = (helm_coefficient * quadrature) * (
                 xx * (yy * zz - yz * yz) - xy * (xy * zz - yz * xz) + xz * (xy * yz - yy * xz)
             )
-            cross = second * third * yz
+            cross = end_j * end_k * yz
             end = float(self.end[i])
             if end != 0.0:
-                cross = cross + end * (second * xy + third * xz)
+                cross = cross + end * (end_j * xy + end_k * xz)
             stiff[at, :] = weighted * xx
-            work[at, :] = (
-                self.along_j(weighted * yy, self.squared.T)
-                + self.along_k(weighted * zz, square)
-                + (2.0 * weighted) * cross
-                + mass
-            )
+            third[at, :] = weighted * zz
+            work[at, :] = self.along_j(weighted * yy, self.squared.T) + (2.0 * weighted) * cross + mass
+        self.along_k(third, square, third)
 
         def add(row, value):
-            work[pl.ds(row, p), :] += value
+            work[row : row + p, :] += value + third[row : row + p, :]
 
         self.along_i(stiff, self.squared.T, add)
         total = dot2(work[...], diagonal[...])
@@ -574,12 +569,13 @@
                     out[row : row + count, :] = total
 
     def start(self, n_x, n_y, n_z, *refs):
-        s4, ind, g, coef, widen, table = refs[:6]
-        z_in = refs[6 : 6 + n_z]
-        t, d, scale, v = refs[6 + n_z : 10 + n_z]
-        refs = refs[10 + n_z :]
+        s4, ind, g, coef, widen, ahead, back = refs[:7]
+        z_in = refs[7 : 7 + n_z]
+        t, d, scale, v = refs[7 + n_z : 11 + n_z]
+        refs = refs[11 + n_z :]
         x_out, y_out = refs[:n_x], refs[n_x : n_x + n_y]
-        upper, lower, r, flag, slope, flux = refs[n_x + n_y :]
+        upper, lower, r, flag = refs[n_x + n_y : n_x + n_y + 4]
+        work = refs[n_x + n_y + 4 :]
         p, block, rows, w3, w4 = self.p, self.block, self.rows, self.w3, self.w4
         step, first_own, end_own = self.step3, HALO * self.step3, self.n3 - HALO * self.step3
         size, part = self.sizes["gz"], self.halo4
@@ -633,7 +629,7 @@
             scaled = factor * r[at, :]
             t[at, :] = scaled
             d[at, :] = scaled * middle
-        self.operator(d, g, v, slope, flux, table)
+        self.operator(d, g, v, *work, ahead, back)
         self.iteration_fold(v)
         self.emit(v, x_out, y_out)
 
@@ -646,19 +642,19 @@
             put(at, keep * d[at, :] + gain * t_new[at, :])
 
     def middle(self, n_x, n_y, which, *refs):
-        t, d, scale, v, total, g, coef, table = refs[:8]
-        refs = refs[8:]
+        t, d, scale, v, total, g, coef, ahead, back = refs[:9]
+        refs = refs[9:]
         x_in, y_in, refs = refs[:n_x], refs[n_x : n_x + n_y], refs[n_x + n_y :]
         t_new, d_new, v_new, total_new = refs[:4]
         x_out, y_out = refs[4 : 4 + n_x], refs[4 + n_x : 4 + n_x + n_y]
-        slope, flux = refs[4 + n_x + n_y :]
+        work = refs[4 + n_x + n_y :]
 
         def put(at, x):
             d_new[at, :] = x
             total_new[at, :] = total[at, :] + x
 
         self.advance(t, t_new, d, v, scale, coef, which, x_in, y_in, put)
-        self.operator(d_new, g, v_new, slope, flux, table)
+        self.operator(d_new, g, v_new, *work, ahead, back)
         self.iteration_fold(v_new)
         self.emit(v_new, x_out, y_out)
 
@@ -715,6 +711,7 @@
 
     lanes = plan.ez * p
     table = jnp.asarray(plan.table)
+    ahead, back = jnp.asarray(plan.third[0]), jnp.asarray(plan.third[1])
     field3, field4 = shape(rows, w3), shape(rows, w4)
     elements = element_slot.shape[-1]
     spread = call(
@@ -730,6 +727,7 @@
         jnp.swapaxes(right_side, 1, 2),
         element_slot,
         jnp.asarray(plan.ids),
+        jnp.asarray(plan.third[2]),
     )
     lhs = FIELDS * block + 2 * plan.c * p
     results = call(
@@ -744,7 +742,7 @@
         + [shape(block + 2 * p, w4)] * n_y
         + [shape(p * plan.ey * p, lanes)] * n_z,
         operands,
-        scratch=[vmem(lhs, plan.ey * lanes, dtype=BF16)] * 2 + [vmem(rows, w3)] * 2,
+        scratch=[vmem(lhs, plan.ey * lanes, dtype=BF16)] * 2 + [vmem(rows, w3)] * 3,
         name="prepare",
     )
     s4, ind, raw, hot3 = results[:4]
@@ -782,9 +780,10 @@
     results = call(
         functools.partial(plan.start, n_x, n_y, n_z),
         [field3] * 4 + messages,
-        [s4, ind, g, coef, jnp.asarray(plan.widen), table] + z_in,
+        [s4, ind, g, coef, jnp.asarray(plan.widen), ahead, back] + z_in,
         scratch=[vmem(rows, 2 * w4, dtype=BF16)] * 2
-        + [vmem(rows, w3), vmem(2 * block, w3), vmem(rows, w3), vmem(rows, w3)],
+        + [vmem(rows, w3), vmem(2 * block, w3)]
+        + [vmem(rows, w3)] * 4,
         name="first_direction",
     )
     t, d, scale, v = results[:4]
@@ -797,8 +796,8 @@
             results = call(
                 functools.partial(plan.middle, n_x, n_y, n),
                 [field3] * 4 + messages,
-                [t, d, scale, v, total, g, coef, table] + x_in + y_in,
-                scratch=[vmem(rows, w3)] * 2,
+                [t, d, scale, v, total, g, coef, ahead, back] + x_in + y_in,
+                scratch=[vmem(rows, w3)] * 4,
                 name="direction",
             )
             t, d, v, total = results[:4]

time: 39 us -> 37.9 us (0.972)
  Pallas kernels: 8.85 us -> 7.7 us
    pallas_call x10, Pallas kernels: 8.85 us -> 7.7 us  [call(): pl.pallas_call(kernel, out_shape=list(outputs), in_specs=specs, out_specs...]
    unnamed x20 -> x26, local copies, waits for them, and re-layouts: 1.03 us -> 1.04 us
where the time goes in v3:
time: 37.9 us; the launch traced here: 37.7 us
  starting transfers between devices  15.4 us (41%)
  waiting for transfers between devices  12.1 us (32%)
  Pallas kernels  7.7 us (20%)
  between operations  1.5 us (4%)
  local copies, waits for them, and re-layouts  1.04 us (3%)
    ppermute x13, starting transfers between devices, send(): return [lax.ppermute(x, axis, pair) for x, pair in zip(arrays, pairs)]  15.4 us
    ppermute x13, waiting for transfers between devices, send(): return [lax.ppermute(x, axis, pair) for x, pair in zip(arrays, pairs)]  12.1 us
    pallas_call x10, Pallas kernels, call(): pl.pallas_call(kernel, out_shape=list(outputs), in_specs=specs, out_specs...  7.7 us
    unnamed x26, local copies, waits for them, and re-layouts  1.04 us
  transfers between devices with their start and end apart: 13, of which 7 were waited for; matrix products, arithmetic and copies ran while one was open for 0% of the time, Pallas kernels for 5%

profile of v3, /device:TPU:0, one launch (start us, length us, event | category | flops | bytes accessed | tf_op | source)
XLA Modules:
  0.0 37.7 jit_solution(7448214762608660640)
XLA Ops:
  0.1 0.2 spread_table.1.refs_2_
  0.3 0.6 %copy-done.2 = f32[192,128]{1,0:T(8,128)S(1)} copy-done((f32[192,128]{1,0:T(8,128)S(1)}, f32[192,128]{1,0:T(8,128)}, u32[]{:S(2)}) %copy-start.2) | copy-done | bytes 98328
  1.0 0.2 copy-done.3
  1.3 2.0 %prepare.1 = (f32[512,128]{1,0:T(8,128)S(1)}, f32[128,128]{1,0:T(8,128)S(1)}, f32[3584,128]{1,0:T(8,128)S(1)}, bf16[96,128]{1,0:T(8,128)(2,1)S(1)}, f32[64,128]{...) custom-call(f32[6,8,16,128]{3,2,1,0:T(8,128)S(1)} %copy-done.3, ...), custom_call_target="tpu_custom_call" | custom-call | tf_op jit(solution)/shard_map/prepare/pallas_call | solution.py:697
  3.3 0.5 %collective-permute-start = (f32[64,128]{1,0:T(8,128)S(1)}, f32[64,128]{1,0:T(8,128)S(1)}, u32[]{:S(2)}, u32[]{:S(2)}) collective-permute-start(f32[64,128]{1,0:T(8,128)S(1)} %get-tuple-element.36), channel_id=1, source_target_pairs={{0,8},{8,0},{16,24},{24,16},{1,9},{9,1},{17,25},{25,17},{2,10},{10... | collective-permute-start | bytes 98312 | tf_op jit(solution)/shard_map/ppermute | solution.py:689
  3.8 2.6 %collective-permute-start.1 = (f32[64,128]{1,0:T(8,128)S(1)}, f32[64,128]{1,0:T(8,128)S(1)}, u32[]{:S(2)}, u32[]{:S(2)}) collective-permute-start(f32[64,128]{1,0:T(8,128)S(1)} %get-tuple-element.37), channel_id=1, source_target_pairs={{0,24},{8,16},{16,8},{24,0},{1,25},{9,17},{17,9},{25,1},{2,26},{10... | collective-permute-start | bytes 98312 | tf_op jit(solution)/shard_map/ppermute | solution.py:689
  6.4 1.7 %collective-permute-done.1.refs_1_.refs_3_ = f32[64,128]{1,0:T(8,128)S(1)} collective-permute-done((f32[64,128]{1,0:T(8,128)S(1)}, f32[64,128]{1,0:T(8,128)S(1)}, u32[]{:S(2)}, u32[]{:S(2)}) %collective-permute-start.1) | collective-permute-done | bytes 32800 | tf_op jit(solution)/shard_map/ppermute | solution.py:689
  8.1 0.1 join.3
  8.2 1.7 %collective-permute-start.2 = (f32[80,128]{1,0:T(8,128)S(1)}, f32[80,128]{1,0:T(8,128)S(1)}, u32[]{:S(2)}, u32[]{:S(2)}) collective-permute-start(f32[80,128]{1,0:T(8,128)S(1)} %join.3), channel_id=1, source_target_pairs={{0,4},{4,0},{1,5},{5,1},{2,6},{6,2},{3,7},{7,3},{8,12},{12,8},{9,1... | collective-permute-start | bytes 122888 | tf_op jit(solution)/shard_map/ppermute | solution.py:689
  9.9 1.6 %collective-permute-start.3 = (f32[128,128]{1,0:T(8,128)S(1)}, f32[128,128]{1,0:T(8,128)S(1)}, u32[]{:S(2)}, u32[]{:S(2)}) collective-permute-start(f32[128,128]{1,0:T(8,128)S(1)} %get-tuple-element.42), channel_id=1, source_target_pairs={{0,1},{1,0},{2,3},{3,2},{4,5},{5,4},{6,7},{7,6},{8,9},{9,8},{10,11... | collective-permute-start | bytes 196616 | tf_op jit(solution)/shard_map/ppermute | solution.py:689
  11.5 0.5 %collective-permute-start.4 = (f32[128,128]{1,0:T(8,128)S(1)}, f32[128,128]{1,0:T(8,128)S(1)}, u32[]{:S(2)}, u32[]{:S(2)}) collective-permute-start(f32[128,128]{1,0:T(8,128)S(1)} %get-tuple-element.43), channel_id=1, source_target_pairs={{0,4},{1,2},{2,1},{3,7},{4,0},{5,6},{6,5},{7,3},{8,12},{9,10},{10,... | collective-permute-start | bytes 196616 | tf_op jit(solution)/shard_map/ppermute | solution.py:689
  12.0 0.3 collective-permute-done.2.refs_4_
  12.3 0.4 pack.1
  12.7 2.4 %collective-permute-start.5 = (f32[80,128]{1,0:T(8,128)S(1)}, f32[80,128]{1,0:T(8,128)S(1)}, u32[]{:S(2)}, u32[]{:S(2)}) collective-permute-start(f32[80,128]{1,0:T(8,128)S(1)} %get-tuple-element.46), channel_id=1, source_target_pairs={{0,1},{1,0},{2,3},{3,2},{4,5},{5,4},{6,7},{7,6},{8,9},{9,8},{10,11... | collective-permute-start | bytes 122888 | tf_op jit(solution)/shard_map/ppermute | solution.py:689
  15.1 0.8 %collective-permute-start.6 = (f32[80,128]{1,0:T(8,128)S(1)}, f32[80,128]{1,0:T(8,128)S(1)}, u32[]{:S(2)}, u32[]{:S(2)}) collective-permute-start(f32[80,128]{1,0:T(8,128)S(1)} %get-tuple-element.47), channel_id=1, source_target_pairs={{0,4},{1,2},{2,1},{3,7},{4,0},{5,6},{6,5},{7,3},{8,12},{9,10},{10,... | collective-permute-start | bytes 122888 | tf_op jit(solution)/shard_map/ppermute | solution.py:689
  17.3 1.4 %halo_geometry.1 = (f32[7,512,128]{2,1,0:T(8,128)S(1)}, f32[40,128]{1,0:T(8,128)S(1)}) custom-call(f32[3584,128]{1,0:T(8,128)S(1)} %get-tuple-element.41.refs_0_, bf16[128,1024]{1,0:T(8,128)(2,1)S(1)} %copy-done.4, f32[192,128]{1,0:T(8,128)S(1)} %copy-done.2, f32[1]{0:T(128)S(6)} %copy.16.refs_3_, f32[1]{0:T(128)S(6)} %copy.17.refs_4_, ...), custom_call_target="tpu_custom_call" | custom-call | flops 2000000 | tf_op jit(solution)/shard_map/halo_geometry/pallas_call | solution.py:697
  18.7 0.4 %collective-permute-done.6.refs_8_ = f32[80,128]{1,0:T(8,128)S(1)} collective-permute-done((f32[80,128]{1,0:T(8,128)S(1)}, f32[80,128]{1,0:T(8,128)S(1)}, u32[]{:S(2)}, u32[]{:S(2)}) %collective-permute-start.6) | collective-permute-done | bytes 40992 | tf_op jit(solution)/shard_map/ppermute | solution.py:689
  19.1 1.4 %first_direction.1 = (f32[512,128]{1,0:T(8,128)S(1)}, f32[512,128]{1,0:T(8,128)S(1)}, f32[512,128]{1,0:T(8,128)S(1)}, f32[512,128]{1,0:T(8,128)S(1)}, f32[64,128...) custom-call(f32[512,128]{1,0:T(8,128)S(1)} %get-tuple-element.39.refs_0_, ...), custom_call_target="tpu_custom_call" | custom-call | tf_op jit(solution)/shard_map/first_direction/pallas_call | solution.py:697
  20.6 0.1 collective-permute-start.7
  20.6 1.6 %collective-permute-start.8 = (f32[64,128]{1,0:T(8,128)S(1)}, f32[64,128]{1,0:T(8,128)S(1)}, u32[]{:S(2)}, u32[]{:S(2)}) collective-permute-start(f32[64,128]{1,0:T(8,128)S(1)} %get-tuple-element.53), channel_id=1, source_target_pairs={{0,24},{8,16},{16,8},{24,0},{1,25},{9,17},{17,9},{25,1},{2,26},{10... | collective-permute-start | bytes 98312 | tf_op jit(solution)/shard_map/ppermute | solution.py:689
  22.2 1.8 %collective-permute-done.8.refs_1_.refs_10_ = f32[64,128]{1,0:T(8,128)S(1)} collective-permute-done((f32[64,128]{1,0:T(8,128)S(1)}, f32[64,128]{1,0:T(8,128)S(1)}, u32[]{:S(2)}, u32[]{:S(2)}) %collective-permute-start.8) | collective-permute-done | bytes 32800 | tf_op jit(solution)/shard_map/ppermute | solution.py:689
  24.0 0.1 join.4
  24.1 0.9 %collective-permute-start.9 = (f32[64,128]{1,0:T(8,128)S(1)}, f32[64,128]{1,0:T(8,128)S(1)}, u32[]{:S(2)}, u32[]{:S(2)}) collective-permute-start(f32[64,128]{1,0:T(8,128)S(1)} %join.4), channel_id=1, source_target_pairs={{0,4},{4,0},{1,5},{5,1},{2,6},{6,2},{3,7},{7,3},{8,12},{12,8},{9,1... | collective-permute-start | bytes 98312 | tf_op jit(solution)/shard_map/ppermute | solution.py:689
  25.0 3.1 %collective-permute-done.9.refs_11_ = f32[64,128]{1,0:T(8,128)S(1)} collective-permute-done((f32[64,128]{1,0:T(8,128)S(1)}, f32[64,128]{1,0:T(8,128)S(1)}, u32[]{:S(2)}, u32[]{:S(2)}) %collective-permute-start.9) | collective-permute-done | bytes 32800 | tf_op jit(solution)/shard_map/ppermute | solution.py:689
  28.1 1.1 %direction.1 = (f32[512,128]{1,0:T(8,128)S(1)}, f32[512,128]{1,0:T(8,128)S(1)}, f32[512,128]{1,0:T(8,128)S(1)}, f32[512,128]{1,0:T(8,128)S(1)}, f32[64,128]{1,0:...) custom-call(f32[512,128]{1,0:T(8,128)S(1)} %get-tuple-element.48.refs_0_, ...), custom_call_target="tpu_custom_call" | custom-call | tf_op jit(solution)/shard_map/direction/pallas_call | solution.py:697
  29.2 0.1 collective-permute-start.10
  29.3 1.6 %collective-permute-start.11 = (f32[64,128]{1,0:T(8,128)S(1)}, f32[64,128]{1,0:T(8,128)S(1)}, u32[]{:S(2)}, u32[]{:S(2)}) collective-permute-start(f32[64,128]{1,0:T(8,128)S(1)} %get-tuple-element.61), channel_id=1, source_target_pairs={{0,24},{8,16},{16,8},{24,0},{1,25},{9,17},{17,9},{25,1},{2,26},{10... | collective-permute-start | bytes 98312 | tf_op jit(solution)/shard_map/ppermute | solution.py:689
  30.9 1.8 %collective-permute-done.11.refs_1_.refs_8_ = f32[64,128]{1,0:T(8,128)S(1)} collective-permute-done((f32[64,128]{1,0:T(8,128)S(1)}, f32[64,128]{1,0:T(8,128)S(1)}, u32[]{:S(2)}, u32[]{:S(2)}) %collective-permute-start.11) | collective-permute-done | bytes 32800 | tf_op jit(solution)/shard_map/ppermute | solution.py:689
  32.7 0.1 join.5
  32.8 0.9 %collective-permute-start.12 = (f32[64,128]{1,0:T(8,128)S(1)}, f32[64,128]{1,0:T(8,128)S(1)}, u32[]{:S(2)}, u32[]{:S(2)}) collective-permute-start(f32[64,128]{1,0:T(8,128)S(1)} %join.5), channel_id=1, source_target_pairs={{0,4},{4,0},{1,5},{5,1},{2,6},{6,2},{3,7},{7,3},{8,12},{12,8},{9,1... | collective-permute-start | bytes 98312 | tf_op jit(solution)/shard_map/ppermute | solution.py:689
  33.7 3.1 %collective-permute-done.12.refs_9_ = f32[64,128]{1,0:T(8,128)S(1)} collective-permute-done((f32[64,128]{1,0:T(8,128)S(1)}, f32[64,128]{1,0:T(8,128)S(1)}, u32[]{:S(2)}, u32[]{:S(2)}) %collective-permute-start.12) | collective-permute-done | bytes 32800 | tf_op jit(solution)/shard_map/ppermute | solution.py:689
  36.7 1.0 %field.1 = f32[3,32,512]{2,1,0:T(8,128)} custom-call(f32[512,128]{1,0:T(8,128)S(1)} %get-tuple-element.55.refs_0_, f32[512,128]{1,0:T(8,128)S(1)} %get-tuple-element.56.refs_1_, f32[512,128]{1,0:T(8,128)S(1)} %get-tuple-element.50.refs_2_, f32[512,128]{1,0:T(8,128)S(1)} %get-tuple-element.57.refs_3_, f32[512,128]{1,0:T(8,128)S(1)} %get-tuple-element.58.refs_4_, ...), custom_call_target="tpu_custom_call" | custom-call | tf_op jit(solution)/shard_map/field/pallas_call | solution.py:697
  (30 shorter events, 0.2 us)
Async XLA Ops:
  0.0 0.9 %copy-start.2 = (f32[192,128]{1,0:T(8,128)S(1)}, f32[192,128]{1,0:T(8,128)}, u32[]{:S(2)}) copy-start(f32[192,128]{1,0:T(8,128)} %constant.16.clone.refs_4_.refs_2_) | copy-start | bytes 294916
  0.0 0.9 %copy-start.7 = (bf16[128,384]{1,0:T(8,128)(2,1)S(1)}, bf16[128,384]{1,0:T(8,128)(2,1)}, u32[]{:S(2)}) copy-start(bf16[128,384]{1,0:T(8,128)(2,1)} %constant.21.clone.refs_9_) | copy-start | bytes 294916
  0.0 0.9 %copy-start.10 = (bf16[128,128]{1,0:T(8,128)(2,1)S(1)}, bf16[128,128]{1,0:T(8,128)(2,1)}, u32[]{:S(2)}) copy-start(bf16[128,128]{1,0:T(8,128)(2,1)} %constant.19.clone.refs_5_) | copy-start | bytes 98308
  0.0 0.9 %copy-start.11 = (s32[6,128]{1,0:T(8,128)S(1)}, s32[6,128]{1,0:T(8,128)}, u32[]{:S(2)}) copy-start(s32[6,128]{1,0:T(8,128)} %constant.20.clone.refs_8_) | copy-start | bytes 9220
  0.0 0.9 %copy-start.9 = (s32[2,3,16,128]{3,2,1,0:T(8,128)S(1)}, s32[2,3,16,128]{3,2,1,0:T(8,128)}, u32[]{:S(2)}) copy-start(s32[2,3,16,128]{3,2,1,0:T(8,128)} %refs_3_.2) | copy-start | bytes 147460
  0.0 0.9 %copy-start.12 = (s32[1,32]{1,0:T(1,128)S(1)}, s32[1,32]{1,0:T(1,128)}, u32[]{:S(2)}) copy-start(s32[1,32]{1,0:T(1,128)} %refs_7_.2) | copy-start | bytes 388
  0.0 1.0 %copy-start.8 = (f32[8,16,128]{2,1,0:T(8,128)S(1)}, f32[8,16,128]{2,1,0:T(8,128)}, u32[]{:S(2)}) copy-start(f32[8,16,128]{2,1,0:T(8,128)} %refs_1_.2) | copy-start | bytes 196612
  0.0 1.2 %copy-start.3 = (f32[6,8,16,128]{3,2,1,0:T(8,128)S(1)}, f32[6,8,16,128]{3,2,1,0:T(8,128)}, u32[]{:S(2)}) copy-start(f32[6,8,16,128]{3,2,1,0:T(8,128)} %refs_0_.1) | copy-start | bytes 1179652
  0.0 1.2 %copy-start.5 = (f32[3,512,32]{1,2,0:T(8,128)S(1)}, f32[3,512,32]{1,2,0:T(8,128)}, u32[]{:S(2)}) copy-start(f32[3,512,32]{1,2,0:T(8,128)} %param.15) | copy-start | bytes 589828
  0.2 17.0 %copy-start.4 = (bf16[128,1024]{1,0:T(8,128)(2,1)S(1)}, bf16[128,1024]{1,0:T(8,128)(2,1)}, u32[]{:S(2)}) copy-start(bf16[128,1024]{1,0:T(8,128)(2,1)} %constant.22.clone.refs_1_) | copy-start | bytes 786436
  3.3 15.8 %copy-start = (bf16[128,384]{1,0:T(8,128)(2,1)S(1)}, bf16[128,384]{1,0:T(8,128)(2,1)}, u32[]{:S(2)}) copy-start(bf16[128,384]{1,0:T(8,128)(2,1)} %constant.18.clone.refs_6_.refs_8_) | copy-start | bytes 294916
  3.3 15.8 %copy-start.1 = (bf16[128,384]{1,0:T(8,128)(2,1)S(1)}, bf16[128,384]{1,0:T(8,128)(2,1)}, u32[]{:S(2)}) copy-start(bf16[128,384]{1,0:T(8,128)(2,1)} %constant.17.clone.refs_5_.refs_7_) | copy-start | bytes 294916
  3.3 15.8 %copy-start.6 = (bf16[256,256]{1,0:T(8,128)(2,1)S(1)}, bf16[256,256]{1,0:T(8,128)(2,1)}, u32[]{:S(2)}) copy-start(bf16[256,256]{1,0:T(8,128)(2,1)} %constant.23.clone.refs_4_) | copy-start | bytes 393220
  3.3 3.1 %collective-permute-start = (f32[64,128]{1,0:T(8,128)S(1)}, f32[64,128]{1,0:T(8,128)S(1)}, u32[]{:S(2)}, u32[]{:S(2)}) collective-permute-start(f32[64,128]{1,0:T(8,128)S(1)} %get-tuple-element.36), channel_id=1, source_target_pairs={{0,8},{8,0},{16,24},{24,16},{1,9},{9,1},{17,25},{25,17},{2,10},{10... | collective-permute-start | bytes 98312 | tf_op jit(solution)/shard_map/ppermute | solution.py:689
  3.8 4.3 %collective-permute-start.1 = (f32[64,128]{1,0:T(8,128)S(1)}, f32[64,128]{1,0:T(8,128)S(1)}, u32[]{:S(2)}, u32[]{:S(2)}) collective-permute-start(f32[64,128]{1,0:T(8,128)S(1)} %get-tuple-element.37), channel_id=1, source_target_pairs={{0,24},{8,16},{16,8},{24,0},{1,25},{9,17},{17,9},{25,1},{2,26},{10... | collective-permute-start | bytes 98312 | tf_op jit(solution)/shard_map/ppermute | solution.py:689
  8.2 4.1 %collective-permute-start.2 = (f32[80,128]{1,0:T(8,128)S(1)}, f32[80,128]{1,0:T(8,128)S(1)}, u32[]{:S(2)}, u32[]{:S(2)}) collective-permute-start(f32[80,128]{1,0:T(8,128)S(1)} %join.3), channel_id=1, source_target_pairs={{0,4},{4,0},{1,5},{5,1},{2,6},{6,2},{3,7},{7,3},{8,12},{12,8},{9,1... | collective-permute-start | bytes 122888 | tf_op jit(solution)/shard_map/ppermute | solution.py:689
  9.9 7.3 %collective-permute-start.3 = (f32[128,128]{1,0:T(8,128)S(1)}, f32[128,128]{1,0:T(8,128)S(1)}, u32[]{:S(2)}, u32[]{:S(2)}) collective-permute-start(f32[128,128]{1,0:T(8,128)S(1)} %get-tuple-element.42), channel_id=1, source_target_pairs={{0,1},{1,0},{2,3},{3,2},{4,5},{5,4},{6,7},{7,6},{8,9},{9,8},{10,11... | collective-permute-start | bytes 196616 | tf_op jit(solution)/shard_map/ppermute | solution.py:689
  11.5 5.8 %collective-permute-start.4 = (f32[128,128]{1,0:T(8,128)S(1)}, f32[128,128]{1,0:T(8,128)S(1)}, u32[]{:S(2)}, u32[]{:S(2)}) collective-permute-start(f32[128,128]{1,0:T(8,128)S(1)} %get-tuple-element.43), channel_id=1, source_target_pairs={{0,4},{1,2},{2,1},{3,7},{4,0},{5,6},{6,5},{7,3},{8,12},{9,10},{10,... | collective-permute-start | bytes 196616 | tf_op jit(solution)/shard_map/ppermute | solution.py:689
  12.7 6.1 %collective-permute-start.5 = (f32[80,128]{1,0:T(8,128)S(1)}, f32[80,128]{1,0:T(8,128)S(1)}, u32[]{:S(2)}, u32[]{:S(2)}) collective-permute-start(f32[80,128]{1,0:T(8,128)S(1)} %get-tuple-element.46), channel_id=1, source_target_pairs={{0,1},{1,0},{2,3},{3,2},{4,5},{5,4},{6,7},{7,6},{8,9},{9,8},{10,11... | collective-permute-start | bytes 122888 | tf_op jit(solution)/shard_map/ppermute | solution.py:689
  15.1 4.0 %collective-permute-start.6 = (f32[80,128]{1,0:T(8,128)S(1)}, f32[80,128]{1,0:T(8,128)S(1)}, u32[]{:S(2)}, u32[]{:S(2)}) collective-permute-start(f32[80,128]{1,0:T(8,128)S(1)} %get-tuple-element.47), channel_id=1, source_target_pairs={{0,4},{1,2},{2,1},{3,7},{4,0},{5,6},{6,5},{7,3},{8,12},{9,10},{10,... | collective-permute-start | bytes 122888 | tf_op jit(solution)/shard_map/ppermute | solution.py:689
  20.6 1.7 %collective-permute-start.7 = (f32[64,128]{1,0:T(8,128)S(1)}, f32[64,128]{1,0:T(8,128)S(1)}, u32[]{:S(2)}, u32[]{:S(2)}) collective-permute-start(f32[64,128]{1,0:T(8,128)S(1)} %get-tuple-element.52), channel_id=1, source_target_pairs={{0,8},{8,0},{16,24},{24,16},{1,9},{9,1},{17,25},{25,17},{2,10},{10... | collective-permute-start | bytes 98312 | tf_op jit(solution)/shard_map/ppermute | solution.py:689
  20.6 3.4 %collective-permute-start.8 = (f32[64,128]{1,0:T(8,128)S(1)}, f32[64,128]{1,0:T(8,128)S(1)}, u32[]{:S(2)}, u32[]{:S(2)}) collective-permute-start(f32[64,128]{1,0:T(8,128)S(1)} %get-tuple-element.53), channel_id=1, source_target_pairs={{0,24},{8,16},{16,8},{24,0},{1,25},{9,17},{17,9},{25,1},{2,26},{10... | collective-permute-start | bytes 98312 | tf_op jit(solution)/shard_map/ppermute | solution.py:689
  24.1 4.0 %collective-permute-start.9 = (f32[64,128]{1,0:T(8,128)S(1)}, f32[64,128]{1,0:T(8,128)S(1)}, u32[]{:S(2)}, u32[]{:S(2)}) collective-permute-start(f32[64,128]{1,0:T(8,128)S(1)} %join.4), channel_id=1, source_target_pairs={{0,4},{4,0},{1,5},{5,1},{2,6},{6,2},{3,7},{7,3},{8,12},{12,8},{9,1... | collective-permute-start | bytes 98312 | tf_op jit(solution)/shard_map/ppermute | solution.py:689
  29.2 1.7 %collective-permute-start.10 = (f32[64,128]{1,0:T(8,128)S(1)}, f32[64,128]{1,0:T(8,128)S(1)}, u32[]{:S(2)}, u32[]{:S(2)}) collective-permute-start(f32[64,128]{1,0:T(8,128)S(1)} %get-tuple-element.60), channel_id=1, source_target_pairs={{0,8},{8,0},{16,24},{24,16},{1,9},{9,1},{17,25},{25,17},{2,10},{10... | collective-permute-start | bytes 98312 | tf_op jit(solution)/shard_map/ppermute | solution.py:689
  29.3 3.4 %collective-permute-start.11 = (f32[64,128]{1,0:T(8,128)S(1)}, f32[64,128]{1,0:T(8,128)S(1)}, u32[]{:S(2)}, u32[]{:S(2)}) collective-permute-start(f32[64,128]{1,0:T(8,128)S(1)} %get-tuple-element.61), channel_id=1, source_target_pairs={{0,24},{8,16},{16,8},{24,0},{1,25},{9,17},{17,9},{25,1},{2,26},{10... | collective-permute-start | bytes 98312 | tf_op jit(solution)/shard_map/ppermute | solution.py:689
  32.8 4.0 %collective-permute-start.12 = (f32[64,128]{1,0:T(8,128)S(1)}, f32[64,128]{1,0:T(8,128)S(1)}, u32[]{:S(2)}, u32[]{:S(2)}) collective-permute-start(f32[64,128]{1,0:T(8,128)S(1)} %join.5), channel_id=1, source_target_pairs={{0,4},{4,0},{1,5},{5,1},{2,6},{6,2},{3,7},{7,3},{8,12},{12,8},{9,1... | collective-permute-start | bytes 98312 | tf_op jit(solution)/shard_map/ppermute | solution.py:689

commit v4 on v3

--- a/solution.py
+++ b/solution.py
@@ -151,11 +151,9 @@
         p, c, ey, ez = self.p, self.c, self.ey, self.ez
         lanes = ez * p
         every = [(g, cc, f) for g in range(ez) for cc in range(c) for f in range(ey)]
-        diagonal = np.zeros((self.w3, self.w4), np.float32)
         widen = np.zeros((2 * self.w4, 2 * self.w3), np.float32)
         ids = np.full((2 * c, 128, 128), -1, np.int32)
         for g, cc, f in every:
-            diagonal[self.lane3(g, 0, f), self.lane4(g, c, f)] = 1
             widen[self.lane4(g, cc, f), self.lane3(g, cc, f)] = 1
             widen[self.lane4(g, c, f), self.w3 + self.lane3(g, cc, f)] = 1
             ids[cc, :, self.lane4(g, cc, f)] = f * ez + g
@@ -176,14 +174,20 @@
                         for k in range(p):
                             halo[(side * ey + f) * part + g * p + k, k, at] = 1
         self.halo = halo.reshape(128, -1).astype(jnp.bfloat16)
-        self.diagonal, self.widen = (x.astype(jnp.bfloat16) for x in (diagonal, widen))
+        self.widen = widen.astype(jnp.bfloat16)
         self.third = [self.block_terms(matrix) for matrix in (self.forward, self.forward.T, self.squared.T)]
-        node = [(j, k) for j in range(p) for k in range(p)]
-        wjk = [self.weights[j] * self.weights[k] for j, k in node]
-        second = [self.end[j] for j, k in node]
-        third = [self.end[k] for j, k in node]
-        column = np.asarray(wjk + second + third, np.float32)
+        column = np.asarray([wj * wk for wj in self.weights for wk in self.weights], np.float32)
         self.table = np.ascontiguousarray(np.broadcast_to(column[:, None], (column.size, 128)))
+        face = (ey * p, lanes)
+        second = np.tile(np.arange(p), ey)[:, None]
+        third = np.tile(np.arange(p), ez)[None, :]
+        self.face_table = np.concatenate(
+            [
+                self.weights[second] * self.weights[third],
+                np.broadcast_to(self.end[second], face),
+                np.broadcast_to(self.end[third], face),
+            ]
+        ).astype(np.float32)
 
     def block_terms(self, matrix):
         size = self.rows // 4
@@ -192,10 +196,6 @@
         lower = (blocks - upper.astype(np.float32)).astype(jnp.bfloat16)
         return np.concatenate([upper, upper, lower], axis=1)
 
-
-    def node_table(self, table, which):
-        start = which * self.block
-        return table[start : start + self.block, :]
 
     def contract(self, x, matrix):
         p = self.p
@@ -303,19 +303,6 @@
                     high, u[start + block - p : start + block, :], u[start : start + p, :]
                 )
 
-    def subtract_shared(self, t, scale, x_in, y_in):
-        p, block, rows = self.p, self.block, self.rows
-        low, high = both_sides([x[...] for x in x_in], roles("gx", self.sizes["gx"]))
-        if x_in:
-            t[:block, :] -= scale[:block, :] * low
-            t[rows - block :, :] -= scale[rows - block :, :] * high
-        low, high = both_sides([y[...] for y in y_in], roles("gy", self.sizes["gy"]))
-        if y_in:
-            for i in range(p):
-                at, end = i * block, (i + 1) * block
-                t[at : at + p, :] -= scale[at : at + p, :] * low[i * p : (i + 1) * p]
-                t[end - p : end, :] -= scale[end - p : end, :] * high[i * p : (i + 1) * p]
-
     def iteration_fold(self, u):
         self.fold_second(u)
         last = self.n3 - self.step3
@@ -335,15 +322,14 @@
                 total = jnp.where(here, jnp.where(high, upper, lower), total)
             target[...] = total
 
-    def by_nodes(self, upper, lower, table, store):
-        w3 = self.w3
+    def by_nodes(self, upper, lower, table, width, store):
         for k in range(0, self.p, 2):
-            columns = table[:, k * w3 : (k + 2) * w3]
-            both = jnp.dot(upper[...], columns, preferred_element_type=F32) + jnp.dot(
-                lower[...], columns, preferred_element_type=F32
-            )
-            store(k, both[:, :w3])
-            store(k + 1, both[:, w3:])
+            columns = table[:, k * width : (k + 2) * width]
+            both = jnp.dot(upper, columns, preferred_element_type=F32) + jnp.dot(
+                lower, columns, preferred_element_type=F32
+            )
+            store(k, both[:, :width])
+            store(k + 1, both[:, width:])
 
     def one_hot(self, slots, ids):
         count = slots.shape[-1]
@@ -355,25 +341,85 @@
             [jnp.where(column == ids[n : n + 1, :].astype(F32), 1.0, 0.0) for n in range(self.c)], axis=0
         ).astype(BF16)
 
-    def spread_table(self, out):
-        p, ey, ez, w3 = self.p, self.ey, self.ez, self.w3
-        shape = (ey * ez * p, w3)
-        row = lax.broadcasted_iota(jnp.int32, shape, 0)
-        lane = lax.broadcasted_iota(jnp.int32, (1, w3), 1)
-        g = lane // self.step3 - HALO
-        element = jnp.where((g >= 0) & (g < ez), lax.rem(lane, ey) * ez + g, -1)
-        same = row // p == element
-        node = lax.rem(row, p)
-        for k in range(p):
-            out[:, k * w3 : (k + 1) * w3] = jnp.where(same & (node == k), 1.0, 0.0).astype(BF16)
-
-    def prepare(self, n_x, n_y, n_z, *refs):
-        geometry, viscosity, spread, dirichlet, table, diagonal, right, slots, ids, square = refs[:10]
-        s4, ind, raw, hot3 = refs[10:14]
-        refs = refs[14:]
-        x_out, y_out, z_out = refs[:n_x], refs[n_x : n_x + n_y], refs[n_x + n_y : n_x + n_y + n_z]
-        upper, lower, stiff, third, work = refs[n_x + n_y + n_z :]
+    def spread_tables(self, out3, out4):
+        p, ey, ez = self.p, self.ey, self.ez
+        for out, width, step, offset, first in (
+            (out3, self.w3, self.step3, HALO, 0),
+            (out4, self.w4, self.step4, 0, self.c * ey),
+        ):
+            row = lax.broadcasted_iota(jnp.int32, (ey * ez * p, width), 0)
+            lane = lax.broadcasted_iota(jnp.int32, (1, width), 1)
+            g = lane // step - offset
+            inside = (g >= 0) & (g < ez) & (lax.rem(lane, step) >= first)
+            same = row // p == jnp.where(inside, lax.rem(lane, ey) * ez + g, -1)
+            node = lax.rem(row, p)
+            for k in range(p):
+                out[:, k * width : (k + 1) * width] = jnp.where(same & (node == k), 1.0, 0.0).astype(BF16)
+
+    def prepare(self, n_x, n_y, *refs):
+        geometry, viscosity, spread, table, right, slots, ids, square = refs[:8]
+        s4, hot3 = refs[8:10]
+        refs = refs[10:]
+        x_out, y_out, work = refs[:n_x], refs[n_x : n_x + n_y], refs[n_x + n_y]
         p, c, block, rows, ey = self.p, self.c, self.block, self.rows, self.ey
+        face = ey * p
+        wjk, end_j, end_k = (table[n * face : (n + 1) * face, :] for n in range(3))
+        stiff, second, third, rest = [], [], [], []
+        for i in range(p):
+            xx, yy, zz, xy, xz, yz = (geometry[q, i] for q in range(6))
+            quadrature = float(self.weights[i]) * wjk
+            weighted = quadrature * viscosity[i]
+            mass = (helm_coefficient * quadrature) * (
+                xx * (yy * zz - yz * yz) - xy * (xy * zz - yz * xz) + xz * (xy * yz - yy * xz)
+            )
+            cross = end_j * end_k * yz
+            end = float(self.end[i])
+            if end != 0.0:
+                cross = cross + end * (end_j * xy + end_k * xz)
+            stiff.append(weighted * xx)
+            second.append(weighted * yy)
+            third.append(weighted * zz)
+            rest.append((2.0 * weighted) * cross + mass)
+        upper, lower = split(jnp.concatenate(second, axis=0))
+        diagonal = jnp.dot(
+            square[...], jnp.concatenate([upper, lower, upper], axis=0), preferred_element_type=F32
+        )
+        upper, lower = split(jnp.concatenate(third, axis=0))
+        diagonal = diagonal + lax.dot_general(
+            jnp.concatenate([upper, lower, upper], axis=1),
+            square[...],
+            (((1,), (1,)), ((), ())),
+            preferred_element_type=F32,
+        )
+        first = self.contract(stiff, self.squared.T)
+        diagonal = diagonal + jnp.concatenate([x + y for x, y in zip(first, rest)], axis=0)
+        width = diagonal.shape[-1]
+        value = diagonal.reshape(p, ey, p, width)
+        value = jnp.concatenate([value[:, f].reshape(block, width) for f in range(ey)], axis=1)
+
+        def store(k, part):
+            work[pl.ds(k, block, stride=p), :] = part
+
+        self.by_nodes(*split(value), spread, self.w4, store)
+        hot = self.one_hot(slots, ids)
+        hot3[...] = self.one_hot(slots, ids[c:, :])
+        total = work[...]
+        for part in split(right[...].reshape(hot.shape[0], rows)):
+            total = total + lax.dot_general(
+                part, hot, (((0,), (0,)), ((), ())), preferred_element_type=F32
+            )
+        s4[...] = total
+        self.fold_second(s4)
+        last = self.n4 - self.step4
+        self.fold_third(s4, self.step4, lambda l: l < last, lambda l: (l >= self.step4) & (l < self.n4))
+        self.emit(s4, x_out, y_out)
+
+    def convert(self, n_y, n_z, *refs):
+        geometry, viscosity, spread, dirichlet = refs[:4]
+        raw, ind = refs[4:6]
+        refs = refs[6:]
+        y_out, z_out, (upper, lower) = refs[:n_y], refs[n_y : n_y + n_z], refs[n_y + n_z :]
+        p, c, block, ey = self.p, self.c, self.block, self.ey
         width = geometry.shape[-1]
 
         def field(q):
@@ -406,42 +452,9 @@
                 total = jnp.where(owner == cc, value[at : at + flags], total)
             ind[pl.ds(k, flags, stride=p), :] = jnp.where(here, total, 0.0)
 
-        self.by_nodes(upper, lower, spread, store)
+        self.by_nodes(upper[...], lower[...], spread, self.w3, store)
         self.pack_geometry(field, z_out)
-        wjk, end_j, end_k = (self.node_table(table, n) for n in range(3))
-        for i in range(p):
-            at = slice(i * block, (i + 1) * block)
-            xx, yy, zz, xy, xz, yz = (raw[q * rows + i * block : q * rows + (i + 1) * block, :] for q in range(6))
-            quadrature = float(self.weights[i]) * wjk
-            weighted = quadrature * raw[6 * rows + i * block : 6 * rows + (i + 1) * block, :]
-            mass = (helm_coefficient * quadrature) * (
-                xx * (yy * zz - yz * yz) - xy * (xy * zz - yz * xz) + xz * (xy * yz - yy * xz)
-            )
-            cross = end_j * end_k * yz
-            end = float(self.end[i])
-            if end != 0.0:
-                cross = cross + end * (end_j * xy + end_k * xz)
-            stiff[at, :] = weighted * xx
-            third[at, :] = weighted * zz
-            work[at, :] = self.along_j(weighted * yy, self.squared.T) + (2.0 * weighted) * cross + mass
-        self.along_k(third, square, third)
-
-        def add(row, value):
-            work[row : row + p, :] += value + third[row : row + p, :]
-
-        self.along_i(stiff, self.squared.T, add)
-        total = dot2(work[...], diagonal[...])
-        hot = self.one_hot(slots, ids)
-        hot3[...] = self.one_hot(slots, ids[c:, :])
-        for part in split(right[...].reshape(hot.shape[0], rows)):
-            total = total + lax.dot_general(
-                part, hot, (((0,), (0,)), ((), ())), preferred_element_type=F32
-            )
-        s4[...] = total
-        self.fold_second(s4)
         self.fold_second(ind)
-        last = self.n4 - self.step4
-        self.fold_third(s4, self.step4, lambda l: l < last, lambda l: (l >= self.step4) & (l < self.n4))
         first_own, end_own = HALO * self.step3, self.n3 - HALO * self.step3
         self.fold_third(
             ind,
@@ -449,29 +462,18 @@
             lambda l: (l >= first_own) & (l < end_own - self.step3),
             lambda l: (l >= first_own + self.step3) & (l < end_own),
         )
-        self.emit(s4, x_out, y_out)
         for out, (up, _, _) in zip(y_out, roles("gy", self.sizes["gy"])):
             for n in range(2):
                 start = n * block
-                out[block + n * p : block + (n + 1) * p, :] = jnp.where(
+                out[n * p : (n + 1) * p, :] = jnp.where(
                     up, ind[start + block - p : start + block, :], ind[start : start + p, :]
                 )
 
     def halo_geometry(self, n_z, *refs):
-        raw, halo, table, low, high = refs[:5]
-        z_in, (g, coef) = refs[5 : 5 + n_z], refs[5 + n_z : 7 + n_z]
-        upper, lower, total = refs[7 + n_z :]
+        raw, halo, table = refs[:3]
+        z_in, g = refs[3 : 3 + n_z], refs[3 + n_z]
+        upper, lower, total = refs[4 + n_z :]
         p, block, rows, ey = self.p, self.block, self.rows, self.ey
-        top, bottom = jnp.full((8, 128), high[0], F32), jnp.full((8, 128), low[0], F32)
-        midpoint, halfwidth = (top + bottom) * 0.5, (top - bottom) * 0.5
-        ratio = midpoint / halfwidth
-        damping = 1.0 / ratio
-        coef[0:8, :] = 1.0 / midpoint
-        for n in range(ITERS - 1):
-            following = 1.0 / (2.0 * ratio - damping)
-            coef[8 * (2 * n + 1) : 8 * (2 * n + 2), :] = following * damping
-            coef[8 * (2 * n + 2) : 8 * (2 * n + 3), :] = 2.0 * following / halfwidth
-            damping = following
         source = raw
         if n_z:
             sides = both_sides([z[...] for z in z_in], roles("gz", self.sizes["gz"]))
@@ -494,9 +496,9 @@
                 at = pl.ds(k, FIELDS * block, stride=p)
                 total[at, :] = raw[at, :] + value
 
-            self.by_nodes(upper, lower, halo, store)
+            self.by_nodes(upper[...], lower[...], halo, self.w3, store)
             source = total
-        wjk = self.node_table(table, 0)
+        wjk = table[...]
         for i in range(p):
             at = slice(i * block, (i + 1) * block)
             entries = [source[q * rows + i * block : q * rows + (i + 1) * block, :] for q in range(FIELDS)]
@@ -509,73 +511,141 @@
             for q in range(6):
                 g[q, at, :] = weighted * entries[q]
 
+    def coefficients(self, low, high, coef):
+        top, bottom = jnp.full((8, 128), high[0], F32), jnp.full((8, 128), low[0], F32)
+        midpoint, halfwidth = (top + bottom) * 0.5, (top - bottom) * 0.5
+        ratio = midpoint / halfwidth
+        damping = 1.0 / ratio
+        coef[0:8, :] = 1.0 / midpoint
+        for n in range(ITERS - 1):
+            following = 1.0 / (2.0 * ratio - damping)
+            coef[8 * (2 * n + 1) : 8 * (2 * n + 2), :] = following * damping
+            coef[8 * (2 * n + 2) : 8 * (2 * n + 3), :] = 2.0 * following / halfwidth
+            damping = following
+
     def join(self, n_x, n_y, *refs):
-        x_in, y_raw, y_out = refs[:n_x], refs[n_x : n_x + n_y], refs[n_x + n_y :]
+        x_in, refs = refs[:n_x], refs[n_x:]
+        y_raw, y_more, y_out = refs[:n_y], refs[n_y:-n_y], refs[-n_y:]
         p, block, ey = self.p, self.block, self.ey
         low, high = both_sides([x[...] for x in x_in], roles("gx", self.sizes["gx"]))
-        for raw, out, (up, _, _) in zip(y_raw, y_out, roles("gy", self.sizes["gy"])):
-            width = raw.shape[-1]
-            face = raw[...]
+        for n, (up, _, _) in enumerate(roles("gy", self.sizes["gy"])):
+            face = y_raw[n][...]
+            width = face.shape[-1]
             if n_x:
                 first, last = (jnp.where(up, x[block - p :], x[:p]) for x in (low, high))
-                parts = [face[:p] + first, face[p : block - p], face[block - p : block] + last]
-                parts += [face[block:]] if face.shape[0] > block else []
-                face = jnp.concatenate(parts, axis=0)
-            f = lax.rem(lax.broadcasted_iota(jnp.int32, face.shape, 1), ey)
+                face = jnp.concatenate([face[:p] + first, face[p : block - p], face[block - p :] + last], axis=0)
+            if y_more:
+                face = jnp.concatenate([face, y_more[n][...]], axis=0)
+            if ey == 1:
+                y_out[n][...] = face
+                continue
+            half = face.shape[0] // 2
+            first, second = face[:half], face[half:]
+            f = lax.rem(lax.broadcasted_iota(jnp.int32, first.shape, 1), ey)
+            below = jnp.where(f == 0, pltpu.roll(first, width - (ey - 1), 1), 0.0) + jnp.where(
+                f == 1, pltpu.roll(second, (width - (ey - 2)) % width, 1) if ey != 2 else second, 0.0
+            )
+            above = jnp.where(f == ey - 1, pltpu.roll(first, ey - 1, 1), 0.0) + jnp.where(
+                f == ey - 2, pltpu.roll(second, ey - 2, 1) if ey != 2 else second, 0.0
+            )
+            y_out[n][...] = jnp.where(up, below, above)
+
+    def second_sides(self, received):
+        role, ey = roles("gy", self.sizes["gy"]), self.ey
+        faces = []
+        for message, (_, from_high, _) in zip(received, role):
+            data = message[...]
             if ey > 1:
-                to_first = jnp.where(f == 0, pltpu.roll(face, width - (ey - 1), 1), 0.0)
-                to_last = jnp.where(f == ey - 1, pltpu.roll(face, ey - 1, 1), 0.0)
-                face = jnp.where(up, to_first, to_last)
-            out[...] = face
-
-    def pack(self, n_x, n_y, *refs):
+                width = data.shape[-1]
+                f = lax.rem(lax.broadcasted_iota(jnp.int32, data.shape, 1), ey)
+                beside = jnp.where(from_high, pltpu.roll(data, 1, 1), pltpu.roll(data, width - 1, 1))
+                here = f == jnp.where(from_high, ey - 1, 0)
+                data = jnp.concatenate([jnp.where(here, x, 0.0) for x in (data, beside)], axis=0)
+            faces.append(data)
+        return both_sides(faces, role)
+
+    def pack_first(self, n_x, *refs):
         s4, ind = refs[:2]
-        x_in, y_in = refs[2 : 2 + n_x], refs[2 + n_x : 2 + n_x + n_y]
-        s_out, i_out = refs[2 + n_x + n_y : 4 + n_x + n_y]
-        z_out = refs[4 + n_x + n_y :]
+        x_in, s_out, z_out = refs[2 : 2 + n_x], refs[2 + n_x], refs[3 + n_x :]
         p, block, rows = self.p, self.block, self.rows
         s_out[...] = s4[...]
-        i_out[...] = ind[...]
         if n_x:
             low, high = both_sides([x[...] for x in x_in], roles("gx", self.sizes["gx"]))
             s_out[:block, :] += low
             s_out[rows - block :, :] += high
+        halo3 = HALO * self.step3
+        for out, (up, _, _) in zip(z_out, roles("gz", self.sizes["gz"])):
+            self.pack(out, s_out, block, 0, self.n4 - self.halo4, up, 0)
+            self.pack(out, ind, p, halo3, self.n3 - 2 * halo3, up, block)
+
+    def pack(self, out, u, count, first, last, up, start):
+        p, width, size = self.p, self.w4, self.halo4
+        lane = lax.broadcasted_iota(jnp.int32, (count, width), 1)
+        for section in range(0, u.shape[0] // count, p):
+            total = jnp.zeros((count, width), F32)
+            for n in range(p):
+                at, shift = (section + n) * count, n * size
+                x = u[at : at + count, :]
+                below = pltpu.roll(x, (shift - first) % width, 1) if (shift - first) % width else x
+                above = pltpu.roll(x, (shift - last) % width, 1)
+                here = (lane >= shift) & (lane < shift + size)
+                total = jnp.where(here, jnp.where(up, above, below), total)
+            row = start + section // p * count
+            out[row : row + count, :] = total
+
+    def pack_second(self, n_y, n_z, *refs):
+        y_in, z_in, z_out = refs[:n_y], refs[n_y : n_y + n_z], refs[n_y + n_z :]
+        p, block, width, size = self.p, self.block, self.w4, self.halo4
+        low, high = self.second_sides(y_in)
+        halo3 = HALO * self.step3
+        lane = lax.broadcasted_iota(jnp.int32, (p, width), 1)
+        for packed, out, (up, _, _) in zip(z_in, z_out, roles("gz", self.sizes["gz"])):
+            out[...] = packed[...]
+            for face, row in ((low, 0), (high, block - p)):
+                total = jnp.zeros((p, width), F32)
+                for n in range(p):
+                    shift = n * size
+                    x = face[n * p : (n + 1) * p]
+                    below = pltpu.roll(x, shift, 1) if shift else x
+                    above = pltpu.roll(x, (shift - self.n4 + size) % width, 1)
+                    here = (lane >= shift) & (lane < shift + size)
+                    total = jnp.where(here, jnp.where(up, above, below), total)
+                out[row : row + p, :] += total
+            for n in range(2):
+                row = block + n * p
+                for face, group in ((low, 0), (high, p - 1)):
+                    shift = group * size
+                    x = face[row : row + p]
+                    below = pltpu.roll(x, (shift - halo3) % width, 1)
+                    above = pltpu.roll(x, (shift - self.n3 + 2 * halo3) % width, 1)
+                    here = (lane >= shift) & (lane < shift + size)
+                    out[row : row + p, :] += jnp.where(here, jnp.where(up, above, below), 0.0)
+
+    def own(self, n_y, *refs):
+        s4, ind, widen = refs[:3]
+        y_in, (r, scale, flag, work) = refs[3 : 3 + n_y], refs[3 + n_y :]
+        p, block, w3 = self.p, self.block, self.w3
+        work[...] = s4[...]
+        flag[...] = ind[...]
         if n_y:
-            low, high = both_sides([y[...] for y in y_in], roles("gy", self.sizes["gy"]))
-            for u, first, count in ((s_out, 0, p), (i_out, p, 2)):
+            low, high = self.second_sides(y_in)
+            for u, first, count in ((work, 0, p), (flag, p, 2)):
                 for i in range(count):
                     at, end, row = i * block, (i + 1) * block, (first + i) * p
                     u[at : at + p, :] += low[row : row + p]
                     u[end - p : end, :] += high[row : row + p]
-        width, size = self.w4, self.halo4
-        own3, halo3 = HALO * self.step3, HALO * self.step3
-        for out, (up, _, _) in zip(z_out, roles("gz", self.sizes["gz"])):
-            for u, count, first, last, start in (
-                (s_out, block, 0, self.n4 - size, 0),
-                (i_out, p, own3, self.n3 - 2 * halo3, block),
-            ):
-                lane = lax.broadcasted_iota(jnp.int32, (count, width), 1)
-                for section in range(0, u.shape[0] // count, p):
-                    total = jnp.zeros((count, width), F32)
-                    for n in range(p):
-                        at = (section + n) * count
-                        x = u[at : at + count, :]
-                        shift = n * size
-                        below = pltpu.roll(x, (shift - first) % width, 1) if (shift - first) % width else x
-                        above = pltpu.roll(x, (shift - last) % width, 1)
-                        here = (lane >= shift) & (lane < shift + size)
-                        total = jnp.where(here, jnp.where(up, above, below), total)
-                    row = start + section // p * count
-                    out[row : row + count, :] = total
+        both = dot2(work[...], widen[: self.w4, :])
+        r[...] = both[:, :w3]
+        scale[...] = both[:, w3:]
 
     def start(self, n_x, n_y, n_z, *refs):
-        s4, ind, g, coef, widen, ahead, back = refs[:7]
+        r_own, diagonal_own, flag_own, g, widen, ahead, back = refs[:7]
         z_in = refs[7 : 7 + n_z]
-        t, d, scale, v = refs[7 + n_z : 11 + n_z]
-        refs = refs[11 + n_z :]
+        t, scale, v = refs[7 + n_z : 10 + n_z]
+        refs = refs[10 + n_z :]
         x_out, y_out = refs[:n_x], refs[n_x : n_x + n_y]
-        upper, lower, r, flag = refs[n_x + n_y : n_x + n_y + 4]
-        work = refs[n_x + n_y + 4 :]
+        beside, r, flag = refs[n_x + n_y : n_x + n_y + 3]
+        work = refs[n_x + n_y + 3 :]
         p, block, rows, w3, w4 = self.p, self.block, self.rows, self.w3, self.w4
         step, first_own, end_own = self.step3, HALO * self.step3, self.n3 - HALO * self.step3
         size, part = self.sizes["gz"], self.halo4
@@ -587,15 +657,12 @@
         for n in range(p):
             first = pltpu.roll(low[:block], w4 - n * part, 1) if n else low[:block]
             second = pltpu.roll(high[:block], (part - n * part) % w4, 1) if n != 1 else high[:block]
-            beside = jnp.where(lane < part, first, jnp.where(lane < 2 * part, second, 0.0))
-            at = slice(n * block, (n + 1) * block)
-            upper[at, :w4], lower[at, :w4] = split(s4[at, :])
-            upper[at, w4:], lower[at, w4:] = split(beside)
-        both = jnp.dot(upper[...], widen[...], preferred_element_type=F32) + jnp.dot(
-            lower[...], widen[...], preferred_element_type=F32
-        )
-        r[...] = both[:, :w3]
-        scale[...] = both[:, w3:]
+            beside[n * block : (n + 1) * block, :] = jnp.where(
+                lane < part, first, jnp.where(lane < 2 * part, second, 0.0)
+            )
+        both = dot2(beside[...], widen[w4:, :])
+        r[...] = r_own[...] + both[:, :w3]
+        scale[...] = diagonal_own[...] + both[:, w3:]
         lane = lax.broadcasted_iota(jnp.int32, (p, w3), 1)
         for n in range(2 * p):
             row, shift = block + n // p * p, n % p * part
@@ -604,7 +671,7 @@
             flag[n * p : (n + 1) * p, :] = jnp.where(
                 lane < first_own,
                 first,
-                jnp.where(lane < end_own, ind[n * p : (n + 1) * p, :], jnp.where(lane < self.n3, second, 0.0)),
+                jnp.where(lane < end_own, flag_own[n * p : (n + 1) * p, :], jnp.where(lane < self.n3, second, 0.0)),
             )
         for u in (r, scale, flag):
             self.fold_third(
@@ -618,7 +685,6 @@
         end = jnp.where(index < size - 1, self.n3, end_own)
         lane = lax.broadcasted_iota(jnp.int32, (block, w3), 1)
         valid = (lane >= begin) & (lane < end)
-        middle = coef[0:1, :]
         for i in range(p):
             at = slice(i * block, (i + 1) * block)
             factor = jnp.where(valid, 1.0 / jnp.where(valid, scale[at, :], 1.0), 0.0)
@@ -626,54 +692,96 @@
                 row = 0 if i == 0 else block
                 factor = jnp.where(flag[row : row + block, :] > 0.5, 0.0, factor)
             scale[at, :] = factor
-            scaled = factor * r[at, :]
-            t[at, :] = scaled
-            d[at, :] = scaled * middle
-        self.operator(d, g, v, *work, ahead, back)
+            t[at, :] = factor * r[at, :]
+        self.operator(t, g, v, *work, ahead, back)
         self.iteration_fold(v)
         self.emit(v, x_out, y_out)
 
-    def advance(self, t, t_new, d, v, scale, coef, which, x_in, y_in, put):
-        t_new[...] = t[...] - scale[...] * v[...]
-        self.subtract_shared(t_new, scale, x_in, y_in)
-        keep, gain = (coef[8 * (2 * which + n) : 8 * (2 * which + n) + 1, :] for n in (1, 2))
-        for i in range(self.p):
-            at = slice(i * self.block, (i + 1) * self.block)
-            put(at, keep * d[at, :] + gain * t_new[at, :])
-
-    def middle(self, n_x, n_y, which, *refs):
-        t, d, scale, v, total, g, coef, ahead, back = refs[:9]
-        refs = refs[9:]
-        x_in, y_in, refs = refs[:n_x], refs[n_x : n_x + n_y], refs[n_x + n_y :]
-        t_new, d_new, v_new, total_new = refs[:4]
-        x_out, y_out = refs[4 : 4 + n_x], refs[4 + n_x : 4 + n_x + n_y]
-        work = refs[4 + n_x + n_y :]
-
-        def put(at, x):
-            d_new[at, :] = x
-            total_new[at, :] = total[at, :] + x
-
-        self.advance(t, t_new, d, v, scale, coef, which, x_in, y_in, put)
-        self.operator(d_new, g, v_new, *work, ahead, back)
-        self.iteration_fold(v_new)
-        self.emit(v_new, x_out, y_out)
-
-    def finish(self, n_x, n_y, which, *refs):
-        t, d, scale, v, total, coef, hot = refs[:7]
+    def factors(self, coef, n):
+        rows = [coef[8 * m : 8 * m + 1, :] for m in (0, 2 * n + 1, 2 * n + 2)]
+        return (rows[0] if n == 0 else None), rows[1], rows[2]
+
+    def shares(self, faces, scale, image, at):
+        low, high = faces
+        p, block = self.p, self.block
+        i = at // block
+        out = []
+        for start, face in ((at, low), (at + block - p, high)):
+            value = scale[start : start + p, :] * face[i * p : (i + 1) * p]
+            out.append((start, -value if image is None else -image * value))
+        return out
+
+    def preview(self, n_x, n_y, n, last, *refs):
+        t, t_old, d, scale, v, coef, hot = refs[:7]
         refs = refs[7:]
-        x_in, y_in, refs = refs[:n_x], refs[n_x : n_x + n_y], refs[n_x + n_y :]
-        out, t_new, field = refs
-
-        def put(at, x):
-            field[at, :] = total[at, :] + x
-
-        self.advance(t, t_new, d, v, scale, coef, which, x_in, y_in, put)
+        x_in, y_old, refs = refs[:n_x], refs[n_x : -2 if not last else -3], refs[-2 if not last else -3 :]
+        p, block, rows = self.p, self.block, self.rows
+        image, keep, gain = self.factors(coef, n)
+        start = coef[0:1, :]
+        if last:
+            out, t_new, field = refs
+        else:
+            t_new, d_new = refs
+        low, high = both_sides([x[...] for x in x_in], roles("gx", self.sizes["gx"]))
+        if n:
+            faces = self.second_sides(y_old) if n_y else None
+            image_old = self.factors(coef, n - 1)[0]
+        for i in range(p):
+            at = slice(i * block, (i + 1) * block)
+            value = v[at, :]
+            if n_x and i in (0, p - 1):
+                value = value + (low if i == 0 else high)
+            value = scale[at, :] * value
+            t_new[at, :] = t_old[at, :] - (value if image is None else image * value)
+            if n and n_y:
+                for row, share in self.shares(faces, scale, image_old, i * block):
+                    t_new[row : row + p, :] += share
+            direction = d[at, :] if n else start * t[at, :]
+            following = keep * direction + gain * t_new[at, :]
+            if last:
+                field[at, :] = start * t[at, :] + following + (direction if n else 0.0)
+            else:
+                d_new[at, :] = following
+        if last:
+            out[...] = self.by_slots(hot, field[...])
+
+    def by_slots(self, hot, field):
         value = None
-        for part in split(field[...]):
+        for part in split(field):
             term = lax.dot_general(
                 hot[...], part, (((1,), (1,)), ((), ())), preferred_element_type=F32
             )
             value = term if value is None else value + term
+        return value
+
+    def middle(self, n_x, n_y, n, *refs):
+        d, scale, g, coef, ahead, back = refs[:6]
+        y_in, refs = refs[6 : 6 + n_y], refs[6 + n_y :]
+        d_new, v = refs[:2]
+        x_out, y_out, work = refs[2 : 2 + n_x], refs[2 + n_x : 2 + n_x + n_y], refs[2 + n_x + n_y :]
+        d_new[...] = d[...]
+        image, _, gain = self.factors(coef, n)
+        if n_y:
+            faces = self.second_sides(y_in)
+            for i in range(self.p):
+                for row, share in self.shares(faces, scale, image, i * self.block):
+                    d_new[row : row + self.p, :] += gain * share
+        self.operator(d_new, g, v, *work, ahead, back)
+        self.iteration_fold(v)
+        self.emit(v, x_out, y_out)
+
+    def finish(self, n_y, n, *refs):
+        part, scale, coef, hot = refs[:4]
+        y_in, (out, field) = refs[4 : 4 + n_y], refs[4 + n_y :]
+        value = part[...]
+        image, _, gain = self.factors(coef, n)
+        if n_y:
+            faces = self.second_sides(y_in)
+            field[...] = jnp.zeros(field.shape, F32)
+            for i in range(self.p):
+                for row, share in self.shares(faces, scale, image, i * self.block):
+                    field[row : row + self.p, :] = gain * share
+            value = value + self.by_slots(hot, field[...])
         out[...] = value.reshape(out.shape)
 
 
@@ -714,102 +822,137 @@
     ahead, back = jnp.asarray(plan.third[0]), jnp.asarray(plan.third[1])
     field3, field4 = shape(rows, w3), shape(rows, w4)
     elements = element_slot.shape[-1]
-    spread = call(
-        plan.spread_table, [shape(plan.ey * lanes, p * w3, dtype=BF16)], (), flops=FLOPS, name="spread_table"
-    )[0]
-    operands = (
-        geometry,
-        viscosity,
-        spread,
-        dirichlet,
-        table,
-        jnp.asarray(plan.diagonal),
-        jnp.swapaxes(right_side, 1, 2),
-        element_slot,
-        jnp.asarray(plan.ids),
-        jnp.asarray(plan.third[2]),
+    spread3, spread4 = call(
+        plan.spread_tables,
+        [shape(plan.ey * lanes, p * w, dtype=BF16) for w in (w3, w4)],
+        (),
+        flops=FLOPS,
+        name="spread_tables",
     )
+    results = call(
+        functools.partial(plan.prepare, n_x, n_y),
+        [field4, shape(plan.c * elements, w3, dtype=BF16)] + [shape(block, w4)] * (n_x + n_y),
+        (
+            geometry,
+            viscosity,
+            spread4,
+            jnp.asarray(plan.face_table),
+            jnp.swapaxes(right_side, 1, 2),
+            element_slot,
+            jnp.asarray(plan.ids),
+            jnp.asarray(plan.third[2]),
+        ),
+        scratch=[vmem(rows, w4)],
+        name="prepare",
+    )
+    s4, hot3 = results[:2]
+    x_out, y_raw = results[2 : 2 + n_x], results[2 + n_x :]
+    x_in = send(x_out, "gx", x_pairs)
+
     lhs = FIELDS * block + 2 * plan.c * p
     results = call(
-        functools.partial(plan.prepare, n_x, n_y, n_z),
-        [
-            field4,
-            shape(2 * block, w3),
-            shape(FIELDS * rows, w3),
-            shape(plan.c * elements, w3, dtype=BF16),
-        ]
-        + [shape(block, w4)] * n_x
-        + [shape(block + 2 * p, w4)] * n_y
+        functools.partial(plan.convert, n_y, n_z),
+        [shape(FIELDS * rows, w3), shape(2 * block, w3)]
+        + [shape(2 * p, w3)] * n_y
         + [shape(p * plan.ey * p, lanes)] * n_z,
-        operands,
-        scratch=[vmem(lhs, plan.ey * lanes, dtype=BF16)] * 2 + [vmem(rows, w3)] * 3,
-        name="prepare",
+        (geometry, viscosity, spread3, dirichlet),
+        scratch=[vmem(lhs, plan.ey * lanes, dtype=BF16)] * 2,
+        name="convert",
     )
-    s4, ind, raw, hot3 = results[:4]
-    results = results[4:]
-    x_out, y_raw, z_geometry = results[:n_x], results[n_x : n_x + n_y], results[n_x + n_y :]
-    x_in = send(x_out, "gx", x_pairs)
-    def joined(x_in, y_raw):
+    raw, ind = results[:2]
+    y_more, z_geometry = results[2 : 2 + n_y], results[2 + n_y :]
+
+    def joined(x_in, y_raw, y_more=()):
         if not y_raw:
             return []
-        faces = [shape(*y.shape) for y in y_raw]
-        return call(functools.partial(plan.join, n_x, n_y), faces, x_in + y_raw, name="join")
-
-    y_in = send(joined(x_in, y_raw), "gy", y_pairs)
+        count = y_raw[0].shape[0] + (y_more[0].shape[0] if y_more else 0)
+        faces = [shape(count // 2 if plan.ey > 1 else count, y.shape[1]) for y in y_raw]
+        return call(functools.partial(plan.join, n_x, n_y), faces, x_in + y_raw + list(y_more), name="join")
+
+    y_in = send(joined(x_in, y_raw, y_more), "gy", y_pairs)
     z_geometry = send(z_geometry, ("gy", "gz"), z_pairs)
-    g, coef = call(
+    g = call(
         functools.partial(plan.halo_geometry, n_z),
-        [shape(FIELDS, rows, w3), shape(8 * (2 * ITERS - 1), 128)],
-        [raw, jnp.asarray(plan.halo), table, eig_low, eig_high] + z_geometry,
+        [shape(FIELDS, rows, w3)],
+        [raw, jnp.asarray(plan.halo), table] + z_geometry,
         scratch=[vmem(FIELDS * block, 128, dtype=BF16)] * 2 + [vmem(FIELDS * rows, w3)],
-        spaces={3: pltpu.SMEM, 4: pltpu.SMEM},
-        flops=2000000,
         name="halo_geometry",
+    )[0]
+    results = call(
+        functools.partial(plan.pack_first, n_x),
+        [field4] + [shape(block + 2 * p, w4)] * n_z,
+        [s4, ind] + x_in,
+        name="pack_first",
     )
-
-    results = call(
-        functools.partial(plan.pack, n_x, n_y),
-        [field4, shape(2 * block, w3)] + [shape(block + 2 * p, w4)] * n_z,
-        [s4, ind] + x_in + y_in,
-        name="pack",
+    s4, z_out = results[0], results[1:]
+    if n_y and n_z:
+        z_out = call(
+            functools.partial(plan.pack_second, n_y, n_z),
+            [shape(*z.shape) for z in z_out],
+            y_in + z_out,
+            flops=FLOPS,
+            name="pack_second",
+        )
+    z_in = send(z_out, ("gy", "gz"), z_pairs)
+    widen = jnp.asarray(plan.widen)
+    own = call(
+        functools.partial(plan.own, n_y),
+        [field3, field3, shape(2 * block, w3)],
+        [s4, ind, widen] + y_in,
+        scratch=[vmem(rows, w4)],
+        name="own",
     )
-    s4, ind = results[:2]
-    z_in = send(results[2:], ("gy", "gz"), z_pairs)
 
     messages = [shape(block, w3)] * (n_x + n_y)
     results = call(
         functools.partial(plan.start, n_x, n_y, n_z),
-        [field3] * 4 + messages,
-        [s4, ind, g, coef, jnp.asarray(plan.widen), ahead, back] + z_in,
-        scratch=[vmem(rows, 2 * w4, dtype=BF16)] * 2
-        + [vmem(rows, w3), vmem(2 * block, w3)]
-        + [vmem(rows, w3)] * 4,
+        [field3] * 3 + messages,
+        own + [g, widen, ahead, back] + z_in,
+        scratch=[vmem(rows, w4), vmem(rows, w3), vmem(2 * block, w3)] + [vmem(rows, w3)] * 4,
         name="first_direction",
     )
-    t, d, scale, v = results[:4]
-    total = d
+    t, scale, v = results[:3]
+    x_out, y_raw = results[3 : 3 + n_x], results[3 + n_x :]
+    x_out, low, high = lax.optimization_barrier((x_out, eig_low, eig_high))
+    coef = call(
+        plan.coefficients,
+        [shape(8 * (2 * ITERS - 1), 128)],
+        (low, high),
+        spaces={0: pltpu.SMEM, 1: pltpu.SMEM},
+        name="coefficients",
+    )[0]
+    t_old, d, y_in = t, t, []
     for n in range(ITERS - 1):
-        x_out, y_raw = results[4 : 4 + n_x], results[4 + n_x :]
+        last = n == ITERS - 2
         x_in = send(x_out, "gx", x_pairs)
-        y_in = send(joined(x_in, y_raw), "gy", y_pairs)
-        if n < ITERS - 2:
-            results = call(
-                functools.partial(plan.middle, n_x, n_y, n),
-                [field3] * 4 + messages,
-                [t, d, scale, v, total, g, coef, ahead, back] + x_in + y_in,
-                scratch=[vmem(rows, w3)] * 4,
-                name="direction",
-            )
-            t, d, v, total = results[:4]
-        else:
-            out = call(
-                functools.partial(plan.finish, n_x, n_y, n),
-                [shape(plan.c, elements, rows)],
-                [t, d, scale, v, total, coef, hot3] + x_in + y_in,
-                scratch=[vmem(rows, w3)] * 2,
-                name="field",
-            )[0]
-            return jnp.swapaxes(out, 1, 2)
+        y_old, y_in = y_in, send(joined(x_in, y_raw), "gy", y_pairs)
+        results = call(
+            functools.partial(plan.preview, n_x, n_y, n, last),
+            [shape(plan.c * elements, rows)] if last else [field3, field3],
+            [t, t_old, d, scale, v, coef, hot3] + x_in + y_old,
+            scratch=[vmem(rows, w3)] * 2 if last else [],
+            name="preview",
+        )
+        if last:
+            break
+        t_old, d = results
+        results = call(
+            functools.partial(plan.middle, n_x, n_y, n),
+            [field3] * 2 + messages,
+            [d, scale, g, coef, ahead, back] + y_in,
+            scratch=[vmem(rows, w3)] * 4,
+            name="direction",
+        )
+        d, v = results[:2]
+        x_out, y_raw = results[2 : 2 + n_x], results[2 + n_x :]
+    out = call(
+        functools.partial(plan.finish, n_y, n),
+        [shape(plan.c, elements, rows)],
+        [results[0], scale, coef, hot3] + y_in,
+        scratch=[vmem(rows, w3)],
+        name="field",
+    )[0]
+    return jnp.swapaxes(out, 1, 2)
 
 
 def solution(mesh):

time: 37.9 us -> 36.1 us (0.953)
  waiting for transfers between devices: 12.1 us -> 10.7 us
  starting transfers between devices: 15.4 us -> 14.6 us
  Pallas kernels: 7.7 us -> 8.23 us
    ppermute x13, waiting for transfers between devices: 12.1 us -> 10.7 us  [send(): return [lax.ppermute(x, axis, pair) for x, pair in zip(arrays, pairs)]]
    ppermute x13, starting transfers between devices: 15.4 us -> 14.6 us  [send(): return [lax.ppermute(x, axis, pair) for x, pair in zip(arrays, pairs)]]
    pallas_call x10 -> x16, Pallas kernels: 7.7 us -> 8.23 us  [call(): pl.pallas_call(kernel, out_shape=list(outputs), in_specs=specs, out_specs...]
  transfers between devices with their start and end apart: 13 -> 13, of which waited for: 7 -> 6; matrix products, arithmetic and copies ran while one was open for 0% -> 0% of each run, Pallas kernels for 5% -> 10%
where the time goes in v4:
time: 36.1 us; the launch traced here: 35.9 us
  starting transfers between devices  14.6 us (40%)
  waiting for transfers between devices  10.7 us (30%)
  Pallas kernels  8.23 us (23%)
  between operations  1.54 us (4%)
  local copies, waits for them, and re-layouts  0.83 us (2%)
    ppermute x13, starting transfers between devices, send(): return [lax.ppermute(x, axis, pair) for x, pair in zip(arrays, pairs)]  14.6 us
    ppermute x13, waiting for transfers between devices, send(): return [lax.ppermute(x, axis, pair) for x, pair in zip(arrays, pairs)]  10.7 us
    pallas_call x16, Pallas kernels, call(): pl.pallas_call(kernel, out_shape=list(outputs), in_specs=specs, out_specs...  8.23 us
    unnamed x26, local copies, waits for them, and re-layouts  0.83 us
  transfers between devices with their start and end apart: 13, of which 6 were waited for; matrix products, arithmetic and copies ran while one was open for 0% of the time, Pallas kernels for 10%

profile of v4, /device:TPU:0, one launch (start us, length us, event | category | flops | bytes accessed | tf_op | source)
XLA Modules:
  0.0 35.9 jit_solution(4011262224435651786)
XLA Ops:
  0.0 0.4 spread_tables.1
  0.4 0.5 %copy-done.7 = bf16[128,384]{1,0:T(8,128)(2,1)S(1)} copy-done((bf16[128,384]{1,0:T(8,128)(2,1)S(1)}, bf16[128,384]{1,0:T(8,128)(2,1)}, u32[]{:S(2)}) %copy-start.7) | copy-done | bytes 98328
  0.9 0.2 copy-done
  1.2 0.8 %prepare.1 = (f32[512,128]{1,0:T(8,128)S(1)}, bf16[96,128]{1,0:T(8,128)(2,1)S(1)}, f32[64,128]{1,0:T(8,128)S(1)}, f32[64,128]{1,0:T(8,128)S(1)}, f32[64,128]{1,0:T(8,128)S(1)}) custom-call(f32[6,8,16,128]{3,2,1,0:T(8,128)S(1)} %copy-done, f32[8,16,128]{2,1,0:T(8,128)S(1)} %copy-done.5, bf16[256,1024]{1,0:T(8,128)(2,1)S(1)} %get-tuple-element.42.refs_2_, ...), custom_call_target="tpu_custom_call" | custom-call | tf_op jit(solution)/shard_map/prepare/pallas_call | solution.py:805
  2.0 0.5 %collective-permute-start = (f32[64,128]{1,0:T(8,128)S(1)}, f32[64,128]{1,0:T(8,128)S(1)}, u32[]{:S(2)}, u32[]{:S(2)}) collective-permute-start(f32[64,128]{1,0:T(8,128)S(1)} %get-tuple-element.46), channel_id=1, source_target_pairs={{0,8},{8,0},{16,24},{24,16},{1,9},{9,1},{17,25},{25,17},{2,10},{10... | collective-permute-start | bytes 98312 | tf_op jit(solution)/shard_map/ppermute | solution.py:797
  2.5 2.6 %collective-permute-start.1 = (f32[64,128]{1,0:T(8,128)S(1)}, f32[64,128]{1,0:T(8,128)S(1)}, u32[]{:S(2)}, u32[]{:S(2)}) collective-permute-start(f32[64,128]{1,0:T(8,128)S(1)} %get-tuple-element.47), channel_id=1, source_target_pairs={{0,24},{8,16},{16,8},{24,0},{1,25},{9,17},{17,9},{25,1},{2,26},{10... | collective-permute-start | bytes 98312 | tf_op jit(solution)/shard_map/ppermute | solution.py:797
  5.1 1.0 %convert.1 = (f32[3584,128]{1,0:T(8,128)S(1)}, f32[128,128]{1,0:T(8,128)S(1)}, f32[16,128]{1,0:T(8,128)S(1)}, f32[128,128]{1,0:T(8,128)S(1)}, f32[128,128]{1,0:T(8,128)S(1)}) custom-call(f32[6,8,16,128]{3,2,1,0:T(8,128)S(1)} %copy-done, f32[8,16,128]{2,1,0:T(8,128)S(1)} %copy-done.5, bf16[256,1024]{1,0:T(8,128)(2,1)S(1)} %get-tuple-element.44.refs_2_, ...), custom_call_target="tpu_custom_call" | custom-call | tf_op jit(solution)/shard_map/convert/pallas_call | solution.py:805
  6.1 0.6 %collective-permute-done.1.refs_3_.refs_1_ = f32[64,128]{1,0:T(8,128)S(1)} collective-permute-done((f32[64,128]{1,0:T(8,128)S(1)}, f32[64,128]{1,0:T(8,128)S(1)}, u32[]{:S(2)}, u32[]{:S(2)}) %collective-permute-start.1) | collective-permute-done | bytes 32800 | tf_op jit(solution)/shard_map/ppermute | solution.py:797
  6.8 1.7 %collective-permute-start.2 = (f32[40,128]{1,0:T(8,128)S(1)}, f32[40,128]{1,0:T(8,128)S(1)}, u32[]{:S(2)}, u32[]{:S(2)}) collective-permute-start(f32[40,128]{1,0:T(8,128)S(1)} %join.3), channel_id=1, source_target_pairs={{0,4},{4,0},{1,5},{5,1},{2,6},{6,2},{3,7},{7,3},{8,12},{12,8},{9,1... | collective-permute-start | bytes 61448 | tf_op jit(solution)/shard_map/ppermute | solution.py:797
  8.6 1.6 %collective-permute-start.3 = (f32[128,128]{1,0:T(8,128)S(1)}, f32[128,128]{1,0:T(8,128)S(1)}, u32[]{:S(2)}, u32[]{:S(2)}) collective-permute-start(f32[128,128]{1,0:T(8,128)S(1)} %get-tuple-element.55), channel_id=1, source_target_pairs={{0,1},{1,0},{2,3},{3,2},{4,5},{5,4},{6,7},{7,6},{8,9},{9,8},{10,11... | collective-permute-start | bytes 196616 | tf_op jit(solution)/shard_map/ppermute | solution.py:797
  10.1 0.5 %collective-permute-start.4 = (f32[128,128]{1,0:T(8,128)S(1)}, f32[128,128]{1,0:T(8,128)S(1)}, u32[]{:S(2)}, u32[]{:S(2)}) collective-permute-start(f32[128,128]{1,0:T(8,128)S(1)} %get-tuple-element.56), channel_id=1, source_target_pairs={{0,4},{1,2},{2,1},{3,7},{4,0},{5,6},{6,5},{7,3},{8,12},{9,10},{10,... | collective-permute-start | bytes 196616 | tf_op jit(solution)/shard_map/ppermute | solution.py:797
  10.7 0.4 %pack_first.1 = (f32[512,128]{1,0:T(8,128)S(1)}, f32[80,128]{1,0:T(8,128)S(1)}, f32[80,128]{1,0:T(8,128)S(1)}) custom-call(f32[512,128]{1,0:T(8,128)S(1)} %get-tuple-element.43.refs_0_, f32[128,128]{1,0:T(8,128)S(1)} %get-tuple-element.45.refs_1_, f32[64,128]{1,0:T(8,128)S(1)} %collective-permute-done.refs_2_.refs_0_, ...), custom_call_target="tpu_custom_call" | custom-call | tf_op jit(solution)/shard_map/pack_first/pallas_call | solution.py:805
  11.1 0.2 pack_second.1
  11.2 2.7 %collective-permute-start.5 = (f32[80,128]{1,0:T(8,128)S(1)}, f32[80,128]{1,0:T(8,128)S(1)}, u32[]{:S(2)}, u32[]{:S(2)}) collective-permute-start(f32[80,128]{1,0:T(8,128)S(1)} %get-tuple-element.59), channel_id=1, source_target_pairs={{0,1},{1,0},{2,3},{3,2},{4,5},{5,4},{6,7},{7,6},{8,9},{9,8},{10,11... | collective-permute-start | bytes 122888 | tf_op jit(solution)/shard_map/ppermute | solution.py:797
  13.9 0.5 %collective-permute-start.6 = (f32[80,128]{1,0:T(8,128)S(1)}, f32[80,128]{1,0:T(8,128)S(1)}, u32[]{:S(2)}, u32[]{:S(2)}) collective-permute-start(f32[80,128]{1,0:T(8,128)S(1)} %get-tuple-element.60), channel_id=1, source_target_pairs={{0,4},{1,2},{2,1},{3,7},{4,0},{5,6},{6,5},{7,3},{8,12},{9,10},{10,... | collective-permute-start | bytes 122888 | tf_op jit(solution)/shard_map/ppermute | solution.py:797
  14.5 0.3 own.1
  14.8 1.4 %halo_geometry.1.refs_3_.refs_2_ = f32[7,512,128]{2,1,0:T(8,128)S(1)} custom-call(f32[3584,128]{1,0:T(8,128)S(1)} %get-tuple-element.54.refs_0_, bf16[128,1024]{1,0:T(8,128)(2,1)S(1)} %copy-done.4, f32[64,128]{1,0:T(8,128)S(1)} %copy-done.9, f32[128,128]{1,0:T(8,128)S(1)} %collective-permute-done.3.refs_3_, f32[128,128]{1,0:T(8,128)S(1)} %collective-permute-done.4.refs_4_), custom_call_target="tpu_custom_call" | custom-call | tf_op jit(solution)/shard_map/halo_geometry/pallas_call | solution.py:805
  16.3 1.7 %collective-permute-done.6.refs_8_ = f32[80,128]{1,0:T(8,128)S(1)} collective-permute-done((f32[80,128]{1,0:T(8,128)S(1)}, f32[80,128]{1,0:T(8,128)S(1)}, u32[]{:S(2)}, u32[]{:S(2)}) %collective-permute-start.6) | collective-permute-done | bytes 40992 | tf_op jit(solution)/shard_map/ppermute | solution.py:797
  18.0 1.4 %first_direction.1 = (f32[512,128]{1,0:T(8,128)S(1)}, f32[512,128]{1,0:T(8,128)S(1)}, f32[512,128]{1,0:T(8,128)S(1)}, f32[64,128]{1,0:T(8,128)S(1)}, f32[64,128]{1,0:T(8,128)S(1)}, /*index=5*/f32[64,128]{1,0:T(8,128)S(1)}) custom-call(f32[512,128]{1,0:T(8,128)S(1)} %get-tuple-element.51.refs_0_, f32[512,128]{1,0:T(8,128)S(1)} %get-tuple-element.52.refs_1_, ...), custom_call_target="tpu_custom_call" | custom-call | tf_op jit(solution)/shard_map/first_direction/pallas_call | solution.py:805
  19.4 1.6 %collective-permute-start.8 = (f32[64,128]{1,0:T(8,128)S(1)}, f32[64,128]{1,0:T(8,128)S(1)}, u32[]{:S(2)}, u32[]{:S(2)}) collective-permute-start(f32[64,128]{1,0:T(8,128)S(1)} %get-tuple-element.70), channel_id=1, source_target_pairs={{0,24},{8,16},{16,8},{24,0},{1,25},{9,17},{17,9},{25,1},{2,26},{10... | collective-permute-start | bytes 98312 | tf_op jit(solution)/shard_map/ppermute | solution.py:797
  21.0 1.8 %collective-permute-done.8.refs_8_.refs_1_ = f32[64,128]{1,0:T(8,128)S(1)} collective-permute-done((f32[64,128]{1,0:T(8,128)S(1)}, f32[64,128]{1,0:T(8,128)S(1)}, u32[]{:S(2)}, u32[]{:S(2)}) %collective-permute-start.8) | collective-permute-done | bytes 32800 | tf_op jit(solution)/shard_map/ppermute | solution.py:797
  22.8 0.1 join.4
  22.9 0.6 %collective-permute-start.9 = (f32[32,128]{1,0:T(8,128)S(1)}, f32[32,128]{1,0:T(8,128)S(1)}, u32[]{:S(2)}, u32[]{:S(2)}) collective-permute-start(f32[32,128]{1,0:T(8,128)S(1)} %join.4), channel_id=1, source_target_pairs={{0,4},{4,0},{1,5},{5,1},{2,6},{6,2},{3,7},{7,3},{8,12},{12,8},{9,1... | collective-permute-start | bytes 49160 | tf_op jit(solution)/shard_map/ppermute | solution.py:797
  24.8 0.1 preview.2
  24.9 1.8 %collective-permute-done.9.refs_6_.refs_9_ = f32[32,128]{1,0:T(8,128)S(1)} collective-permute-done((f32[32,128]{1,0:T(8,128)S(1)}, f32[32,128]{1,0:T(8,128)S(1)}, u32[]{:S(2)}, u32[]{:S(2)}) %collective-permute-start.9) | collective-permute-done | bytes 16416 | tf_op jit(solution)/shard_map/ppermute | solution.py:797
  26.7 0.8 %direction.1 = (f32[512,128]{1,0:T(8,128)S(1)}, f32[512,128]{1,0:T(8,128)S(1)}, f32[64,128]{1,0:T(8,128)S(1)}, f32[64,128]{1,0:T(8,128)S(1)}, f32[64,128]{1,0:T(8,128)S(1)}) custom-call(f32[512,128]{1,0:T(8,128)S(1)} %get-tuple-element.72.refs_0_, f32[512,128]{1,0:T(8,128)S(1)} %get-tuple-element.62.refs_3_.refs_1_, ...), custom_call_target="tpu_custom_call" | custom-call | tf_op jit(solution)/shard_map/direction/pallas_call | solution.py:805
  27.6 1.6 %collective-permute-start.11 = (f32[64,128]{1,0:T(8,128)S(1)}, f32[64,128]{1,0:T(8,128)S(1)}, u32[]{:S(2)}, u32[]{:S(2)}) collective-permute-start(f32[64,128]{1,0:T(8,128)S(1)} %get-tuple-element.77), channel_id=1, source_target_pairs={{0,24},{8,16},{16,8},{24,0},{1,25},{9,17},{17,9},{25,1},{2,26},{10... | collective-permute-start | bytes 98312 | tf_op jit(solution)/shard_map/ppermute | solution.py:797
  29.2 1.8 %collective-permute-done.11.refs_8_.refs_1_ = f32[64,128]{1,0:T(8,128)S(1)} collective-permute-done((f32[64,128]{1,0:T(8,128)S(1)}, f32[64,128]{1,0:T(8,128)S(1)}, u32[]{:S(2)}, u32[]{:S(2)}) %collective-permute-start.11) | collective-permute-done | bytes 32800 | tf_op jit(solution)/shard_map/ppermute | solution.py:797
  31.1 0.6 %collective-permute-start.12 = (f32[32,128]{1,0:T(8,128)S(1)}, f32[32,128]{1,0:T(8,128)S(1)}, u32[]{:S(2)}, u32[]{:S(2)}) collective-permute-start(f32[32,128]{1,0:T(8,128)S(1)} %join.5), channel_id=1, source_target_pairs={{0,4},{4,0},{1,5},{5,1},{2,6},{6,2},{3,7},{7,3},{8,12},{12,8},{9,1... | collective-permute-start | bytes 49160 | tf_op jit(solution)/shard_map/ppermute | solution.py:797
  31.7 0.3 preview.3.refs_0_
  32.0 2.9 %collective-permute-done.12.refs_4_ = f32[32,128]{1,0:T(8,128)S(1)} collective-permute-done((f32[32,128]{1,0:T(8,128)S(1)}, f32[32,128]{1,0:T(8,128)S(1)}, u32[]{:S(2)}, u32[]{:S(2)}) %collective-permute-start.12) | collective-permute-done | bytes 16416 | tf_op jit(solution)/shard_map/ppermute | solution.py:797
  34.9 1.0 %field.1 = f32[3,32,512]{2,1,0:T(8,128)} custom-call(f32[96,512]{1,0:T(8,128)S(1)} %preview.3.refs_0_, f32[512,128]{1,0:T(8,128)S(1)} %get-tuple-element.62.refs_3_.refs_1_, f32[40,128]{1,0:T(8,128)S(1)} %coefficients.1.refs_5_.refs_3_.refs_2_, bf16[96,128]{1,0:T(8,128)(2,1)S(1)} %get-tuple-element.68.refs_6_.refs_3_, ...), custom_call_target="tpu_custom_call" | custom-call | tf_op jit(solution)/shard_map/field/pallas_call | solution.py:805
  (36 shorter events, 0.5 us)
Async XLA Ops:
  0.0 0.9 %copy-start.7 = (bf16[128,384]{1,0:T(8,128)(2,1)S(1)}, bf16[128,384]{1,0:T(8,128)(2,1)}, u32[]{:S(2)}) copy-start(bf16[128,384]{1,0:T(8,128)(2,1)} %constant.21.clone.refs_7_) | copy-start | bytes 294916
  0.0 0.9 %copy-start.10 = (f32[48,128]{1,0:T(8,128)S(1)}, f32[48,128]{1,0:T(8,128)}, u32[]{:S(2)}) copy-start(f32[48,128]{1,0:T(8,128)} %constant.19.clone.refs_3_) | copy-start | bytes 73732
  0.0 0.9 %copy-start.11 = (s32[6,128]{1,0:T(8,128)S(1)}, s32[6,128]{1,0:T(8,128)}, u32[]{:S(2)}) copy-start(s32[6,128]{1,0:T(8,128)} %constant.20.clone.refs_6_) | copy-start | bytes 9220
  0.0 0.9 %copy-start.5 = (f32[8,16,128]{2,1,0:T(8,128)S(1)}, f32[8,16,128]{2,1,0:T(8,128)}, u32[]{:S(2)}) copy-start(f32[8,16,128]{2,1,0:T(8,128)} %refs_1_.4) | copy-start | bytes 196612
  0.0 1.1 %copy-start = (f32[6,8,16,128]{3,2,1,0:T(8,128)S(1)}, f32[6,8,16,128]{3,2,1,0:T(8,128)}, u32[]{:S(2)}) copy-start(f32[6,8,16,128]{3,2,1,0:T(8,128)} %refs_0_.3) | copy-start | bytes 1179652
  0.0 1.1 %copy-start.12 = (s32[1,32]{1,0:T(1,128)S(1)}, s32[1,32]{1,0:T(1,128)}, u32[]{:S(2)}) copy-start(s32[1,32]{1,0:T(1,128)} %refs_5_.3) | copy-start | bytes 388
  0.0 1.2 %copy-start.6 = (f32[3,512,32]{1,2,0:T(8,128)S(1)}, f32[3,512,32]{1,2,0:T(8,128)}, u32[]{:S(2)}) copy-start(f32[3,512,32]{1,2,0:T(8,128)} %param.15) | copy-start | bytes 589828
  0.0 5.1 %copy-start.8 = (s32[2,3,16,128]{3,2,1,0:T(8,128)S(1)}, s32[2,3,16,128]{3,2,1,0:T(8,128)}, u32[]{:S(2)}) copy-start(s32[2,3,16,128]{3,2,1,0:T(8,128)} %refs_3_.2) | copy-start | bytes 147460
  2.0 4.1 %collective-permute-start = (f32[64,128]{1,0:T(8,128)S(1)}, f32[64,128]{1,0:T(8,128)S(1)}, u32[]{:S(2)}, u32[]{:S(2)}) collective-permute-start(f32[64,128]{1,0:T(8,128)S(1)} %get-tuple-element.46), channel_id=1, source_target_pairs={{0,8},{8,0},{16,24},{24,16},{1,9},{9,1},{17,25},{25,17},{2,10},{10... | collective-permute-start | bytes 98312 | tf_op jit(solution)/shard_map/ppermute | solution.py:797
  2.5 4.3 %collective-permute-start.1 = (f32[64,128]{1,0:T(8,128)S(1)}, f32[64,128]{1,0:T(8,128)S(1)}, u32[]{:S(2)}, u32[]{:S(2)}) collective-permute-start(f32[64,128]{1,0:T(8,128)S(1)} %get-tuple-element.47), channel_id=1, source_target_pairs={{0,24},{8,16},{16,8},{24,0},{1,25},{9,17},{17,9},{25,1},{2,26},{10... | collective-permute-start | bytes 98312 | tf_op jit(solution)/shard_map/ppermute | solution.py:797
  6.8 4.2 %collective-permute-start.2 = (f32[40,128]{1,0:T(8,128)S(1)}, f32[40,128]{1,0:T(8,128)S(1)}, u32[]{:S(2)}, u32[]{:S(2)}) collective-permute-start(f32[40,128]{1,0:T(8,128)S(1)} %join.3), channel_id=1, source_target_pairs={{0,4},{4,0},{1,5},{5,1},{2,6},{6,2},{3,7},{7,3},{8,12},{12,8},{9,1... | collective-permute-start | bytes 61448 | tf_op jit(solution)/shard_map/ppermute | solution.py:797
  8.6 6.2 %collective-permute-start.3 = (f32[128,128]{1,0:T(8,128)S(1)}, f32[128,128]{1,0:T(8,128)S(1)}, u32[]{:S(2)}, u32[]{:S(2)}) collective-permute-start(f32[128,128]{1,0:T(8,128)S(1)} %get-tuple-element.55), channel_id=1, source_target_pairs={{0,1},{1,0},{2,3},{3,2},{4,5},{5,4},{6,7},{7,6},{8,9},{9,8},{10,11... | collective-permute-start | bytes 196616 | tf_op jit(solution)/shard_map/ppermute | solution.py:797
  10.1 4.6 %collective-permute-start.4 = (f32[128,128]{1,0:T(8,128)S(1)}, f32[128,128]{1,0:T(8,128)S(1)}, u32[]{:S(2)}, u32[]{:S(2)}) collective-permute-start(f32[128,128]{1,0:T(8,128)S(1)} %get-tuple-element.56), channel_id=1, source_target_pairs={{0,4},{1,2},{2,1},{3,7},{4,0},{5,6},{6,5},{7,3},{8,12},{9,10},{10,... | collective-permute-start | bytes 196616 | tf_op jit(solution)/shard_map/ppermute | solution.py:797
  11.0 3.4 %copy-start.1 = (bf16[256,256]{1,0:T(8,128)(2,1)S(1)}, bf16[256,256]{1,0:T(8,128)(2,1)}, u32[]{:S(2)}) copy-start(bf16[256,256]{1,0:T(8,128)(2,1)} %constant.23.clone.refs_2_.refs_4_) | copy-start | bytes 393220
  11.0 3.7 %copy-start.4 = (bf16[128,1024]{1,0:T(8,128)(2,1)S(1)}, bf16[128,1024]{1,0:T(8,128)(2,1)}, u32[]{:S(2)}) copy-start(bf16[128,1024]{1,0:T(8,128)(2,1)} %constant.22.clone.refs_1_) | copy-start | bytes 786436
  11.1 3.7 %copy-start.9 = (f32[64,128]{1,0:T(8,128)S(1)}, f32[64,128]{1,0:T(8,128)}, u32[]{:S(2)}) copy-start(f32[64,128]{1,0:T(8,128)} %constant.16.clone.refs_2_) | copy-start | bytes 98308
  11.2 5.0 %collective-permute-start.5 = (f32[80,128]{1,0:T(8,128)S(1)}, f32[80,128]{1,0:T(8,128)S(1)}, u32[]{:S(2)}, u32[]{:S(2)}) collective-permute-start(f32[80,128]{1,0:T(8,128)S(1)} %get-tuple-element.59), channel_id=1, source_target_pairs={{0,1},{1,0},{2,3},{3,2},{4,5},{5,4},{6,7},{7,6},{8,9},{9,8},{10,11... | collective-permute-start | bytes 122888 | tf_op jit(solution)/shard_map/ppermute | solution.py:797
  13.9 4.0 %collective-permute-start.6 = (f32[80,128]{1,0:T(8,128)S(1)}, f32[80,128]{1,0:T(8,128)S(1)}, u32[]{:S(2)}, u32[]{:S(2)}) collective-permute-start(f32[80,128]{1,0:T(8,128)S(1)} %get-tuple-element.60), channel_id=1, source_target_pairs={{0,4},{1,2},{2,1},{3,7},{4,0},{5,6},{6,5},{7,3},{8,12},{9,10},{10,... | collective-permute-start | bytes 122888 | tf_op jit(solution)/shard_map/ppermute | solution.py:797
  14.8 3.2 %copy-start.2 = (bf16[128,384]{1,0:T(8,128)(2,1)S(1)}, bf16[128,384]{1,0:T(8,128)(2,1)}, u32[]{:S(2)}) copy-start(bf16[128,384]{1,0:T(8,128)(2,1)} %constant.18.clone.refs_6_.refs_5_) | copy-start | bytes 294916
  14.8 3.1 %copy-start.3 = (bf16[128,384]{1,0:T(8,128)(2,1)S(1)}, bf16[128,384]{1,0:T(8,128)(2,1)}, u32[]{:S(2)}) copy-start(bf16[128,384]{1,0:T(8,128)(2,1)} %constant.17.clone.refs_5_.refs_4_) | copy-start | bytes 294916
  19.3 1.7 %collective-permute-start.7 = (f32[64,128]{1,0:T(8,128)S(1)}, f32[64,128]{1,0:T(8,128)S(1)}, u32[]{:S(2)}, u32[]{:S(2)}) collective-permute-start(f32[64,128]{1,0:T(8,128)S(1)} %get-tuple-element.69), channel_id=1, source_target_pairs={{0,8},{8,0},{16,24},{24,16},{1,9},{9,1},{17,25},{25,17},{2,10},{10... | collective-permute-start | bytes 98312 | tf_op jit(solution)/shard_map/ppermute | solution.py:797
  19.4 3.4 %collective-permute-start.8 = (f32[64,128]{1,0:T(8,128)S(1)}, f32[64,128]{1,0:T(8,128)S(1)}, u32[]{:S(2)}, u32[]{:S(2)}) collective-permute-start(f32[64,128]{1,0:T(8,128)S(1)} %get-tuple-element.70), channel_id=1, source_target_pairs={{0,24},{8,16},{16,8},{24,0},{1,25},{9,17},{17,9},{25,1},{2,26},{10... | collective-permute-start | bytes 98312 | tf_op jit(solution)/shard_map/ppermute | solution.py:797
  22.9 3.8 %collective-permute-start.9 = (f32[32,128]{1,0:T(8,128)S(1)}, f32[32,128]{1,0:T(8,128)S(1)}, u32[]{:S(2)}, u32[]{:S(2)}) collective-permute-start(f32[32,128]{1,0:T(8,128)S(1)} %join.4), channel_id=1, source_target_pairs={{0,4},{4,0},{1,5},{5,1},{2,6},{6,2},{3,7},{7,3},{8,12},{12,8},{9,1... | collective-permute-start | bytes 49160 | tf_op jit(solution)/shard_map/ppermute | solution.py:797
  27.6 1.7 %collective-permute-start.10 = (f32[64,128]{1,0:T(8,128)S(1)}, f32[64,128]{1,0:T(8,128)S(1)}, u32[]{:S(2)}, u32[]{:S(2)}) collective-permute-start(f32[64,128]{1,0:T(8,128)S(1)} %get-tuple-element.76), channel_id=1, source_target_pairs={{0,8},{8,0},{16,24},{24,16},{1,9},{9,1},{17,25},{25,17},{2,10},{10... | collective-permute-start | bytes 98312 | tf_op jit(solution)/shard_map/ppermute | solution.py:797
  27.6 3.4 %collective-permute-start.11 = (f32[64,128]{1,0:T(8,128)S(1)}, f32[64,128]{1,0:T(8,128)S(1)}, u32[]{:S(2)}, u32[]{:S(2)}) collective-permute-start(f32[64,128]{1,0:T(8,128)S(1)} %get-tuple-element.77), channel_id=1, source_target_pairs={{0,24},{8,16},{16,8},{24,0},{1,25},{9,17},{17,9},{25,1},{2,26},{10... | collective-permute-start | bytes 98312 | tf_op jit(solution)/shard_map/ppermute | solution.py:797
  31.1 3.8 %collective-permute-start.12 = (f32[32,128]{1,0:T(8,128)S(1)}, f32[32,128]{1,0:T(8,128)S(1)}, u32[]{:S(2)}, u32[]{:S(2)}) collective-permute-start(f32[32,128]{1,0:T(8,128)S(1)} %join.5), channel_id=1, source_target_pairs={{0,4},{4,0},{1,5},{5,1},{2,6},{6,2},{3,7},{7,3},{8,12},{12,8},{9,1... | collective-permute-start | bytes 49160 | tf_op jit(solution)/shard_map/ppermute | solution.py:797

commit v5 on v4

--- a/solution.py
+++ b/solution.py
@@ -790,7 +790,7 @@
     p, block, rows, w3, w4 = plan.p, plan.block, plan.rows, plan.w3, plan.w4
     x_pairs = pairings(("gx",), (sizes["gx"],), 0)
     y_pairs = pairings(("gy",), (sizes["gy"],), 0)
-    z_pairs = pairings(("gy", "gz"), (sizes["gy"], sizes["gz"]), 1)
+    z_pairs = pairings(("gx", "gz"), (sizes["gx"], sizes["gz"]), 1)
     n_x, n_y, n_z = len(x_pairs), len(y_pairs), len(z_pairs)
 
     def send(arrays, axis, pairs):
@@ -870,7 +870,7 @@
         return call(functools.partial(plan.join, n_x, n_y), faces, x_in + y_raw + list(y_more), name="join")
 
     y_in = send(joined(x_in, y_raw, y_more), "gy", y_pairs)
-    z_geometry = send(z_geometry, ("gy", "gz"), z_pairs)
+    z_geometry = send(z_geometry, ("gx", "gz"), z_pairs)
     g = call(
         functools.partial(plan.halo_geometry, n_z),
         [shape(FIELDS, rows, w3)],
@@ -893,7 +893,7 @@
             flops=FLOPS,
             name="pack_second",
         )
-    z_in = send(z_out, ("gy", "gz"), z_pairs)
+    z_in = send(z_out, ("gx", "gz"), z_pairs)
     widen = jnp.asarray(plan.widen)
     own = call(
         functools.partial(plan.own, n_y),

time: 36.1 us -> 34.4 us (0.953)
  waiting for transfers between devices: 10.7 us -> 9.68 us
  starting transfers between devices: 14.6 us -> 14 us
    ppermute x13, waiting for transfers between devices: 10.7 us -> 9.68 us  [send(): return [lax.ppermute(x, axis, pair) for x, pair in zip(arrays, pairs)]]
    ppermute x13, starting transfers between devices: 14.6 us -> 14 us  [send(): return [lax.ppermute(x, axis, pair) for x, pair in zip(arrays, pairs)]]
  transfers between devices with their start and end apart: 13 -> 13, of which waited for: 6 -> 7; matrix products, arithmetic and copies ran while one was open for 0% -> 0% of each run, Pallas kernels for 10% -> 11%
where the time goes in v5:
time: 34.4 us; the launch traced here: 34.2 us
  starting transfers between devices  14 us (41%)
  waiting for transfers between devices  9.68 us (28%)
  Pallas kernels  8.23 us (24%)
  between operations  1.5 us (4%)
  local copies, waits for them, and re-layouts  0.82 us (2%)
    ppermute x13, starting transfers between devices, send(): return [lax.ppermute(x, axis, pair) for x, pair in zip(arrays, pairs)]  14 us
    ppermute x13, waiting for transfers between devices, send(): return [lax.ppermute(x, axis, pair) for x, pair in zip(arrays, pairs)]  9.68 us
    pallas_call x16, Pallas kernels, call(): pl.pallas_call(kernel, out_shape=list(outputs), in_specs=specs, out_specs...  8.23 us
    unnamed x26, local copies, waits for them, and re-layouts  0.82 us
  transfers between devices with their start and end apart: 13, of which 7 were waited for; matrix products, arithmetic and copies ran while one was open for 0% of the time, Pallas kernels for 11%

profile of v5, /device:TPU:0, one launch (start us, length us, event | category | flops | bytes accessed | tf_op | source)
XLA Modules:
  0.0 34.2 jit_solution(7520670412152558061)
XLA Ops:
  0.0 0.4 %spread_tables.1 = (bf16[256,1024]{1,0:T(8,128)(2,1)S(1)}, bf16[256,1024]{1,0:T(8,128)(2,1)S(1)}) custom-call(), custom_call_target="tpu_custom_call" | custom-call | flops 3000000000 | tf_op jit(solution)/shard_map/spread_tables/pallas_call | solution.py:805
  0.4 0.5 %copy-done.7 = bf16[128,384]{1,0:T(8,128)(2,1)S(1)} copy-done((bf16[128,384]{1,0:T(8,128)(2,1)S(1)}, bf16[128,384]{1,0:T(8,128)(2,1)}, u32[]{:S(2)}) %copy-start.7) | copy-done | bytes 98328
  0.9 0.2 copy-done
  1.2 0.8 %prepare.1 = (f32[512,128]{1,0:T(8,128)S(1)}, bf16[96,128]{1,0:T(8,128)(2,1)S(1)}, f32[64,128]{1,0:T(8,128)S(1)}, f32[64,128]{1,0:T(8,128)S(1)}, f32[64,128]{1,0:T(8,128)S(1)}) custom-call(f32[6,8,16,128]{3,2,1,0:T(8,128)S(1)} %copy-done, f32[8,16,128]{2,1,0:T(8,128)S(1)} %copy-done.5, bf16[256,1024]{1,0:T(8,128)(2,1)S(1)} %get-tuple-element.42.refs_2_, ...), custom_call_target="tpu_custom_call" | custom-call | tf_op jit(solution)/shard_map/prepare/pallas_call | solution.py:805
  2.0 0.5 %collective-permute-start = (f32[64,128]{1,0:T(8,128)S(1)}, f32[64,128]{1,0:T(8,128)S(1)}, u32[]{:S(2)}, u32[]{:S(2)}) collective-permute-start(f32[64,128]{1,0:T(8,128)S(1)} %get-tuple-element.46), channel_id=1, source_target_pairs={{0,8},{8,0},{16,24},{24,16},{1,9},{9,1},{17,25},{25,17},{2,10},{10... | collective-permute-start | bytes 98312 | tf_op jit(solution)/shard_map/ppermute | solution.py:797
  2.5 2.6 %collective-permute-start.1 = (f32[64,128]{1,0:T(8,128)S(1)}, f32[64,128]{1,0:T(8,128)S(1)}, u32[]{:S(2)}, u32[]{:S(2)}) collective-permute-start(f32[64,128]{1,0:T(8,128)S(1)} %get-tuple-element.47), channel_id=1, source_target_pairs={{0,24},{8,16},{16,8},{24,0},{1,25},{9,17},{17,9},{25,1},{2,26},{10... | collective-permute-start | bytes 98312 | tf_op jit(solution)/shard_map/ppermute | solution.py:797
  5.1 1.0 %convert.1 = (f32[3584,128]{1,0:T(8,128)S(1)}, f32[128,128]{1,0:T(8,128)S(1)}, f32[16,128]{1,0:T(8,128)S(1)}, f32[128,128]{1,0:T(8,128)S(1)}, f32[128,128]{1,0:T(8,128)S(1)}) custom-call(f32[6,8,16,128]{3,2,1,0:T(8,128)S(1)} %copy-done, f32[8,16,128]{2,1,0:T(8,128)S(1)} %copy-done.5, bf16[256,1024]{1,0:T(8,128)(2,1)S(1)} %get-tuple-element.44.refs_2_, ...), custom_call_target="tpu_custom_call" | custom-call | tf_op jit(solution)/shard_map/convert/pallas_call | solution.py:805
  6.1 0.6 %collective-permute-done.1.refs_3_.refs_1_ = f32[64,128]{1,0:T(8,128)S(1)} collective-permute-done((f32[64,128]{1,0:T(8,128)S(1)}, f32[64,128]{1,0:T(8,128)S(1)}, u32[]{:S(2)}, u32[]{:S(2)}) %collective-permute-start.1) | collective-permute-done | bytes 32800 | tf_op jit(solution)/shard_map/ppermute | solution.py:797
  6.8 1.7 %collective-permute-start.2 = (f32[40,128]{1,0:T(8,128)S(1)}, f32[40,128]{1,0:T(8,128)S(1)}, u32[]{:S(2)}, u32[]{:S(2)}) collective-permute-start(f32[40,128]{1,0:T(8,128)S(1)} %join.3), channel_id=1, source_target_pairs={{0,4},{4,0},{1,5},{5,1},{2,6},{6,2},{3,7},{7,3},{8,12},{12,8},{9,1... | collective-permute-start | bytes 61448 | tf_op jit(solution)/shard_map/ppermute | solution.py:797
  8.6 1.6 %collective-permute-start.3 = (f32[128,128]{1,0:T(8,128)S(1)}, f32[128,128]{1,0:T(8,128)S(1)}, u32[]{:S(2)}, u32[]{:S(2)}) collective-permute-start(f32[128,128]{1,0:T(8,128)S(1)} %get-tuple-element.55), channel_id=1, source_target_pairs={{0,1},{1,0},{2,3},{3,2},{8,9},{9,8},{10,11},{11,10},{16,17},{17,16... | collective-permute-start | bytes 196616 | tf_op jit(solution)/shard_map/ppermute | solution.py:797
  10.1 0.4 %pack_first.1 = (f32[512,128]{1,0:T(8,128)S(1)}, f32[80,128]{1,0:T(8,128)S(1)}, f32[80,128]{1,0:T(8,128)S(1)}) custom-call(f32[512,128]{1,0:T(8,128)S(1)} %get-tuple-element.43.refs_0_, f32[128,128]{1,0:T(8,128)S(1)} %get-tuple-element.45.refs_1_, f32[64,128]{1,0:T(8,128)S(1)} %collective-permute-done.refs_2_.refs_0_, ...), custom_call_target="tpu_custom_call" | custom-call | tf_op jit(solution)/shard_map/pack_first/pallas_call | solution.py:805
  10.5 0.2 collective-permute-done.2.refs_3_.refs_0_
  10.7 0.2 pack_second.1
  10.9 3.1 %collective-permute-start.5 = (f32[80,128]{1,0:T(8,128)S(1)}, f32[80,128]{1,0:T(8,128)S(1)}, u32[]{:S(2)}, u32[]{:S(2)}) collective-permute-start(f32[80,128]{1,0:T(8,128)S(1)} %get-tuple-element.59), channel_id=1, source_target_pairs={{0,1},{1,0},{2,3},{3,2},{8,9},{9,8},{10,11},{11,10},{16,17},{17,16... | collective-permute-start | bytes 122888 | tf_op jit(solution)/shard_map/ppermute | solution.py:797
  13.9 0.3 own.1
  14.3 1.4 %halo_geometry.1.refs_3_.refs_2_ = f32[7,512,128]{2,1,0:T(8,128)S(1)} custom-call(f32[3584,128]{1,0:T(8,128)S(1)} %get-tuple-element.54.refs_0_, bf16[128,1024]{1,0:T(8,128)(2,1)S(1)} %copy-done.4, f32[64,128]{1,0:T(8,128)S(1)} %copy-done.9, f32[128,128]{1,0:T(8,128)S(1)} %collective-permute-done.3.refs_3_, f32[128,128]{1,0:T(8,128)S(1)} %collective-permute-done.4.refs_4_), custom_call_target="tpu_custom_call" | custom-call | tf_op jit(solution)/shard_map/halo_geometry/pallas_call | solution.py:805
  15.8 0.2 collective-permute-done.5.refs_7_
  15.9 1.4 %first_direction.1 = (f32[512,128]{1,0:T(8,128)S(1)}, f32[512,128]{1,0:T(8,128)S(1)}, f32[512,128]{1,0:T(8,128)S(1)}, f32[64,128]{1,0:T(8,128)S(1)}, f32[64,128]{1,0:T(8,128)S(1)}, /*index=5*/f32[64,128]{1,0:T(8,128)S(1)}) custom-call(f32[512,128]{1,0:T(8,128)S(1)} %get-tuple-element.51.refs_0_, f32[512,128]{1,0:T(8,128)S(1)} %get-tuple-element.52.refs_1_, ...), custom_call_target="tpu_custom_call" | custom-call | tf_op jit(solution)/shard_map/first_direction/pallas_call | solution.py:805
  17.3 0.4 %collective-permute-start.7 = (f32[64,128]{1,0:T(8,128)S(1)}, f32[64,128]{1,0:T(8,128)S(1)}, u32[]{:S(2)}, u32[]{:S(2)}) collective-permute-start(f32[64,128]{1,0:T(8,128)S(1)} %get-tuple-element.69), channel_id=1, source_target_pairs={{0,8},{8,0},{16,24},{24,16},{1,9},{9,1},{17,25},{25,17},{2,10},{10... | collective-permute-start | bytes 98312 | tf_op jit(solution)/shard_map/ppermute | solution.py:797
  17.8 1.2 %collective-permute-start.8 = (f32[64,128]{1,0:T(8,128)S(1)}, f32[64,128]{1,0:T(8,128)S(1)}, u32[]{:S(2)}, u32[]{:S(2)}) collective-permute-start(f32[64,128]{1,0:T(8,128)S(1)} %get-tuple-element.70), channel_id=1, source_target_pairs={{0,24},{8,16},{16,8},{24,0},{1,25},{9,17},{17,9},{25,1},{2,26},{10... | collective-permute-start | bytes 98312 | tf_op jit(solution)/shard_map/ppermute | solution.py:797
  19.0 2.1 %collective-permute-done.8.refs_8_.refs_1_ = f32[64,128]{1,0:T(8,128)S(1)} collective-permute-done((f32[64,128]{1,0:T(8,128)S(1)}, f32[64,128]{1,0:T(8,128)S(1)}, u32[]{:S(2)}, u32[]{:S(2)}) %collective-permute-start.8) | collective-permute-done | bytes 32800 | tf_op jit(solution)/shard_map/ppermute | solution.py:797
  21.1 0.1 join.4
  21.2 0.6 %collective-permute-start.9 = (f32[32,128]{1,0:T(8,128)S(1)}, f32[32,128]{1,0:T(8,128)S(1)}, u32[]{:S(2)}, u32[]{:S(2)}) collective-permute-start(f32[32,128]{1,0:T(8,128)S(1)} %join.4), channel_id=1, source_target_pairs={{0,4},{4,0},{1,5},{5,1},{2,6},{6,2},{3,7},{7,3},{8,12},{12,8},{9,1... | collective-permute-start | bytes 49160 | tf_op jit(solution)/shard_map/ppermute | solution.py:797
  23.1 0.1 preview.2
  23.2 1.8 %collective-permute-done.9.refs_6_.refs_9_ = f32[32,128]{1,0:T(8,128)S(1)} collective-permute-done((f32[32,128]{1,0:T(8,128)S(1)}, f32[32,128]{1,0:T(8,128)S(1)}, u32[]{:S(2)}, u32[]{:S(2)}) %collective-permute-start.9) | collective-permute-done | bytes 16416 | tf_op jit(solution)/shard_map/ppermute | solution.py:797
  25.0 0.8 %direction.1 = (f32[512,128]{1,0:T(8,128)S(1)}, f32[512,128]{1,0:T(8,128)S(1)}, f32[64,128]{1,0:T(8,128)S(1)}, f32[64,128]{1,0:T(8,128)S(1)}, f32[64,128]{1,0:T(8,128)S(1)}) custom-call(f32[512,128]{1,0:T(8,128)S(1)} %get-tuple-element.72.refs_0_, f32[512,128]{1,0:T(8,128)S(1)} %get-tuple-element.62.refs_3_.refs_1_, ...), custom_call_target="tpu_custom_call" | custom-call | tf_op jit(solution)/shard_map/direction/pallas_call | solution.py:805
  25.9 1.6 %collective-permute-start.11 = (f32[64,128]{1,0:T(8,128)S(1)}, f32[64,128]{1,0:T(8,128)S(1)}, u32[]{:S(2)}, u32[]{:S(2)}) collective-permute-start(f32[64,128]{1,0:T(8,128)S(1)} %get-tuple-element.77), channel_id=1, source_target_pairs={{0,24},{8,16},{16,8},{24,0},{1,25},{9,17},{17,9},{25,1},{2,26},{10... | collective-permute-start | bytes 98312 | tf_op jit(solution)/shard_map/ppermute | solution.py:797
  27.5 1.8 %collective-permute-done.11.refs_8_.refs_1_ = f32[64,128]{1,0:T(8,128)S(1)} collective-permute-done((f32[64,128]{1,0:T(8,128)S(1)}, f32[64,128]{1,0:T(8,128)S(1)}, u32[]{:S(2)}, u32[]{:S(2)}) %collective-permute-start.11) | collective-permute-done | bytes 32800 | tf_op jit(solution)/shard_map/ppermute | solution.py:797
  29.4 0.6 %collective-permute-start.12 = (f32[32,128]{1,0:T(8,128)S(1)}, f32[32,128]{1,0:T(8,128)S(1)}, u32[]{:S(2)}, u32[]{:S(2)}) collective-permute-start(f32[32,128]{1,0:T(8,128)S(1)} %join.5), channel_id=1, source_target_pairs={{0,4},{4,0},{1,5},{5,1},{2,6},{6,2},{3,7},{7,3},{8,12},{12,8},{9,1... | collective-permute-start | bytes 49160 | tf_op jit(solution)/shard_map/ppermute | solution.py:797
  30.0 0.3 preview.3.refs_0_
  30.3 2.9 %collective-permute-done.12.refs_4_ = f32[32,128]{1,0:T(8,128)S(1)} collective-permute-done((f32[32,128]{1,0:T(8,128)S(1)}, f32[32,128]{1,0:T(8,128)S(1)}, u32[]{:S(2)}, u32[]{:S(2)}) %collective-permute-start.12) | collective-permute-done | bytes 16416 | tf_op jit(solution)/shard_map/ppermute | solution.py:797
  33.2 1.0 %field.1 = f32[3,32,512]{2,1,0:T(8,128)} custom-call(f32[96,512]{1,0:T(8,128)S(1)} %preview.3.refs_0_, f32[512,128]{1,0:T(8,128)S(1)} %get-tuple-element.62.refs_3_.refs_1_, f32[40,128]{1,0:T(8,128)S(1)} %coefficients.1.refs_5_.refs_3_.refs_2_, bf16[96,128]{1,0:T(8,128)(2,1)S(1)} %get-tuple-element.68.refs_6_.refs_3_, ...), custom_call_target="tpu_custom_call" | custom-call | tf_op jit(solution)/shard_map/field/pallas_call | solution.py:805
  (36 shorter events, 0.4 us)
Async XLA Ops:
  0.0 0.9 %copy-start.7 = (bf16[128,384]{1,0:T(8,128)(2,1)S(1)}, bf16[128,384]{1,0:T(8,128)(2,1)}, u32[]{:S(2)}) copy-start(bf16[128,384]{1,0:T(8,128)(2,1)} %constant.21.clone.refs_7_) | copy-start | bytes 294916
  0.0 0.9 %copy-start.10 = (f32[48,128]{1,0:T(8,128)S(1)}, f32[48,128]{1,0:T(8,128)}, u32[]{:S(2)}) copy-start(f32[48,128]{1,0:T(8,128)} %constant.19.clone.refs_3_) | copy-start | bytes 73732
  0.0 0.9 %copy-start.11 = (s32[6,128]{1,0:T(8,128)S(1)}, s32[6,128]{1,0:T(8,128)}, u32[]{:S(2)}) copy-start(s32[6,128]{1,0:T(8,128)} %constant.20.clone.refs_6_) | copy-start | bytes 9220
  0.0 0.9 %copy-start.5 = (f32[8,16,128]{2,1,0:T(8,128)S(1)}, f32[8,16,128]{2,1,0:T(8,128)}, u32[]{:S(2)}) copy-start(f32[8,16,128]{2,1,0:T(8,128)} %refs_1_.4) | copy-start | bytes 196612
  0.0 1.1 %copy-start = (f32[6,8,16,128]{3,2,1,0:T(8,128)S(1)}, f32[6,8,16,128]{3,2,1,0:T(8,128)}, u32[]{:S(2)}) copy-start(f32[6,8,16,128]{3,2,1,0:T(8,128)} %refs_0_.3) | copy-start | bytes 1179652
  0.0 1.1 %copy-start.12 = (s32[1,32]{1,0:T(1,128)S(1)}, s32[1,32]{1,0:T(1,128)}, u32[]{:S(2)}) copy-start(s32[1,32]{1,0:T(1,128)} %refs_5_.3) | copy-start | bytes 388
  0.0 1.2 %copy-start.6 = (f32[3,512,32]{1,2,0:T(8,128)S(1)}, f32[3,512,32]{1,2,0:T(8,128)}, u32[]{:S(2)}) copy-start(f32[3,512,32]{1,2,0:T(8,128)} %param.15) | copy-start | bytes 589828
  0.0 5.1 %copy-start.8 = (s32[2,3,16,128]{3,2,1,0:T(8,128)S(1)}, s32[2,3,16,128]{3,2,1,0:T(8,128)}, u32[]{:S(2)}) copy-start(s32[2,3,16,128]{3,2,1,0:T(8,128)} %refs_3_.2) | copy-start | bytes 147460
  2.0 4.1 %collective-permute-start = (f32[64,128]{1,0:T(8,128)S(1)}, f32[64,128]{1,0:T(8,128)S(1)}, u32[]{:S(2)}, u32[]{:S(2)}) collective-permute-start(f32[64,128]{1,0:T(8,128)S(1)} %get-tuple-element.46), channel_id=1, source_target_pairs={{0,8},{8,0},{16,24},{24,16},{1,9},{9,1},{17,25},{25,17},{2,10},{10... | collective-permute-start | bytes 98312 | tf_op jit(solution)/shard_map/ppermute | solution.py:797
  2.5 4.3 %collective-permute-start.1 = (f32[64,128]{1,0:T(8,128)S(1)}, f32[64,128]{1,0:T(8,128)S(1)}, u32[]{:S(2)}, u32[]{:S(2)}) collective-permute-start(f32[64,128]{1,0:T(8,128)S(1)} %get-tuple-element.47), channel_id=1, source_target_pairs={{0,24},{8,16},{16,8},{24,0},{1,25},{9,17},{17,9},{25,1},{2,26},{10... | collective-permute-start | bytes 98312 | tf_op jit(solution)/shard_map/ppermute | solution.py:797
  6.8 3.8 %collective-permute-start.2 = (f32[40,128]{1,0:T(8,128)S(1)}, f32[40,128]{1,0:T(8,128)S(1)}, u32[]{:S(2)}, u32[]{:S(2)}) collective-permute-start(f32[40,128]{1,0:T(8,128)S(1)} %join.3), channel_id=1, source_target_pairs={{0,4},{4,0},{1,5},{5,1},{2,6},{6,2},{3,7},{7,3},{8,12},{12,8},{9,1... | collective-permute-start | bytes 61448 | tf_op jit(solution)/shard_map/ppermute | solution.py:797
  8.6 5.7 %collective-permute-start.3 = (f32[128,128]{1,0:T(8,128)S(1)}, f32[128,128]{1,0:T(8,128)S(1)}, u32[]{:S(2)}, u32[]{:S(2)}) collective-permute-start(f32[128,128]{1,0:T(8,128)S(1)} %get-tuple-element.55), channel_id=1, source_target_pairs={{0,1},{1,0},{2,3},{3,2},{8,9},{9,8},{10,11},{11,10},{16,17},{17,16... | collective-permute-start | bytes 196616 | tf_op jit(solution)/shard_map/ppermute | solution.py:797
  10.1 4.1 %collective-permute-start.4 = (f32[128,128]{1,0:T(8,128)S(1)}, f32[128,128]{1,0:T(8,128)S(1)}, u32[]{:S(2)}, u32[]{:S(2)}) collective-permute-start(f32[128,128]{1,0:T(8,128)S(1)} %get-tuple-element.56), channel_id=1, source_target_pairs={{0,8},{1,2},{2,1},{3,11},{8,0},{9,10},{10,9},{11,3},{16,24},{17,18... | collective-permute-start | bytes 196616 | tf_op jit(solution)/shard_map/ppermute | solution.py:797
  10.7 3.3 %copy-start.1 = (bf16[256,256]{1,0:T(8,128)(2,1)S(1)}, bf16[256,256]{1,0:T(8,128)(2,1)}, u32[]{:S(2)}) copy-start(bf16[256,256]{1,0:T(8,128)(2,1)} %constant.23.clone.refs_2_.refs_4_) | copy-start | bytes 393220
  10.7 3.6 %copy-start.4 = (bf16[128,1024]{1,0:T(8,128)(2,1)S(1)}, bf16[128,1024]{1,0:T(8,128)(2,1)}, u32[]{:S(2)}) copy-start(bf16[128,1024]{1,0:T(8,128)(2,1)} %constant.22.clone.refs_1_) | copy-start | bytes 786436
  10.7 3.6 %copy-start.9 = (f32[64,128]{1,0:T(8,128)S(1)}, f32[64,128]{1,0:T(8,128)}, u32[]{:S(2)}) copy-start(f32[64,128]{1,0:T(8,128)} %constant.16.clone.refs_2_) | copy-start | bytes 98308
  10.9 5.1 %collective-permute-start.5 = (f32[80,128]{1,0:T(8,128)S(1)}, f32[80,128]{1,0:T(8,128)S(1)}, u32[]{:S(2)}, u32[]{:S(2)}) collective-permute-start(f32[80,128]{1,0:T(8,128)S(1)} %get-tuple-element.59), channel_id=1, source_target_pairs={{0,1},{1,0},{2,3},{3,2},{8,9},{9,8},{10,11},{11,10},{16,17},{17,16... | collective-permute-start | bytes 122888 | tf_op jit(solution)/shard_map/ppermute | solution.py:797
  13.9 2.0 %collective-permute-start.6 = (f32[80,128]{1,0:T(8,128)S(1)}, f32[80,128]{1,0:T(8,128)S(1)}, u32[]{:S(2)}, u32[]{:S(2)}) collective-permute-start(f32[80,128]{1,0:T(8,128)S(1)} %get-tuple-element.60), channel_id=1, source_target_pairs={{0,8},{1,2},{2,1},{3,11},{8,0},{9,10},{10,9},{11,3},{16,24},{17,18... | collective-permute-start | bytes 122888 | tf_op jit(solution)/shard_map/ppermute | solution.py:797
  14.3 1.6 %copy-start.2 = (bf16[128,384]{1,0:T(8,128)(2,1)S(1)}, bf16[128,384]{1,0:T(8,128)(2,1)}, u32[]{:S(2)}) copy-start(bf16[128,384]{1,0:T(8,128)(2,1)} %constant.18.clone.refs_6_.refs_5_) | copy-start | bytes 294916
  14.3 1.6 %copy-start.3 = (bf16[128,384]{1,0:T(8,128)(2,1)S(1)}, bf16[128,384]{1,0:T(8,128)(2,1)}, u32[]{:S(2)}) copy-start(bf16[128,384]{1,0:T(8,128)(2,1)} %constant.17.clone.refs_5_.refs_4_) | copy-start | bytes 294916
  17.3 1.7 %collective-permute-start.7 = (f32[64,128]{1,0:T(8,128)S(1)}, f32[64,128]{1,0:T(8,128)S(1)}, u32[]{:S(2)}, u32[]{:S(2)}) collective-permute-start(f32[64,128]{1,0:T(8,128)S(1)} %get-tuple-element.69), channel_id=1, source_target_pairs={{0,8},{8,0},{16,24},{24,16},{1,9},{9,1},{17,25},{25,17},{2,10},{10... | collective-permute-start | bytes 98312 | tf_op jit(solution)/shard_map/ppermute | solution.py:797
  17.8 3.4 %collective-permute-start.8 = (f32[64,128]{1,0:T(8,128)S(1)}, f32[64,128]{1,0:T(8,128)S(1)}, u32[]{:S(2)}, u32[]{:S(2)}) collective-permute-start(f32[64,128]{1,0:T(8,128)S(1)} %get-tuple-element.70), channel_id=1, source_target_pairs={{0,24},{8,16},{16,8},{24,0},{1,25},{9,17},{17,9},{25,1},{2,26},{10... | collective-permute-start | bytes 98312 | tf_op jit(solution)/shard_map/ppermute | solution.py:797
  21.2 3.8 %collective-permute-start.9 = (f32[32,128]{1,0:T(8,128)S(1)}, f32[32,128]{1,0:T(8,128)S(1)}, u32[]{:S(2)}, u32[]{:S(2)}) collective-permute-start(f32[32,128]{1,0:T(8,128)S(1)} %join.4), channel_id=1, source_target_pairs={{0,4},{4,0},{1,5},{5,1},{2,6},{6,2},{3,7},{7,3},{8,12},{12,8},{9,1... | collective-permute-start | bytes 49160 | tf_op jit(solution)/shard_map/ppermute | solution.py:797
  25.9 1.7 %collective-permute-start.10 = (f32[64,128]{1,0:T(8,128)S(1)}, f32[64,128]{1,0:T(8,128)S(1)}, u32[]{:S(2)}, u32[]{:S(2)}) collective-permute-start(f32[64,128]{1,0:T(8,128)S(1)} %get-tuple-element.76), channel_id=1, source_target_pairs={{0,8},{8,0},{16,24},{24,16},{1,9},{9,1},{17,25},{25,17},{2,10},{10... | collective-permute-start | bytes 98312 | tf_op jit(solution)/shard_map/ppermute | solution.py:797
  25.9 3.4 %collective-permute-start.11 = (f32[64,128]{1,0:T(8,128)S(1)}, f32[64,128]{1,0:T(8,128)S(1)}, u32[]{:S(2)}, u32[]{:S(2)}) collective-permute-start(f32[64,128]{1,0:T(8,128)S(1)} %get-tuple-element.77), channel_id=1, source_target_pairs={{0,24},{8,16},{16,8},{24,0},{1,25},{9,17},{17,9},{25,1},{2,26},{10... | collective-permute-start | bytes 98312 | tf_op jit(solution)/shard_map/ppermute | solution.py:797
  29.4 3.8 %collective-permute-start.12 = (f32[32,128]{1,0:T(8,128)S(1)}, f32[32,128]{1,0:T(8,128)S(1)}, u32[]{:S(2)}, u32[]{:S(2)}) collective-permute-start(f32[32,128]{1,0:T(8,128)S(1)} %join.5), channel_id=1, source_target_pairs={{0,4},{4,0},{1,5},{5,1},{2,6},{6,2},{3,7},{7,3},{8,12},{12,8},{9,1... | collective-permute-start | bytes 49160 | tf_op jit(solution)/shard_map/ppermute | solution.py:797

commit v6 on v5

--- a/solution.py
+++ b/solution.py
@@ -113,9 +113,10 @@
 
 
 def dot2(x, table):
-    upper, lower = split(x)
-    return jnp.dot(upper, table, preferred_element_type=F32) + jnp.dot(
-        lower, table, preferred_element_type=F32
+    return jnp.dot(
+        jnp.concatenate(split(x), axis=1),
+        jnp.concatenate([table, table], axis=0),
+        preferred_element_type=F32,
     )
 
 
@@ -161,8 +162,8 @@
         self.ids = np.ascontiguousarray(ids[:, :1, :]).reshape(2 * c, 128)
         part = HALO * p
         self.part = part
-        assert FIELDS * part <= lanes and 2 * ey * part <= 128
-        halo = np.zeros((128, p, self.w3), np.float32)
+        assert FIELDS * part <= lanes and 2 * ey * part <= lanes // 2
+        halo = np.zeros((lanes, p, self.w3), np.float32)
         for side, first in ((0, -HALO), (1, ez)):
             for g in range(HALO):
                 for cc in range(c):
@@ -172,12 +173,11 @@
                         widen[row + cc * ey + f, at] = 1
                         widen[row + c * ey + f, self.w3 + at] = 1
                         for k in range(p):
-                            halo[(side * ey + f) * part + g * p + k, k, at] = 1
-        self.halo = halo.reshape(128, -1).astype(jnp.bfloat16)
+                            for half in range(2):
+                                halo[half * lanes // 2 + (side * ey + f) * part + g * p + k, k, at] = 1
+        self.halo = halo.reshape(lanes, -1).astype(jnp.bfloat16)
         self.widen = widen.astype(jnp.bfloat16)
         self.third = [self.block_terms(matrix) for matrix in (self.forward, self.forward.T, self.squared.T)]
-        column = np.asarray([wj * wk for wj in self.weights for wk in self.weights], np.float32)
-        self.table = np.ascontiguousarray(np.broadcast_to(column[:, None], (column.size, 128)))
         face = (ey * p, lanes)
         second = np.tile(np.arange(p), ey)[:, None]
         third = np.tile(np.arange(p), ez)[None, :]
@@ -197,14 +197,14 @@
         return np.concatenate([upper, upper, lower], axis=1)
 
 
-    def contract(self, x, matrix):
+    def contract(self, x, matrix, wanted=None):
         p = self.p
         sign = 1.0 if matrix[0, 0] * matrix[p - 1, p - 1] > 0 else -1.0
         half = p // 2
         sums = [x[i] + x[p - 1 - i] for i in range(half)]
         differences = [x[i] - x[p - 1 - i] for i in range(half)]
         out = [None] * p
-        for a in range(half):
+        for a in range(half) if wanted is None else wanted:
             even, odd = None, None
             for i in range(half):
                 first, second = float(matrix[a, i]), float(matrix[a, p - 1 - i])
@@ -212,7 +212,7 @@
                 odd = self.gather(odd, 0.5 * (first - second), differences[i])
             out[a] = odd + even
             out[p - 1 - a] = even - odd if sign > 0 else odd - even
-        return out
+        return [x for x in out if x is not None]
 
     @staticmethod
     def gather(total, factor, x):
@@ -231,41 +231,66 @@
             for row, value in zip(rows, self.contract([source[r : r + p, :] for r in rows], matrix)):
                 write(row, value)
 
-    def along_k(self, source, table, out):
+    def along_k(self, source, table, out, start, end):
         size = table.shape[0]
-        for start in range(0, self.rows, 2 * size):
-            pieces = [split(source[at : at + size, :]) for at in (start, start + size)]
+        width = source.shape[-1]
+        while start < end:
+            count = min(2, (end - start) // size)
+            pieces = [split(source[start + n * size : start + (n + 1) * size, :]) for n in range(count)]
             upper, lower = (jnp.concatenate([piece[n] for piece in pieces], axis=1) for n in range(2))
             both = jnp.dot(
                 table[...], jnp.concatenate([upper, lower, upper], axis=0), preferred_element_type=F32
             )
-            width = source.shape[-1]
-            out[start : start + size, :] = both[:, :width]
-            out[start + size : start + 2 * size, :] = both[:, width:]
-
-    def operator(self, v, g, out, slope, flux, third, work, ahead, back):
-        block = self.block
+            for n in range(count):
+                out[start + n * size : start + (n + 1) * size, :] = both[:, n * width : (n + 1) * width]
+            start += count * size
+
+    def rows_of(self, g, q, at):
+        return g[q * self.rows + at.start : q * self.rows + at.stop, :]
+
+    def operator_first(self, v, g, ends, f1, f2, f3, slope, third, ahead, back):
+        p, block, rows = self.p, self.block, self.rows
 
         def store(row, value):
-            slope[row : row + self.p, :] = value
+            slope[row : row + p, :] = value
 
         self.along_i(v, self.forward, store)
-        self.along_k(v, ahead, third)
-        for i in range(self.p):
+        self.along_k(v, ahead, third, 0, rows)
+        for i in range(p):
             at = slice(i * block, (i + 1) * block)
             x, s1, s3 = v[at, :], slope[at, :], third[at, :]
             s2 = self.along_j(x, self.forward)
-            xy, xz, yz = g[3, at, :], g[4, at, :], g[5, at, :]
-            flux[at, :] = g[0, at, :] * s1 + xy * s2 + xz * s3
-            f2 = xy * s1 + g[1, at, :] * s2 + yz * s3
-            work[at, :] = xz * s1 + yz * s2 + g[2, at, :] * s3
-            out[at, :] = self.along_j(f2, self.forward.T) + g[6, at, :] * x
-        self.along_k(work, back, third)
-
-        def add(row, value):
-            out[row : row + self.p, :] += value + third[row : row + self.p, :]
-
-        self.along_i(flux, self.forward.T, add)
+            xy, xz, yz = self.rows_of(g, 3, at), self.rows_of(g, 4, at), self.rows_of(g, 5, at)
+            f1[at, :] = self.rows_of(g, 0, at) * s1 + xy * s2 + xz * s3
+            f2[at, :] = xy * s1 + self.rows_of(g, 1, at) * s2 + yz * s3
+            f3[at, :] = xz * s1 + yz * s2 + self.rows_of(g, 2, at) * s3
+        for n, start in enumerate((0, rows - block)):
+            at = slice(start, start + block)
+            ends[n * block : (n + 1) * block, :] = self.along_j(f2[at, :], self.forward.T) + self.rows_of(g, 6, at) * v[at, :]
+            slope[n * block : (n + 1) * block, :] = f3[at, :]
+        self.along_k(slope, back, third, 0, 2 * block)
+        for j in range(p):
+            x = [f1[i * block + j * p : i * block + (j + 1) * p, :] for i in range(p)]
+            first, last = self.contract(x, self.forward.T, (0,))
+            for row, value in ((j * p, first), (block + j * p, last)):
+                ends[row : row + p, :] += value + third[row : row + p, :]
+
+    def operator_second(self, n_x, n_y, *refs):
+        v, g, ends, f1, f2, f3, back = refs[:7]
+        out, y_out, third = refs[7], refs[8 : 8 + n_y], refs[8 + n_y]
+        p, block, rows = self.p, self.block, self.rows
+        out[:block, :], out[rows - block :, :] = ends[:block, :], ends[block:, :]
+        self.along_k(f3, back, third, block, rows - block)
+        for i in range(1, p - 1):
+            at = slice(i * block, (i + 1) * block)
+            out[at, :] = self.along_j(f2[at, :], self.forward.T) + self.rows_of(g, 6, at) * v[at, :] + third[at, :]
+        for j in range(p):
+            at = [slice(i * block + j * p, i * block + (j + 1) * p) for i in range(p)]
+            values = self.contract([f1[r, :] for r in at], self.forward.T, range(1, p // 2))
+            for r, value in zip(at[1 : p - 1], values):
+                out[r, :] += value
+        self.iteration_fold(out.at[block : rows - block, :])
+        self.emit_second(out, y_out)
 
     def fold_second(self, u):
         if self.ey == 1:
@@ -292,10 +317,12 @@
             take_lower(lane), pltpu.roll(last, step, 1), 0.0
         )
 
-    def emit(self, u, x_out, y_out):
+    def emit_first(self, ends, x_out):
+        for out, (high, _, _) in zip(x_out, roles("gx", self.sizes["gx"])):
+            out[...] = jnp.where(high, ends[1], ends[0])
+
+    def emit_second(self, u, y_out):
         p, block = self.p, self.block
-        for out, (high, _, _) in zip(x_out, roles("gx", self.sizes["gx"])):
-            out[...] = jnp.where(high, u[self.rows - block :, :], u[:block, :])
         for out, (high, _, _) in zip(y_out, roles("gy", self.sizes["gy"])):
             for i in range(p):
                 start = i * block
@@ -309,15 +336,15 @@
         self.fold_third(u, self.step3, lambda l: l < last, lambda l: (l >= self.step3) & (l < self.n3))
 
 
-    def pack_geometry(self, field, out):
+    def pack_fields(self, fields, out):
         for target, (high, _, _) in zip(out, roles("gz", self.sizes["gz"])):
             rows, width = target.shape
             lane = lax.broadcasted_iota(jnp.int32, (rows, width), 1)
             total = jnp.zeros((rows, width), F32)
             for q in range(FIELDS):
                 start = q * self.part
-                upper = pltpu.roll(field(q), start + self.part, 1)
-                lower = pltpu.roll(field(q), start, 1) if start else field(q)
+                upper = pltpu.roll(fields[q], start + self.part, 1)
+                lower = pltpu.roll(fields[q], start, 1) if start else fields[q]
                 here = (lane >= start) & (lane < start + self.part)
                 total = jnp.where(here, jnp.where(high, upper, lower), total)
             target[...] = total
@@ -358,8 +385,8 @@
 
     def prepare(self, n_x, n_y, *refs):
         geometry, viscosity, spread, table, right, slots, ids, square = refs[:8]
-        s4, hot3 = refs[8:10]
-        refs = refs[10:]
+        s4, hot3, fields = refs[8:11]
+        refs = refs[11:]
         x_out, y_out, work = refs[:n_x], refs[n_x : n_x + n_y], refs[n_x + n_y]
         p, c, block, rows, ey = self.p, self.c, self.block, self.rows, self.ey
         face = ey * p
@@ -376,9 +403,12 @@
             end = float(self.end[i])
             if end != 0.0:
                 cross = cross + end * (end_j * xy + end_k * xz)
-            stiff.append(weighted * xx)
-            second.append(weighted * yy)
-            third.append(weighted * zz)
+            entries = [weighted * entry for entry in (xx, yy, zz, xy, xz, yz)] + [mass]
+            for q, entry in enumerate(entries):
+                fields[q, i * face : (i + 1) * face, :] = entry
+            stiff.append(entries[0])
+            second.append(entries[1])
+            third.append(entries[2])
             rest.append((2.0 * weighted) * cross + mass)
         upper, lower = split(jnp.concatenate(second, axis=0))
         diagonal = jnp.dot(
@@ -412,21 +442,19 @@
         self.fold_second(s4)
         last = self.n4 - self.step4
         self.fold_third(s4, self.step4, lambda l: l < last, lambda l: (l >= self.step4) & (l < self.n4))
-        self.emit(s4, x_out, y_out)
+        self.emit_first((s4[:block, :], s4[rows - block :, :]), x_out)
+        self.emit_second(s4, y_out)
 
     def convert(self, n_y, n_z, *refs):
-        geometry, viscosity, spread, dirichlet = refs[:4]
-        raw, ind = refs[4:6]
+        fields, spread, dirichlet, s4 = refs[:4]
+        g, ind = refs[4:6]
         refs = refs[6:]
-        y_out, z_out, (upper, lower) = refs[:n_y], refs[n_y : n_y + n_z], refs[n_y + n_z :]
+        y_out, z_out, packed = refs[:n_y], refs[n_y : n_y + n_z], refs[n_y + n_z : n_y + 2 * n_z]
+        upper, lower = refs[n_y + 2 * n_z :]
         p, c, block, ey = self.p, self.c, self.block, self.ey
-        width = geometry.shape[-1]
-
-        def field(q):
-            return (geometry[q] if q < FIELDS - 1 else viscosity[...]).reshape(p * ey * p, width)
-
+        width = fields.shape[-1]
         for q in range(FIELDS):
-            value = field(q).reshape(p, ey, p, width)
+            value = fields[q].reshape(p, ey, p, width)
             for f in range(ey):
                 at = (slice(q * block, (q + 1) * block), slice(f * width, (f + 1) * width))
                 upper[at], lower[at] = split(value[:, f].reshape(block, width))
@@ -445,7 +473,7 @@
         owner = lax.rem(lane, self.step3) // ey
 
         def store(k, value):
-            raw[pl.ds(k, first_flag, stride=p), :] = value[:first_flag]
+            g[pl.ds(k, first_flag, stride=p), :] = value[:first_flag]
             total = jnp.zeros((flags, self.w3), F32)
             for cc in range(c):
                 at = first_flag + cc * flags
@@ -453,7 +481,7 @@
             ind[pl.ds(k, flags, stride=p), :] = jnp.where(here, total, 0.0)
 
         self.by_nodes(upper[...], lower[...], spread, self.w3, store)
-        self.pack_geometry(field, z_out)
+        self.pack_fields(fields, z_out)
         self.fold_second(ind)
         first_own, end_own = HALO * self.step3, self.n3 - HALO * self.step3
         self.fold_third(
@@ -468,48 +496,37 @@
                 out[n * p : (n + 1) * p, :] = jnp.where(
                     up, ind[start + block - p : start + block, :], ind[start : start + p, :]
                 )
-
-    def halo_geometry(self, n_z, *refs):
-        raw, halo, table = refs[:3]
-        z_in, g = refs[3 : 3 + n_z], refs[3 + n_z]
-        upper, lower, total = refs[4 + n_z :]
-        p, block, rows, ey = self.p, self.block, self.rows, self.ey
-        source = raw
-        if n_z:
-            sides = both_sides([z[...] for z in z_in], roles("gz", self.sizes["gz"]))
-            width, part = sides[0].shape[-1], self.part
-            sides = [side.reshape(p, ey, p, width) for side in sides]
-            lane = lax.broadcasted_iota(jnp.int32, (block, width), 1)
-            for q in range(FIELDS):
-                value = jnp.zeros((block, width), F32)
-                for side in range(2):
-                    for f in range(ey):
-                        to = (side * ey + f) * part
-                        shift = (to - q * part) % width
-                        x = sides[side][:, f].reshape(block, width)
-                        x = pltpu.roll(x, shift, 1) if shift else x
-                        value = jnp.where((lane >= to) & (lane < to + part), x, value)
-                at = slice(q * block, (q + 1) * block)
-                upper[at, :], lower[at, :] = split(value)
-
-            def store(k, value):
-                at = pl.ds(k, FIELDS * block, stride=p)
-                total[at, :] = raw[at, :] + value
-
-            self.by_nodes(upper[...], lower[...], halo, self.w3, store)
-            source = total
-        wjk = table[...]
-        for i in range(p):
-            at = slice(i * block, (i + 1) * block)
-            entries = [source[q * rows + i * block : q * rows + (i + 1) * block, :] for q in range(FIELDS)]
-            xx, yy, zz, xy, xz, yz = entries[:6]
-            quadrature = float(self.weights[i]) * wjk
-            weighted = quadrature * entries[6]
-            g[6, at, :] = (helm_coefficient * quadrature) * (
-                xx * (yy * zz - yz * yz) - xy * (xy * zz - yz * xz) + xz * (xy * yz - yy * xz)
-            )
-            for q in range(6):
-                g[q, at, :] = weighted * entries[q]
+        for out, (up, _, _) in zip(packed, roles("gz", self.sizes["gz"])):
+            self.pack(out, s4, block, 0, self.n4 - self.halo4, up, 0)
+            self.pack(out, ind, p, first_own, end_own - first_own, up, block)
+
+    def halo_fields(self, n_z, *refs):
+        own, halo = refs[:2]
+        z_in, g, terms = refs[2 : 2 + n_z], refs[2 + n_z], refs[3 + n_z]
+        p, block, ey, part = self.p, self.block, self.ey, self.part
+        sides = both_sides([z[...] for z in z_in], roles("gz", self.sizes["gz"]))
+        width = sides[0].shape[-1]
+        sides = [side.reshape(p, ey, p, width) for side in sides]
+        lane = lax.broadcasted_iota(jnp.int32, (block, width), 1)
+        for q in range(FIELDS):
+            value = jnp.zeros((block, width), F32)
+            for side in range(2):
+                for f in range(ey):
+                    to = (side * ey + f) * part
+                    shift = (to - q * part) % width
+                    x = sides[side][:, f].reshape(block, width)
+                    x = pltpu.roll(x, shift, 1) if shift else x
+                    value = jnp.where((lane >= to) & (lane < to + part), x, value)
+            upper, lower = split(value)
+            lower = pltpu.roll(lower.astype(F32), width // 2, 1).astype(BF16)
+            terms[q * block : (q + 1) * block, :] = upper + lower
+
+        for k in range(0, p, 2):
+            columns = halo[:, k * self.w3 : (k + 2) * self.w3]
+            both = jnp.dot(terms[...], columns, preferred_element_type=F32)
+            for n in range(2):
+                at = pl.ds(k + n, FIELDS * block, stride=p)
+                g[at, :] = own[at, :] + both[:, n * self.w3 : (n + 1) * self.w3]
 
     def coefficients(self, low, high, coef):
         top, bottom = jnp.full((8, 128), high[0], F32), jnp.full((8, 128), low[0], F32)
@@ -564,20 +581,6 @@
             faces.append(data)
         return both_sides(faces, role)
 
-    def pack_first(self, n_x, *refs):
-        s4, ind = refs[:2]
-        x_in, s_out, z_out = refs[2 : 2 + n_x], refs[2 + n_x], refs[3 + n_x :]
-        p, block, rows = self.p, self.block, self.rows
-        s_out[...] = s4[...]
-        if n_x:
-            low, high = both_sides([x[...] for x in x_in], roles("gx", self.sizes["gx"]))
-            s_out[:block, :] += low
-            s_out[rows - block :, :] += high
-        halo3 = HALO * self.step3
-        for out, (up, _, _) in zip(z_out, roles("gz", self.sizes["gz"])):
-            self.pack(out, s_out, block, 0, self.n4 - self.halo4, up, 0)
-            self.pack(out, ind, p, halo3, self.n3 - 2 * halo3, up, block)
-
     def pack(self, out, u, count, first, last, up, start):
         p, width, size = self.p, self.w4, self.halo4
         lane = lax.broadcasted_iota(jnp.int32, (count, width), 1)
@@ -593,14 +596,29 @@
             row = start + section // p * count
             out[row : row + count, :] = total
 
-    def pack_second(self, n_y, n_z, *refs):
-        y_in, z_in, z_out = refs[:n_y], refs[n_y : n_y + n_z], refs[n_y + n_z :]
+    def pack_second(self, n_x, n_y, n_z, *refs):
+        x_in, y_in, refs = refs[:n_x], refs[n_x : n_x + n_y], refs[n_x + n_y :]
+        z_in, z_out = refs[:n_z], refs[n_z:]
         p, block, width, size = self.p, self.block, self.w4, self.halo4
+        ends = both_sides([x[...] for x in x_in], roles("gx", self.sizes["gx"]))
         low, high = self.second_sides(y_in)
         halo3 = HALO * self.step3
         lane = lax.broadcasted_iota(jnp.int32, (p, width), 1)
         for packed, out, (up, _, _) in zip(z_in, z_out, roles("gz", self.sizes["gz"])):
             out[...] = packed[...]
+            if n_x:
+                total = 0.0
+                for x, group in zip(ends, (0, p - 1)):
+                    shift = group * size
+                    below = pltpu.roll(x, shift, 1) if shift else x
+                    back = (shift - self.n4 + size) % width
+                    above = pltpu.roll(x, back, 1) if back else x
+                    wide = lax.broadcasted_iota(jnp.int32, x.shape, 1)
+                    here = (wide >= shift) & (wide < shift + size)
+                    total = total + jnp.where(here, jnp.where(up, above, below), 0.0)
+                out[:block, :] += total
+            if not n_y:
+                continue
             for face, row in ((low, 0), (high, block - p)):
                 total = jnp.zeros((p, width), F32)
                 for n in range(p):
@@ -621,11 +639,15 @@
                     here = (lane >= shift) & (lane < shift + size)
                     out[row : row + p, :] += jnp.where(here, jnp.where(up, above, below), 0.0)
 
-    def own(self, n_y, *refs):
+    def own(self, n_x, n_y, *refs):
         s4, ind, widen = refs[:3]
-        y_in, (r, scale, flag, work) = refs[3 : 3 + n_y], refs[3 + n_y :]
-        p, block, w3 = self.p, self.block, self.w3
+        x_in, y_in, (r, scale, flag, work) = refs[3 : 3 + n_x], refs[3 + n_x : 3 + n_x + n_y], refs[3 + n_x + n_y :]
+        p, block, rows, w3 = self.p, self.block, self.rows, self.w3
         work[...] = s4[...]
+        if n_x:
+            low, high = both_sides([x[...] for x in x_in], roles("gx", self.sizes["gx"]))
+            work[:block, :] += low
+            work[rows - block :, :] += high
         flag[...] = ind[...]
         if n_y:
             low, high = self.second_sides(y_in)
@@ -638,14 +660,12 @@
         r[...] = both[:, :w3]
         scale[...] = both[:, w3:]
 
-    def start(self, n_x, n_y, n_z, *refs):
+    def start(self, n_x, n_z, *refs):
         r_own, diagonal_own, flag_own, g, widen, ahead, back = refs[:7]
         z_in = refs[7 : 7 + n_z]
-        t, scale, v = refs[7 + n_z : 10 + n_z]
-        refs = refs[10 + n_z :]
-        x_out, y_out = refs[:n_x], refs[n_x : n_x + n_y]
-        beside, r, flag = refs[n_x + n_y : n_x + n_y + 3]
-        work = refs[n_x + n_y + 3 :]
+        t, scale, ends, f1, f2, f3 = refs[7 + n_z : 13 + n_z]
+        x_out, refs = refs[13 + n_z : 13 + n_z + n_x], refs[13 + n_z + n_x :]
+        beside, r, flag, slope, third = refs
         p, block, rows, w3, w4 = self.p, self.block, self.rows, self.w3, self.w4
         step, first_own, end_own = self.step3, HALO * self.step3, self.n3 - HALO * self.step3
         size, part = self.sizes["gz"], self.halo4
@@ -693,9 +713,9 @@
                 factor = jnp.where(flag[row : row + block, :] > 0.5, 0.0, factor)
             scale[at, :] = factor
             t[at, :] = factor * r[at, :]
-        self.operator(t, g, v, *work, ahead, back)
-        self.iteration_fold(v)
-        self.emit(v, x_out, y_out)
+        self.operator_first(t, g, ends, f1, f2, f3, slope, third, ahead, back)
+        self.iteration_fold(ends)
+        self.emit_first((ends[:block, :], ends[block:, :]), x_out)
 
     def factors(self, coef, n):
         rows = [coef[8 * m : 8 * m + 1, :] for m in (0, 2 * n + 1, 2 * n + 2)]
@@ -746,19 +766,18 @@
             out[...] = self.by_slots(hot, field[...])
 
     def by_slots(self, hot, field):
-        value = None
-        for part in split(field):
-            term = lax.dot_general(
-                hot[...], part, (((1,), (1,)), ((), ())), preferred_element_type=F32
-            )
-            value = term if value is None else value + term
-        return value
+        return lax.dot_general(
+            jnp.concatenate([hot[...], hot[...]], axis=1),
+            jnp.concatenate(split(field), axis=1),
+            (((1,), (1,)), ((), ())),
+            preferred_element_type=F32,
+        )
 
     def middle(self, n_x, n_y, n, *refs):
         d, scale, g, coef, ahead, back = refs[:6]
         y_in, refs = refs[6 : 6 + n_y], refs[6 + n_y :]
-        d_new, v = refs[:2]
-        x_out, y_out, work = refs[2 : 2 + n_x], refs[2 + n_x : 2 + n_x + n_y], refs[2 + n_x + n_y :]
+        d_new, ends, f1, f2, f3 = refs[:5]
+        x_out, (slope, third) = refs[5 : 5 + n_x], refs[5 + n_x :]
         d_new[...] = d[...]
         image, _, gain = self.factors(coef, n)
         if n_y:
@@ -766,9 +785,9 @@
             for i in range(self.p):
                 for row, share in self.shares(faces, scale, image, i * self.block):
                     d_new[row : row + self.p, :] += gain * share
-        self.operator(d_new, g, v, *work, ahead, back)
-        self.iteration_fold(v)
-        self.emit(v, x_out, y_out)
+        self.operator_first(d_new, g, ends, f1, f2, f3, slope, third, ahead, back)
+        self.iteration_fold(ends)
+        self.emit_first((ends[: self.block, :], ends[self.block :, :]), x_out)
 
     def finish(self, n_y, n, *refs):
         part, scale, coef, hot = refs[:4]
@@ -818,7 +837,6 @@
         return pltpu.VMEM(size, dtype)
 
     lanes = plan.ez * p
-    table = jnp.asarray(plan.table)
     ahead, back = jnp.asarray(plan.third[0]), jnp.asarray(plan.third[1])
     field3, field4 = shape(rows, w3), shape(rows, w4)
     elements = element_slot.shape[-1]
@@ -831,7 +849,8 @@
     )
     results = call(
         functools.partial(plan.prepare, n_x, n_y),
-        [field4, shape(plan.c * elements, w3, dtype=BF16)] + [shape(block, w4)] * (n_x + n_y),
+        [field4, shape(plan.c * elements, w3, dtype=BF16), shape(FIELDS, p * plan.ey * p, lanes)]
+        + [shape(block, w4)] * (n_x + n_y),
         (
             geometry,
             viscosity,
@@ -845,8 +864,8 @@
         scratch=[vmem(rows, w4)],
         name="prepare",
     )
-    s4, hot3 = results[:2]
-    x_out, y_raw = results[2 : 2 + n_x], results[2 + n_x :]
+    s4, hot3, fields = results[:3]
+    x_out, y_raw = results[3 : 3 + n_x], results[3 + n_x :]
     x_in = send(x_out, "gx", x_pairs)
 
     lhs = FIELDS * block + 2 * plan.c * p
@@ -854,13 +873,15 @@
         functools.partial(plan.convert, n_y, n_z),
         [shape(FIELDS * rows, w3), shape(2 * block, w3)]
         + [shape(2 * p, w3)] * n_y
-        + [shape(p * plan.ey * p, lanes)] * n_z,
-        (geometry, viscosity, spread3, dirichlet),
+        + [shape(p * plan.ey * p, lanes)] * n_z
+        + [shape(block + 2 * p, w4)] * n_z,
+        (fields, spread3, dirichlet, s4),
         scratch=[vmem(lhs, plan.ey * lanes, dtype=BF16)] * 2,
         name="convert",
     )
-    raw, ind = results[:2]
-    y_more, z_geometry = results[2 : 2 + n_y], results[2 + n_y :]
+    g, ind = results[:2]
+    y_more, results = results[2 : 2 + n_y], results[2 + n_y :]
+    z_fields, z_out = results[:n_z], results[n_z:]
 
     def joined(x_in, y_raw, y_more=()):
         if not y_raw:
@@ -870,49 +891,44 @@
         return call(functools.partial(plan.join, n_x, n_y), faces, x_in + y_raw + list(y_more), name="join")
 
     y_in = send(joined(x_in, y_raw, y_more), "gy", y_pairs)
-    z_geometry = send(z_geometry, ("gx", "gz"), z_pairs)
-    g = call(
-        functools.partial(plan.halo_geometry, n_z),
-        [shape(FIELDS, rows, w3)],
-        [raw, jnp.asarray(plan.halo), table] + z_geometry,
-        scratch=[vmem(FIELDS * block, 128, dtype=BF16)] * 2 + [vmem(FIELDS * rows, w3)],
-        name="halo_geometry",
-    )[0]
-    results = call(
-        functools.partial(plan.pack_first, n_x),
-        [field4] + [shape(block + 2 * p, w4)] * n_z,
-        [s4, ind] + x_in,
-        name="pack_first",
-    )
-    s4, z_out = results[0], results[1:]
-    if n_y and n_z:
+    z_fields = send(z_fields, ("gx", "gz"), z_pairs)
+    if n_z:
+        g = call(
+            functools.partial(plan.halo_fields, n_z),
+            [shape(FIELDS * rows, w3)],
+            [g, jnp.asarray(plan.halo)] + z_fields,
+            scratch=[vmem(FIELDS * block, lanes, dtype=BF16)],
+            name="halo_fields",
+        )[0]
+    if n_z:
         z_out = call(
-            functools.partial(plan.pack_second, n_y, n_z),
+            functools.partial(plan.pack_second, n_x, n_y, n_z),
             [shape(*z.shape) for z in z_out],
-            y_in + z_out,
+            x_in + y_in + z_out,
             flops=FLOPS,
             name="pack_second",
         )
     z_in = send(z_out, ("gx", "gz"), z_pairs)
     widen = jnp.asarray(plan.widen)
     own = call(
-        functools.partial(plan.own, n_y),
+        functools.partial(plan.own, n_x, n_y),
         [field3, field3, shape(2 * block, w3)],
-        [s4, ind, widen] + y_in,
+        [s4, ind, widen] + x_in + y_in,
         scratch=[vmem(rows, w4)],
         name="own",
     )
 
-    messages = [shape(block, w3)] * (n_x + n_y)
+    fluxes = [shape(2 * block, w3)] + [field3] * 3 + [shape(block, w3)] * n_x
     results = call(
-        functools.partial(plan.start, n_x, n_y, n_z),
-        [field3] * 3 + messages,
+        functools.partial(plan.start, n_x, n_z),
+        [field3] * 2 + fluxes,
         own + [g, widen, ahead, back] + z_in,
-        scratch=[vmem(rows, w4), vmem(rows, w3), vmem(2 * block, w3)] + [vmem(rows, w3)] * 4,
+        scratch=[vmem(rows, w4), vmem(rows, w3), vmem(2 * block, w3)] + [vmem(rows, w3)] * 2,
         name="first_direction",
     )
-    t, scale, v = results[:3]
-    x_out, y_raw = results[3 : 3 + n_x], results[3 + n_x :]
+    t, scale = results[:2]
+    ends, f1, f2, f3 = results[2:6]
+    x_out = results[6:]
     x_out, low, high = lax.optimization_barrier((x_out, eig_low, eig_high))
     coef = call(
         plan.coefficients,
@@ -925,6 +941,14 @@
     for n in range(ITERS - 1):
         last = n == ITERS - 2
         x_in = send(x_out, "gx", x_pairs)
+        results = call(
+            functools.partial(plan.operator_second, n_x, n_y),
+            [field3] + [shape(block, w3)] * n_y,
+            [d, g, ends, f1, f2, f3, back],
+            scratch=[vmem(rows, w3)],
+            name="operator_second",
+        )
+        v, y_raw = results[0], results[1:]
         y_old, y_in = y_in, send(joined(x_in, y_raw), "gy", y_pairs)
         results = call(
             functools.partial(plan.preview, n_x, n_y, n, last),
@@ -938,13 +962,13 @@
         t_old, d = results
         results = call(
             functools.partial(plan.middle, n_x, n_y, n),
-            [field3] * 2 + messages,
+            [field3] + fluxes,
             [d, scale, g, coef, ahead, back] + y_in,
-            scratch=[vmem(rows, w3)] * 4,
+            scratch=[vmem(rows, w3)] * 2,
             name="direction",
         )
-        d, v = results[:2]
-        x_out, y_raw = results[2 : 2 + n_x], results[2 + n_x :]
+        d, ends, f1, f2, f3 = results[:5]
+        x_out = results[5:]
     out = call(
         functools.partial(plan.finish, n_y, n),
         [shape(plan.c, elements, rows)],

time: 34.4 us -> 33.2 us (0.965)
  waiting for transfers between devices: 9.68 us -> 8.23 us
  starting transfers between devices: 14 us -> 14.7 us
  Pallas kernels: 8.23 us -> 7.78 us
    ppermute x13, waiting for transfers between devices: 9.68 us -> 8.23 us  [send(): return [lax.ppermute(x, axis, pair) for x, pair in zip(arrays, pairs)]]
    ppermute x13, starting transfers between devices: 14 us -> 14.7 us  [send(): return [lax.ppermute(x, axis, pair) for x, pair in zip(arrays, pairs)]]
    pallas_call x16 -> x17, Pallas kernels: 8.23 us -> 7.78 us  [call(): pl.pallas_call(kernel, out_shape=list(outputs), in_specs=specs, out_specs...]
    unnamed x26 -> x24, local copies, waits for them, and re-layouts: 0.82 us -> 0.81 us
where the time goes in v6:
time: 33.2 us; the launch traced here: 33 us
  starting transfers between devices  14.7 us (44%)
  waiting for transfers between devices  8.23 us (25%)
  Pallas kernels  7.78 us (23%)
  between operations  1.51 us (5%)
  local copies, waits for them, and re-layouts  0.81 us (2%)
    ppermute x13, starting transfers between devices, send(): return [lax.ppermute(x, axis, pair) for x, pair in zip(arrays, pairs)]  14.7 us
    ppermute x13, waiting for transfers between devices, send(): return [lax.ppermute(x, axis, pair) for x, pair in zip(arrays, pairs)]  8.23 us
    pallas_call x17, Pallas kernels, call(): pl.pallas_call(kernel, out_shape=list(outputs), in_specs=specs, out_specs...  7.78 us
    unnamed x24, local copies, waits for them, and re-layouts  0.81 us
  transfers between devices with their start and end apart: 13, of which 7 were waited for; matrix products, arithmetic and copies ran while one was open for 0% of the time, Pallas kernels for 11%

profile of v6, /device:TPU:0, one launch (start us, length us, event | category | flops | bytes accessed | tf_op | source)
XLA Modules:
  0.0 33.0 jit_solution(18140797130527645994)
XLA Ops:
  0.0 0.4 %spread_tables.1 = (bf16[256,1024]{1,0:T(8,128)(2,1)S(1)}, bf16[256,1024]{1,0:T(8,128)(2,1)S(1)}) custom-call(), custom_call_target="tpu_custom_call" | custom-call | flops 3000000000 | tf_op jit(solution)/shard_map/spread_tables/pallas_call | solution.py:824
  0.4 0.5 %copy-done.6 = bf16[128,384]{1,0:T(8,128)(2,1)S(1)} copy-done((bf16[128,384]{1,0:T(8,128)(2,1)S(1)}, bf16[128,384]{1,0:T(8,128)(2,1)}, u32[]{:S(2)}) %copy-start.6) | copy-done | bytes 98328
  0.9 0.2 copy-done.3
  1.2 0.8 %prepare.1 = (f32[512,128]{1,0:T(8,128)S(1)}, bf16[96,128]{1,0:T(8,128)(2,1)S(1)}, f32[7,128,128]{2,1,0:T(8,128)S(1)}, f32[64,128]{1,0:T(8,128)S(1)}, f32[64,128]{1,0:T(8,128)S(1)}, /*index=5*/f32[64,128]{1,0:T(8,128)S(1)}) custom-call(f32[6,8,16,128]{3,2,1,0:T(8,128)S(1)} %copy-done.3, f32[8,16,128]{2,1,0:T(8,128)S(1)} %copy-done.7, ...), custom_call_target="tpu_custom_call" | custom-call | tf_op jit(solution)/shard_map/prepare/pallas_call | solution.py:824
  2.0 0.5 %collective-permute-start = (f32[64,128]{1,0:T(8,128)S(1)}, f32[64,128]{1,0:T(8,128)S(1)}, u32[]{:S(2)}, u32[]{:S(2)}) collective-permute-start(f32[64,128]{1,0:T(8,128)S(1)} %get-tuple-element.55), channel_id=1, source_target_pairs={{0,8},{8,0},{16,24},{24,16},{1,9},{9,1},{17,25},{25,17},{2,10},{10... | collective-permute-start | bytes 98312 | tf_op jit(solution)/shard_map/ppermute | solution.py:816
  2.5 2.6 %collective-permute-start.1 = (f32[64,128]{1,0:T(8,128)S(1)}, f32[64,128]{1,0:T(8,128)S(1)}, u32[]{:S(2)}, u32[]{:S(2)}) collective-permute-start(f32[64,128]{1,0:T(8,128)S(1)} %get-tuple-element.56), channel_id=1, source_target_pairs={{0,24},{8,16},{16,8},{24,0},{1,25},{9,17},{17,9},{25,1},{2,26},{10... | collective-permute-start | bytes 98312 | tf_op jit(solution)/shard_map/ppermute | solution.py:816
  5.1 1.1 %convert.1 = (f32[3584,128]{1,0:T(8,128)S(1)}, f32[128,128]{1,0:T(8,128)S(1)}, f32[16,128]{1,0:T(8,128)S(1)}, f32[128,128]{1,0:T(8,128)S(1)}, f32[128,128]{1,0:T...) custom-call(f32[7,128,128]{2,1,0:T(8,128)S(1)} %get-tuple-element.52.refs_0_, ...), custom_call_target="tpu_custom_call" | custom-call | tf_op jit(solution)/shard_map/convert/pallas_call | solution.py:824
  6.2 0.5 %collective-permute-done.1.refs_1_.refs_4_ = f32[64,128]{1,0:T(8,128)S(1)} collective-permute-done((f32[64,128]{1,0:T(8,128)S(1)}, f32[64,128]{1,0:T(8,128)S(1)}, u32[]{:S(2)}, u32[]{:S(2)}) %collective-permute-start.1) | collective-permute-done | bytes 32800 | tf_op jit(solution)/shard_map/ppermute | solution.py:816
  6.8 0.1 join.3
  6.8 1.7 %collective-permute-start.2 = (f32[40,128]{1,0:T(8,128)S(1)}, f32[40,128]{1,0:T(8,128)S(1)}, u32[]{:S(2)}, u32[]{:S(2)}) collective-permute-start(f32[40,128]{1,0:T(8,128)S(1)} %join.3), channel_id=1, source_target_pairs={{0,4},{4,0},{1,5},{5,1},{2,6},{6,2},{3,7},{7,3},{8,12},{12,8},{9,1... | collective-permute-start | bytes 61448 | tf_op jit(solution)/shard_map/ppermute | solution.py:816
  8.6 1.6 %collective-permute-start.3 = (f32[128,128]{1,0:T(8,128)S(1)}, f32[128,128]{1,0:T(8,128)S(1)}, u32[]{:S(2)}, u32[]{:S(2)}) collective-permute-start(f32[128,128]{1,0:T(8,128)S(1)} %get-tuple-element.63), channel_id=1, source_target_pairs={{0,1},{1,0},{2,3},{3,2},{8,9},{9,8},{10,11},{11,10},{16,17},{17,16... | collective-permute-start | bytes 196616 | tf_op jit(solution)/shard_map/ppermute | solution.py:816
  10.1 0.6 %collective-permute-done.2.refs_5_.refs_2_ = f32[40,128]{1,0:T(8,128)S(1)} collective-permute-done((f32[40,128]{1,0:T(8,128)S(1)}, f32[40,128]{1,0:T(8,128)S(1)}, u32[]{:S(2)}, u32[]{:S(2)}) %collective-permute-start.2) | collective-permute-done | bytes 20512 | tf_op jit(solution)/shard_map/ppermute | solution.py:816
  10.7 0.2 pack_second.1
  10.9 2.7 %collective-permute-start.5 = (f32[80,128]{1,0:T(8,128)S(1)}, f32[80,128]{1,0:T(8,128)S(1)}, u32[]{:S(2)}, u32[]{:S(2)}) collective-permute-start(f32[80,128]{1,0:T(8,128)S(1)} %get-tuple-element.67), channel_id=1, source_target_pairs={{0,1},{1,0},{2,3},{3,2},{8,9},{9,8},{10,11},{11,10},{16,17},{17,16... | collective-permute-start | bytes 122888 | tf_op jit(solution)/shard_map/ppermute | solution.py:816
  13.5 0.3 own.1
  13.8 0.9 %halo_fields.1.refs_3_.refs_1_.refs_2_ = f32[3584,128]{1,0:T(8,128)S(1)} custom-call(f32[3584,128]{1,0:T(8,128)S(1)} %get-tuple-element.62.refs_0_, bf16[128,1024]{1,0:T(8,128)(2,1)S(1)} %copy-done.4, f32[128,128]{1,0:T(8,128)S(1)} %collective-permute-done.3.refs_2_, f32[128,128]{1,0:T(8,128)S(1)} %collective-permute-done.4.refs_3_), custom_call_target="tpu_custom_call" | custom-call | tf_op jit(solution)/shard_map/halo_fields/pallas_call | solution.py:824
  14.7 0.8 %collective-permute-done.5.refs_7_ = f32[80,128]{1,0:T(8,128)S(1)} collective-permute-done((f32[80,128]{1,0:T(8,128)S(1)}, f32[80,128]{1,0:T(8,128)S(1)}, u32[]{:S(2)}, u32[]{:S(2)}) %collective-permute-start.5) | collective-permute-done | bytes 40992 | tf_op jit(solution)/shard_map/ppermute | solution.py:816
  15.5 1.1 %first_direction.1 = (f32[512,128]{1,0:T(8,128)S(1)}, f32[512,128]{1,0:T(8,128)S(1)}, f32[128,128]{1,0:T(8,128)S(1)}, f32[512,128]{1,0:T(8,128)S(1)}, f32[512,12...) custom-call(f32[512,128]{1,0:T(8,128)S(1)} %get-tuple-element.59.refs_0_, ...), custom_call_target="tpu_custom_call" | custom-call | tf_op jit(solution)/shard_map/first_direction/pallas_call | solution.py:824
  16.7 1.6 %collective-permute-start.8 = (f32[64,128]{1,0:T(8,128)S(1)}, f32[64,128]{1,0:T(8,128)S(1)}, u32[]{:S(2)}, u32[]{:S(2)}) collective-permute-start(f32[64,128]{1,0:T(8,128)S(1)} %get-tuple-element.82), channel_id=1, source_target_pairs={{0,24},{8,16},{16,8},{24,0},{1,25},{9,17},{17,9},{25,1},{2,26},{10... | collective-permute-start | bytes 98312 | tf_op jit(solution)/shard_map/ppermute | solution.py:816
  18.3 0.4 %operator_second.2 = (f32[512,128]{1,0:T(8,128)S(1)}, f32[64,128]{1,0:T(8,128)S(1)}) custom-call(f32[512,128]{1,0:T(8,128)S(1)} %get-tuple-element.69.refs_0_.refs_1_.refs_2_, f32[3584,128]{1,0:T(8,128)S(1)} %halo_fields.1.refs_3_.refs_1_.refs_2_, f32[128,128]{1,0:T(8,128)S(1)} %get-tuple-element.71.refs_2_, f32[512,128]{1,0:T(8,128)S(1)} %get-tuple-element.72.refs_3_, ...), custom_call_target="tpu_custom_call" | custom-call | tf_op jit(solution)/shard_map/operator_second/pallas_call | solution.py:824
  18.7 1.4 %collective-permute-done.8.refs_8_.refs_1_ = f32[64,128]{1,0:T(8,128)S(1)} collective-permute-done((f32[64,128]{1,0:T(8,128)S(1)}, f32[64,128]{1,0:T(8,128)S(1)}, u32[]{:S(2)}, u32[]{:S(2)}) %collective-permute-start.8) | collective-permute-done | bytes 32800 | tf_op jit(solution)/shard_map/ppermute | solution.py:816
  20.2 1.1 %collective-permute-start.9 = (f32[32,128]{1,0:T(8,128)S(1)}, f32[32,128]{1,0:T(8,128)S(1)}, u32[]{:S(2)}, u32[]{:S(2)}) collective-permute-start(f32[32,128]{1,0:T(8,128)S(1)} %join.4), channel_id=1, source_target_pairs={{0,4},{4,0},{1,5},{5,1},{2,6},{6,2},{3,7},{7,3},{8,12},{12,8},{9,1... | collective-permute-start | bytes 49160 | tf_op jit(solution)/shard_map/ppermute | solution.py:816
  22.7 0.1 preview.2
  22.8 1.2 %collective-permute-done.9.refs_6_.refs_9_ = f32[32,128]{1,0:T(8,128)S(1)} collective-permute-done((f32[32,128]{1,0:T(8,128)S(1)}, f32[32,128]{1,0:T(8,128)S(1)}, u32[]{:S(2)}, u32[]{:S(2)}) %collective-permute-start.9) | collective-permute-done | bytes 16416 | tf_op jit(solution)/shard_map/ppermute | solution.py:816
  24.0 0.7 %direction.1 = (f32[512,128]{1,0:T(8,128)S(1)}, f32[128,128]{1,0:T(8,128)S(1)}, f32[512,128]{1,0:T(8,128)S(1)}, f32[512,128]{1,0:T(8,128)S(1)}, f32[512,128]{1,0...) custom-call(f32[512,128]{1,0:T(8,128)S(1)} %get-tuple-element.84.refs_0_, ...), custom_call_target="tpu_custom_call" | custom-call | tf_op jit(solution)/shard_map/direction/pallas_call | solution.py:824
  24.8 1.6 %collective-permute-start.11 = (f32[64,128]{1,0:T(8,128)S(1)}, f32[64,128]{1,0:T(8,128)S(1)}, u32[]{:S(2)}, u32[]{:S(2)}) collective-permute-start(f32[64,128]{1,0:T(8,128)S(1)} %get-tuple-element.93), channel_id=1, source_target_pairs={{0,24},{8,16},{16,8},{24,0},{1,25},{9,17},{17,9},{25,1},{2,26},{10... | collective-permute-start | bytes 98312 | tf_op jit(solution)/shard_map/ppermute | solution.py:816
  26.4 0.4 %operator_second.3 = (f32[512,128]{1,0:T(8,128)S(1)}, f32[64,128]{1,0:T(8,128)S(1)}) custom-call(f32[512,128]{1,0:T(8,128)S(1)} %get-tuple-element.86.refs_0_.refs_2_, f32[3584,128]{1,0:T(8,128)S(1)} %halo_fields.1.refs_3_.refs_1_.refs_2_, f32[128,128]{1,0:T(8,128)S(1)} %get-tuple-element.87.refs_2_, f32[512,128]{1,0:T(8,128)S(1)} %get-tuple-element.88.refs_3_, ...), custom_call_target="tpu_custom_call" | custom-call | tf_op jit(solution)/shard_map/operator_second/pallas_call | solution.py:824
  26.8 1.4 %collective-permute-done.11.refs_8_.refs_1_ = f32[64,128]{1,0:T(8,128)S(1)} collective-permute-done((f32[64,128]{1,0:T(8,128)S(1)}, f32[64,128]{1,0:T(8,128)S(1)}, u32[]{:S(2)}, u32[]{:S(2)}) %collective-permute-start.11) | collective-permute-done | bytes 32800 | tf_op jit(solution)/shard_map/ppermute | solution.py:816
  28.3 1.1 %collective-permute-start.12 = (f32[32,128]{1,0:T(8,128)S(1)}, f32[32,128]{1,0:T(8,128)S(1)}, u32[]{:S(2)}, u32[]{:S(2)}) collective-permute-start(f32[32,128]{1,0:T(8,128)S(1)} %join.5), channel_id=1, source_target_pairs={{0,4},{4,0},{1,5},{5,1},{2,6},{6,2},{3,7},{7,3},{8,12},{12,8},{9,1... | collective-permute-start | bytes 49160 | tf_op jit(solution)/shard_map/ppermute | solution.py:816
  29.4 0.3 preview.3.refs_0_
  29.7 2.4 %collective-permute-done.12.refs_4_ = f32[32,128]{1,0:T(8,128)S(1)} collective-permute-done((f32[32,128]{1,0:T(8,128)S(1)}, f32[32,128]{1,0:T(8,128)S(1)}, u32[]{:S(2)}, u32[]{:S(2)}) %collective-permute-start.12) | collective-permute-done | bytes 16416 | tf_op jit(solution)/shard_map/ppermute | solution.py:816
  32.1 1.0 %field.1 = f32[3,32,512]{2,1,0:T(8,128)} custom-call(f32[96,512]{1,0:T(8,128)S(1)} %preview.3.refs_0_, f32[512,128]{1,0:T(8,128)S(1)} %get-tuple-element.70.refs_3_.refs_1_, f32[40,128]{1,0:T(8,128)S(1)} %coefficients.1.refs_5_.refs_3_.refs_2_, bf16[96,128]{1,0:T(8,128)(2,1)S(1)} %get-tuple-element.80.refs_6_.refs_3_, ...), custom_call_target="tpu_custom_call" | custom-call | tf_op jit(solution)/shard_map/field/pallas_call | solution.py:824
  (35 shorter events, 0.5 us)
Async XLA Ops:
  0.0 0.9 %copy-start.6 = (bf16[128,384]{1,0:T(8,128)(2,1)S(1)}, bf16[128,384]{1,0:T(8,128)(2,1)}, u32[]{:S(2)}) copy-start(bf16[128,384]{1,0:T(8,128)(2,1)} %constant.18.clone.refs_7_) | copy-start | bytes 294916
  0.0 0.9 %copy-start.9 = (f32[48,128]{1,0:T(8,128)S(1)}, f32[48,128]{1,0:T(8,128)}, u32[]{:S(2)}) copy-start(f32[48,128]{1,0:T(8,128)} %constant.16.clone.refs_3_) | copy-start | bytes 73732
  0.0 0.9 %copy-start.10 = (s32[6,128]{1,0:T(8,128)S(1)}, s32[6,128]{1,0:T(8,128)}, u32[]{:S(2)}) copy-start(s32[6,128]{1,0:T(8,128)} %constant.17.clone.refs_6_) | copy-start | bytes 9220
  0.0 0.9 %copy-start.11 = (s32[1,32]{1,0:T(1,128)S(1)}, s32[1,32]{1,0:T(1,128)}, u32[]{:S(2)}) copy-start(s32[1,32]{1,0:T(1,128)} %refs_5_.3) | copy-start | bytes 388
  0.0 0.9 %copy-start.7 = (f32[8,16,128]{2,1,0:T(8,128)S(1)}, f32[8,16,128]{2,1,0:T(8,128)}, u32[]{:S(2)}) copy-start(f32[8,16,128]{2,1,0:T(8,128)} %refs_1_.2) | copy-start | bytes 196612
  0.0 1.1 %copy-start.3 = (f32[6,8,16,128]{3,2,1,0:T(8,128)S(1)}, f32[6,8,16,128]{3,2,1,0:T(8,128)}, u32[]{:S(2)}) copy-start(f32[6,8,16,128]{3,2,1,0:T(8,128)} %refs_0_.1) | copy-start | bytes 1179652
  0.0 1.2 %copy-start.5 = (f32[3,512,32]{1,2,0:T(8,128)S(1)}, f32[3,512,32]{1,2,0:T(8,128)}, u32[]{:S(2)}) copy-start(f32[3,512,32]{1,2,0:T(8,128)} %param.14) | copy-start | bytes 589828
  0.0 5.1 %copy-start.8 = (s32[2,3,16,128]{3,2,1,0:T(8,128)S(1)}, s32[2,3,16,128]{3,2,1,0:T(8,128)}, u32[]{:S(2)}) copy-start(s32[2,3,16,128]{3,2,1,0:T(8,128)} %refs_2_.2) | copy-start | bytes 147460
  2.0 4.3 %collective-permute-start = (f32[64,128]{1,0:T(8,128)S(1)}, f32[64,128]{1,0:T(8,128)S(1)}, u32[]{:S(2)}, u32[]{:S(2)}) collective-permute-start(f32[64,128]{1,0:T(8,128)S(1)} %get-tuple-element.55), channel_id=1, source_target_pairs={{0,8},{8,0},{16,24},{24,16},{1,9},{9,1},{17,25},{25,17},{2,10},{10... | collective-permute-start | bytes 98312 | tf_op jit(solution)/shard_map/ppermute | solution.py:816
  2.5 4.3 %collective-permute-start.1 = (f32[64,128]{1,0:T(8,128)S(1)}, f32[64,128]{1,0:T(8,128)S(1)}, u32[]{:S(2)}, u32[]{:S(2)}) collective-permute-start(f32[64,128]{1,0:T(8,128)S(1)} %get-tuple-element.56), channel_id=1, source_target_pairs={{0,24},{8,16},{16,8},{24,0},{1,25},{9,17},{17,9},{25,1},{2,26},{10... | collective-permute-start | bytes 98312 | tf_op jit(solution)/shard_map/ppermute | solution.py:816
  6.8 3.8 %collective-permute-start.2 = (f32[40,128]{1,0:T(8,128)S(1)}, f32[40,128]{1,0:T(8,128)S(1)}, u32[]{:S(2)}, u32[]{:S(2)}) collective-permute-start(f32[40,128]{1,0:T(8,128)S(1)} %join.3), channel_id=1, source_target_pairs={{0,4},{4,0},{1,5},{5,1},{2,6},{6,2},{3,7},{7,3},{8,12},{12,8},{9,1... | collective-permute-start | bytes 61448 | tf_op jit(solution)/shard_map/ppermute | solution.py:816
  8.6 5.2 %collective-permute-start.3 = (f32[128,128]{1,0:T(8,128)S(1)}, f32[128,128]{1,0:T(8,128)S(1)}, u32[]{:S(2)}, u32[]{:S(2)}) collective-permute-start(f32[128,128]{1,0:T(8,128)S(1)} %get-tuple-element.63), channel_id=1, source_target_pairs={{0,1},{1,0},{2,3},{3,2},{8,9},{9,8},{10,11},{11,10},{16,17},{17,16... | collective-permute-start | bytes 196616 | tf_op jit(solution)/shard_map/ppermute | solution.py:816
  10.1 3.7 %collective-permute-start.4 = (f32[128,128]{1,0:T(8,128)S(1)}, f32[128,128]{1,0:T(8,128)S(1)}, u32[]{:S(2)}, u32[]{:S(2)}) collective-permute-start(f32[128,128]{1,0:T(8,128)S(1)} %get-tuple-element.64), channel_id=1, source_target_pairs={{0,8},{1,2},{2,1},{3,11},{8,0},{9,10},{10,9},{11,3},{16,24},{17,18... | collective-permute-start | bytes 196616 | tf_op jit(solution)/shard_map/ppermute | solution.py:816
  10.7 2.8 %copy-start.1 = (bf16[256,256]{1,0:T(8,128)(2,1)S(1)}, bf16[256,256]{1,0:T(8,128)(2,1)}, u32[]{:S(2)}) copy-start(bf16[256,256]{1,0:T(8,128)(2,1)} %constant.20.clone.refs_2_.refs_4_) | copy-start | bytes 393220
  10.7 3.1 %copy-start.4 = (bf16[128,1024]{1,0:T(8,128)(2,1)S(1)}, bf16[128,1024]{1,0:T(8,128)(2,1)}, u32[]{:S(2)}) copy-start(bf16[128,1024]{1,0:T(8,128)(2,1)} %constant.19.clone.refs_1_) | copy-start | bytes 786436
  10.9 4.6 %collective-permute-start.5 = (f32[80,128]{1,0:T(8,128)S(1)}, f32[80,128]{1,0:T(8,128)S(1)}, u32[]{:S(2)}, u32[]{:S(2)}) collective-permute-start(f32[80,128]{1,0:T(8,128)S(1)} %get-tuple-element.67), channel_id=1, source_target_pairs={{0,1},{1,0},{2,3},{3,2},{8,9},{9,8},{10,11},{11,10},{16,17},{17,16... | collective-permute-start | bytes 122888 | tf_op jit(solution)/shard_map/ppermute | solution.py:816
  13.5 2.0 %collective-permute-start.6 = (f32[80,128]{1,0:T(8,128)S(1)}, f32[80,128]{1,0:T(8,128)S(1)}, u32[]{:S(2)}, u32[]{:S(2)}) collective-permute-start(f32[80,128]{1,0:T(8,128)S(1)} %get-tuple-element.68), channel_id=1, source_target_pairs={{0,8},{1,2},{2,1},{3,11},{8,0},{9,10},{10,9},{11,3},{16,24},{17,18... | collective-permute-start | bytes 122888 | tf_op jit(solution)/shard_map/ppermute | solution.py:816
  13.8 1.7 %copy-start = (bf16[128,384]{1,0:T(8,128)(2,1)S(1)}, bf16[128,384]{1,0:T(8,128)(2,1)}, u32[]{:S(2)}) copy-start(bf16[128,384]{1,0:T(8,128)(2,1)} %constant.15.clone.refs_6_.refs_5_) | copy-start | bytes 294916
  13.8 1.7 %copy-start.2 = (bf16[128,384]{1,0:T(8,128)(2,1)S(1)}, bf16[128,384]{1,0:T(8,128)(2,1)}, u32[]{:S(2)}) copy-start(bf16[128,384]{1,0:T(8,128)(2,1)} %constant.14.clone.refs_5_.refs_4_) | copy-start | bytes 294916
  16.6 2.1 %collective-permute-start.7 = (f32[64,128]{1,0:T(8,128)S(1)}, f32[64,128]{1,0:T(8,128)S(1)}, u32[]{:S(2)}, u32[]{:S(2)}) collective-permute-start(f32[64,128]{1,0:T(8,128)S(1)} %get-tuple-element.81), channel_id=1, source_target_pairs={{0,8},{8,0},{16,24},{24,16},{1,9},{9,1},{17,25},{25,17},{2,10},{10... | collective-permute-start | bytes 98312 | tf_op jit(solution)/shard_map/ppermute | solution.py:816
  16.7 3.4 %collective-permute-start.8 = (f32[64,128]{1,0:T(8,128)S(1)}, f32[64,128]{1,0:T(8,128)S(1)}, u32[]{:S(2)}, u32[]{:S(2)}) collective-permute-start(f32[64,128]{1,0:T(8,128)S(1)} %get-tuple-element.82), channel_id=1, source_target_pairs={{0,24},{8,16},{16,8},{24,0},{1,25},{9,17},{17,9},{25,1},{2,26},{10... | collective-permute-start | bytes 98312 | tf_op jit(solution)/shard_map/ppermute | solution.py:816
  20.2 3.8 %collective-permute-start.9 = (f32[32,128]{1,0:T(8,128)S(1)}, f32[32,128]{1,0:T(8,128)S(1)}, u32[]{:S(2)}, u32[]{:S(2)}) collective-permute-start(f32[32,128]{1,0:T(8,128)S(1)} %join.4), channel_id=1, source_target_pairs={{0,4},{4,0},{1,5},{5,1},{2,6},{6,2},{3,7},{7,3},{8,12},{12,8},{9,1... | collective-permute-start | bytes 49160 | tf_op jit(solution)/shard_map/ppermute | solution.py:816
  24.7 2.1 %collective-permute-start.10 = (f32[64,128]{1,0:T(8,128)S(1)}, f32[64,128]{1,0:T(8,128)S(1)}, u32[]{:S(2)}, u32[]{:S(2)}) collective-permute-start(f32[64,128]{1,0:T(8,128)S(1)} %get-tuple-element.92), channel_id=1, source_target_pairs={{0,8},{8,0},{16,24},{24,16},{1,9},{9,1},{17,25},{25,17},{2,10},{10... | collective-permute-start | bytes 98312 | tf_op jit(solution)/shard_map/ppermute | solution.py:816
  24.8 3.4 %collective-permute-start.11 = (f32[64,128]{1,0:T(8,128)S(1)}, f32[64,128]{1,0:T(8,128)S(1)}, u32[]{:S(2)}, u32[]{:S(2)}) collective-permute-start(f32[64,128]{1,0:T(8,128)S(1)} %get-tuple-element.93), channel_id=1, source_target_pairs={{0,24},{8,16},{16,8},{24,0},{1,25},{9,17},{17,9},{25,1},{2,26},{10... | collective-permute-start | bytes 98312 | tf_op jit(solution)/shard_map/ppermute | solution.py:816
  28.3 3.8 %collective-permute-start.12 = (f32[32,128]{1,0:T(8,128)S(1)}, f32[32,128]{1,0:T(8,128)S(1)}, u32[]{:S(2)}, u32[]{:S(2)}) collective-permute-start(f32[32,128]{1,0:T(8,128)S(1)} %join.5), channel_id=1, source_target_pairs={{0,4},{4,0},{1,5},{5,1},{2,6},{6,2},{3,7},{7,3},{8,12},{12,8},{9,1... | collective-permute-start | bytes 49160 | tf_op jit(solution)/shard_map/ppermute | solution.py:816

commit v7 on v6

--- a/solution.py
+++ b/solution.py
@@ -248,7 +248,7 @@
     def rows_of(self, g, q, at):
         return g[q * self.rows + at.start : q * self.rows + at.stop, :]
 
-    def operator_first(self, v, g, ends, f1, f2, f3, slope, third, ahead, back):
+    def fluxes(self, v, g, f1, f2, f3, slope, third, ahead):
         p, block, rows = self.p, self.block, self.rows
 
         def store(row, value):
@@ -260,13 +260,42 @@
             at = slice(i * block, (i + 1) * block)
             x, s1, s3 = v[at, :], slope[at, :], third[at, :]
             s2 = self.along_j(x, self.forward)
-            xy, xz, yz = self.rows_of(g, 3, at), self.rows_of(g, 4, at), self.rows_of(g, 5, at)
+            xy, xz, yz = (self.rows_of(g, q, at) for q in (3, 4, 5))
             f1[at, :] = self.rows_of(g, 0, at) * s1 + xy * s2 + xz * s3
             f2[at, :] = xy * s1 + self.rows_of(g, 1, at) * s2 + yz * s3
             f3[at, :] = xz * s1 + yz * s2 + self.rows_of(g, 2, at) * s3
+
+    def share_fluxes(self, shares, g, third, ahead, whole, write):
+        p, block = self.p, self.block
+        x = shares[...]
+        ends = [[x[(2 * i + n) * p : (2 * i + n + 1) * p] for i in range(p)] for n in range(2)]
+        s1 = [self.contract(column, self.forward) for column in ends]
+        self.along_k(shares, ahead, third, 0, 2 * block)
+        for i in range(p):
+            first, last = ends[0][i], ends[1][i]
+            count = 3 if whole or i in (0, p - 1) else 1
+            for j in range(p):
+                at = slice(i * block + j * p, i * block + (j + 1) * p)
+                s2 = float(self.forward[j, 0]) * first + float(self.forward[j, p - 1]) * last
+                rows = ((0, 3, 4), (3, 1, 5), (4, 5, 2))[:count]
+                values = [self.rows_of(g, row[1], at) * s2 for row in rows]
+                if j in (0, p - 1):
+                    n = int(j > 0)
+                    line = (2 * i + n) * p
+                    e1, e3 = s1[n][i], third[line : line + p, :]
+                    values = [
+                        value + self.rows_of(g, row[0], at) * e1 + self.rows_of(g, row[2], at) * e3
+                        for value, row in zip(values, rows)
+                    ]
+                write(i, j, values)
+
+    def end_planes(self, v, g, ends, f1, f2, f3, slope, third, back):
+        p, block, rows = self.p, self.block, self.rows
         for n, start in enumerate((0, rows - block)):
             at = slice(start, start + block)
-            ends[n * block : (n + 1) * block, :] = self.along_j(f2[at, :], self.forward.T) + self.rows_of(g, 6, at) * v[at, :]
+            ends[n * block : (n + 1) * block, :] = (
+                self.along_j(f2[at, :], self.forward.T) + self.rows_of(g, 6, at) * v[at, :]
+            )
             slope[n * block : (n + 1) * block, :] = f3[at, :]
         self.along_k(slope, back, third, 0, 2 * block)
         for j in range(p):
@@ -275,15 +304,34 @@
             for row, value in ((j * p, first), (block + j * p, last)):
                 ends[row : row + p, :] += value + third[row : row + p, :]
 
-    def operator_second(self, n_x, n_y, *refs):
+    def operator_second(self, n_x, n_y, shared, *refs):
         v, g, ends, f1, f2, f3, back = refs[:7]
-        out, y_out, third = refs[7], refs[8 : 8 + n_y], refs[8 + n_y]
+        refs = refs[7:]
         p, block, rows = self.p, self.block, self.rows
+        if shared:
+            shares, ahead, out = refs[:3]
+            y_out, (v_new, third, *new) = refs[3 : 3 + n_y], refs[3 + n_y :]
+
+            def write(i, j, values):
+                at = slice(i * block + j * p, i * block + (j + 1) * p)
+                for f_old, f_new, value in zip((f1, f2, f3), new, values):
+                    f_new[at, :] = f_old[at, :] + value
+
+            self.share_fluxes(shares, g, third, ahead, True, write)
+            v_new[...] = v[...]
+            for i in range(p):
+                for m, row in enumerate((i * block, (i + 1) * block - p)):
+                    v_new[row : row + p, :] += shares[(2 * i + m) * p : (2 * i + m + 1) * p, :]
+            v, (f1, f2, f3) = v_new, new
+        else:
+            out, y_out, third = refs[0], refs[1 : 1 + n_y], refs[1 + n_y]
         out[:block, :], out[rows - block :, :] = ends[:block, :], ends[block:, :]
         self.along_k(f3, back, third, block, rows - block)
         for i in range(1, p - 1):
             at = slice(i * block, (i + 1) * block)
-            out[at, :] = self.along_j(f2[at, :], self.forward.T) + self.rows_of(g, 6, at) * v[at, :] + third[at, :]
+            out[at, :] = (
+                self.along_j(f2[at, :], self.forward.T) + self.rows_of(g, 6, at) * v[at, :] + third[at, :]
+            )
         for j in range(p):
             at = [slice(i * block + j * p, i * block + (j + 1) * p) for i in range(p)]
             values = self.contract([f1[r, :] for r in at], self.forward.T, range(1, p // 2))
@@ -713,7 +761,8 @@
                 factor = jnp.where(flag[row : row + block, :] > 0.5, 0.0, factor)
             scale[at, :] = factor
             t[at, :] = factor * r[at, :]
-        self.operator_first(t, g, ends, f1, f2, f3, slope, third, ahead, back)
+        self.fluxes(t, g, f1, f2, f3, slope, third, ahead)
+        self.end_planes(t, g, ends, f1, f2, f3, slope, third, back)
         self.iteration_fold(ends)
         self.emit_first((ends[:block, :], ends[block:, :]), x_out)
 
@@ -732,16 +781,16 @@
         return out
 
     def preview(self, n_x, n_y, n, last, *refs):
-        t, t_old, d, scale, v, coef, hot = refs[:7]
-        refs = refs[7:]
-        x_in, y_old, refs = refs[:n_x], refs[n_x : -2 if not last else -3], refs[-2 if not last else -3 :]
+        t, t_old, d, scale, v, coef = refs[:6]
+        refs = refs[6:]
+        x_in, y_old, refs = refs[:n_x], refs[n_x : n_x + (n_y if n else 0)], refs[n_x + (n_y if n else 0) :]
         p, block, rows = self.p, self.block, self.rows
         image, keep, gain = self.factors(coef, n)
         start = coef[0:1, :]
         if last:
-            out, t_new, field = refs
+            hot, out, t_new, field = refs
         else:
-            t_new, d_new = refs
+            g, ahead, back, t_new, d_new, f1, f2, f3, ends, slope, third = refs
         low, high = both_sides([x[...] for x in x_in], roles("gx", self.sizes["gx"]))
         if n:
             faces = self.second_sides(y_old) if n_y else None
@@ -764,6 +813,9 @@
                 d_new[at, :] = following
         if last:
             out[...] = self.by_slots(hot, field[...])
+        else:
+            self.fluxes(d_new, g, f1, f2, f3, slope, third, ahead)
+            self.end_planes(d_new, g, ends, f1, f2, f3, slope, third, back)
 
     def by_slots(self, hot, field):
         return lax.dot_general(
@@ -774,20 +826,42 @@
         )
 
     def middle(self, n_x, n_y, n, *refs):
-        d, scale, g, coef, ahead, back = refs[:6]
+        part, scale, g, coef, ahead, back = refs[:6]
         y_in, refs = refs[6 : 6 + n_y], refs[6 + n_y :]
-        d_new, ends, f1, f2, f3 = refs[:5]
-        x_out, (slope, third) = refs[5 : 5 + n_x], refs[5 + n_x :]
-        d_new[...] = d[...]
+        ends, shares, refs = refs[0], refs[1], refs[2:]
+        x_out, (f1, f2, f3, third) = refs[:n_x], refs[n_x:]
+        p, block, rows = self.p, self.block, self.rows
         image, _, gain = self.factors(coef, n)
+        ends[...] = part[...]
         if n_y:
             faces = self.second_sides(y_in)
-            for i in range(self.p):
-                for row, share in self.shares(faces, scale, image, i * self.block):
-                    d_new[row : row + self.p, :] += gain * share
-        self.operator_first(d_new, g, ends, f1, f2, f3, slope, third, ahead, back)
+            for i in range(p):
+                for m, (_, share) in enumerate(self.shares(faces, scale, image, i * block)):
+                    shares[(2 * i + m) * p : (2 * i + m + 1) * p, :] = gain * share
+
+            def write(i, j, values):
+                f1[i * block + j * p : i * block + (j + 1) * p, :] = values[0]
+                if len(values) > 1:
+                    row = (block if i else 0) + j * p
+                    f2[row : row + p, :], f3[row : row + p, :] = values[1], values[2]
+
+            self.share_fluxes(shares, g, third, ahead, False, write)
+            self.along_k(f3, back, third, 0, 2 * block)
+            for m, i in enumerate((0, p - 1)):
+                at = slice(m * block, (m + 1) * block)
+                ends[at, :] += self.along_j(f2[at, :], self.forward.T) + third[at, :]
+                for n_face, j in enumerate((0, p - 1)):
+                    row, at = m * block + j * p, slice(i * block + j * p, i * block + (j + 1) * p)
+                    line = (2 * i + n_face) * p
+                    ends[row : row + p, :] += self.rows_of(g, 6, at) * shares[line : line + p, :]
+            for j in range(p):
+                x = [f1[i * block + j * p : i * block + (j + 1) * p, :] for i in range(p)]
+                for row, value in zip((j * p, block + j * p), self.contract(x, self.forward.T, (0,))):
+                    ends[row : row + p, :] += value
+        else:
+            shares[...] = jnp.zeros(shares.shape, F32)
         self.iteration_fold(ends)
-        self.emit_first((ends[: self.block, :], ends[self.block :, :]), x_out)
+        self.emit_first((ends[:block, :], ends[block:, :]), x_out)
 
     def finish(self, n_y, n, *refs):
         part, scale, coef, hot = refs[:4]
@@ -941,34 +1015,44 @@
     for n in range(ITERS - 1):
         last = n == ITERS - 2
         x_in = send(x_out, "gx", x_pairs)
-        results = call(
-            functools.partial(plan.operator_second, n_x, n_y),
-            [field3] + [shape(block, w3)] * n_y,
-            [d, g, ends, f1, f2, f3, back],
-            scratch=[vmem(rows, w3)],
-            name="operator_second",
-        )
-        v, y_raw = results[0], results[1:]
+        outputs = [field3] + [shape(block, w3)] * n_y
+        if n:
+            results = call(
+                functools.partial(plan.operator_second, n_x, n_y, True),
+                outputs + [field3],
+                [d, g, ends, f1, f2, f3, back, shares, ahead],
+                scratch=[vmem(rows, w3)] * 4,
+                name="operator_second",
+            )
+            v, y_raw, d = results[0], results[1 : 1 + n_y], results[1 + n_y]
+        else:
+            results = call(
+                functools.partial(plan.operator_second, n_x, n_y, False),
+                outputs,
+                [d, g, ends, f1, f2, f3, back],
+                scratch=[vmem(rows, w3)],
+                name="operator_second",
+            )
+            v, y_raw = results[0], results[1:]
         y_old, y_in = y_in, send(joined(x_in, y_raw), "gy", y_pairs)
         results = call(
             functools.partial(plan.preview, n_x, n_y, n, last),
-            [shape(plan.c * elements, rows)] if last else [field3, field3],
-            [t, t_old, d, scale, v, coef, hot3] + x_in + y_old,
-            scratch=[vmem(rows, w3)] * 2 if last else [],
+            [shape(plan.c * elements, rows)] if last else [field3] * 5 + [shape(2 * block, w3)],
+            [t, t_old, d, scale, v, coef] + x_in + y_old + ([hot3] if last else [g, ahead, back]),
+            scratch=[vmem(rows, w3)] * 2,
             name="preview",
         )
         if last:
             break
-        t_old, d = results
+        t_old, d, f1, f2, f3, ends = results
         results = call(
             functools.partial(plan.middle, n_x, n_y, n),
-            [field3] + fluxes,
-            [d, scale, g, coef, ahead, back] + y_in,
-            scratch=[vmem(rows, w3)] * 2,
+            [shape(2 * block, w3)] * 2 + [shape(block, w3)] * n_x,
+            [ends, scale, g, coef, ahead, back] + y_in,
+            scratch=[vmem(rows, w3)] + [vmem(2 * block, w3)] * 3,
             name="direction",
         )
-        d, ends, f1, f2, f3 = results[:5]
-        x_out = results[5:]
+        ends, shares, x_out = results[0], results[1], results[2:]
     out = call(
         functools.partial(plan.finish, n_y, n),
         [shape(plan.c, elements, rows)],

time: 33.2 us -> 33.1 us (level)
  waiting for transfers between devices: 8.23 us -> 7.41 us
  Pallas kernels: 7.78 us -> 8.5 us
    ppermute x13, waiting for transfers between devices: 8.23 us -> 7.41 us  [send(): return [lax.ppermute(x, axis, pair) for x, pair in zip(arrays, pairs)]]
    pallas_call x17, Pallas kernels: 7.78 us -> 8.5 us  [call(): pl.pallas_call(kernel, out_shape=list(outputs), in_specs=specs, out_specs...]
  transfers between devices with their start and end apart: 13 -> 13, of which waited for: 7 -> 7; matrix products, arithmetic and copies ran while one was open for 0% -> 0% of each run, Pallas kernels for 11% -> 14%
where the time goes in v7:
time: 33.1 us; the launch traced here: 32.9 us
  starting transfers between devices  14.7 us (44%)
  Pallas kernels  8.5 us (26%)
  waiting for transfers between devices  7.41 us (22%)
  between operations  1.51 us (5%)
  local copies, waits for them, and re-layouts  0.81 us (2%)
    ppermute x13, starting transfers between devices, send(): return [lax.ppermute(x, axis, pair) for x, pair in zip(arrays, pairs)]  14.7 us
    pallas_call x17, Pallas kernels, call(): pl.pallas_call(kernel, out_shape=list(outputs), in_specs=specs, out_specs...  8.5 us
    ppermute x13, waiting for transfers between devices, send(): return [lax.ppermute(x, axis, pair) for x, pair in zip(arrays, pairs)]  7.41 us
    unnamed x24, local copies, waits for them, and re-layouts  0.81 us
  transfers between devices with their start and end apart: 13, of which 7 were waited for; matrix products, arithmetic and copies ran while one was open for 0% of the time, Pallas kernels for 14%

profile of v7, /device:TPU:0, one launch (start us, length us, event | category | flops | bytes accessed | tf_op | source)
XLA Modules:
  0.0 32.9 jit_solution(6455209815833643034)
XLA Ops:
  0.0 0.4 %spread_tables.1 = (bf16[256,1024]{1,0:T(8,128)(2,1)S(1)}, bf16[256,1024]{1,0:T(8,128)(2,1)S(1)}) custom-call(), custom_call_target="tpu_custom_call" | custom-call | flops 3000000000 | tf_op jit(solution)/shard_map/spread_tables/pallas_call | solution.py:898
  0.4 0.5 %copy-done.6 = bf16[128,384]{1,0:T(8,128)(2,1)S(1)} copy-done((bf16[128,384]{1,0:T(8,128)(2,1)S(1)}, bf16[128,384]{1,0:T(8,128)(2,1)}, u32[]{:S(2)}) %copy-start.6) | copy-done | bytes 98328
  0.9 0.2 copy-done.3
  1.2 0.8 %prepare.1 = (f32[512,128]{1,0:T(8,128)S(1)}, bf16[96,128]{1,0:T(8,128)(2,1)S(1)}, f32[7,128,128]{2,1,0:T(8,128)S(1)}, f32[64,128]{1,0:T(8,128)S(1)}, f32[64,128]{1,0:T(8,128)S(1)}, /*index=5*/f32[64,128]{1,0:T(8,128)S(1)}) custom-call(f32[6,8,16,128]{3,2,1,0:T(8,128)S(1)} %copy-done.3, f32[8,16,128]{2,1,0:T(8,128)S(1)} %copy-done.7, ...), custom_call_target="tpu_custom_call" | custom-call | tf_op jit(solution)/shard_map/prepare/pallas_call | solution.py:898
  2.0 0.5 %collective-permute-start = (f32[64,128]{1,0:T(8,128)S(1)}, f32[64,128]{1,0:T(8,128)S(1)}, u32[]{:S(2)}, u32[]{:S(2)}) collective-permute-start(f32[64,128]{1,0:T(8,128)S(1)} %get-tuple-element.57), channel_id=1, source_target_pairs={{0,8},{8,0},{16,24},{24,16},{1,9},{9,1},{17,25},{25,17},{2,10},{10... | collective-permute-start | bytes 98312 | tf_op jit(solution)/shard_map/ppermute | solution.py:890
  2.5 2.6 %collective-permute-start.1 = (f32[64,128]{1,0:T(8,128)S(1)}, f32[64,128]{1,0:T(8,128)S(1)}, u32[]{:S(2)}, u32[]{:S(2)}) collective-permute-start(f32[64,128]{1,0:T(8,128)S(1)} %get-tuple-element.58), channel_id=1, source_target_pairs={{0,24},{8,16},{16,8},{24,0},{1,25},{9,17},{17,9},{25,1},{2,26},{10... | collective-permute-start | bytes 98312 | tf_op jit(solution)/shard_map/ppermute | solution.py:890
  5.1 1.1 %convert.1 = (f32[3584,128]{1,0:T(8,128)S(1)}, f32[128,128]{1,0:T(8,128)S(1)}, f32[16,128]{1,0:T(8,128)S(1)}, f32[128,128]{1,0:T(8,128)S(1)}, f32[128,128]{1,0:T...) custom-call(f32[7,128,128]{2,1,0:T(8,128)S(1)} %get-tuple-element.54.refs_0_, ...), custom_call_target="tpu_custom_call" | custom-call | tf_op jit(solution)/shard_map/convert/pallas_call | solution.py:898
  6.2 0.5 %collective-permute-done.1.refs_1_.refs_4_ = f32[64,128]{1,0:T(8,128)S(1)} collective-permute-done((f32[64,128]{1,0:T(8,128)S(1)}, f32[64,128]{1,0:T(8,128)S(1)}, u32[]{:S(2)}, u32[]{:S(2)}) %collective-permute-start.1) | collective-permute-done | bytes 32800 | tf_op jit(solution)/shard_map/ppermute | solution.py:890
  6.8 0.1 join.3
  6.8 1.7 %collective-permute-start.2 = (f32[40,128]{1,0:T(8,128)S(1)}, f32[40,128]{1,0:T(8,128)S(1)}, u32[]{:S(2)}, u32[]{:S(2)}) collective-permute-start(f32[40,128]{1,0:T(8,128)S(1)} %join.3), channel_id=1, source_target_pairs={{0,4},{4,0},{1,5},{5,1},{2,6},{6,2},{3,7},{7,3},{8,12},{12,8},{9,1... | collective-permute-start | bytes 61448 | tf_op jit(solution)/shard_map/ppermute | solution.py:890
  8.6 1.6 %collective-permute-start.3 = (f32[128,128]{1,0:T(8,128)S(1)}, f32[128,128]{1,0:T(8,128)S(1)}, u32[]{:S(2)}, u32[]{:S(2)}) collective-permute-start(f32[128,128]{1,0:T(8,128)S(1)} %get-tuple-element.65), channel_id=1, source_target_pairs={{0,1},{1,0},{2,3},{3,2},{8,9},{9,8},{10,11},{11,10},{16,17},{17,16... | collective-permute-start | bytes 196616 | tf_op jit(solution)/shard_map/ppermute | solution.py:890
  10.1 0.6 %collective-permute-done.2.refs_5_.refs_2_ = f32[40,128]{1,0:T(8,128)S(1)} collective-permute-done((f32[40,128]{1,0:T(8,128)S(1)}, f32[40,128]{1,0:T(8,128)S(1)}, u32[]{:S(2)}, u32[]{:S(2)}) %collective-permute-start.2) | collective-permute-done | bytes 20512 | tf_op jit(solution)/shard_map/ppermute | solution.py:890
  10.7 0.2 pack_second.1
  10.9 2.7 %collective-permute-start.5 = (f32[80,128]{1,0:T(8,128)S(1)}, f32[80,128]{1,0:T(8,128)S(1)}, u32[]{:S(2)}, u32[]{:S(2)}) collective-permute-start(f32[80,128]{1,0:T(8,128)S(1)} %get-tuple-element.69), channel_id=1, source_target_pairs={{0,1},{1,0},{2,3},{3,2},{8,9},{9,8},{10,11},{11,10},{16,17},{17,16... | collective-permute-start | bytes 122888 | tf_op jit(solution)/shard_map/ppermute | solution.py:890
  13.5 0.3 own.1
  13.8 0.9 %halo_fields.1.refs_3_.refs_1_.refs_8_.refs_2_ = f32[3584,128]{1,0:T(8,128)S(1)} custom-call(f32[3584,128]{1,0:T(8,128)S(1)} %get-tuple-element.64.refs_0_, bf16[128,1024]{1,0:T(8,128)(2,1)S(1)} %copy-done.4, f32[128,128]{1,0:T(8,128)S(1)} %collective-permute-done.3.refs_2_, f32[128,128]{1,0:T(8,128)S(1)} %collective-permute-done.4.refs_3_), custom_call_target="tpu_custom_call" | custom-call | tf_op jit(solution)/shard_map/halo_fields/pallas_call | solution.py:898
  14.7 0.8 %collective-permute-done.5.refs_7_ = f32[80,128]{1,0:T(8,128)S(1)} collective-permute-done((f32[80,128]{1,0:T(8,128)S(1)}, f32[80,128]{1,0:T(8,128)S(1)}, u32[]{:S(2)}, u32[]{:S(2)}) %collective-permute-start.5) | collective-permute-done | bytes 40992 | tf_op jit(solution)/shard_map/ppermute | solution.py:890
  15.5 1.2 %first_direction.1 = (f32[512,128]{1,0:T(8,128)S(1)}, f32[512,128]{1,0:T(8,128)S(1)}, f32[128,128]{1,0:T(8,128)S(1)}, f32[512,128]{1,0:T(8,128)S(1)}, f32[512,12...) custom-call(f32[512,128]{1,0:T(8,128)S(1)} %get-tuple-element.61.refs_0_, ...), custom_call_target="tpu_custom_call" | custom-call | tf_op jit(solution)/shard_map/first_direction/pallas_call | solution.py:898
  16.7 1.6 %collective-permute-start.8 = (f32[64,128]{1,0:T(8,128)S(1)}, f32[64,128]{1,0:T(8,128)S(1)}, u32[]{:S(2)}, u32[]{:S(2)}) collective-permute-start(f32[64,128]{1,0:T(8,128)S(1)} %get-tuple-element.83), channel_id=1, source_target_pairs={{0,24},{8,16},{16,8},{24,0},{1,25},{9,17},{17,9},{25,1},{2,26},{10... | collective-permute-start | bytes 98312 | tf_op jit(solution)/shard_map/ppermute | solution.py:890
  18.3 0.4 %operator_second.2 = (f32[512,128]{1,0:T(8,128)S(1)}, f32[64,128]{1,0:T(8,128)S(1)}) custom-call(f32[512,128]{1,0:T(8,128)S(1)} %get-tuple-element.71.refs_0_.refs_1_.refs_2_, f32[3584,128]{1,0:T(8,128)S(1)} %halo_fields.1.refs_3_.refs_1_.refs_8_.refs_2_, f32[128,128]{1,0:T(8,128)S(1)} %get-tuple-element.73.refs_2_, ...), custom_call_target="tpu_custom_call" | custom-call | tf_op jit(solution)/shard_map/operator_second/pallas_call | solution.py:898
  18.8 1.4 %collective-permute-done.8.refs_7_.refs_1_ = f32[64,128]{1,0:T(8,128)S(1)} collective-permute-done((f32[64,128]{1,0:T(8,128)S(1)}, f32[64,128]{1,0:T(8,128)S(1)}, u32[]{:S(2)}, u32[]{:S(2)}) %collective-permute-start.8) | collective-permute-done | bytes 32800 | tf_op jit(solution)/shard_map/ppermute | solution.py:890
  20.2 1.1 %collective-permute-start.9 = (f32[32,128]{1,0:T(8,128)S(1)}, f32[32,128]{1,0:T(8,128)S(1)}, u32[]{:S(2)}, u32[]{:S(2)}) collective-permute-start(f32[32,128]{1,0:T(8,128)S(1)} %join.4), channel_id=1, source_target_pairs={{0,4},{4,0},{1,5},{5,1},{2,6},{6,2},{3,7},{7,3},{8,12},{12,8},{9,1... | collective-permute-start | bytes 49160 | tf_op jit(solution)/shard_map/ppermute | solution.py:890
  22.7 0.7 %preview.2 = (f32[512,128]{1,0:T(8,128)S(1)}, f32[512,128]{1,0:T(8,128)S(1)}, f32[512,128]{1,0:T(8,128)S(1)}, f32[512,128]{1,0:T(8,128)S(1)}, f32[512,128]{1,0:T(8,128)S(1)}, /*index=5*/f32[128,128]{1,0:T(8,128)S(1)}) custom-call(f32[512,128]{1,0:T(8,128)S(1)} %get-tuple-element.71.refs_0_.refs_1_.refs_2_, ...), custom_call_target="tpu_custom_call" | custom-call | tf_op jit(solution)/shard_map/preview/pallas_call | solution.py:898
  23.4 0.6 %collective-permute-done.9.refs_6_.refs_8_ = f32[32,128]{1,0:T(8,128)S(1)} collective-permute-done((f32[32,128]{1,0:T(8,128)S(1)}, f32[32,128]{1,0:T(8,128)S(1)}, u32[]{:S(2)}, u32[]{:S(2)}) %collective-permute-start.9) | collective-permute-done | bytes 16416 | tf_op jit(solution)/shard_map/ppermute | solution.py:890
  24.0 0.6 %direction.1 = (f32[128,128]{1,0:T(8,128)S(1)}, f32[128,128]{1,0:T(8,128)S(1)}, f32[64,128]{1,0:T(8,128)S(1)}, f32[64,128]{1,0:T(8,128)S(1)}) custom-call(f32[128,128]{1,0:T(8,128)S(1)} %get-tuple-element.86.refs_0_, f32[512,128]{1,0:T(8,128)S(1)} %get-tuple-element.72.refs_3_.refs_1_, f32[3584,128]{1,0:T(8,128)S(1)} %halo_fields.1.refs_3_.refs_1_.refs_8_.refs_2_, ...), custom_call_target="tpu_custom_call" | custom-call | tf_op jit(solution)/shard_map/direction/pallas_call | solution.py:898
  24.7 1.6 %collective-permute-start.11 = (f32[64,128]{1,0:T(8,128)S(1)}, f32[64,128]{1,0:T(8,128)S(1)}, u32[]{:S(2)}, u32[]{:S(2)}) collective-permute-start(f32[64,128]{1,0:T(8,128)S(1)} %get-tuple-element.96), channel_id=1, source_target_pairs={{0,24},{8,16},{16,8},{24,0},{1,25},{9,17},{17,9},{25,1},{2,26},{10... | collective-permute-start | bytes 98312 | tf_op jit(solution)/shard_map/ppermute | solution.py:890
  26.3 0.6 %operator_second.3 = (f32[512,128]{1,0:T(8,128)S(1)}, f32[64,128]{1,0:T(8,128)S(1)}, f32[512,128]{1,0:T(8,128)S(1)}) custom-call(f32[512,128]{1,0:T(8,128)S(1)} %get-tuple-element.85.refs_0_, f32[3584,128]{1,0:T(8,128)S(1)} %halo_fields.1.refs_3_.refs_1_.refs_8_.refs_2_, f32[128,128]{1,0:T(8,128)S(1)} %get-tuple-element.88.refs_2_, ...), custom_call_target="tpu_custom_call" | custom-call | tf_op jit(solution)/shard_map/operator_second/pallas_call | solution.py:898
  26.9 1.2 %collective-permute-done.11.refs_7_.refs_1_ = f32[64,128]{1,0:T(8,128)S(1)} collective-permute-done((f32[64,128]{1,0:T(8,128)S(1)}, f32[64,128]{1,0:T(8,128)S(1)}, u32[]{:S(2)}, u32[]{:S(2)}) %collective-permute-start.11) | collective-permute-done | bytes 32800 | tf_op jit(solution)/shard_map/ppermute | solution.py:890
  28.2 1.1 %collective-permute-start.12 = (f32[32,128]{1,0:T(8,128)S(1)}, f32[32,128]{1,0:T(8,128)S(1)}, u32[]{:S(2)}, u32[]{:S(2)}) collective-permute-start(f32[32,128]{1,0:T(8,128)S(1)} %join.5), channel_id=1, source_target_pairs={{0,4},{4,0},{1,5},{5,1},{2,6},{6,2},{3,7},{7,3},{8,12},{12,8},{9,1... | collective-permute-start | bytes 49160 | tf_op jit(solution)/shard_map/ppermute | solution.py:890
  29.3 0.3 preview.3.refs_0_
  29.6 2.4 %collective-permute-done.12.refs_4_ = f32[32,128]{1,0:T(8,128)S(1)} collective-permute-done((f32[32,128]{1,0:T(8,128)S(1)}, f32[32,128]{1,0:T(8,128)S(1)}, u32[]{:S(2)}, u32[]{:S(2)}) %collective-permute-start.12) | collective-permute-done | bytes 16416 | tf_op jit(solution)/shard_map/ppermute | solution.py:890
  32.0 1.0 %field.1 = f32[3,32,512]{2,1,0:T(8,128)} custom-call(f32[96,512]{1,0:T(8,128)S(1)} %preview.3.refs_0_, f32[512,128]{1,0:T(8,128)S(1)} %get-tuple-element.72.refs_3_.refs_1_, f32[40,128]{1,0:T(8,128)S(1)} %coefficients.1.refs_5_.refs_3_.refs_2_, bf16[96,128]{1,0:T(8,128)(2,1)S(1)} %get-tuple-element.97.refs_9_.refs_3_, ...), custom_call_target="tpu_custom_call" | custom-call | tf_op jit(solution)/shard_map/field/pallas_call | solution.py:898
  (35 shorter events, 0.5 us)
Async XLA Ops:
  0.0 0.9 %copy-start.6 = (bf16[128,384]{1,0:T(8,128)(2,1)S(1)}, bf16[128,384]{1,0:T(8,128)(2,1)}, u32[]{:S(2)}) copy-start(bf16[128,384]{1,0:T(8,128)(2,1)} %constant.18.clone.refs_7_) | copy-start | bytes 294916
  0.0 0.9 %copy-start.9 = (f32[48,128]{1,0:T(8,128)S(1)}, f32[48,128]{1,0:T(8,128)}, u32[]{:S(2)}) copy-start(f32[48,128]{1,0:T(8,128)} %constant.16.clone.refs_3_) | copy-start | bytes 73732
  0.0 0.9 %copy-start.10 = (s32[6,128]{1,0:T(8,128)S(1)}, s32[6,128]{1,0:T(8,128)}, u32[]{:S(2)}) copy-start(s32[6,128]{1,0:T(8,128)} %constant.17.clone.refs_6_) | copy-start | bytes 9220
  0.0 0.9 %copy-start.11 = (s32[1,32]{1,0:T(1,128)S(1)}, s32[1,32]{1,0:T(1,128)}, u32[]{:S(2)}) copy-start(s32[1,32]{1,0:T(1,128)} %refs_5_.3) | copy-start | bytes 388
  0.0 0.9 %copy-start.7 = (f32[8,16,128]{2,1,0:T(8,128)S(1)}, f32[8,16,128]{2,1,0:T(8,128)}, u32[]{:S(2)}) copy-start(f32[8,16,128]{2,1,0:T(8,128)} %refs_1_.2) | copy-start | bytes 196612
  0.0 1.1 %copy-start.3 = (f32[6,8,16,128]{3,2,1,0:T(8,128)S(1)}, f32[6,8,16,128]{3,2,1,0:T(8,128)}, u32[]{:S(2)}) copy-start(f32[6,8,16,128]{3,2,1,0:T(8,128)} %refs_0_.1) | copy-start | bytes 1179652
  0.0 1.2 %copy-start.5 = (f32[3,512,32]{1,2,0:T(8,128)S(1)}, f32[3,512,32]{1,2,0:T(8,128)}, u32[]{:S(2)}) copy-start(f32[3,512,32]{1,2,0:T(8,128)} %param.14) | copy-start | bytes 589828
  0.0 5.1 %copy-start.8 = (s32[2,3,16,128]{3,2,1,0:T(8,128)S(1)}, s32[2,3,16,128]{3,2,1,0:T(8,128)}, u32[]{:S(2)}) copy-start(s32[2,3,16,128]{3,2,1,0:T(8,128)} %refs_2_.2) | copy-start | bytes 147460
  2.0 4.3 %collective-permute-start = (f32[64,128]{1,0:T(8,128)S(1)}, f32[64,128]{1,0:T(8,128)S(1)}, u32[]{:S(2)}, u32[]{:S(2)}) collective-permute-start(f32[64,128]{1,0:T(8,128)S(1)} %get-tuple-element.57), channel_id=1, source_target_pairs={{0,8},{8,0},{16,24},{24,16},{1,9},{9,1},{17,25},{25,17},{2,10},{10... | collective-permute-start | bytes 98312 | tf_op jit(solution)/shard_map/ppermute | solution.py:890
  2.5 4.3 %collective-permute-start.1 = (f32[64,128]{1,0:T(8,128)S(1)}, f32[64,128]{1,0:T(8,128)S(1)}, u32[]{:S(2)}, u32[]{:S(2)}) collective-permute-start(f32[64,128]{1,0:T(8,128)S(1)} %get-tuple-element.58), channel_id=1, source_target_pairs={{0,24},{8,16},{16,8},{24,0},{1,25},{9,17},{17,9},{25,1},{2,26},{10... | collective-permute-start | bytes 98312 | tf_op jit(solution)/shard_map/ppermute | solution.py:890
  6.8 3.8 %collective-permute-start.2 = (f32[40,128]{1,0:T(8,128)S(1)}, f32[40,128]{1,0:T(8,128)S(1)}, u32[]{:S(2)}, u32[]{:S(2)}) collective-permute-start(f32[40,128]{1,0:T(8,128)S(1)} %join.3), channel_id=1, source_target_pairs={{0,4},{4,0},{1,5},{5,1},{2,6},{6,2},{3,7},{7,3},{8,12},{12,8},{9,1... | collective-permute-start | bytes 61448 | tf_op jit(solution)/shard_map/ppermute | solution.py:890
  8.6 5.2 %collective-permute-start.3 = (f32[128,128]{1,0:T(8,128)S(1)}, f32[128,128]{1,0:T(8,128)S(1)}, u32[]{:S(2)}, u32[]{:S(2)}) collective-permute-start(f32[128,128]{1,0:T(8,128)S(1)} %get-tuple-element.65), channel_id=1, source_target_pairs={{0,1},{1,0},{2,3},{3,2},{8,9},{9,8},{10,11},{11,10},{16,17},{17,16... | collective-permute-start | bytes 196616 | tf_op jit(solution)/shard_map/ppermute | solution.py:890
  10.1 3.7 %collective-permute-start.4 = (f32[128,128]{1,0:T(8,128)S(1)}, f32[128,128]{1,0:T(8,128)S(1)}, u32[]{:S(2)}, u32[]{:S(2)}) collective-permute-start(f32[128,128]{1,0:T(8,128)S(1)} %get-tuple-element.66), channel_id=1, source_target_pairs={{0,8},{1,2},{2,1},{3,11},{8,0},{9,10},{10,9},{11,3},{16,24},{17,18... | collective-permute-start | bytes 196616 | tf_op jit(solution)/shard_map/ppermute | solution.py:890
  10.7 2.8 %copy-start.2 = (bf16[256,256]{1,0:T(8,128)(2,1)S(1)}, bf16[256,256]{1,0:T(8,128)(2,1)}, u32[]{:S(2)}) copy-start(bf16[256,256]{1,0:T(8,128)(2,1)} %constant.20.clone.refs_2_.refs_4_) | copy-start | bytes 393220
  10.7 3.1 %copy-start.4 = (bf16[128,1024]{1,0:T(8,128)(2,1)S(1)}, bf16[128,1024]{1,0:T(8,128)(2,1)}, u32[]{:S(2)}) copy-start(bf16[128,1024]{1,0:T(8,128)(2,1)} %constant.19.clone.refs_1_) | copy-start | bytes 786436
  10.9 4.6 %collective-permute-start.5 = (f32[80,128]{1,0:T(8,128)S(1)}, f32[80,128]{1,0:T(8,128)S(1)}, u32[]{:S(2)}, u32[]{:S(2)}) collective-permute-start(f32[80,128]{1,0:T(8,128)S(1)} %get-tuple-element.69), channel_id=1, source_target_pairs={{0,1},{1,0},{2,3},{3,2},{8,9},{9,8},{10,11},{11,10},{16,17},{17,16... | collective-permute-start | bytes 122888 | tf_op jit(solution)/shard_map/ppermute | solution.py:890
  13.5 2.0 %collective-permute-start.6 = (f32[80,128]{1,0:T(8,128)S(1)}, f32[80,128]{1,0:T(8,128)S(1)}, u32[]{:S(2)}, u32[]{:S(2)}) collective-permute-start(f32[80,128]{1,0:T(8,128)S(1)} %get-tuple-element.70), channel_id=1, source_target_pairs={{0,8},{1,2},{2,1},{3,11},{8,0},{9,10},{10,9},{11,3},{16,24},{17,18... | collective-permute-start | bytes 122888 | tf_op jit(solution)/shard_map/ppermute | solution.py:890
  13.8 1.7 %copy-start = (bf16[128,384]{1,0:T(8,128)(2,1)S(1)}, bf16[128,384]{1,0:T(8,128)(2,1)}, u32[]{:S(2)}) copy-start(bf16[128,384]{1,0:T(8,128)(2,1)} %constant.15.clone.refs_6_.refs_10_.refs_5_) | copy-start | bytes 294916
  13.8 1.7 %copy-start.1 = (bf16[128,384]{1,0:T(8,128)(2,1)S(1)}, bf16[128,384]{1,0:T(8,128)(2,1)}, u32[]{:S(2)}) copy-start(bf16[128,384]{1,0:T(8,128)(2,1)} %constant.14.clone.refs_5_.refs_9_.refs_4_.refs_8_) | copy-start | bytes 294916
  16.7 2.1 %collective-permute-start.7 = (f32[64,128]{1,0:T(8,128)S(1)}, f32[64,128]{1,0:T(8,128)S(1)}, u32[]{:S(2)}, u32[]{:S(2)}) collective-permute-start(f32[64,128]{1,0:T(8,128)S(1)} %get-tuple-element.82), channel_id=1, source_target_pairs={{0,8},{8,0},{16,24},{24,16},{1,9},{9,1},{17,25},{25,17},{2,10},{10... | collective-permute-start | bytes 98312 | tf_op jit(solution)/shard_map/ppermute | solution.py:890
  16.7 3.4 %collective-permute-start.8 = (f32[64,128]{1,0:T(8,128)S(1)}, f32[64,128]{1,0:T(8,128)S(1)}, u32[]{:S(2)}, u32[]{:S(2)}) collective-permute-start(f32[64,128]{1,0:T(8,128)S(1)} %get-tuple-element.83), channel_id=1, source_target_pairs={{0,24},{8,16},{16,8},{24,0},{1,25},{9,17},{17,9},{25,1},{2,26},{10... | collective-permute-start | bytes 98312 | tf_op jit(solution)/shard_map/ppermute | solution.py:890
  20.2 3.8 %collective-permute-start.9 = (f32[32,128]{1,0:T(8,128)S(1)}, f32[32,128]{1,0:T(8,128)S(1)}, u32[]{:S(2)}, u32[]{:S(2)}) collective-permute-start(f32[32,128]{1,0:T(8,128)S(1)} %join.4), channel_id=1, source_target_pairs={{0,4},{4,0},{1,5},{5,1},{2,6},{6,2},{3,7},{7,3},{8,12},{12,8},{9,1... | collective-permute-start | bytes 49160 | tf_op jit(solution)/shard_map/ppermute | solution.py:890
  24.6 2.3 %collective-permute-start.10 = (f32[64,128]{1,0:T(8,128)S(1)}, f32[64,128]{1,0:T(8,128)S(1)}, u32[]{:S(2)}, u32[]{:S(2)}) collective-permute-start(f32[64,128]{1,0:T(8,128)S(1)} %get-tuple-element.95), channel_id=1, source_target_pairs={{0,8},{8,0},{16,24},{24,16},{1,9},{9,1},{17,25},{25,17},{2,10},{10... | collective-permute-start | bytes 98312 | tf_op jit(solution)/shard_map/ppermute | solution.py:890
  24.7 3.4 %collective-permute-start.11 = (f32[64,128]{1,0:T(8,128)S(1)}, f32[64,128]{1,0:T(8,128)S(1)}, u32[]{:S(2)}, u32[]{:S(2)}) collective-permute-start(f32[64,128]{1,0:T(8,128)S(1)} %get-tuple-element.96), channel_id=1, source_target_pairs={{0,24},{8,16},{16,8},{24,0},{1,25},{9,17},{17,9},{25,1},{2,26},{10... | collective-permute-start | bytes 98312 | tf_op jit(solution)/shard_map/ppermute | solution.py:890
  28.2 3.8 %collective-permute-start.12 = (f32[32,128]{1,0:T(8,128)S(1)}, f32[32,128]{1,0:T(8,128)S(1)}, u32[]{:S(2)}, u32[]{:S(2)}) collective-permute-start(f32[32,128]{1,0:T(8,128)S(1)} %join.5), channel_id=1, source_target_pairs={{0,4},{4,0},{1,5},{5,1},{2,6},{6,2},{3,7},{7,3},{8,12},{12,8},{9,1... | collective-permute-start | bytes 49160 | tf_op jit(solution)/shard_map/ppermute | solution.py:890

commit v8 on v7

--- a/solution.py
+++ b/solution.py
@@ -177,7 +177,7 @@
                                 halo[half * lanes // 2 + (side * ey + f) * part + g * p + k, k, at] = 1
         self.halo = halo.reshape(lanes, -1).astype(jnp.bfloat16)
         self.widen = widen.astype(jnp.bfloat16)
-        self.third = [self.block_terms(matrix) for matrix in (self.forward, self.forward.T, self.squared.T)]
+        self.third = [self.block_terms(matrix) for matrix in (self.forward, self.forward.T)]
         face = (ey * p, lanes)
         second = np.tile(np.arange(p), ey)[:, None]
         third = np.tile(np.arange(p), ez)[None, :]
@@ -416,7 +416,25 @@
             [jnp.where(column == ids[n : n + 1, :].astype(F32), 1.0, 0.0) for n in range(self.c)], axis=0
         ).astype(BF16)
 
-    def spread_tables(self, out3, out4):
+    def block_table(self, matrix, out):
+        p, size = self.p, out.shape[0]
+        row = lax.broadcasted_iota(jnp.int32, (p, size), 0)
+        node = lax.rem(lax.broadcasted_iota(jnp.int32, (p, size), 1), p)
+        tile = jnp.zeros((p, size), F32)
+        for a in range(p):
+            line = jnp.zeros((p, size), F32)
+            for i in range(p):
+                line = jnp.where(node == i, float(matrix[a, i]), line)
+            tile = jnp.where(row == a, line, tile)
+        whole = jnp.concatenate([tile] * (size // p), axis=0)
+        same = lax.broadcasted_iota(jnp.int32, (size, size), 0) // p == (
+            lax.broadcasted_iota(jnp.int32, (size, size), 1) // p
+        )
+        upper, lower = split(jnp.where(same, whole, 0.0))
+        out[...] = jnp.concatenate([upper, upper, lower], axis=1)
+
+    def spread_tables(self, out3, out4, square):
+        self.block_table(self.squared.T, square)
         p, ey, ez = self.p, self.ey, self.ez
         for out, width, step, offset, first in (
             (out3, self.w3, self.step3, HALO, 0),
@@ -914,9 +932,10 @@
     ahead, back = jnp.asarray(plan.third[0]), jnp.asarray(plan.third[1])
     field3, field4 = shape(rows, w3), shape(rows, w4)
     elements = element_slot.shape[-1]
-    spread3, spread4 = call(
+    spread3, spread4, square = call(
         plan.spread_tables,
-        [shape(plan.ey * lanes, p * w, dtype=BF16) for w in (w3, w4)],
+        [shape(plan.ey * lanes, p * w, dtype=BF16) for w in (w3, w4)]
+        + [shape(*plan.third[0].shape, dtype=BF16)],
         (),
         flops=FLOPS,
         name="spread_tables",
@@ -933,7 +952,7 @@
             jnp.swapaxes(right_side, 1, 2),
             element_slot,
             jnp.asarray(plan.ids),
-            jnp.asarray(plan.third[2]),
+            square,
         ),
         scratch=[vmem(rows, w4)],
         name="prepare",

time: 33.1 us -> 33 us (level)
    unnamed x24 -> x22, local copies, waits for them, and re-layouts: 0.81 us -> 0.74 us
where the time goes in v8:
time: 33 us; the launch traced here: 32.9 us
  starting transfers between devices  14.7 us (45%)
  Pallas kernels  8.53 us (26%)
  waiting for transfers between devices  7.4 us (22%)
  between operations  1.5 us (5%)
  local copies, waits for them, and re-layouts  0.74 us (2%)
    ppermute x13, starting transfers between devices, send(): return [lax.ppermute(x, axis, pair) for x, pair in zip(arrays, pairs)]  14.7 us
    pallas_call x17, Pallas kernels, call(): pl.pallas_call(kernel, out_shape=list(outputs), in_specs=specs, out_specs...  8.53 us
    ppermute x13, waiting for transfers between devices, send(): return [lax.ppermute(x, axis, pair) for x, pair in zip(arrays, pairs)]  7.4 us
    unnamed x22, local copies, waits for them, and re-layouts  0.74 us
  transfers between devices with their start and end apart: 13, of which 7 were waited for; matrix products, arithmetic and copies ran while one was open for 0% of the time, Pallas kernels for 14%

profile of v8, /device:TPU:0, one launch (start us, length us, event | category | flops | bytes accessed | tf_op | source)
XLA Modules:
  0.0 32.9 jit_solution(7972533874829919275)
XLA Ops:
  0.0 0.4 %spread_tables.1 = (bf16[256,1024]{1,0:T(8,128)(2,1)S(1)}, bf16[256,1024]{1,0:T(8,128)(2,1)S(1)}, bf16[128,384]{1,0:T(8,128)(2,1)S(1)}) custom-call(), custom_call_target="tpu_custom_call" | custom-call | flops 3000000000 | tf_op jit(solution)/shard_map/spread_tables/pallas_call | solution.py:916
  0.4 0.3 copy-done.8
  0.7 0.1 copy-done.6
  0.9 0.2 copy-done.3
  1.1 0.8 %prepare.1 = (f32[512,128]{1,0:T(8,128)S(1)}, bf16[96,128]{1,0:T(8,128)(2,1)S(1)}, f32[7,128,128]{2,1,0:T(8,128)S(1)}, f32[64,128]{1,0:T(8,128)S(1)}, f32[64,128]{1,0:T(8,128)S(1)}, /*index=5*/f32[64,128]{1,0:T(8,128)S(1)}) custom-call(f32[6,8,16,128]{3,2,1,0:T(8,128)S(1)} %copy-done.3, f32[8,16,128]{2,1,0:T(8,128)S(1)} %copy-done.6, ...), custom_call_target="tpu_custom_call" | custom-call | tf_op jit(solution)/shard_map/prepare/pallas_call | solution.py:916
  1.9 0.5 %collective-permute-start = (f32[64,128]{1,0:T(8,128)S(1)}, f32[64,128]{1,0:T(8,128)S(1)}, u32[]{:S(2)}, u32[]{:S(2)}) collective-permute-start(f32[64,128]{1,0:T(8,128)S(1)} %get-tuple-element.59), channel_id=1, source_target_pairs={{0,8},{8,0},{16,24},{24,16},{1,9},{9,1},{17,25},{25,17},{2,10},{10... | collective-permute-start | bytes 98312 | tf_op jit(solution)/shard_map/ppermute | solution.py:908
  2.4 2.6 %collective-permute-start.1 = (f32[64,128]{1,0:T(8,128)S(1)}, f32[64,128]{1,0:T(8,128)S(1)}, u32[]{:S(2)}, u32[]{:S(2)}) collective-permute-start(f32[64,128]{1,0:T(8,128)S(1)} %get-tuple-element.60), channel_id=1, source_target_pairs={{0,24},{8,16},{16,8},{24,0},{1,25},{9,17},{17,9},{25,1},{2,26},{10... | collective-permute-start | bytes 98312 | tf_op jit(solution)/shard_map/ppermute | solution.py:908
  5.0 1.1 %convert.1 = (f32[3584,128]{1,0:T(8,128)S(1)}, f32[128,128]{1,0:T(8,128)S(1)}, f32[16,128]{1,0:T(8,128)S(1)}, f32[128,128]{1,0:T(8,128)S(1)}, f32[128,128]{1,0:T...) custom-call(f32[7,128,128]{2,1,0:T(8,128)S(1)} %get-tuple-element.56.refs_0_, ...), custom_call_target="tpu_custom_call" | custom-call | tf_op jit(solution)/shard_map/convert/pallas_call | solution.py:916
  6.2 0.5 %collective-permute-done.1.refs_1_.refs_4_ = f32[64,128]{1,0:T(8,128)S(1)} collective-permute-done((f32[64,128]{1,0:T(8,128)S(1)}, f32[64,128]{1,0:T(8,128)S(1)}, u32[]{:S(2)}, u32[]{:S(2)}) %collective-permute-start.1) | collective-permute-done | bytes 32800 | tf_op jit(solution)/shard_map/ppermute | solution.py:908
  6.8 1.7 %collective-permute-start.2 = (f32[40,128]{1,0:T(8,128)S(1)}, f32[40,128]{1,0:T(8,128)S(1)}, u32[]{:S(2)}, u32[]{:S(2)}) collective-permute-start(f32[40,128]{1,0:T(8,128)S(1)} %join.3), channel_id=1, source_target_pairs={{0,4},{4,0},{1,5},{5,1},{2,6},{6,2},{3,7},{7,3},{8,12},{12,8},{9,1... | collective-permute-start | bytes 61448 | tf_op jit(solution)/shard_map/ppermute | solution.py:908
  8.5 1.6 %collective-permute-start.3 = (f32[128,128]{1,0:T(8,128)S(1)}, f32[128,128]{1,0:T(8,128)S(1)}, u32[]{:S(2)}, u32[]{:S(2)}) collective-permute-start(f32[128,128]{1,0:T(8,128)S(1)} %get-tuple-element.67), channel_id=1, source_target_pairs={{0,1},{1,0},{2,3},{3,2},{8,9},{9,8},{10,11},{11,10},{16,17},{17,16... | collective-permute-start | bytes 196616 | tf_op jit(solution)/shard_map/ppermute | solution.py:908
  10.1 0.6 %collective-permute-done.2.refs_5_.refs_2_ = f32[40,128]{1,0:T(8,128)S(1)} collective-permute-done((f32[40,128]{1,0:T(8,128)S(1)}, f32[40,128]{1,0:T(8,128)S(1)}, u32[]{:S(2)}, u32[]{:S(2)}) %collective-permute-start.2) | collective-permute-done | bytes 20512 | tf_op jit(solution)/shard_map/ppermute | solution.py:908
  10.6 0.2 pack_second.1
  10.8 2.7 %collective-permute-start.5 = (f32[80,128]{1,0:T(8,128)S(1)}, f32[80,128]{1,0:T(8,128)S(1)}, u32[]{:S(2)}, u32[]{:S(2)}) collective-permute-start(f32[80,128]{1,0:T(8,128)S(1)} %get-tuple-element.71), channel_id=1, source_target_pairs={{0,1},{1,0},{2,3},{3,2},{8,9},{9,8},{10,11},{11,10},{16,17},{17,16... | collective-permute-start | bytes 122888 | tf_op jit(solution)/shard_map/ppermute | solution.py:908
  13.5 0.3 own.1
  13.8 0.9 %halo_fields.1.refs_3_.refs_1_.refs_8_.refs_2_ = f32[3584,128]{1,0:T(8,128)S(1)} custom-call(f32[3584,128]{1,0:T(8,128)S(1)} %get-tuple-element.66.refs_0_, bf16[128,1024]{1,0:T(8,128)(2,1)S(1)} %copy-done.4, f32[128,128]{1,0:T(8,128)S(1)} %collective-permute-done.3.refs_2_, f32[128,128]{1,0:T(8,128)S(1)} %collective-permute-done.4.refs_3_), custom_call_target="tpu_custom_call" | custom-call | tf_op jit(solution)/shard_map/halo_fields/pallas_call | solution.py:916
  14.7 0.8 %collective-permute-done.5.refs_7_ = f32[80,128]{1,0:T(8,128)S(1)} collective-permute-done((f32[80,128]{1,0:T(8,128)S(1)}, f32[80,128]{1,0:T(8,128)S(1)}, u32[]{:S(2)}, u32[]{:S(2)}) %collective-permute-start.5) | collective-permute-done | bytes 40992 | tf_op jit(solution)/shard_map/ppermute | solution.py:908
  15.5 1.2 %first_direction.1 = (f32[512,128]{1,0:T(8,128)S(1)}, f32[512,128]{1,0:T(8,128)S(1)}, f32[128,128]{1,0:T(8,128)S(1)}, f32[512,128]{1,0:T(8,128)S(1)}, f32[512,12...) custom-call(f32[512,128]{1,0:T(8,128)S(1)} %get-tuple-element.63.refs_0_, ...), custom_call_target="tpu_custom_call" | custom-call | tf_op jit(solution)/shard_map/first_direction/pallas_call | solution.py:916
  16.7 1.6 %collective-permute-start.8 = (f32[64,128]{1,0:T(8,128)S(1)}, f32[64,128]{1,0:T(8,128)S(1)}, u32[]{:S(2)}, u32[]{:S(2)}) collective-permute-start(f32[64,128]{1,0:T(8,128)S(1)} %get-tuple-element.85), channel_id=1, source_target_pairs={{0,24},{8,16},{16,8},{24,0},{1,25},{9,17},{17,9},{25,1},{2,26},{10... | collective-permute-start | bytes 98312 | tf_op jit(solution)/shard_map/ppermute | solution.py:908
  18.3 0.4 %operator_second.2 = (f32[512,128]{1,0:T(8,128)S(1)}, f32[64,128]{1,0:T(8,128)S(1)}) custom-call(f32[512,128]{1,0:T(8,128)S(1)} %get-tuple-element.73.refs_0_.refs_1_.refs_2_, f32[3584,128]{1,0:T(8,128)S(1)} %halo_fields.1.refs_3_.refs_1_.refs_8_.refs_2_, f32[128,128]{1,0:T(8,128)S(1)} %get-tuple-element.75.refs_2_, ...), custom_call_target="tpu_custom_call" | custom-call | tf_op jit(solution)/shard_map/operator_second/pallas_call | solution.py:916
  18.7 1.4 %collective-permute-done.8.refs_7_.refs_1_ = f32[64,128]{1,0:T(8,128)S(1)} collective-permute-done((f32[64,128]{1,0:T(8,128)S(1)}, f32[64,128]{1,0:T(8,128)S(1)}, u32[]{:S(2)}, u32[]{:S(2)}) %collective-permute-start.8) | collective-permute-done | bytes 32800 | tf_op jit(solution)/shard_map/ppermute | solution.py:908
  20.2 1.1 %collective-permute-start.9 = (f32[32,128]{1,0:T(8,128)S(1)}, f32[32,128]{1,0:T(8,128)S(1)}, u32[]{:S(2)}, u32[]{:S(2)}) collective-permute-start(f32[32,128]{1,0:T(8,128)S(1)} %join.4), channel_id=1, source_target_pairs={{0,4},{4,0},{1,5},{5,1},{2,6},{6,2},{3,7},{7,3},{8,12},{12,8},{9,1... | collective-permute-start | bytes 49160 | tf_op jit(solution)/shard_map/ppermute | solution.py:908
  22.6 0.7 %preview.2 = (f32[512,128]{1,0:T(8,128)S(1)}, f32[512,128]{1,0:T(8,128)S(1)}, f32[512,128]{1,0:T(8,128)S(1)}, f32[512,128]{1,0:T(8,128)S(1)}, f32[512,128]{1,0:T(8,128)S(1)}, /*index=5*/f32[128,128]{1,0:T(8,128)S(1)}) custom-call(f32[512,128]{1,0:T(8,128)S(1)} %get-tuple-element.73.refs_0_.refs_1_.refs_2_, ...), custom_call_target="tpu_custom_call" | custom-call | tf_op jit(solution)/shard_map/preview/pallas_call | solution.py:916
  23.3 0.6 %collective-permute-done.9.refs_6_.refs_8_ = f32[32,128]{1,0:T(8,128)S(1)} collective-permute-done((f32[32,128]{1,0:T(8,128)S(1)}, f32[32,128]{1,0:T(8,128)S(1)}, u32[]{:S(2)}, u32[]{:S(2)}) %collective-permute-start.9) | collective-permute-done | bytes 16416 | tf_op jit(solution)/shard_map/ppermute | solution.py:908
  24.0 0.6 %direction.1 = (f32[128,128]{1,0:T(8,128)S(1)}, f32[128,128]{1,0:T(8,128)S(1)}, f32[64,128]{1,0:T(8,128)S(1)}, f32[64,128]{1,0:T(8,128)S(1)}) custom-call(f32[128,128]{1,0:T(8,128)S(1)} %get-tuple-element.88.refs_0_, f32[512,128]{1,0:T(8,128)S(1)} %get-tuple-element.74.refs_3_.refs_1_, f32[3584,128]{1,0:T(8,128)S(1)} %halo_fields.1.refs_3_.refs_1_.refs_8_.refs_2_, ...), custom_call_target="tpu_custom_call" | custom-call | tf_op jit(solution)/shard_map/direction/pallas_call | solution.py:916
  24.6 1.6 %collective-permute-start.11 = (f32[64,128]{1,0:T(8,128)S(1)}, f32[64,128]{1,0:T(8,128)S(1)}, u32[]{:S(2)}, u32[]{:S(2)}) collective-permute-start(f32[64,128]{1,0:T(8,128)S(1)} %get-tuple-element.98), channel_id=1, source_target_pairs={{0,24},{8,16},{16,8},{24,0},{1,25},{9,17},{17,9},{25,1},{2,26},{10... | collective-permute-start | bytes 98312 | tf_op jit(solution)/shard_map/ppermute | solution.py:908
  26.2 0.6 %operator_second.3 = (f32[512,128]{1,0:T(8,128)S(1)}, f32[64,128]{1,0:T(8,128)S(1)}, f32[512,128]{1,0:T(8,128)S(1)}) custom-call(f32[512,128]{1,0:T(8,128)S(1)} %get-tuple-element.87.refs_0_, f32[3584,128]{1,0:T(8,128)S(1)} %halo_fields.1.refs_3_.refs_1_.refs_8_.refs_2_, f32[128,128]{1,0:T(8,128)S(1)} %get-tuple-element.90.refs_2_, ...), custom_call_target="tpu_custom_call" | custom-call | tf_op jit(solution)/shard_map/operator_second/pallas_call | solution.py:916
  26.9 1.2 %collective-permute-done.11.refs_7_.refs_1_ = f32[64,128]{1,0:T(8,128)S(1)} collective-permute-done((f32[64,128]{1,0:T(8,128)S(1)}, f32[64,128]{1,0:T(8,128)S(1)}, u32[]{:S(2)}, u32[]{:S(2)}) %collective-permute-start.11) | collective-permute-done | bytes 32800 | tf_op jit(solution)/shard_map/ppermute | solution.py:908
  28.1 1.1 %collective-permute-start.12 = (f32[32,128]{1,0:T(8,128)S(1)}, f32[32,128]{1,0:T(8,128)S(1)}, u32[]{:S(2)}, u32[]{:S(2)}) collective-permute-start(f32[32,128]{1,0:T(8,128)S(1)} %join.5), channel_id=1, source_target_pairs={{0,4},{4,0},{1,5},{5,1},{2,6},{6,2},{3,7},{7,3},{8,12},{12,8},{9,1... | collective-permute-start | bytes 49160 | tf_op jit(solution)/shard_map/ppermute | solution.py:908
  29.3 0.3 preview.3.refs_0_
  29.6 2.4 %collective-permute-done.12.refs_4_ = f32[32,128]{1,0:T(8,128)S(1)} collective-permute-done((f32[32,128]{1,0:T(8,128)S(1)}, f32[32,128]{1,0:T(8,128)S(1)}, u32[]{:S(2)}, u32[]{:S(2)}) %collective-permute-start.12) | collective-permute-done | bytes 16416 | tf_op jit(solution)/shard_map/ppermute | solution.py:908
  31.9 1.0 %field.1 = f32[3,32,512]{2,1,0:T(8,128)} custom-call(f32[96,512]{1,0:T(8,128)S(1)} %preview.3.refs_0_, f32[512,128]{1,0:T(8,128)S(1)} %get-tuple-element.74.refs_3_.refs_1_, f32[40,128]{1,0:T(8,128)S(1)} %coefficients.1.refs_5_.refs_3_.refs_2_, bf16[96,128]{1,0:T(8,128)(2,1)S(1)} %get-tuple-element.99.refs_9_.refs_3_, ...), custom_call_target="tpu_custom_call" | custom-call | tf_op jit(solution)/shard_map/field/pallas_call | solution.py:916
  (33 shorter events, 0.5 us)
Async XLA Ops:
  0.0 0.7 %copy-start.8 = (f32[48,128]{1,0:T(8,128)S(1)}, f32[48,128]{1,0:T(8,128)}, u32[]{:S(2)}) copy-start(f32[48,128]{1,0:T(8,128)} %constant.14.clone.refs_3_) | copy-start | bytes 73732
  0.0 0.7 %copy-start.9 = (s32[6,128]{1,0:T(8,128)S(1)}, s32[6,128]{1,0:T(8,128)}, u32[]{:S(2)}) copy-start(s32[6,128]{1,0:T(8,128)} %constant.15.clone.refs_6_) | copy-start | bytes 9220
  0.0 0.7 %copy-start.10 = (s32[1,32]{1,0:T(1,128)S(1)}, s32[1,32]{1,0:T(1,128)}, u32[]{:S(2)}) copy-start(s32[1,32]{1,0:T(1,128)} %refs_5_.3) | copy-start | bytes 388
  0.0 0.9 %copy-start.6 = (f32[8,16,128]{2,1,0:T(8,128)S(1)}, f32[8,16,128]{2,1,0:T(8,128)}, u32[]{:S(2)}) copy-start(f32[8,16,128]{2,1,0:T(8,128)} %refs_1_.2) | copy-start | bytes 196612
  0.0 1.1 %copy-start.3 = (f32[6,8,16,128]{3,2,1,0:T(8,128)S(1)}, f32[6,8,16,128]{3,2,1,0:T(8,128)}, u32[]{:S(2)}) copy-start(f32[6,8,16,128]{3,2,1,0:T(8,128)} %refs_0_.1) | copy-start | bytes 1179652
  0.0 1.1 %copy-start.5 = (f32[3,512,32]{1,2,0:T(8,128)S(1)}, f32[3,512,32]{1,2,0:T(8,128)}, u32[]{:S(2)}) copy-start(f32[3,512,32]{1,2,0:T(8,128)} %param.13) | copy-start | bytes 589828
  0.0 5.0 %copy-start.7 = (s32[2,3,16,128]{3,2,1,0:T(8,128)S(1)}, s32[2,3,16,128]{3,2,1,0:T(8,128)}, u32[]{:S(2)}) copy-start(s32[2,3,16,128]{3,2,1,0:T(8,128)} %refs_2_.2) | copy-start | bytes 147460
  1.9 4.3 %collective-permute-start = (f32[64,128]{1,0:T(8,128)S(1)}, f32[64,128]{1,0:T(8,128)S(1)}, u32[]{:S(2)}, u32[]{:S(2)}) collective-permute-start(f32[64,128]{1,0:T(8,128)S(1)} %get-tuple-element.59), channel_id=1, source_target_pairs={{0,8},{8,0},{16,24},{24,16},{1,9},{9,1},{17,25},{25,17},{2,10},{10... | collective-permute-start | bytes 98312 | tf_op jit(solution)/shard_map/ppermute | solution.py:908
  2.4 4.3 %collective-permute-start.1 = (f32[64,128]{1,0:T(8,128)S(1)}, f32[64,128]{1,0:T(8,128)S(1)}, u32[]{:S(2)}, u32[]{:S(2)}) collective-permute-start(f32[64,128]{1,0:T(8,128)S(1)} %get-tuple-element.60), channel_id=1, source_target_pairs={{0,24},{8,16},{16,8},{24,0},{1,25},{9,17},{17,9},{25,1},{2,26},{10... | collective-permute-start | bytes 98312 | tf_op jit(solution)/shard_map/ppermute | solution.py:908
  6.8 3.8 %collective-permute-start.2 = (f32[40,128]{1,0:T(8,128)S(1)}, f32[40,128]{1,0:T(8,128)S(1)}, u32[]{:S(2)}, u32[]{:S(2)}) collective-permute-start(f32[40,128]{1,0:T(8,128)S(1)} %join.3), channel_id=1, source_target_pairs={{0,4},{4,0},{1,5},{5,1},{2,6},{6,2},{3,7},{7,3},{8,12},{12,8},{9,1... | collective-permute-start | bytes 61448 | tf_op jit(solution)/shard_map/ppermute | solution.py:908
  8.5 5.2 %collective-permute-start.3 = (f32[128,128]{1,0:T(8,128)S(1)}, f32[128,128]{1,0:T(8,128)S(1)}, u32[]{:S(2)}, u32[]{:S(2)}) collective-permute-start(f32[128,128]{1,0:T(8,128)S(1)} %get-tuple-element.67), channel_id=1, source_target_pairs={{0,1},{1,0},{2,3},{3,2},{8,9},{9,8},{10,11},{11,10},{16,17},{17,16... | collective-permute-start | bytes 196616 | tf_op jit(solution)/shard_map/ppermute | solution.py:908
  10.1 3.7 %collective-permute-start.4 = (f32[128,128]{1,0:T(8,128)S(1)}, f32[128,128]{1,0:T(8,128)S(1)}, u32[]{:S(2)}, u32[]{:S(2)}) collective-permute-start(f32[128,128]{1,0:T(8,128)S(1)} %get-tuple-element.68), channel_id=1, source_target_pairs={{0,8},{1,2},{2,1},{3,11},{8,0},{9,10},{10,9},{11,3},{16,24},{17,18... | collective-permute-start | bytes 196616 | tf_op jit(solution)/shard_map/ppermute | solution.py:908
  10.6 2.8 %copy-start.2 = (bf16[256,256]{1,0:T(8,128)(2,1)S(1)}, bf16[256,256]{1,0:T(8,128)(2,1)}, u32[]{:S(2)}) copy-start(bf16[256,256]{1,0:T(8,128)(2,1)} %constant.17.clone.refs_2_.refs_4_) | copy-start | bytes 393220
  10.6 3.1 %copy-start.4 = (bf16[128,1024]{1,0:T(8,128)(2,1)S(1)}, bf16[128,1024]{1,0:T(8,128)(2,1)}, u32[]{:S(2)}) copy-start(bf16[128,1024]{1,0:T(8,128)(2,1)} %constant.16.clone.refs_1_) | copy-start | bytes 786436
  10.8 4.6 %collective-permute-start.5 = (f32[80,128]{1,0:T(8,128)S(1)}, f32[80,128]{1,0:T(8,128)S(1)}, u32[]{:S(2)}, u32[]{:S(2)}) collective-permute-start(f32[80,128]{1,0:T(8,128)S(1)} %get-tuple-element.71), channel_id=1, source_target_pairs={{0,1},{1,0},{2,3},{3,2},{8,9},{9,8},{10,11},{11,10},{16,17},{17,16... | collective-permute-start | bytes 122888 | tf_op jit(solution)/shard_map/ppermute | solution.py:908
  13.5 2.0 %collective-permute-start.6 = (f32[80,128]{1,0:T(8,128)S(1)}, f32[80,128]{1,0:T(8,128)S(1)}, u32[]{:S(2)}, u32[]{:S(2)}) collective-permute-start(f32[80,128]{1,0:T(8,128)S(1)} %get-tuple-element.72), channel_id=1, source_target_pairs={{0,8},{1,2},{2,1},{3,11},{8,0},{9,10},{10,9},{11,3},{16,24},{17,18... | collective-permute-start | bytes 122888 | tf_op jit(solution)/shard_map/ppermute | solution.py:908
  13.8 1.7 %copy-start = (bf16[128,384]{1,0:T(8,128)(2,1)S(1)}, bf16[128,384]{1,0:T(8,128)(2,1)}, u32[]{:S(2)}) copy-start(bf16[128,384]{1,0:T(8,128)(2,1)} %constant.13.clone.refs_6_.refs_10_.refs_5_) | copy-start | bytes 294916
  13.8 1.7 %copy-start.1 = (bf16[128,384]{1,0:T(8,128)(2,1)S(1)}, bf16[128,384]{1,0:T(8,128)(2,1)}, u32[]{:S(2)}) copy-start(bf16[128,384]{1,0:T(8,128)(2,1)} %constant.12.clone.refs_5_.refs_9_.refs_4_.refs_8_) | copy-start | bytes 294916
  16.6 2.1 %collective-permute-start.7 = (f32[64,128]{1,0:T(8,128)S(1)}, f32[64,128]{1,0:T(8,128)S(1)}, u32[]{:S(2)}, u32[]{:S(2)}) collective-permute-start(f32[64,128]{1,0:T(8,128)S(1)} %get-tuple-element.84), channel_id=1, source_target_pairs={{0,8},{8,0},{16,24},{24,16},{1,9},{9,1},{17,25},{25,17},{2,10},{10... | collective-permute-start | bytes 98312 | tf_op jit(solution)/shard_map/ppermute | solution.py:908
  16.7 3.4 %collective-permute-start.8 = (f32[64,128]{1,0:T(8,128)S(1)}, f32[64,128]{1,0:T(8,128)S(1)}, u32[]{:S(2)}, u32[]{:S(2)}) collective-permute-start(f32[64,128]{1,0:T(8,128)S(1)} %get-tuple-element.85), channel_id=1, source_target_pairs={{0,24},{8,16},{16,8},{24,0},{1,25},{9,17},{17,9},{25,1},{2,26},{10... | collective-permute-start | bytes 98312 | tf_op jit(solution)/shard_map/ppermute | solution.py:908
  20.2 3.8 %collective-permute-start.9 = (f32[32,128]{1,0:T(8,128)S(1)}, f32[32,128]{1,0:T(8,128)S(1)}, u32[]{:S(2)}, u32[]{:S(2)}) collective-permute-start(f32[32,128]{1,0:T(8,128)S(1)} %join.4), channel_id=1, source_target_pairs={{0,4},{4,0},{1,5},{5,1},{2,6},{6,2},{3,7},{7,3},{8,12},{12,8},{9,1... | collective-permute-start | bytes 49160 | tf_op jit(solution)/shard_map/ppermute | solution.py:908
  24.5 2.3 %collective-permute-start.10 = (f32[64,128]{1,0:T(8,128)S(1)}, f32[64,128]{1,0:T(8,128)S(1)}, u32[]{:S(2)}, u32[]{:S(2)}) collective-permute-start(f32[64,128]{1,0:T(8,128)S(1)} %get-tuple-element.97), channel_id=1, source_target_pairs={{0,8},{8,0},{16,24},{24,16},{1,9},{9,1},{17,25},{25,17},{2,10},{10... | collective-permute-start | bytes 98312 | tf_op jit(solution)/shard_map/ppermute | solution.py:908
  24.6 3.4 %collective-permute-start.11 = (f32[64,128]{1,0:T(8,128)S(1)}, f32[64,128]{1,0:T(8,128)S(1)}, u32[]{:S(2)}, u32[]{:S(2)}) collective-permute-start(f32[64,128]{1,0:T(8,128)S(1)} %get-tuple-element.98), channel_id=1, source_target_pairs={{0,24},{8,16},{16,8},{24,0},{1,25},{9,17},{17,9},{25,1},{2,26},{10... | collective-permute-start | bytes 98312 | tf_op jit(solution)/shard_map/ppermute | solution.py:908
  28.1 3.8 %collective-permute-start.12 = (f32[32,128]{1,0:T(8,128)S(1)}, f32[32,128]{1,0:T(8,128)S(1)}, u32[]{:S(2)}, u32[]{:S(2)}) collective-permute-start(f32[32,128]{1,0:T(8,128)S(1)} %join.5), channel_id=1, source_target_pairs={{0,4},{4,0},{1,5},{5,1},{2,6},{6,2},{3,7},{7,3},{8,12},{12,8},{9,1... | collective-permute-start | bytes 49160 | tf_op jit(solution)/shard_map/ppermute | solution.py:908

commit v9 on v8

--- a/solution.py
+++ b/solution.py
@@ -162,7 +162,7 @@
         self.ids = np.ascontiguousarray(ids[:, :1, :]).reshape(2 * c, 128)
         part = HALO * p
         self.part = part
-        assert FIELDS * part <= lanes and 2 * ey * part <= lanes // 2
+        assert FIELDS * part + part == lanes == p * ey * p and 2 * ey * part <= lanes // 2
         halo = np.zeros((lanes, p, self.w3), np.float32)
         for side, first in ((0, -HALO), (1, ez)):
             for g in range(HALO):
@@ -385,17 +385,36 @@
 
 
     def pack_fields(self, fields, out):
+        part = self.part
         for target, (high, _, _) in zip(out, roles("gz", self.sizes["gz"])):
-            rows, width = target.shape
+            _, rows, width = fields.shape
             lane = lax.broadcasted_iota(jnp.int32, (rows, width), 1)
             total = jnp.zeros((rows, width), F32)
             for q in range(FIELDS):
-                start = q * self.part
-                upper = pltpu.roll(fields[q], start + self.part, 1)
+                start = q * part
+                upper = pltpu.roll(fields[q], start + part, 1)
                 lower = pltpu.roll(fields[q], start, 1) if start else fields[q]
-                here = (lane >= start) & (lane < start + self.part)
+                here = (lane >= start) & (lane < start + part)
                 total = jnp.where(here, jnp.where(high, upper, lower), total)
-            target[...] = total
+            kept = FIELDS * part
+            free = lane[:part] >= kept
+            target[...] = jnp.concatenate(
+                [
+                    jnp.where(free, pltpu.roll(total[kept:], kept - q * part, 1), total[q * part : (q + 1) * part])
+                    for q in range(FIELDS)
+                ],
+                axis=0,
+            )
+
+    def unpack_fields(self, message):
+        part = self.part
+        kept, width = message.shape
+        lane = lax.broadcasted_iota(jnp.int32, (part, width), 1)
+        last = jnp.zeros((part, width), F32)
+        for q in range(FIELDS):
+            x = pltpu.roll(message[q * part : (q + 1) * part], width - (kept - q * part), 1)
+            last = jnp.where((lane >= q * part) & (lane < (q + 1) * part), x, last)
+        return jnp.concatenate([message, last], axis=0)
 
     def by_nodes(self, upper, lower, table, width, store):
         for k in range(0, self.p, 2):
@@ -571,6 +590,7 @@
         z_in, g, terms = refs[2 : 2 + n_z], refs[2 + n_z], refs[3 + n_z]
         p, block, ey, part = self.p, self.block, self.ey, self.part
         sides = both_sides([z[...] for z in z_in], roles("gz", self.sizes["gz"]))
+        sides = [self.unpack_fields(side) for side in sides]
         width = sides[0].shape[-1]
         sides = [side.reshape(p, ey, p, width) for side in sides]
         lane = lax.broadcasted_iota(jnp.int32, (block, width), 1)
@@ -966,7 +986,7 @@
         functools.partial(plan.convert, n_y, n_z),
         [shape(FIELDS * rows, w3), shape(2 * block, w3)]
         + [shape(2 * p, w3)] * n_y
-        + [shape(p * plan.ey * p, lanes)] * n_z
+        + [shape(FIELDS * plan.part, lanes)] * n_z
         + [shape(block + 2 * p, w4)] * n_z,
         (fields, spread3, dirichlet, s4),
         scratch=[vmem(lhs, plan.ey * lanes, dtype=BF16)] * 2,

time: 33 us -> 33 us (level)
  no operation moved by 1% of the time
where the time goes in v9:
time: 33 us; the launch traced here: 32.9 us
  starting transfers between devices  14.7 us (45%)
  Pallas kernels  8.74 us (26%)
  waiting for transfers between devices  7.19 us (22%)
  between operations  1.5 us (5%)
  local copies, waits for them, and re-layouts  0.74 us (2%)
    ppermute x13, starting transfers between devices, send(): return [lax.ppermute(x, axis, pair) for x, pair in zip(arrays, pairs)]  14.7 us
    pallas_call x17, Pallas kernels, call(): pl.pallas_call(kernel, out_shape=list(outputs), in_specs=specs, out_specs...  8.74 us
    ppermute x13, waiting for transfers between devices, send(): return [lax.ppermute(x, axis, pair) for x, pair in zip(arrays, pairs)]  7.19 us
    unnamed x22, local copies, waits for them, and re-layouts  0.74 us
  transfers between devices with their start and end apart: 13, of which 7 were waited for; matrix products, arithmetic and copies ran while one was open for 0% of the time, Pallas kernels for 14%

profile of v9, /device:TPU:0, one launch (start us, length us, event | category | flops | bytes accessed | tf_op | source)
XLA Modules:
  0.0 32.9 jit_solution(7940592690308662453)
XLA Ops:
  0.0 0.4 %spread_tables.1 = (bf16[256,1024]{1,0:T(8,128)(2,1)S(1)}, bf16[256,1024]{1,0:T(8,128)(2,1)S(1)}, bf16[128,384]{1,0:T(8,128)(2,1)S(1)}) custom-call(), custom_call_target="tpu_custom_call" | custom-call | flops 3000000000 | tf_op jit(solution)/shard_map/spread_tables/pallas_call | solution.py:936
  0.4 0.3 copy-done.8
  0.7 0.1 copy-done.6
  0.9 0.2 copy-done.3
  1.1 0.8 %prepare.1 = (f32[512,128]{1,0:T(8,128)S(1)}, bf16[96,128]{1,0:T(8,128)(2,1)S(1)}, f32[7,128,128]{2,1,0:T(8,128)S(1)}, f32[64,128]{1,0:T(8,128)S(1)}, f32[64,128]{1,0:T(8,128)S(1)}, /*index=5*/f32[64,128]{1,0:T(8,128)S(1)}) custom-call(f32[6,8,16,128]{3,2,1,0:T(8,128)S(1)} %copy-done.3, f32[8,16,128]{2,1,0:T(8,128)S(1)} %copy-done.6, ...), custom_call_target="tpu_custom_call" | custom-call | tf_op jit(solution)/shard_map/prepare/pallas_call | solution.py:936
  1.9 0.5 %collective-permute-start = (f32[64,128]{1,0:T(8,128)S(1)}, f32[64,128]{1,0:T(8,128)S(1)}, u32[]{:S(2)}, u32[]{:S(2)}) collective-permute-start(f32[64,128]{1,0:T(8,128)S(1)} %get-tuple-element.59), channel_id=1, source_target_pairs={{0,8},{8,0},{16,24},{24,16},{1,9},{9,1},{17,25},{25,17},{2,10},{10... | collective-permute-start | bytes 98312 | tf_op jit(solution)/shard_map/ppermute | solution.py:928
  2.4 2.6 %collective-permute-start.1 = (f32[64,128]{1,0:T(8,128)S(1)}, f32[64,128]{1,0:T(8,128)S(1)}, u32[]{:S(2)}, u32[]{:S(2)}) collective-permute-start(f32[64,128]{1,0:T(8,128)S(1)} %get-tuple-element.60), channel_id=1, source_target_pairs={{0,24},{8,16},{16,8},{24,0},{1,25},{9,17},{17,9},{25,1},{2,26},{10... | collective-permute-start | bytes 98312 | tf_op jit(solution)/shard_map/ppermute | solution.py:928
  5.0 1.3 %convert.1 = (f32[3584,128]{1,0:T(8,128)S(1)}, f32[128,128]{1,0:T(8,128)S(1)}, f32[16,128]{1,0:T(8,128)S(1)}, f32[112,128]{1,0:T(8,128)S(1)}, f32[112,128]{1,0:T...) custom-call(f32[7,128,128]{2,1,0:T(8,128)S(1)} %get-tuple-element.56.refs_0_, ...), custom_call_target="tpu_custom_call" | custom-call | tf_op jit(solution)/shard_map/convert/pallas_call | solution.py:936
  6.3 0.4 %collective-permute-done.1.refs_1_.refs_4_ = f32[64,128]{1,0:T(8,128)S(1)} collective-permute-done((f32[64,128]{1,0:T(8,128)S(1)}, f32[64,128]{1,0:T(8,128)S(1)}, u32[]{:S(2)}, u32[]{:S(2)}) %collective-permute-start.1) | collective-permute-done | bytes 32800 | tf_op jit(solution)/shard_map/ppermute | solution.py:928
  6.8 1.7 %collective-permute-start.2 = (f32[40,128]{1,0:T(8,128)S(1)}, f32[40,128]{1,0:T(8,128)S(1)}, u32[]{:S(2)}, u32[]{:S(2)}) collective-permute-start(f32[40,128]{1,0:T(8,128)S(1)} %join.3), channel_id=1, source_target_pairs={{0,4},{4,0},{1,5},{5,1},{2,6},{6,2},{3,7},{7,3},{8,12},{12,8},{9,1... | collective-permute-start | bytes 61448 | tf_op jit(solution)/shard_map/ppermute | solution.py:928
  8.5 1.6 %collective-permute-start.3 = (f32[112,128]{1,0:T(8,128)S(1)}, f32[112,128]{1,0:T(8,128)S(1)}, u32[]{:S(2)}, u32[]{:S(2)}) collective-permute-start(f32[112,128]{1,0:T(8,128)S(1)} %get-tuple-element.67), channel_id=1, source_target_pairs={{0,1},{1,0},{2,3},{3,2},{8,9},{9,8},{10,11},{11,10},{16,17},{17,16... | collective-permute-start | bytes 172040 | tf_op jit(solution)/shard_map/ppermute | solution.py:928
  10.1 0.6 %collective-permute-done.2.refs_5_.refs_2_ = f32[40,128]{1,0:T(8,128)S(1)} collective-permute-done((f32[40,128]{1,0:T(8,128)S(1)}, f32[40,128]{1,0:T(8,128)S(1)}, u32[]{:S(2)}, u32[]{:S(2)}) %collective-permute-start.2) | collective-permute-done | bytes 20512 | tf_op jit(solution)/shard_map/ppermute | solution.py:928
  10.6 0.2 pack_second.1
  10.8 2.7 %collective-permute-start.5 = (f32[80,128]{1,0:T(8,128)S(1)}, f32[80,128]{1,0:T(8,128)S(1)}, u32[]{:S(2)}, u32[]{:S(2)}) collective-permute-start(f32[80,128]{1,0:T(8,128)S(1)} %get-tuple-element.71), channel_id=1, source_target_pairs={{0,1},{1,0},{2,3},{3,2},{8,9},{9,8},{10,11},{11,10},{16,17},{17,16... | collective-permute-start | bytes 122888 | tf_op jit(solution)/shard_map/ppermute | solution.py:928
  13.5 0.3 own.1
  13.8 0.9 %halo_fields.1.refs_3_.refs_1_.refs_8_.refs_2_ = f32[3584,128]{1,0:T(8,128)S(1)} custom-call(f32[3584,128]{1,0:T(8,128)S(1)} %get-tuple-element.66.refs_0_, bf16[128,1024]{1,0:T(8,128)(2,1)S(1)} %copy-done.4, f32[112,128]{1,0:T(8,128)S(1)} %collective-permute-done.3.refs_2_, f32[112,128]{1,0:T(8,128)S(1)} %collective-permute-done.4.refs_3_), custom_call_target="tpu_custom_call" | custom-call | tf_op jit(solution)/shard_map/halo_fields/pallas_call | solution.py:936
  14.7 0.7 %collective-permute-done.5.refs_7_ = f32[80,128]{1,0:T(8,128)S(1)} collective-permute-done((f32[80,128]{1,0:T(8,128)S(1)}, f32[80,128]{1,0:T(8,128)S(1)}, u32[]{:S(2)}, u32[]{:S(2)}) %collective-permute-start.5) | collective-permute-done | bytes 40992 | tf_op jit(solution)/shard_map/ppermute | solution.py:928
  15.5 1.2 %first_direction.1 = (f32[512,128]{1,0:T(8,128)S(1)}, f32[512,128]{1,0:T(8,128)S(1)}, f32[128,128]{1,0:T(8,128)S(1)}, f32[512,128]{1,0:T(8,128)S(1)}, f32[512,12...) custom-call(f32[512,128]{1,0:T(8,128)S(1)} %get-tuple-element.63.refs_0_, ...), custom_call_target="tpu_custom_call" | custom-call | tf_op jit(solution)/shard_map/first_direction/pallas_call | solution.py:936
  16.7 1.6 %collective-permute-start.8 = (f32[64,128]{1,0:T(8,128)S(1)}, f32[64,128]{1,0:T(8,128)S(1)}, u32[]{:S(2)}, u32[]{:S(2)}) collective-permute-start(f32[64,128]{1,0:T(8,128)S(1)} %get-tuple-element.85), channel_id=1, source_target_pairs={{0,24},{8,16},{16,8},{24,0},{1,25},{9,17},{17,9},{25,1},{2,26},{10... | collective-permute-start | bytes 98312 | tf_op jit(solution)/shard_map/ppermute | solution.py:928
  18.3 0.4 %operator_second.2 = (f32[512,128]{1,0:T(8,128)S(1)}, f32[64,128]{1,0:T(8,128)S(1)}) custom-call(f32[512,128]{1,0:T(8,128)S(1)} %get-tuple-element.73.refs_0_.refs_1_.refs_2_, f32[3584,128]{1,0:T(8,128)S(1)} %halo_fields.1.refs_3_.refs_1_.refs_8_.refs_2_, f32[128,128]{1,0:T(8,128)S(1)} %get-tuple-element.75.refs_2_, ...), custom_call_target="tpu_custom_call" | custom-call | tf_op jit(solution)/shard_map/operator_second/pallas_call | solution.py:936
  18.7 1.4 %collective-permute-done.8.refs_7_.refs_1_ = f32[64,128]{1,0:T(8,128)S(1)} collective-permute-done((f32[64,128]{1,0:T(8,128)S(1)}, f32[64,128]{1,0:T(8,128)S(1)}, u32[]{:S(2)}, u32[]{:S(2)}) %collective-permute-start.8) | collective-permute-done | bytes 32800 | tf_op jit(solution)/shard_map/ppermute | solution.py:928
  20.2 1.1 %collective-permute-start.9 = (f32[32,128]{1,0:T(8,128)S(1)}, f32[32,128]{1,0:T(8,128)S(1)}, u32[]{:S(2)}, u32[]{:S(2)}) collective-permute-start(f32[32,128]{1,0:T(8,128)S(1)} %join.4), channel_id=1, source_target_pairs={{0,4},{4,0},{1,5},{5,1},{2,6},{6,2},{3,7},{7,3},{8,12},{12,8},{9,1... | collective-permute-start | bytes 49160 | tf_op jit(solution)/shard_map/ppermute | solution.py:928
  22.6 0.7 %preview.2 = (f32[512,128]{1,0:T(8,128)S(1)}, f32[512,128]{1,0:T(8,128)S(1)}, f32[512,128]{1,0:T(8,128)S(1)}, f32[512,128]{1,0:T(8,128)S(1)}, f32[512,128]{1,0:T(8,128)S(1)}, /*index=5*/f32[128,128]{1,0:T(8,128)S(1)}) custom-call(f32[512,128]{1,0:T(8,128)S(1)} %get-tuple-element.73.refs_0_.refs_1_.refs_2_, ...), custom_call_target="tpu_custom_call" | custom-call | tf_op jit(solution)/shard_map/preview/pallas_call | solution.py:936
  23.3 0.6 %collective-permute-done.9.refs_6_.refs_8_ = f32[32,128]{1,0:T(8,128)S(1)} collective-permute-done((f32[32,128]{1,0:T(8,128)S(1)}, f32[32,128]{1,0:T(8,128)S(1)}, u32[]{:S(2)}, u32[]{:S(2)}) %collective-permute-start.9) | collective-permute-done | bytes 16416 | tf_op jit(solution)/shard_map/ppermute | solution.py:928
  24.0 0.6 %direction.1 = (f32[128,128]{1,0:T(8,128)S(1)}, f32[128,128]{1,0:T(8,128)S(1)}, f32[64,128]{1,0:T(8,128)S(1)}, f32[64,128]{1,0:T(8,128)S(1)}) custom-call(f32[128,128]{1,0:T(8,128)S(1)} %get-tuple-element.88.refs_0_, f32[512,128]{1,0:T(8,128)S(1)} %get-tuple-element.74.refs_3_.refs_1_, f32[3584,128]{1,0:T(8,128)S(1)} %halo_fields.1.refs_3_.refs_1_.refs_8_.refs_2_, ...), custom_call_target="tpu_custom_call" | custom-call | tf_op jit(solution)/shard_map/direction/pallas_call | solution.py:936
  24.6 1.6 %collective-permute-start.11 = (f32[64,128]{1,0:T(8,128)S(1)}, f32[64,128]{1,0:T(8,128)S(1)}, u32[]{:S(2)}, u32[]{:S(2)}) collective-permute-start(f32[64,128]{1,0:T(8,128)S(1)} %get-tuple-element.98), channel_id=1, source_target_pairs={{0,24},{8,16},{16,8},{24,0},{1,25},{9,17},{17,9},{25,1},{2,26},{10... | collective-permute-start | bytes 98312 | tf_op jit(solution)/shard_map/ppermute | solution.py:928
  26.2 0.6 %operator_second.3 = (f32[512,128]{1,0:T(8,128)S(1)}, f32[64,128]{1,0:T(8,128)S(1)}, f32[512,128]{1,0:T(8,128)S(1)}) custom-call(f32[512,128]{1,0:T(8,128)S(1)} %get-tuple-element.87.refs_0_, f32[3584,128]{1,0:T(8,128)S(1)} %halo_fields.1.refs_3_.refs_1_.refs_8_.refs_2_, f32[128,128]{1,0:T(8,128)S(1)} %get-tuple-element.90.refs_2_, ...), custom_call_target="tpu_custom_call" | custom-call | tf_op jit(solution)/shard_map/operator_second/pallas_call | solution.py:936
  26.9 1.2 %collective-permute-done.11.refs_7_.refs_1_ = f32[64,128]{1,0:T(8,128)S(1)} collective-permute-done((f32[64,128]{1,0:T(8,128)S(1)}, f32[64,128]{1,0:T(8,128)S(1)}, u32[]{:S(2)}, u32[]{:S(2)}) %collective-permute-start.11) | collective-permute-done | bytes 32800 | tf_op jit(solution)/shard_map/ppermute | solution.py:928
  28.1 1.1 %collective-permute-start.12 = (f32[32,128]{1,0:T(8,128)S(1)}, f32[32,128]{1,0:T(8,128)S(1)}, u32[]{:S(2)}, u32[]{:S(2)}) collective-permute-start(f32[32,128]{1,0:T(8,128)S(1)} %join.5), channel_id=1, source_target_pairs={{0,4},{4,0},{1,5},{5,1},{2,6},{6,2},{3,7},{7,3},{8,12},{12,8},{9,1... | collective-permute-start | bytes 49160 | tf_op jit(solution)/shard_map/ppermute | solution.py:928
  29.3 0.3 preview.3.refs_0_
  29.6 2.4 %collective-permute-done.12.refs_4_ = f32[32,128]{1,0:T(8,128)S(1)} collective-permute-done((f32[32,128]{1,0:T(8,128)S(1)}, f32[32,128]{1,0:T(8,128)S(1)}, u32[]{:S(2)}, u32[]{:S(2)}) %collective-permute-start.12) | collective-permute-done | bytes 16416 | tf_op jit(solution)/shard_map/ppermute | solution.py:928
  31.9 1.0 %field.1 = f32[3,32,512]{2,1,0:T(8,128)} custom-call(f32[96,512]{1,0:T(8,128)S(1)} %preview.3.refs_0_, f32[512,128]{1,0:T(8,128)S(1)} %get-tuple-element.74.refs_3_.refs_1_, f32[40,128]{1,0:T(8,128)S(1)} %coefficients.1.refs_5_.refs_3_.refs_2_, bf16[96,128]{1,0:T(8,128)(2,1)S(1)} %get-tuple-element.99.refs_9_.refs_3_, ...), custom_call_target="tpu_custom_call" | custom-call | tf_op jit(solution)/shard_map/field/pallas_call | solution.py:936
  (33 shorter events, 0.5 us)
Async XLA Ops:
  0.0 0.7 %copy-start.8 = (f32[48,128]{1,0:T(8,128)S(1)}, f32[48,128]{1,0:T(8,128)}, u32[]{:S(2)}) copy-start(f32[48,128]{1,0:T(8,128)} %constant.14.clone.refs_3_) | copy-start | bytes 73732
  0.0 0.7 %copy-start.9 = (s32[6,128]{1,0:T(8,128)S(1)}, s32[6,128]{1,0:T(8,128)}, u32[]{:S(2)}) copy-start(s32[6,128]{1,0:T(8,128)} %constant.15.clone.refs_6_) | copy-start | bytes 9220
  0.0 0.7 %copy-start.10 = (s32[1,32]{1,0:T(1,128)S(1)}, s32[1,32]{1,0:T(1,128)}, u32[]{:S(2)}) copy-start(s32[1,32]{1,0:T(1,128)} %refs_5_.3) | copy-start | bytes 388
  0.0 0.9 %copy-start.6 = (f32[8,16,128]{2,1,0:T(8,128)S(1)}, f32[8,16,128]{2,1,0:T(8,128)}, u32[]{:S(2)}) copy-start(f32[8,16,128]{2,1,0:T(8,128)} %refs_1_.2) | copy-start | bytes 196612
  0.0 1.1 %copy-start.3 = (f32[6,8,16,128]{3,2,1,0:T(8,128)S(1)}, f32[6,8,16,128]{3,2,1,0:T(8,128)}, u32[]{:S(2)}) copy-start(f32[6,8,16,128]{3,2,1,0:T(8,128)} %refs_0_.1) | copy-start | bytes 1179652
  0.0 1.1 %copy-start.5 = (f32[3,512,32]{1,2,0:T(8,128)S(1)}, f32[3,512,32]{1,2,0:T(8,128)}, u32[]{:S(2)}) copy-start(f32[3,512,32]{1,2,0:T(8,128)} %param.13) | copy-start | bytes 589828
  0.0 5.0 %copy-start.7 = (s32[2,3,16,128]{3,2,1,0:T(8,128)S(1)}, s32[2,3,16,128]{3,2,1,0:T(8,128)}, u32[]{:S(2)}) copy-start(s32[2,3,16,128]{3,2,1,0:T(8,128)} %refs_2_.2) | copy-start | bytes 147460
  1.9 4.4 %collective-permute-start = (f32[64,128]{1,0:T(8,128)S(1)}, f32[64,128]{1,0:T(8,128)S(1)}, u32[]{:S(2)}, u32[]{:S(2)}) collective-permute-start(f32[64,128]{1,0:T(8,128)S(1)} %get-tuple-element.59), channel_id=1, source_target_pairs={{0,8},{8,0},{16,24},{24,16},{1,9},{9,1},{17,25},{25,17},{2,10},{10... | collective-permute-start | bytes 98312 | tf_op jit(solution)/shard_map/ppermute | solution.py:928
  2.4 4.3 %collective-permute-start.1 = (f32[64,128]{1,0:T(8,128)S(1)}, f32[64,128]{1,0:T(8,128)S(1)}, u32[]{:S(2)}, u32[]{:S(2)}) collective-permute-start(f32[64,128]{1,0:T(8,128)S(1)} %get-tuple-element.60), channel_id=1, source_target_pairs={{0,24},{8,16},{16,8},{24,0},{1,25},{9,17},{17,9},{25,1},{2,26},{10... | collective-permute-start | bytes 98312 | tf_op jit(solution)/shard_map/ppermute | solution.py:928
  6.8 3.8 %collective-permute-start.2 = (f32[40,128]{1,0:T(8,128)S(1)}, f32[40,128]{1,0:T(8,128)S(1)}, u32[]{:S(2)}, u32[]{:S(2)}) collective-permute-start(f32[40,128]{1,0:T(8,128)S(1)} %join.3), channel_id=1, source_target_pairs={{0,4},{4,0},{1,5},{5,1},{2,6},{6,2},{3,7},{7,3},{8,12},{12,8},{9,1... | collective-permute-start | bytes 61448 | tf_op jit(solution)/shard_map/ppermute | solution.py:928
  8.5 5.2 %collective-permute-start.3 = (f32[112,128]{1,0:T(8,128)S(1)}, f32[112,128]{1,0:T(8,128)S(1)}, u32[]{:S(2)}, u32[]{:S(2)}) collective-permute-start(f32[112,128]{1,0:T(8,128)S(1)} %get-tuple-element.67), channel_id=1, source_target_pairs={{0,1},{1,0},{2,3},{3,2},{8,9},{9,8},{10,11},{11,10},{16,17},{17,16... | collective-permute-start | bytes 172040 | tf_op jit(solution)/shard_map/ppermute | solution.py:928
  10.1 3.7 %collective-permute-start.4 = (f32[112,128]{1,0:T(8,128)S(1)}, f32[112,128]{1,0:T(8,128)S(1)}, u32[]{:S(2)}, u32[]{:S(2)}) collective-permute-start(f32[112,128]{1,0:T(8,128)S(1)} %get-tuple-element.68), channel_id=1, source_target_pairs={{0,8},{1,2},{2,1},{3,11},{8,0},{9,10},{10,9},{11,3},{16,24},{17,18... | collective-permute-start | bytes 172040 | tf_op jit(solution)/shard_map/ppermute | solution.py:928
  10.6 2.8 %copy-start.2 = (bf16[256,256]{1,0:T(8,128)(2,1)S(1)}, bf16[256,256]{1,0:T(8,128)(2,1)}, u32[]{:S(2)}) copy-start(bf16[256,256]{1,0:T(8,128)(2,1)} %constant.17.clone.refs_2_.refs_4_) | copy-start | bytes 393220
  10.6 3.1 %copy-start.4 = (bf16[128,1024]{1,0:T(8,128)(2,1)S(1)}, bf16[128,1024]{1,0:T(8,128)(2,1)}, u32[]{:S(2)}) copy-start(bf16[128,1024]{1,0:T(8,128)(2,1)} %constant.16.clone.refs_1_) | copy-start | bytes 786436
  10.8 4.6 %collective-permute-start.5 = (f32[80,128]{1,0:T(8,128)S(1)}, f32[80,128]{1,0:T(8,128)S(1)}, u32[]{:S(2)}, u32[]{:S(2)}) collective-permute-start(f32[80,128]{1,0:T(8,128)S(1)} %get-tuple-element.71), channel_id=1, source_target_pairs={{0,1},{1,0},{2,3},{3,2},{8,9},{9,8},{10,11},{11,10},{16,17},{17,16... | collective-permute-start | bytes 122888 | tf_op jit(solution)/shard_map/ppermute | solution.py:928
  13.5 2.0 %collective-permute-start.6 = (f32[80,128]{1,0:T(8,128)S(1)}, f32[80,128]{1,0:T(8,128)S(1)}, u32[]{:S(2)}, u32[]{:S(2)}) collective-permute-start(f32[80,128]{1,0:T(8,128)S(1)} %get-tuple-element.72), channel_id=1, source_target_pairs={{0,8},{1,2},{2,1},{3,11},{8,0},{9,10},{10,9},{11,3},{16,24},{17,18... | collective-permute-start | bytes 122888 | tf_op jit(solution)/shard_map/ppermute | solution.py:928
  13.8 1.7 %copy-start = (bf16[128,384]{1,0:T(8,128)(2,1)S(1)}, bf16[128,384]{1,0:T(8,128)(2,1)}, u32[]{:S(2)}) copy-start(bf16[128,384]{1,0:T(8,128)(2,1)} %constant.13.clone.refs_6_.refs_10_.refs_5_) | copy-start | bytes 294916
  13.8 1.7 %copy-start.1 = (bf16[128,384]{1,0:T(8,128)(2,1)S(1)}, bf16[128,384]{1,0:T(8,128)(2,1)}, u32[]{:S(2)}) copy-start(bf16[128,384]{1,0:T(8,128)(2,1)} %constant.12.clone.refs_5_.refs_9_.refs_4_.refs_8_) | copy-start | bytes 294916
  16.6 2.1 %collective-permute-start.7 = (f32[64,128]{1,0:T(8,128)S(1)}, f32[64,128]{1,0:T(8,128)S(1)}, u32[]{:S(2)}, u32[]{:S(2)}) collective-permute-start(f32[64,128]{1,0:T(8,128)S(1)} %get-tuple-element.84), channel_id=1, source_target_pairs={{0,8},{8,0},{16,24},{24,16},{1,9},{9,1},{17,25},{25,17},{2,10},{10... | collective-permute-start | bytes 98312 | tf_op jit(solution)/shard_map/ppermute | solution.py:928
  16.7 3.4 %collective-permute-start.8 = (f32[64,128]{1,0:T(8,128)S(1)}, f32[64,128]{1,0:T(8,128)S(1)}, u32[]{:S(2)}, u32[]{:S(2)}) collective-permute-start(f32[64,128]{1,0:T(8,128)S(1)} %get-tuple-element.85), channel_id=1, source_target_pairs={{0,24},{8,16},{16,8},{24,0},{1,25},{9,17},{17,9},{25,1},{2,26},{10... | collective-permute-start | bytes 98312 | tf_op jit(solution)/shard_map/ppermute | solution.py:928
  20.2 3.8 %collective-permute-start.9 = (f32[32,128]{1,0:T(8,128)S(1)}, f32[32,128]{1,0:T(8,128)S(1)}, u32[]{:S(2)}, u32[]{:S(2)}) collective-permute-start(f32[32,128]{1,0:T(8,128)S(1)} %join.4), channel_id=1, source_target_pairs={{0,4},{4,0},{1,5},{5,1},{2,6},{6,2},{3,7},{7,3},{8,12},{12,8},{9,1... | collective-permute-start | bytes 49160 | tf_op jit(solution)/shard_map/ppermute | solution.py:928
  24.5 2.3 %collective-permute-start.10 = (f32[64,128]{1,0:T(8,128)S(1)}, f32[64,128]{1,0:T(8,128)S(1)}, u32[]{:S(2)}, u32[]{:S(2)}) collective-permute-start(f32[64,128]{1,0:T(8,128)S(1)} %get-tuple-element.97), channel_id=1, source_target_pairs={{0,8},{8,0},{16,24},{24,16},{1,9},{9,1},{17,25},{25,17},{2,10},{10... | collective-permute-start | bytes 98312 | tf_op jit(solution)/shard_map/ppermute | solution.py:928
  24.6 3.4 %collective-permute-start.11 = (f32[64,128]{1,0:T(8,128)S(1)}, f32[64,128]{1,0:T(8,128)S(1)}, u32[]{:S(2)}, u32[]{:S(2)}) collective-permute-start(f32[64,128]{1,0:T(8,128)S(1)} %get-tuple-element.98), channel_id=1, source_target_pairs={{0,24},{8,16},{16,8},{24,0},{1,25},{9,17},{17,9},{25,1},{2,26},{10... | collective-permute-start | bytes 98312 | tf_op jit(solution)/shard_map/ppermute | solution.py:928
  28.1 3.8 %collective-permute-start.12 = (f32[32,128]{1,0:T(8,128)S(1)}, f32[32,128]{1,0:T(8,128)S(1)}, u32[]{:S(2)}, u32[]{:S(2)}) collective-permute-start(f32[32,128]{1,0:T(8,128)S(1)} %join.5), channel_id=1, source_target_pairs={{0,4},{4,0},{1,5},{5,1},{2,6},{6,2},{3,7},{7,3},{8,12},{12,8},{9,1... | collective-permute-start | bytes 49160 | tf_op jit(solution)/shard_map/ppermute | solution.py:928

commit v10 on v9

--- a/solution.py
+++ b/solution.py
@@ -452,8 +452,10 @@
         upper, lower = split(jnp.where(same, whole, 0.0))
         out[...] = jnp.concatenate([upper, upper, lower], axis=1)
 
-    def spread_tables(self, out3, out4, square):
+    def spread_tables(self, out3, out4, square, ahead, back):
         self.block_table(self.squared.T, square)
+        self.block_table(self.forward, ahead)
+        self.block_table(self.forward.T, back)
         p, ey, ez = self.p, self.ey, self.ez
         for out, width, step, offset, first in (
             (out3, self.w3, self.step3, HALO, 0),
@@ -949,13 +951,12 @@
         return pltpu.VMEM(size, dtype)
 
     lanes = plan.ez * p
-    ahead, back = jnp.asarray(plan.third[0]), jnp.asarray(plan.third[1])
     field3, field4 = shape(rows, w3), shape(rows, w4)
     elements = element_slot.shape[-1]
-    spread3, spread4, square = call(
+    spread3, spread4, square, ahead, back = call(
         plan.spread_tables,
         [shape(plan.ey * lanes, p * w, dtype=BF16) for w in (w3, w4)]
-        + [shape(*plan.third[0].shape, dtype=BF16)],
+        + [shape(*plan.third[0].shape, dtype=BF16)] * 3,
         (),
         flops=FLOPS,
         name="spread_tables",

time: 33 us -> 33 us (level)
    unnamed x22 -> x18, local copies, waits for them, and re-layouts: 0.74 us -> 0.67 us
where the time goes in v10:
time: 33 us; the launch traced here: 32.9 us
  starting transfers between devices  14.7 us (45%)
  Pallas kernels  8.81 us (27%)
  waiting for transfers between devices  7.21 us (22%)
  between operations  1.48 us (4%)
  local copies, waits for them, and re-layouts  0.67 us (2%)
    ppermute x13, starting transfers between devices, send(): return [lax.ppermute(x, axis, pair) for x, pair in zip(arrays, pairs)]  14.7 us
    pallas_call x17, Pallas kernels, call(): pl.pallas_call(kernel, out_shape=list(outputs), in_specs=specs, out_specs...  8.81 us
    ppermute x13, waiting for transfers between devices, send(): return [lax.ppermute(x, axis, pair) for x, pair in zip(arrays, pairs)]  7.21 us
    unnamed x18, local copies, waits for them, and re-layouts  0.67 us
  transfers between devices with their start and end apart: 13, of which 7 were waited for; matrix products, arithmetic and copies ran while one was open for 0% of the time, Pallas kernels for 14%

profile of v10, /device:TPU:0, one launch (start us, length us, event | category | flops | bytes accessed | tf_op | source)
XLA Modules:
  0.0 32.9 jit_solution(11604211055775907600)
XLA Ops:
  0.0 0.4 %spread_tables.1 = (bf16[256,1024]{1,0:T(8,128)(2,1)S(1)}, bf16[256,1024]{1,0:T(8,128)(2,1)S(1)}, bf16[128,384]{1,0:T(8,128)(2,1)S(1)}, bf16[128,384]{1,0:T(8,128)(2,1)S(1)}, bf16[128,384]{1,0:T(8,128)(2,1)S(1)}) custom-call(), custom_call_target="tpu_custom_call" | custom-call | flops 3000000000 | tf_op jit(solution)/shard_map/spread_tables/pallas_call | solution.py:938
  0.5 0.3 copy-done.6
  0.7 0.1 copy-done.4
  0.9 0.2 copy-done.1
  1.1 0.8 %prepare.1 = (f32[512,128]{1,0:T(8,128)S(1)}, bf16[96,128]{1,0:T(8,128)(2,1)S(1)}, f32[7,128,128]{2,1,0:T(8,128)S(1)}, f32[64,128]{1,0:T(8,128)S(1)}, f32[64,128]{1,0:T(8,128)S(1)}, /*index=5*/f32[64,128]{1,0:T(8,128)S(1)}) custom-call(f32[6,8,16,128]{3,2,1,0:T(8,128)S(1)} %copy-done.1, f32[8,16,128]{2,1,0:T(8,128)S(1)} %copy-done.4, ...), custom_call_target="tpu_custom_call" | custom-call | tf_op jit(solution)/shard_map/prepare/pallas_call | solution.py:938
  1.9 0.5 %collective-permute-start = (f32[64,128]{1,0:T(8,128)S(1)}, f32[64,128]{1,0:T(8,128)S(1)}, u32[]{:S(2)}, u32[]{:S(2)}) collective-permute-start(f32[64,128]{1,0:T(8,128)S(1)} %get-tuple-element.61), channel_id=1, source_target_pairs={{0,8},{8,0},{16,24},{24,16},{1,9},{9,1},{17,25},{25,17},{2,10},{10... | collective-permute-start | bytes 98312 | tf_op jit(solution)/shard_map/ppermute | solution.py:930
  2.4 2.6 %collective-permute-start.1 = (f32[64,128]{1,0:T(8,128)S(1)}, f32[64,128]{1,0:T(8,128)S(1)}, u32[]{:S(2)}, u32[]{:S(2)}) collective-permute-start(f32[64,128]{1,0:T(8,128)S(1)} %get-tuple-element.62), channel_id=1, source_target_pairs={{0,24},{8,16},{16,8},{24,0},{1,25},{9,17},{17,9},{25,1},{2,26},{10... | collective-permute-start | bytes 98312 | tf_op jit(solution)/shard_map/ppermute | solution.py:930
  5.0 1.3 %convert.1 = (f32[3584,128]{1,0:T(8,128)S(1)}, f32[128,128]{1,0:T(8,128)S(1)}, f32[16,128]{1,0:T(8,128)S(1)}, f32[112,128]{1,0:T(8,128)S(1)}, f32[112,128]{1,0:T...) custom-call(f32[7,128,128]{2,1,0:T(8,128)S(1)} %get-tuple-element.58.refs_0_, ...), custom_call_target="tpu_custom_call" | custom-call | tf_op jit(solution)/shard_map/convert/pallas_call | solution.py:938
  6.3 0.4 %collective-permute-done.1.refs_1_.refs_4_ = f32[64,128]{1,0:T(8,128)S(1)} collective-permute-done((f32[64,128]{1,0:T(8,128)S(1)}, f32[64,128]{1,0:T(8,128)S(1)}, u32[]{:S(2)}, u32[]{:S(2)}) %collective-permute-start.1) | collective-permute-done | bytes 32800 | tf_op jit(solution)/shard_map/ppermute | solution.py:930
  6.8 1.7 %collective-permute-start.2 = (f32[40,128]{1,0:T(8,128)S(1)}, f32[40,128]{1,0:T(8,128)S(1)}, u32[]{:S(2)}, u32[]{:S(2)}) collective-permute-start(f32[40,128]{1,0:T(8,128)S(1)} %join.3), channel_id=1, source_target_pairs={{0,4},{4,0},{1,5},{5,1},{2,6},{6,2},{3,7},{7,3},{8,12},{12,8},{9,1... | collective-permute-start | bytes 61448 | tf_op jit(solution)/shard_map/ppermute | solution.py:930
  8.5 1.6 %collective-permute-start.3 = (f32[112,128]{1,0:T(8,128)S(1)}, f32[112,128]{1,0:T(8,128)S(1)}, u32[]{:S(2)}, u32[]{:S(2)}) collective-permute-start(f32[112,128]{1,0:T(8,128)S(1)} %get-tuple-element.69), channel_id=1, source_target_pairs={{0,1},{1,0},{2,3},{3,2},{8,9},{9,8},{10,11},{11,10},{16,17},{17,16... | collective-permute-start | bytes 172040 | tf_op jit(solution)/shard_map/ppermute | solution.py:930
  10.1 0.6 %collective-permute-done.2.refs_5_.refs_2_ = f32[40,128]{1,0:T(8,128)S(1)} collective-permute-done((f32[40,128]{1,0:T(8,128)S(1)}, f32[40,128]{1,0:T(8,128)S(1)}, u32[]{:S(2)}, u32[]{:S(2)}) %collective-permute-start.2) | collective-permute-done | bytes 20512 | tf_op jit(solution)/shard_map/ppermute | solution.py:930
  10.6 0.2 pack_second.1
  10.8 2.7 %collective-permute-start.5 = (f32[80,128]{1,0:T(8,128)S(1)}, f32[80,128]{1,0:T(8,128)S(1)}, u32[]{:S(2)}, u32[]{:S(2)}) collective-permute-start(f32[80,128]{1,0:T(8,128)S(1)} %get-tuple-element.75), channel_id=1, source_target_pairs={{0,1},{1,0},{2,3},{3,2},{8,9},{9,8},{10,11},{11,10},{16,17},{17,16... | collective-permute-start | bytes 122888 | tf_op jit(solution)/shard_map/ppermute | solution.py:930
  13.5 0.3 own.1
  13.8 0.9 %halo_fields.1.refs_3_.refs_1_.refs_8_.refs_2_ = f32[3584,128]{1,0:T(8,128)S(1)} custom-call(f32[3584,128]{1,0:T(8,128)S(1)} %get-tuple-element.68.refs_0_, bf16[128,1024]{1,0:T(8,128)(2,1)S(1)} %copy-done.2, f32[112,128]{1,0:T(8,128)S(1)} %collective-permute-done.3.refs_2_, f32[112,128]{1,0:T(8,128)S(1)} %collective-permute-done.4.refs_3_), custom_call_target="tpu_custom_call" | custom-call | tf_op jit(solution)/shard_map/halo_fields/pallas_call | solution.py:938
  14.7 0.7 %collective-permute-done.5.refs_7_ = f32[80,128]{1,0:T(8,128)S(1)} collective-permute-done((f32[80,128]{1,0:T(8,128)S(1)}, f32[80,128]{1,0:T(8,128)S(1)}, u32[]{:S(2)}, u32[]{:S(2)}) %collective-permute-start.5) | collective-permute-done | bytes 40992 | tf_op jit(solution)/shard_map/ppermute | solution.py:930
  15.4 1.2 %first_direction.1 = (f32[512,128]{1,0:T(8,128)S(1)}, f32[512,128]{1,0:T(8,128)S(1)}, f32[128,128]{1,0:T(8,128)S(1)}, f32[512,128]{1,0:T(8,128)S(1)}, f32[512,12...) custom-call(f32[512,128]{1,0:T(8,128)S(1)} %get-tuple-element.65.refs_0_, ...), custom_call_target="tpu_custom_call" | custom-call | tf_op jit(solution)/shard_map/first_direction/pallas_call | solution.py:938
  16.7 1.6 %collective-permute-start.8 = (f32[64,128]{1,0:T(8,128)S(1)}, f32[64,128]{1,0:T(8,128)S(1)}, u32[]{:S(2)}, u32[]{:S(2)}) collective-permute-start(f32[64,128]{1,0:T(8,128)S(1)} %get-tuple-element.89), channel_id=1, source_target_pairs={{0,24},{8,16},{16,8},{24,0},{1,25},{9,17},{17,9},{25,1},{2,26},{10... | collective-permute-start | bytes 98312 | tf_op jit(solution)/shard_map/ppermute | solution.py:930
  18.3 0.4 %operator_second.2 = (f32[512,128]{1,0:T(8,128)S(1)}, f32[64,128]{1,0:T(8,128)S(1)}) custom-call(f32[512,128]{1,0:T(8,128)S(1)} %get-tuple-element.77.refs_0_.refs_1_.refs_2_, f32[3584,128]{1,0:T(8,128)S(1)} %halo_fields.1.refs_3_.refs_1_.refs_8_.refs_2_, f32[128,128]{1,0:T(8,128)S(1)} %get-tuple-element.79.refs_2_, ...), custom_call_target="tpu_custom_call" | custom-call | tf_op jit(solution)/shard_map/operator_second/pallas_call | solution.py:938
  18.7 1.4 %collective-permute-done.8.refs_7_.refs_1_ = f32[64,128]{1,0:T(8,128)S(1)} collective-permute-done((f32[64,128]{1,0:T(8,128)S(1)}, f32[64,128]{1,0:T(8,128)S(1)}, u32[]{:S(2)}, u32[]{:S(2)}) %collective-permute-start.8) | collective-permute-done | bytes 32800 | tf_op jit(solution)/shard_map/ppermute | solution.py:930
  20.2 1.1 %collective-permute-start.9 = (f32[32,128]{1,0:T(8,128)S(1)}, f32[32,128]{1,0:T(8,128)S(1)}, u32[]{:S(2)}, u32[]{:S(2)}) collective-permute-start(f32[32,128]{1,0:T(8,128)S(1)} %join.4), channel_id=1, source_target_pairs={{0,4},{4,0},{1,5},{5,1},{2,6},{6,2},{3,7},{7,3},{8,12},{12,8},{9,1... | collective-permute-start | bytes 49160 | tf_op jit(solution)/shard_map/ppermute | solution.py:930
  22.6 0.7 %preview.2 = (f32[512,128]{1,0:T(8,128)S(1)}, f32[512,128]{1,0:T(8,128)S(1)}, f32[512,128]{1,0:T(8,128)S(1)}, f32[512,128]{1,0:T(8,128)S(1)}, f32[512,128]{1,0:T(8,128)S(1)}, /*index=5*/f32[128,128]{1,0:T(8,128)S(1)}) custom-call(f32[512,128]{1,0:T(8,128)S(1)} %get-tuple-element.77.refs_0_.refs_1_.refs_2_, ...), custom_call_target="tpu_custom_call" | custom-call | tf_op jit(solution)/shard_map/preview/pallas_call | solution.py:938
  23.3 0.6 %collective-permute-done.9.refs_6_.refs_8_ = f32[32,128]{1,0:T(8,128)S(1)} collective-permute-done((f32[32,128]{1,0:T(8,128)S(1)}, f32[32,128]{1,0:T(8,128)S(1)}, u32[]{:S(2)}, u32[]{:S(2)}) %collective-permute-start.9) | collective-permute-done | bytes 16416 | tf_op jit(solution)/shard_map/ppermute | solution.py:930
  24.0 0.6 %direction.1 = (f32[128,128]{1,0:T(8,128)S(1)}, f32[128,128]{1,0:T(8,128)S(1)}, f32[64,128]{1,0:T(8,128)S(1)}, f32[64,128]{1,0:T(8,128)S(1)}) custom-call(f32[128,128]{1,0:T(8,128)S(1)} %get-tuple-element.92.refs_0_, f32[512,128]{1,0:T(8,128)S(1)} %get-tuple-element.78.refs_3_.refs_1_, f32[3584,128]{1,0:T(8,128)S(1)} %halo_fields.1.refs_3_.refs_1_.refs_8_.refs_2_, ...), custom_call_target="tpu_custom_call" | custom-call | tf_op jit(solution)/shard_map/direction/pallas_call | solution.py:938
  24.6 1.6 %collective-permute-start.11 = (f32[64,128]{1,0:T(8,128)S(1)}, f32[64,128]{1,0:T(8,128)S(1)}, u32[]{:S(2)}, u32[]{:S(2)}) collective-permute-start(f32[64,128]{1,0:T(8,128)S(1)} %get-tuple-element.102), channel_id=1, source_target_pairs={{0,24},{8,16},{16,8},{24,0},{1,25},{9,17},{17,9},{25,1},{2,26},{10... | collective-permute-start | bytes 98312 | tf_op jit(solution)/shard_map/ppermute | solution.py:930
  26.2 0.6 %operator_second.3 = (f32[512,128]{1,0:T(8,128)S(1)}, f32[64,128]{1,0:T(8,128)S(1)}, f32[512,128]{1,0:T(8,128)S(1)}) custom-call(f32[512,128]{1,0:T(8,128)S(1)} %get-tuple-element.91.refs_0_, f32[3584,128]{1,0:T(8,128)S(1)} %halo_fields.1.refs_3_.refs_1_.refs_8_.refs_2_, f32[128,128]{1,0:T(8,128)S(1)} %get-tuple-element.94.refs_2_, ...), custom_call_target="tpu_custom_call" | custom-call | tf_op jit(solution)/shard_map/operator_second/pallas_call | solution.py:938
  26.8 1.2 %collective-permute-done.11.refs_7_.refs_1_ = f32[64,128]{1,0:T(8,128)S(1)} collective-permute-done((f32[64,128]{1,0:T(8,128)S(1)}, f32[64,128]{1,0:T(8,128)S(1)}, u32[]{:S(2)}, u32[]{:S(2)}) %collective-permute-start.11) | collective-permute-done | bytes 32800 | tf_op jit(solution)/shard_map/ppermute | solution.py:930
  28.1 1.1 %collective-permute-start.12 = (f32[32,128]{1,0:T(8,128)S(1)}, f32[32,128]{1,0:T(8,128)S(1)}, u32[]{:S(2)}, u32[]{:S(2)}) collective-permute-start(f32[32,128]{1,0:T(8,128)S(1)} %join.5), channel_id=1, source_target_pairs={{0,4},{4,0},{1,5},{5,1},{2,6},{6,2},{3,7},{7,3},{8,12},{12,8},{9,1... | collective-permute-start | bytes 49160 | tf_op jit(solution)/shard_map/ppermute | solution.py:930
  29.3 0.3 preview.3.refs_0_
  29.6 2.4 %collective-permute-done.12.refs_4_ = f32[32,128]{1,0:T(8,128)S(1)} collective-permute-done((f32[32,128]{1,0:T(8,128)S(1)}, f32[32,128]{1,0:T(8,128)S(1)}, u32[]{:S(2)}, u32[]{:S(2)}) %collective-permute-start.12) | collective-permute-done | bytes 16416 | tf_op jit(solution)/shard_map/ppermute | solution.py:930
  31.9 1.0 %field.1 = f32[3,32,512]{2,1,0:T(8,128)} custom-call(f32[96,512]{1,0:T(8,128)S(1)} %preview.3.refs_0_, f32[512,128]{1,0:T(8,128)S(1)} %get-tuple-element.78.refs_3_.refs_1_, f32[40,128]{1,0:T(8,128)S(1)} %coefficients.1.refs_5_.refs_3_.refs_2_, bf16[96,128]{1,0:T(8,128)(2,1)S(1)} %get-tuple-element.103.refs_9_.refs_3_, ...), custom_call_target="tpu_custom_call" | custom-call | tf_op jit(solution)/shard_map/field/pallas_call | solution.py:938
  (29 shorter events, 0.5 us)
Async XLA Ops:
  0.0 0.7 %copy-start.6 = (f32[48,128]{1,0:T(8,128)S(1)}, f32[48,128]{1,0:T(8,128)}, u32[]{:S(2)}) copy-start(f32[48,128]{1,0:T(8,128)} %constant.8.clone.refs_3_) | copy-start | bytes 73732
  0.0 0.7 %copy-start.7 = (s32[6,128]{1,0:T(8,128)S(1)}, s32[6,128]{1,0:T(8,128)}, u32[]{:S(2)}) copy-start(s32[6,128]{1,0:T(8,128)} %constant.9.clone.refs_6_) | copy-start | bytes 9220
  0.0 0.7 %copy-start.8 = (s32[1,32]{1,0:T(1,128)S(1)}, s32[1,32]{1,0:T(1,128)}, u32[]{:S(2)}) copy-start(s32[1,32]{1,0:T(1,128)} %refs_5_.1) | copy-start | bytes 388
  0.0 0.9 %copy-start.4 = (f32[8,16,128]{2,1,0:T(8,128)S(1)}, f32[8,16,128]{2,1,0:T(8,128)}, u32[]{:S(2)}) copy-start(f32[8,16,128]{2,1,0:T(8,128)} %refs_1_.2) | copy-start | bytes 196612
  0.0 1.1 %copy-start.1 = (f32[6,8,16,128]{3,2,1,0:T(8,128)S(1)}, f32[6,8,16,128]{3,2,1,0:T(8,128)}, u32[]{:S(2)}) copy-start(f32[6,8,16,128]{3,2,1,0:T(8,128)} %refs_0_.1) | copy-start | bytes 1179652
  0.0 1.1 %copy-start.3 = (f32[3,512,32]{1,2,0:T(8,128)S(1)}, f32[3,512,32]{1,2,0:T(8,128)}, u32[]{:S(2)}) copy-start(f32[3,512,32]{1,2,0:T(8,128)} %param.11) | copy-start | bytes 589828
  0.0 5.0 %copy-start.5 = (s32[2,3,16,128]{3,2,1,0:T(8,128)S(1)}, s32[2,3,16,128]{3,2,1,0:T(8,128)}, u32[]{:S(2)}) copy-start(s32[2,3,16,128]{3,2,1,0:T(8,128)} %refs_2_.2) | copy-start | bytes 147460
  1.9 4.4 %collective-permute-start = (f32[64,128]{1,0:T(8,128)S(1)}, f32[64,128]{1,0:T(8,128)S(1)}, u32[]{:S(2)}, u32[]{:S(2)}) collective-permute-start(f32[64,128]{1,0:T(8,128)S(1)} %get-tuple-element.61), channel_id=1, source_target_pairs={{0,8},{8,0},{16,24},{24,16},{1,9},{9,1},{17,25},{25,17},{2,10},{10... | collective-permute-start | bytes 98312 | tf_op jit(solution)/shard_map/ppermute | solution.py:930
  2.4 4.3 %collective-permute-start.1 = (f32[64,128]{1,0:T(8,128)S(1)}, f32[64,128]{1,0:T(8,128)S(1)}, u32[]{:S(2)}, u32[]{:S(2)}) collective-permute-start(f32[64,128]{1,0:T(8,128)S(1)} %get-tuple-element.62), channel_id=1, source_target_pairs={{0,24},{8,16},{16,8},{24,0},{1,25},{9,17},{17,9},{25,1},{2,26},{10... | collective-permute-start | bytes 98312 | tf_op jit(solution)/shard_map/ppermute | solution.py:930
  6.8 3.8 %collective-permute-start.2 = (f32[40,128]{1,0:T(8,128)S(1)}, f32[40,128]{1,0:T(8,128)S(1)}, u32[]{:S(2)}, u32[]{:S(2)}) collective-permute-start(f32[40,128]{1,0:T(8,128)S(1)} %join.3), channel_id=1, source_target_pairs={{0,4},{4,0},{1,5},{5,1},{2,6},{6,2},{3,7},{7,3},{8,12},{12,8},{9,1... | collective-permute-start | bytes 61448 | tf_op jit(solution)/shard_map/ppermute | solution.py:930
  8.5 5.2 %collective-permute-start.3 = (f32[112,128]{1,0:T(8,128)S(1)}, f32[112,128]{1,0:T(8,128)S(1)}, u32[]{:S(2)}, u32[]{:S(2)}) collective-permute-start(f32[112,128]{1,0:T(8,128)S(1)} %get-tuple-element.69), channel_id=1, source_target_pairs={{0,1},{1,0},{2,3},{3,2},{8,9},{9,8},{10,11},{11,10},{16,17},{17,16... | collective-permute-start | bytes 172040 | tf_op jit(solution)/shard_map/ppermute | solution.py:930
  10.1 3.7 %collective-permute-start.4 = (f32[112,128]{1,0:T(8,128)S(1)}, f32[112,128]{1,0:T(8,128)S(1)}, u32[]{:S(2)}, u32[]{:S(2)}) collective-permute-start(f32[112,128]{1,0:T(8,128)S(1)} %get-tuple-element.70), channel_id=1, source_target_pairs={{0,8},{1,2},{2,1},{3,11},{8,0},{9,10},{10,9},{11,3},{16,24},{17,18... | collective-permute-start | bytes 172040 | tf_op jit(solution)/shard_map/ppermute | solution.py:930
  10.6 2.8 %copy-start = (bf16[256,256]{1,0:T(8,128)(2,1)S(1)}, bf16[256,256]{1,0:T(8,128)(2,1)}, u32[]{:S(2)}) copy-start(bf16[256,256]{1,0:T(8,128)(2,1)} %constant.11.clone.refs_2_.refs_4_) | copy-start | bytes 393220
  10.6 3.1 %copy-start.2 = (bf16[128,1024]{1,0:T(8,128)(2,1)S(1)}, bf16[128,1024]{1,0:T(8,128)(2,1)}, u32[]{:S(2)}) copy-start(bf16[128,1024]{1,0:T(8,128)(2,1)} %constant.10.clone.refs_1_) | copy-start | bytes 786436
  10.8 4.6 %collective-permute-start.5 = (f32[80,128]{1,0:T(8,128)S(1)}, f32[80,128]{1,0:T(8,128)S(1)}, u32[]{:S(2)}, u32[]{:S(2)}) collective-permute-start(f32[80,128]{1,0:T(8,128)S(1)} %get-tuple-element.75), channel_id=1, source_target_pairs={{0,1},{1,0},{2,3},{3,2},{8,9},{9,8},{10,11},{11,10},{16,17},{17,16... | collective-permute-start | bytes 122888 | tf_op jit(solution)/shard_map/ppermute | solution.py:930
  13.5 2.0 %collective-permute-start.6 = (f32[80,128]{1,0:T(8,128)S(1)}, f32[80,128]{1,0:T(8,128)S(1)}, u32[]{:S(2)}, u32[]{:S(2)}) collective-permute-start(f32[80,128]{1,0:T(8,128)S(1)} %get-tuple-element.76), channel_id=1, source_target_pairs={{0,8},{1,2},{2,1},{3,11},{8,0},{9,10},{10,9},{11,3},{16,24},{17,18... | collective-permute-start | bytes 122888 | tf_op jit(solution)/shard_map/ppermute | solution.py:930
  16.6 2.1 %collective-permute-start.7 = (f32[64,128]{1,0:T(8,128)S(1)}, f32[64,128]{1,0:T(8,128)S(1)}, u32[]{:S(2)}, u32[]{:S(2)}) collective-permute-start(f32[64,128]{1,0:T(8,128)S(1)} %get-tuple-element.88), channel_id=1, source_target_pairs={{0,8},{8,0},{16,24},{24,16},{1,9},{9,1},{17,25},{25,17},{2,10},{10... | collective-permute-start | bytes 98312 | tf_op jit(solution)/shard_map/ppermute | solution.py:930
  16.7 3.4 %collective-permute-start.8 = (f32[64,128]{1,0:T(8,128)S(1)}, f32[64,128]{1,0:T(8,128)S(1)}, u32[]{:S(2)}, u32[]{:S(2)}) collective-permute-start(f32[64,128]{1,0:T(8,128)S(1)} %get-tuple-element.89), channel_id=1, source_target_pairs={{0,24},{8,16},{16,8},{24,0},{1,25},{9,17},{17,9},{25,1},{2,26},{10... | collective-permute-start | bytes 98312 | tf_op jit(solution)/shard_map/ppermute | solution.py:930
  20.2 3.8 %collective-permute-start.9 = (f32[32,128]{1,0:T(8,128)S(1)}, f32[32,128]{1,0:T(8,128)S(1)}, u32[]{:S(2)}, u32[]{:S(2)}) collective-permute-start(f32[32,128]{1,0:T(8,128)S(1)} %join.4), channel_id=1, source_target_pairs={{0,4},{4,0},{1,5},{5,1},{2,6},{6,2},{3,7},{7,3},{8,12},{12,8},{9,1... | collective-permute-start | bytes 49160 | tf_op jit(solution)/shard_map/ppermute | solution.py:930
  24.5 2.3 %collective-permute-start.10 = (f32[64,128]{1,0:T(8,128)S(1)}, f32[64,128]{1,0:T(8,128)S(1)}, u32[]{:S(2)}, u32[]{:S(2)}) collective-permute-start(f32[64,128]{1,0:T(8,128)S(1)} %get-tuple-element.101), channel_id=1, source_target_pairs={{0,8},{8,0},{16,24},{24,16},{1,9},{9,1},{17,25},{25,17},{2,10},{10... | collective-permute-start | bytes 98312 | tf_op jit(solution)/shard_map/ppermute | solution.py:930
  24.6 3.4 %collective-permute-start.11 = (f32[64,128]{1,0:T(8,128)S(1)}, f32[64,128]{1,0:T(8,128)S(1)}, u32[]{:S(2)}, u32[]{:S(2)}) collective-permute-start(f32[64,128]{1,0:T(8,128)S(1)} %get-tuple-element.102), channel_id=1, source_target_pairs={{0,24},{8,16},{16,8},{24,0},{1,25},{9,17},{17,9},{25,1},{2,26},{10... | collective-permute-start | bytes 98312 | tf_op jit(solution)/shard_map/ppermute | solution.py:930
  28.1 3.8 %collective-permute-start.12 = (f32[32,128]{1,0:T(8,128)S(1)}, f32[32,128]{1,0:T(8,128)S(1)}, u32[]{:S(2)}, u32[]{:S(2)}) collective-permute-start(f32[32,128]{1,0:T(8,128)S(1)} %join.5), channel_id=1, source_target_pairs={{0,4},{4,0},{1,5},{5,1},{2,6},{6,2},{3,7},{7,3},{8,12},{12,8},{9,1... | collective-permute-start | bytes 49160 | tf_op jit(solution)/shard_map/ppermute | solution.py:930
